TPU v7x, 32 devices: a whole 2x2x4 slice. The times are simulated.
32 devices in a mesh: rep: 4 (over y, x), fsdp: 8 (over z, core).
Axes of the slice: x: 2, y: 2, z: 4, core: 2. Of those that a mesh axis runs over, the one named last changes fastest.
Arguments:
- hidden_in: bfloat16 [16384, 1536], P(('rep', 'fsdp')), may hold values from -6 to 6
- lengths: int32 [32, 2], P(('rep', 'fsdp')), may hold values from 128 to 384, as said below
- norm_gain: bfloat16 [1536], P('fsdp'), may hold values from 0.5 to 1.5
- in_weight: bfloat16 [1536, 6448], P('fsdp'), may hold values from -0.15625 to 0.15625
- conv_weight: bfloat16 [4, 3328], P(None, 'fsdp'), may hold values from -3 to 3
- conv_bias: bfloat16 [3328], P('fsdp'), may hold values from -0.5 to 0.5
- dt_bias: bfloat16 [48], P('fsdp'), may hold values from -6 to -3
- a_log: bfloat16 [48], P('fsdp'), may hold values from 0 to 1.3984375
- skip_gain: bfloat16 [48], P('fsdp'), may hold values from 0.5 to 1.5
- gate_gain: bfloat16 [3072], P('fsdp'), may hold values from 0.5 to 1.5
- out_weight: bfloat16 [3072, 1536], P(None, 'fsdp'), may hold values from -0.109375 to 0.109375
- cotangent: bfloat16 [16384, 1536], P(('rep', 'fsdp')), may hold values from -12 to 12
Outputs:
- mixed: bfloat16 [16384, 1536], P(('rep', 'fsdp'))
- grad_hidden: float32 [16384, 1536], P(('rep', 'fsdp'))
- grad_norm_gain: float32 [1536], P('fsdp')
- grad_in_weight: float32 [1536, 6448], P('fsdp')
- grad_conv_weight: float32 [4, 3328], P(None, 'fsdp')
- grad_conv_bias: float32 [3328], P('fsdp')
- grad_dt_bias: float32 [48], P('fsdp')
- grad_a_log: float32 [48], P('fsdp')
- grad_skip_gain: float32 [48], P('fsdp')
- grad_gate_gain: float32 [3072], P('fsdp')
- grad_out_weight: float32 [3072, 1536], P(None, 'fsdp')
Inputs may be any that keep to these rules, and one draw needn't show every extreme that they name: Each row gives the lengths of the two sequences of one device's block of 512 token slots, which fill its first rows in order; the remaining rows are padding. Every block fills at least half of its rows, and in some block a first sequence of 128 tokens and a second one fill all rows.
All inputs are finite; a program needn't handle non-finite values.
Results may differ from a plain program's by a relative error of at most 0.0068.
Values may be sent and summed in bfloat16 or wider, within the bound.
No kernel may reach another device: no remote copies, remote signals or barrier semaphores. Data moves between devices by JAX's collectives and lax.ppermute only.
A program may use at most 256 MiB of HBM per device.

v0:
```python
import jax
import jax.numpy as jnp
from jax import lax
from jax.sharding import PartitionSpec as P

SPAN = 256


highest = lax.Precision.HIGHEST
epsilon = 1e-05


def segments_of(lengths_row, token_count):
    seq_ends = jnp.cumsum(lengths_row)
    positions = jnp.arange(token_count, dtype=jnp.int32)
    return (positions[:, None] >= seq_ends[None, :]).sum(axis=1)


def normalize(inputs, scales):
    factor = lax.rsqrt(jnp.mean(inputs * inputs, axis=-1, keepdims=True) + epsilon)
    return inputs * factor * scales


def convolve(channels_in, segment, kernel, offsets):
    taps = kernel.shape[0]
    result = offsets + kernel[taps - 1] * channels_in
    for delay in range(1, taps):
        shifted = jnp.concatenate(
            [jnp.zeros((delay, channels_in.shape[1]), channels_in.dtype), channels_in[:-delay]], 0
        )
        earlier = jnp.concatenate([jnp.full((delay,), -1, jnp.int32), segment[:-delay]])
        result = result + kernel[taps - 1 - delay] * jnp.where(
            (earlier == segment)[:, None], shifted, 0.0
        )
    return jax.nn.silu(result)


def blockwise(values, keys, queries, rates, steps, segment, skip):
    token_count = values.shape[0]
    pieces_count = token_count // SPAN
    heads, head_size = (values.shape[1], values.shape[2])
    state_size = keys.shape[1]
    positions = jnp.arange(SPAN, dtype=jnp.int32)
    causal = positions[:, None] >= positions[None, :]

    def split_rows(array):
        return array.reshape((pieces_count, SPAN) + array.shape[1:])

    def advance(carry, pieces):
        state, last_segment = carry
        vals, key_rows, query_rows, rate_rows, step_rows, seg_rows = pieces
        running = jnp.cumsum(rate_rows, axis=0)
        allowed = causal & (seg_rows[:, None] == seg_rows[None, :])
        scores = jnp.dot(query_rows, key_rows.T, precision=highest)
        decay = jnp.exp(
            jnp.where(allowed[:, :, None], running[:, None, :] - running[None, :, :], -jnp.inf)
        )
        weights = scores[:, :, None] * decay * step_rows[None, :, :]
        inside = jnp.einsum("tsh,shp->thp", weights, vals, precision=highest)
        reach = jnp.where((seg_rows == last_segment)[:, None], jnp.exp(running), 0.0)
        carried = (
            jnp.einsum("tn,hpn->thp", query_rows, state, precision=highest) * reach[:, :, None]
        )
        final_segment = seg_rows[-1]
        whole_decay = running[-1]
        source_weight = jnp.where(
            (seg_rows == final_segment)[:, None],
            jnp.exp(whole_decay[None, :] - running) * step_rows,
            0.0,
        )
        fresh = jnp.einsum(
            "shp,sn->hpn", source_weight[:, :, None] * vals, key_rows, precision=highest
        )
        kept_decay = jnp.where(final_segment == last_segment, jnp.exp(whole_decay), 0.0)
        state = state * kept_decay[:, None, None] + fresh
        return ((state, final_segment), inside + carried + skip[None, :, None] * vals)

    start_state = (jnp.zeros((heads, head_size, state_size), jnp.float32), jnp.int32(-1))
    pieces = (
        split_rows(values),
        split_rows(keys),
        split_rows(queries),
        split_rows(rates),
        split_rows(steps),
        split_rows(segment),
    )
    unused, outputs = lax.scan(jax.checkpoint(advance), start_state, pieces)
    return outputs.reshape(values.shape)


def mixer(projected, segment, kernel, offsets, step_bias, decay_log, skip, gate_scale):
    inner = gate_scale.shape[0]
    channels = offsets.shape[0]
    heads = step_bias.shape[0]
    state_size = (channels - inner) // 2
    gate = projected[:, :inner]
    conv_in = projected[:, inner : inner + channels]
    step_raw = projected[:, inner + channels :]
    conv_out = convolve(conv_in, segment, kernel, offsets)
    steps = jax.nn.softplus(step_raw + step_bias)
    rates = -jnp.exp(decay_log) * steps
    values = conv_out[:, :inner].reshape(-1, heads, inner // heads)
    keys = conv_out[:, inner : inner + state_size]
    queries = conv_out[:, inner + state_size :]
    ssd_out = blockwise(values, keys, queries, rates, steps, segment, skip).reshape(-1, inner)
    return normalize(ssd_out * jax.nn.silu(gate), gate_scale)


def per_device(
    hidden_in,
    lengths,
    norm_gain,
    in_weight,
    conv_weight,
    conv_bias,
    dt_bias,
    a_log,
    skip_gain,
    gate_gain,
    out_weight,
    cotangent,
):
    token_count = hidden_in.shape[0]
    segment = segments_of(lengths[0], token_count)
    is_valid = (segment < 2)[:, None]
    w_in, w_out, kernel, offsets, step_bias, decay_log, skip, gate_scale, n_gain = (
        lax.all_gather(in_weight, "fsdp", axis=0, tiled=True),
        lax.all_gather(out_weight, "fsdp", axis=1, tiled=True),
        lax.all_gather(conv_weight, "fsdp", axis=1, tiled=True),
        lax.all_gather(conv_bias, "fsdp", axis=0, tiled=True),
        lax.all_gather(dt_bias, "fsdp", axis=0, tiled=True),
        lax.all_gather(a_log, "fsdp", axis=0, tiled=True),
        lax.all_gather(skip_gain, "fsdp", axis=0, tiled=True),
        lax.all_gather(gate_gain, "fsdp", axis=0, tiled=True),
        lax.all_gather(norm_gain, "fsdp", axis=0, tiled=True),
    )
    small_floats = tuple(
        (a.astype(jnp.float32) for a in (kernel, offsets, step_bias, decay_log, skip, gate_scale))
    )
    hidden = hidden_in.astype(jnp.float32)
    normed, norm_pull = jax.vjp(normalize, hidden, n_gain.astype(jnp.float32))
    normed_low = normed.astype(jnp.bfloat16)
    projected = jnp.dot(normed_low, w_in, preferred_element_type=jnp.float32)

    def local_mixer(proj_rows, kernel_f, offsets_f, bias_f, decay_f, skip_f, gate_f):
        return mixer(proj_rows, segment, kernel_f, offsets_f, bias_f, decay_f, skip_f, gate_f)

    branch, mixer_pull = jax.vjp(local_mixer, projected, *small_floats)
    branch_low = branch.astype(jnp.bfloat16)
    summed = hidden + jnp.dot(branch_low, w_out, preferred_element_type=jnp.float32)
    mixed = jnp.where(is_valid, summed, 0.0).astype(jnp.bfloat16)
    back_low = jnp.where(is_valid, cotangent, jnp.zeros_like(cotangent))
    w_in, w_out = (
        lax.all_gather(in_weight, "fsdp", axis=0, tiled=True),
        lax.all_gather(out_weight, "fsdp", axis=1, tiled=True),
    )
    d_branch = jnp.einsum("te,de->td", back_low, w_out, preferred_element_type=jnp.float32)
    d_projected, g_kernel, g_offsets, g_bias, g_decay, g_skip, g_gate = mixer_pull(d_branch)
    d_proj_low = d_projected.astype(jnp.bfloat16)
    d_normed = jnp.einsum("te,de->td", d_proj_low, w_in, preferred_element_type=jnp.float32)
    d_hidden, g_norm = norm_pull(d_normed)
    grad_hidden = back_low.astype(jnp.float32) + d_hidden
    s_kernel, s_offsets, s_bias, s_decay, s_skip, s_gate, s_norm = (
        lax.psum_scatter(g_kernel, "fsdp", scatter_dimension=1, tiled=True),
        lax.psum_scatter(g_offsets, "fsdp", scatter_dimension=0, tiled=True),
        lax.psum_scatter(g_bias, "fsdp", scatter_dimension=0, tiled=True),
        lax.psum_scatter(g_decay, "fsdp", scatter_dimension=0, tiled=True),
        lax.psum_scatter(g_skip, "fsdp", scatter_dimension=0, tiled=True),
        lax.psum_scatter(g_gate, "fsdp", scatter_dimension=0, tiled=True),
        lax.psum_scatter(g_norm, "fsdp", scatter_dimension=0, tiled=True),
    )
    columns = normed_low
    part_in = lax.psum_scatter(
        jnp.einsum("td,te->de", columns, d_proj_low, preferred_element_type=jnp.float32),
        "fsdp",
        scatter_dimension=0,
        tiled=True,
    )
    columns = back_low
    part_out = lax.psum_scatter(
        jnp.einsum("td,tf->df", columns, branch_low, preferred_element_type=jnp.float32),
        "fsdp",
        scatter_dimension=0,
        tiled=True,
    )
    g_in, g_out_rows, s_kernel, s_offsets, s_bias, s_decay, s_skip, s_gate, s_norm = lax.psum(
        (part_in, part_out, s_kernel, s_offsets, s_bias, s_decay, s_skip, s_gate, s_norm), "rep"
    )
    return (
        mixed,
        grad_hidden,
        s_norm,
        g_in,
        s_kernel,
        s_offsets,
        s_bias,
        s_decay,
        s_skip,
        s_gate,
        g_out_rows.T,
    )


def solution(mesh):
    return jax.shard_map(
        per_device,
        mesh=mesh,
        in_specs=(
            P(("rep", "fsdp"), None),
            P(("rep", "fsdp"), None),
            P("fsdp"),
            P("fsdp", None),
            P(None, "fsdp"),
            P("fsdp"),
            P("fsdp"),
            P("fsdp"),
            P("fsdp"),
            P("fsdp"),
            P(None, "fsdp"),
            P(("rep", "fsdp"), None),
        ),
        out_specs=(
            P(("rep", "fsdp"), None),
            P(("rep", "fsdp"), None),
            P("fsdp"),
            P("fsdp", None),
            P(None, "fsdp"),
            P("fsdp"),
            P("fsdp"),
            P("fsdp"),
            P("fsdp"),
            P("fsdp"),
            P(None, "fsdp"),
        ),
        check_vma=False,
    )
```

profile of v0, /device:TPU:0, one launch (start us, length us, event | category | flops | bytes accessed | tf_op | source)
XLA Modules:
  0.0 1604.6 jit_solution(4947056089663793834)
XLA Ops:
  17.9 31.5 %all-reduce.33 = (bf16[1536]{0:T(1024)(128)(2,1)S(1)}, bf16[48]{0:T(256)(128)(2,1)S(1)}, bf16[48]{0:T(256)(128)(2,1)S(1)}, bf16[3328]{0:T(1024)(128)(2,1)S(1)}, bf16[48]{0:T(256)(128)(2,1)S(1)}) all-reduce(bf16[1536]{0:T(1024)(128)(2,1)S(1)} %dynamic-update-slice.1, ...), channel_id=1, replica_groups=mesh['rep'=4,'fsdp'=8] {'fsdp'}, use_global_device_ids=true, to_apply=%add.20 | all-reduce | flops 5008 | bytes 20032
  49.5 18.8 %all-gather.1 = bf16[8,1,384]{2,1,0:T(2,128)(2,1)S(1)} all-gather(bf16[1,1,384]{2,1,0:T(2,128)(2,1)S(1)} %reshape.451), channel_id=1, replica_groups=mesh['rep'=4,'fsdp'=8] {'fsdp'}, dimensions={0}, use_global_device_ids=true | all-gather | bytes 6912 | tf_op jit(solution)/shard_map/all_gather | solution.py:134
  68.9 15.6 all-gather
  87.7 103.4 %all-gather.5.cloned.1.call-done = bf16[1536,6448]{1,0:T(8,128)(2,1)} async-done(((bf16[192,6448]{1,0:T(8,128)(2,1)}), bf16[1536,6448]{1,0:T(8,128)(2,1)}) %all-gather.5.cloned.1.call-update) | async-done | bytes 19808272 | tf_op jit(solution)/shard_map/all_gather | solution.py:127
  191.1 18.4 %fusion.119 = f32[512,6448]{0,1:T(8,128)} fusion(bf16[1536,6448]{1,0:T(8,128)(2,1)} %all-gather.5.cloned.1.call-done, bf16[512,1536]{1,0:T(8,128)(2,1)} %param.16, f32[1536]{0:T(1024)S(1)} %convert_element_type.45, f32[512]{0:T(512)S(1)} %fusion.125), kind=kOutput, calls=%fused_computation.195 | convolution fusion | flops 10144972800 | bytes 34594816 | tf_op jit(solution)/shard_map/dot_general | solution.py:143
  227.6 14.6 fusion.102
  271.8 206.8 %while.48 = (s32[]{:T(128)}, f32[48,64,128]{2,1,0:T(8,128)S(1)}, s32[]{:T(128)}, f32[2,256,48,64]{1,0,3,2:T(2,128)}, f32[2,48,64,128]{3,2,1,0:T(8,128)}, /*index...) while((s32[]{:T(128)}, f32[48,64,128]{2,1,0:T(8,128)S(1)}, ...), condition=%wide.region_6.7_spmd.clone, body=%wide.region_3.6_spmd.clone.sunk | while | flops 4952814592 | bytes 60323644 | solution.py:87
  279.6 15.9 fusion.206
  304.6 63.5 %dynamic_update_slice.89 = f32[2,256,48,64]{1,0,3,2:T(2,128)} dynamic-update-slice(f32[2,256,48,64]{1,0,3,2:T(2,128)} %get-tuple-element.1318, f32[1,256,48,64]{1,0,3,2:T(1,128)} %copy.334, s32[]{:T(128)S(6)} %copy.371, s32[]{:T(128)} %constant.155.clone.1..sunk, s32[]{:T(128)} %constant.155.clone.1..sunk, s32[]{:T(128)} %constant.155.clone.1..sunk) | dynamic-update-slice | bytes 6291460 | tf_op jit(solution)/shard_map/jvp()/while/body/jit(dynamic_update_index_in_dim)/dynamic_update_slice | solution.py:87
  382.9 15.9 fusion.206
  407.9 63.5 %dynamic_update_slice.89 = f32[2,256,48,64]{1,0,3,2:T(2,128)} dynamic-update-slice(f32[2,256,48,64]{1,0,3,2:T(2,128)} %get-tuple-element.1318, f32[1,256,48,64]{1,0,3,2:T(1,128)} %copy.334, s32[]{:T(128)S(6)} %copy.371, s32[]{:T(128)} %constant.155.clone.1..sunk, s32[]{:T(128)} %constant.155.clone.1..sunk, s32[]{:T(128)} %constant.155.clone.1..sunk) | dynamic-update-slice | bytes 6291460 | tf_op jit(solution)/shard_map/jvp()/while/body/jit(dynamic_update_index_in_dim)/dynamic_update_slice | solution.py:87
  515.5 13.5 fusion.114
  545.7 391.3 %while.49 = (s32[]{:T(128)}, f32[48]{0:T(128)}, f32[48,64,128]{2,1,0:T(8,128)}, f32[2,256,48,64]{1,0,3,2:T(2,128)}, f32[2,256,128]{2,1,0:T(8,128)}, /*index=5*/f...) while((s32[]{:T(128)}, f32[48]{0:T(128)}, ...), condition=%wide.region_23.24_spmd.clone, body=%wide.region_9.23_spmd.clone.sunk | while | flops 11242868736 | bytes 124601600 | solution.py:87
  588.1 21.6 %fusion.229 = (f32[256,48]{0,1:T(8,128)}, f32[256,48]{0,1:T(8,128)}, f32[256,48]{0,1:T(8,128)}, f32[256,256]{1,0:T(8,128)}) fusion(f32[256,48]{0,1:T(8,128)} %copy.339, f32[256,48]{0,1:T(8,128)} %copy.341, f32[256,256]{1,0:T(8,128)S(1)} %fusion.228, pred[256,256]{1,0:T(8,128)(4,1)} %compare_and_fusion.2, f32[256,48,64]{0,2,1:T(8,128)} %get-tuple-element.1274, ...), kind=kOutput, calls=%fused_computation.71.clone.1 | convolution fusion | flops 2456711168 | bytes 7127040 | tf_op jit(solution)/shard_map/transpose(jvp())/while/body/eval_jaxpr/checkpoint/tsh,shp->thp/dot_general | solution.py:59
  673.6 63.3 %dynamic_update_slice.94 = f32[2,256,48,64]{1,0,3,2:T(2,128)} dynamic-update-slice(f32[2,256,48,64]{1,0,3,2:T(2,128)} %get-tuple-element.1373, f32[1,256,48,64]{1,0,3,2:T(1,128)S(1)} %copy.348, s32[]{:T(128)S(6)} %sub.249, s32[]{:T(128)} %constant.155.clone.1..sunk.1, s32[]{:T(128)} %constant.155.clone.1..sunk.1, s32[]{:T(128)} %constant.155.clone.1..sunk.1) | dynamic-update-slice | bytes 6291460 | tf_op jit(solution)/shard_map/transpose(jvp())/while/body/jit(dynamic_update_index_in_dim)/dynamic_update_slice | solution.py:87
  780.4 21.6 %fusion.229 = (f32[256,48]{0,1:T(8,128)}, f32[256,48]{0,1:T(8,128)}, f32[256,48]{0,1:T(8,128)}, f32[256,256]{1,0:T(8,128)}) fusion(f32[256,48]{0,1:T(8,128)} %copy.339, f32[256,48]{0,1:T(8,128)} %copy.341, f32[256,256]{1,0:T(8,128)S(1)} %fusion.228, pred[256,256]{1,0:T(8,128)(4,1)} %compare_and_fusion.2, f32[256,48,64]{0,2,1:T(8,128)} %get-tuple-element.1274, ...), kind=kOutput, calls=%fused_computation.71.clone.1 | convolution fusion | flops 2456711168 | bytes 7127040 | tf_op jit(solution)/shard_map/transpose(jvp())/while/body/eval_jaxpr/checkpoint/tsh,shp->thp/dot_general | solution.py:59
  866.0 63.3 %dynamic_update_slice.94 = f32[2,256,48,64]{1,0,3,2:T(2,128)} dynamic-update-slice(f32[2,256,48,64]{1,0,3,2:T(2,128)} %get-tuple-element.1373, f32[1,256,48,64]{1,0,3,2:T(1,128)S(1)} %copy.348, s32[]{:T(128)S(6)} %sub.249, s32[]{:T(128)} %constant.155.clone.1..sunk.1, s32[]{:T(128)} %constant.155.clone.1..sunk.1, s32[]{:T(128)} %constant.155.clone.1..sunk.1) | dynamic-update-slice | bytes 6291460 | tf_op jit(solution)/shard_map/transpose(jvp())/while/body/jit(dynamic_update_index_in_dim)/dynamic_update_slice | solution.py:87
  948.8 18.3 %fusion.131 = (f32[3328]{0:T(1024)S(1)}, f32[3328]{0:T(1024)S(1)}, f32[3328]{0:T(1024)S(1)}, f32[3328]{0:T(1024)S(1)}, f32[3328]{0:T(1024)S(1)}, /*index=5*/f32[512,3328]{0,1:T(8,128)S(1)}) fusion(f32[512,6448]{0,1:T(8,128)} %fusion.119, f32[511,3328]{0,1:T(8,128)} %slice.163, pred[512]{0:T(512)(128)(4,1)S(1)} %copy-done.40, f32[510,3328]{0,1:T(8,128)} %slice.165, ...), kind=kLoop, calls=%fused_computation.231 | loop fusion | flops 39173888 | bytes 47698432 | tf_op jit(solution)/shard_map/transpose(jvp())/reduce_sum | solution.py:26
  988.7 22.5 %fusion.117 = f32[1536,6448]{1,0:T(8,128)} fusion(bf16[512,1536]{1,0:T(8,128)(2,1)S(1)} %copy-done.10, f32[1536]{0:T(1024)S(1)} %copy-done.29, f32[512]{0:T(512)S(1)} %copy-done.36, f32[512,3072]{0,1:T(8,128)} %get-tuple-element.1032, f32[512,3328]{0,1:T(8,128)} %multiply_add_fusion.2, f32[512,48]{0,1:T(8,128)S(1)} %get-tuple-element.1009), kind=kOutput, calls=%fused_computation.194 | convolution fusion | flops 10154876928 | bytes 54403072 | tf_op jit(solution)/shard_map/td,te->de/dot_general | solution.py:174
  1013.2 382.8 %reduce-scatter.6.cloned.1.call-done = f32[192,6448]{1,0:T(8,128)} async-done(((f32[1536,6448]{1,0:T(8,128)}), f32[192,6448]{1,0:T(8,128)}) %reduce-scatter.6.cloned.1.call-update) | async-done | bytes 4952080 | tf_op jit(solution)/shard_map/reduce_scatter | solution.py:173
  1398.5 24.0 %fusion.110 = (f32[1536]{0:T(1024)S(1)}, f32[512]{0:T(512)S(1)}, f32[512,1536]{1,0:T(8,128)}) fusion(bf16[512,1536]{1,0:T(8,128)(2,1)S(1)} %copy-done.10, f32[512]{0:T(512)S(1)} %copy-done.36, f32[1536]{0:T(1024)S(1)} %copy-done.29, bf16[1536,6448]{1,0:T(8,128)(2,1)} %all-gather.5.cloned.1.call-done, f32[512,3072]{0,1:T(8,128)} %get-tuple-element.1032, ...), kind=kOutput, calls=%fused_computation.186 | convolution fusion | flops 10157234176 | bytes 37748736 | tf_op jit(solution)/shard_map/te,de->td/dot_general | solution.py:160
  1422.5 26.7 %all-reduce.30 = (f32[1536]{0:T(1024)S(1)}, f32[3328]{0:T(1024)S(1)}, f32[48]{0:T(128)S(1)}, f32[48]{0:T(128)S(1)}, f32[48]{0:T(128)S(1)}, /*index=5*/f32[3072]{0:T(1024)S(1)}) all-reduce(f32[1536]{0:T(1024)S(1)} %get-tuple-element.920, f32[3328]{0:T(1024)S(1)} %get-tuple-element.915, ...), channel_id=2, replica_groups=mesh['rep'=4,'fsdp'=8] {'fsdp'}, use_global_device_ids=true, to_apply=%region_26.27.clone | all-reduce | flops 8080 | bytes 64640
  1468.8 17.1 %all-reduce.31 = (f32[192]{0:T(256)}, f32[4,416]{1,0:T(4,128)}, f32[416]{0:T(512)}, f32[6]{0:T(128)}, f32[6]{0:T(128)}, /*index=5*/f32[6]{0:T(128)}, f32[384]{0:T(512)}) all-reduce(f32[192]{0:T(256)S(1)} %dynamic-slice.6, f32[4,416]{1,0:T(4,128)S(1)} %copy.243, f32[416]{0:T(512)S(1)} %dynamic-slice.8, ...), channel_id=1, replica_groups=mesh['rep'=4,'fsdp'=8] {'rep'}, use_global_device_ids=true, to_apply=%region_27.28 | all-reduce | flops 2674 | bytes 21392 | tf_op jit(solution)/shard_map/psum | solution.py:186
  1485.8 104.8 %all-reduce.36.cloned.1.call-done = (f32[192,6448]{1,0:T(8,128)}, f32[3072,192]{0,1:T(8,128)}) async-done(((f32[192,6448]{1,0:T(8,128)}, f32[3072,192]{0,1:T(8,128)}), (f32[192,6448]{1,0:T(8,128)}, f32[3072,192]{0,1:T(8,128)})) %all-reduce.36.cloned.1.call-update) | async-done | bytes 7311376 | tf_op jit(solution)/shard_map/psum | solution.py:186
  (415 shorter events, 429.7 us)
Async XLA Ops:
  7.2 184.0 %all-gather.5.cloned.1.call-start = ((), (), s32[]{:S(2)}) async-start(), calls=%async_computation.3 | async-start | bytes 22560768 | tf_op jit(solution)/shard_map/all_gather | solution.py:127
  7.9 495.6 %all-gather.7.cloned.1.call-start = ((), (), s32[]{:S(2)}) async-start(), calls=%async_computation.4 | async-start | bytes 10616832 | tf_op jit(solution)/shard_map/all_gather | solution.py:128
  8.7 1004.5 %reduce-scatter.8.cloned.1.call-start = ((), (), s32[]{:S(2)}) async-start(), calls=%async_computation.6 | async-start | bytes 21233664 | tf_op jit(solution)/shard_map/reduce_scatter | solution.py:180
  49.4 160.1 %copy-start.54 = (bf16[48]{0:T(256)(128)(2,1)}, bf16[48]{0:T(256)(128)(2,1)S(1)}, u32[]{:S(2)}) copy-start(bf16[48]{0:T(256)(128)(2,1)S(1)} %get-tuple-element.1005) | copy-start | bytes 292
  49.5 176.7 %copy-start.47 = (f32[48]{0:T(128)}, f32[48]{0:T(128)S(1)}, u32[]{:S(2)}) copy-start(f32[48]{0:T(128)S(1)} %convert_element_type.47) | copy-start | bytes 580
  49.5 160.1 %copy-start.28 = (f32[1536]{0:T(1024)}, f32[1536]{0:T(1024)S(1)}, u32[]{:S(2)}) copy-start(f32[1536]{0:T(1024)S(1)} %convert_element_type.45) | copy-start | bytes 18436
  84.8 142.8 %copy-start.17 = (f32[3328]{0:T(1024)}, f32[3328]{0:T(1024)S(1)}, u32[]{:S(2)}) copy-start(f32[3328]{0:T(1024)S(1)} %get-tuple-element.922) | copy-start | bytes 39940
  84.8 142.8 %copy-start.19 = (f32[3328]{0:T(1024)}, f32[3328]{0:T(1024)S(1)}, u32[]{:S(2)}) copy-start(f32[3328]{0:T(1024)S(1)} %get-tuple-element.923) | copy-start | bytes 39940
  84.8 142.8 %copy-start.21 = (f32[3328]{0:T(1024)}, f32[3328]{0:T(1024)S(1)}, u32[]{:S(2)}) copy-start(f32[3328]{0:T(1024)S(1)} %get-tuple-element.924) | copy-start | bytes 39940
  84.8 142.8 %copy-start.23 = (f32[3328]{0:T(1024)}, f32[3328]{0:T(1024)S(1)}, u32[]{:S(2)}) copy-start(f32[3328]{0:T(1024)S(1)} %get-tuple-element.925) | copy-start | bytes 39940
  86.7 122.9 %copy-start.30 = (f32[512]{0:T(512)}, f32[512]{0:T(512)S(1)}, u32[]{:S(2)}) copy-start(f32[512]{0:T(512)S(1)} %fusion.112) | copy-start | bytes 6148
  86.7 139.4 %copy-start.49 = (f32[48]{0:T(128)}, f32[48]{0:T(128)S(1)}, u32[]{:S(2)}) copy-start(f32[48]{0:T(128)S(1)} %fusion.127) | copy-start | bytes 580
  87.2 122.4 %copy-start.35 = (f32[512]{0:T(512)}, f32[512]{0:T(512)S(1)}, u32[]{:S(2)}) copy-start(f32[512]{0:T(512)S(1)} %fusion.125) | copy-start | bytes 6148
  87.7 414.0 %copy-start.39 = (pred[512]{0:T(512)(128)(4,1)}, pred[512]{0:T(512)(128)(4,1)S(1)}, u32[]{:S(2)}) copy-start(pred[512]{0:T(512)(128)(4,1)S(1)} %get-tuple-element.1036) | copy-start | bytes 1540
  87.7 414.6 %copy-start.41 = (pred[512]{0:T(512)(128)(4,1)}, pred[512]{0:T(512)(128)(4,1)S(1)}, u32[]{:S(2)}) copy-start(pred[512]{0:T(512)(128)(4,1)S(1)} %get-tuple-element.1037) | copy-start | bytes 1540
  87.7 415.3 %copy-start.43 = (pred[512]{0:T(512)(128)(4,1)}, pred[512]{0:T(512)(128)(4,1)S(1)}, u32[]{:S(2)}) copy-start(pred[512]{0:T(512)(128)(4,1)S(1)} %get-tuple-element.1038) | copy-start | bytes 1540
  501.7 894.3 %reduce-scatter.6.cloned.1.call-start = ((), (), s32[]{:S(2)}) async-start(), calls=%async_computation.5 | async-start | bytes 45121536 | tf_op jit(solution)/shard_map/reduce_scatter | solution.py:173
  673.6 63.3 %copy-start.16 = (f32[2,256,48]{1,0,2:T(2,128)}, f32[2,256,48]{1,0,2:T(2,128)S(1)}, u32[]{:S(2)}) copy-start(f32[2,256,48]{1,0,2:T(2,128)S(1)} %dynamic_update_slice.95) | copy-start | bytes 294916 | tf_op jit(solution)/shard_map/transpose(jvp())/while
  865.9 63.3 %copy-start.16 = (f32[2,256,48]{1,0,2:T(2,128)}, f32[2,256,48]{1,0,2:T(2,128)S(1)}, u32[]{:S(2)}) copy-start(f32[2,256,48]{1,0,2:T(2,128)S(1)} %dynamic_update_slice.95) | copy-start | bytes 294916 | tf_op jit(solution)/shard_map/transpose(jvp())/while
  1011.2 387.3 %copy-start.55 = (bf16[48]{0:T(256)(128)(2,1)S(1)}, bf16[48]{0:T(256)(128)(2,1)}, u32[]{:S(2)}) copy-start(bf16[48]{0:T(256)(128)(2,1)} %copy-done.54) | copy-start | bytes 292
  1011.2 456.6 %reduce-scatter.10.cloned.1.call-start = ((), (), s32[]{:S(2)}) async-start(), calls=%async_computation.7 | async-start | bytes 1916928
  1013.1 577.6 %all-reduce.36.cloned.1.call-start = ((), (), s32[]{:S(2)}) async-start(), calls=%async_computation.8 | async-start | bytes 14745600 | tf_op jit(solution)/shard_map/psum | solution.py:186
  1398.5 51.2 %copy-start.31 = (f32[512]{0:T(512)S(1)}, f32[512]{0:T(512)}, u32[]{:S(2)}) copy-start(f32[512]{0:T(512)} %copy-done.30) | copy-start | bytes 6148
  1398.5 51.2 %copy-start.46 = (pred[512]{0:T(512)(128)(4,1)S(1)}, pred[512]{0:T(512)(128)(4,1)}, u32[]{:S(2)}) copy-start(pred[512]{0:T(512)(128)(4,1)} %get-tuple-element.1039) | copy-start | bytes 1540
  (58 other events, 714.4 us)
Sparse Core Ops, SparseCore 0:
  9.7 181.4 all-gather.4
  192.8 89.1 all-gather.6
  501.8 186.5 reduce-scatter.7
  1011.3 384.6 reduce-scatter.5
  1398.7 33.2 reduce-scatter.9
  1435.8 154.8 all-reduce.35
where the time goes:
time: 1630 us; the launch traced here: 1600 us
  waiting for transfers between devices  592 us (36%)
  local copies, waits for them, and re-layouts  444 us (27%)
  matrix products  290 us (18%)
  other arithmetic  134 us (8%)
  blocking collectives  110 us (7%)
  between operations  19.7 us (1%)
    reduce_scatter x1, waiting for transfers between devices, per_device(): lax.psum_scatter(jnp.einsum('td,te->de', columns, d_proj_low, preferred_e...  383 us
    dynamic_update_slice x14, local copies, waits for them, and re-layouts, blockwise(): unused, outputs = lax.scan(jax.checkpoint(advance), start_state, pieces)  275 us
    psum x1, waiting for transfers between devices, per_device(): lax.psum((part_in, part_out, s_kernel, s_offsets, s_bias, s_decay, s_skip...  105 us
    all_gather x1, waiting for transfers between devices, per_device(): lax.all_gather(in_weight, 'fsdp', axis=0, tiled=True)  103 us
    dot_general x6, matrix products, advance(): inside = jnp.einsum('tsh,shp->thp', weights, vals, precision=highest)  101 us
    unnamed x2, blocking collectives  58.2 us
    unnamed x124, local copies, waits for them, and re-layouts  42.4 us
    dot_general x6, matrix products, advance(): jnp.einsum('shp,sn->hpn', source_weight[:, :, None] * vals, key_rows, pre...  40.9 us
  transfers between devices with their start and end apart: 6, of which 3 were waited for; matrix products, arithmetic and copies ran while one was open for 53% of the time, Pallas kernels for 0%

commit v1 on v0

v1 whole, which is shorter than its diff:
```python
import functools

import jax
import jax.numpy as jnp
from jax import lax
from jax.experimental import pallas as pl
from jax.experimental.pallas import tpu as pltpu
from jax.sharding import PartitionSpec as P

EPS = 1e-05
CHUNK = 128
LANES = 128
HIGHEST = lax.Precision.HIGHEST
F32 = jnp.float32
BF16 = jnp.bfloat16


def dot(left, right, precision=None):
    return lax.dot_general(
        left, right, (((1,), (0,)), ((), ())), precision=precision, preferred_element_type=F32
    )


def dot_nt(left, right):
    return lax.dot_general(left, right, (((1,), (1,)), ((), ())), preferred_element_type=F32)


def sigmoid(v):
    return 1.0 / (1.0 + jnp.exp(-v))


def softplus(v):
    return jnp.maximum(v, 0.0) + jnp.log1p(jnp.exp(-jnp.abs(v)))


def begin_of(position, first, both):
    return jnp.where(position >= both, both, jnp.where(position >= first, first, 0))


def iotas(rows, columns):
    return (
        lax.broadcasted_iota(jnp.int32, (rows, columns), 0),
        lax.broadcasted_iota(jnp.int32, (rows, columns), 1),
    )


def conv_tile(u_ref, cw_ref, start, columns, masks):
    inputs = [u_ref[start : start + CHUNK, columns]]
    for delay in range(1, 4):
        if start:
            shifted = u_ref[start - delay : start - delay + CHUNK, columns]
        else:
            shifted = pltpu.roll(inputs[0], delay, 0)
        inputs.append(jnp.where(masks[delay - 1], shifted, 0.0))
    pre = cw_ref[4:5, columns] + cw_ref[3:4, columns] * inputs[0]
    for delay in range(1, 4):
        pre = pre + cw_ref[3 - delay : 4 - delay, columns] * inputs[delay]
    return pre, inputs


def chunk_rates(dt_ref, hp_ref, start):
    raw = dt_ref[start : start + CHUNK, :] + hp_ref[0:1, :]
    step = softplus(raw)
    rate = -jnp.exp(hp_ref[1:2, :]) * step
    row, column = iotas(CHUNK, CHUNK)
    running = dot((row >= column).astype(F32), rate, HIGHEST)
    return raw, step, rate, running


def pair_of(low, matrix, head):
    return jnp.where(low, matrix[:, head : head + 1], matrix[:, head + 1 : head + 2])


def forward_kernel(heads, size, len_ref, u_ref, dt_ref, kq_ref, cw_ref, hp_ref, y_ref, st_ref, state):
    block = pl.program_id(0)
    first = len_ref[block, 0]
    both = first + len_ref[block, 1]
    tokens = u_ref.shape[0]
    chunks = tokens // CHUNK
    row, column = iotas(CHUNK, CHUNK)
    low = column < size
    low_row = low[0:1, :]
    for ci in range(chunks):
        start = ci * CHUNK
        position = row + start
        begin = begin_of(position, first, both)
        masks = [position - delay >= begin for delay in range(1, 4)]
        raw, step, rate, running = chunk_rates(dt_ref, hp_ref, start)
        running_t = running.T
        keys = kq_ref[start : start + CHUNK, :LANES]
        queries = kq_ref[start : start + CHUNK, LANES:]
        keys_t = keys.astype(F32).T.astype(BF16)
        allowed = (column <= row) & (column + start >= begin)
        scores = jnp.where(allowed, dot_nt(queries, keys), 0.0)
        last_begin = begin_of(start + CHUNK - 1, first, both)
        source = position >= last_begin
        reached = begin < start
        ending = running[CHUNK - 1 : CHUNK, :]
        kept = jnp.where(last_begin < start, jnp.exp(ending), 0.0)
        for pair in range(heads // 2):
            h = 2 * pair
            columns = slice(pair * LANES, (pair + 1) * LANES)
            pre, _ = conv_tile(u_ref, cw_ref, start, columns, masks)
            values = pre * sigmoid(pre)
            scaled = values * pair_of(low, step, h)
            weights = []
            for head in (h, h + 1):
                gap = running[:, head : head + 1] - running_t[head : head + 1, :]
                weights.append((scores * jnp.exp(jnp.minimum(gap, 0.0))).astype(BF16))
            stacked = jnp.concatenate(
                [jnp.where(low, scaled, 0.0), jnp.where(low, 0.0, scaled)], axis=0
            ).astype(BF16)
            out = dot(jnp.concatenate(weights, axis=1), stacked)
            out = out + cw_ref[5:6, columns] * values
            across = pair_of(low, running, h)
            if ci:
                carried = dot(queries, state[:, columns].astype(BF16))
                out = out + jnp.where(reached, carried * jnp.exp(across), 0.0)
            y_ref[start : start + CHUNK, columns] = out
            if ci < chunks - 1:
                left = pair_of(low_row, ending, h) - across
                source_in = jnp.where(source, scaled * jnp.exp(left), 0.0).astype(BF16)
                fresh = dot(keys_t, source_in)
                if ci:
                    fresh = fresh + state[:, columns] * pair_of(low_row, kept, h)
                state[:, columns] = fresh
                st_ref[0, ci, :, columns] = fresh.astype(BF16)


def backward_kernel(
    heads,
    size,
    first_head,
    len_ref,
    u_ref,
    dt_ref,
    kq_ref,
    dy_ref,
    st_ref,
    cw_ref,
    hp_ref,
    du_ref,
    ddt_ref,
    dkq_ref,
    cg_ref,
    hg_ref,
    d_state,
    d_pre,
    out_in,
    source_in,
):
    block = pl.program_id(0)
    first = len_ref[block, 0]
    both = first + len_ref[block, 1]
    tokens, width = u_ref.shape
    chunks = tokens // CHUNK
    row, column = iotas(CHUNK, CHUNK)
    low = column < size
    low_row = low[0:1, :]
    wide_row, wide_column = iotas(2 * CHUNK, LANES)
    pick_row, pick_column = iotas(16, 2 * CHUNK)

    @pl.when(block == 0)
    def _():
        cg_ref[...] = jnp.zeros_like(cg_ref)
        hg_ref[...] = jnp.zeros_like(hg_ref)

    d_pre[tokens : tokens + 8, :] = jnp.zeros((8, width), F32)
    for ci in reversed(range(chunks)):
        start = ci * CHUNK
        has_later = ci < chunks - 1
        position = row + start
        begin = begin_of(position, first, both)
        masks = [position - delay >= begin for delay in range(1, 4)]
        ahead = [begin_of(position + delay, first, both) <= position for delay in range(1, 4)]
        raw, step, rate, running = chunk_rates(dt_ref, hp_ref, start)
        running_t = running.T
        keys = kq_ref[start : start + CHUNK, :LANES]
        queries = kq_ref[start : start + CHUNK, LANES:]
        allowed = (row <= column) & (position >= begin_of(column + start, first, both))
        scores = jnp.where(allowed, dot_nt(keys, queries), 0.0)
        last_begin = begin_of(start + CHUNK - 1, first, both)
        source = position >= last_begin
        reached = begin < start
        ending = running[CHUNK - 1 : CHUNK, :]
        kept = jnp.where(last_begin < start, jnp.exp(ending), 0.0)
        d_scores = jnp.zeros((CHUNK, CHUNK), F32)
        later_sums = jnp.zeros((16, CHUNK), F32)
        early_sums = jnp.zeros((CHUNK, LANES), F32)
        out_sums = jnp.zeros((CHUNK, LANES), F32)
        source_sums = jnp.zeros((CHUNK, LANES), F32)
        direct_sums = jnp.zeros((CHUNK, LANES), F32)
        kept_sums = jnp.zeros((8, LANES), F32)
        for pair in range(heads // 2):
            h = first_head + 2 * pair
            columns = slice(pair * LANES, (pair + 1) * LANES)
            to_head = (column == h + (row >= size).astype(jnp.int32)).astype(BF16)
            pre, inputs = conv_tile(u_ref, cw_ref, start, columns, masks)
            gate = sigmoid(pre)
            values = pre * gate
            steps = pair_of(low, step, h)
            scaled = values * steps
            d_out = dy_ref[start : start + CHUNK, columns].astype(F32)
            d_low = d_out.astype(BF16)
            stacked = jnp.concatenate(
                [jnp.where(low, scaled, 0.0), jnp.where(low, 0.0, scaled)], axis=0
            ).astype(BF16)
            d_weights = dot_nt(stacked, d_low)
            weights, products = [], []
            for at, head in enumerate((h, h + 1)):
                gap = running_t[head : head + 1, :] - running[:, head : head + 1]
                decay = jnp.exp(jnp.minimum(gap, 0.0))
                d_decayed = decay * d_weights[at * CHUNK : (at + 1) * CHUNK]
                d_scores = d_scores + d_decayed
                products.append((scores * d_decayed).astype(BF16))
                weights.append((scores * decay).astype(BF16))
            early = wide_column == h + (wide_row >= CHUNK).astype(jnp.int32)
            early_sums = early_sums + dot(jnp.concatenate(products, axis=1), early.astype(BF16))
            later = pick_row == h + (pick_column >= CHUNK).astype(jnp.int32)
            later_sums = later_sums + dot(later.astype(BF16), jnp.concatenate(products, axis=0))
            d_stacked = jnp.concatenate(
                [jnp.where(low, d_out, 0.0), jnp.where(low, 0.0, d_out)], axis=0
            ).astype(BF16)
            d_scaled = dot(jnp.concatenate(weights, axis=1), d_stacked)
            across = pair_of(low, running, h)
            if has_later:
                left = jnp.exp(pair_of(low_row, ending, h) - across)
                left = jnp.where(source, left, 0.0)
                d_state_here = d_state[:, columns]
                d_source = dot(keys, d_state_here.astype(BF16)) * left
                d_scaled = d_scaled + d_source
                source_sums = source_sums + dot((scaled * d_source).astype(BF16), to_head)
                source_in[:, columns] = (scaled * left).astype(BF16)
            if ci:
                before = st_ref[0, ci - 1, :, columns]
                d_reach = jnp.where(reached, d_out * jnp.exp(across), 0.0)
                out_sums = out_sums + dot((d_reach * dot(queries, before)).astype(BF16), to_head)
                out_in[:, columns] = d_reach.astype(BF16)
                if has_later:
                    held = jnp.sum(d_state_here * before.astype(F32), axis=0, keepdims=True)
                    held = held * pair_of(low_row, kept, h)
                    kept_sums = kept_sums + dot(
                        jnp.broadcast_to(held, (8, LANES)), to_head.astype(F32), HIGHEST
                    )
            direct_sums = direct_sums + dot((d_scaled * values).astype(BF16), to_head)
            d_values = d_scaled * steps + cw_ref[5:6, columns] * d_out
            cg_ref[5:6, columns] += jnp.sum(d_out * values, axis=0, keepdims=True)
            d_here = d_values * (gate * (1.0 + pre * (1.0 - gate)))
            d_pre[start : start + CHUNK, columns] = d_here
            d_in = cw_ref[3:4, columns] * d_here
            for delay in range(1, 4):
                shifted = d_pre[start + delay : start + delay + CHUNK, columns]
                d_in = d_in + cw_ref[3 - delay : 4 - delay, columns] * jnp.where(
                    ahead[delay - 1], shifted, 0.0
                )
            du_ref[start : start + CHUNK, columns] = d_in.astype(BF16)
            for delay in range(4):
                cg_ref[3 - delay : 4 - delay, columns] += jnp.sum(
                    inputs[delay] * d_here, axis=0, keepdims=True
                )
            cg_ref[4:5, columns] += jnp.sum(d_here, axis=0, keepdims=True)
        d_scores = jnp.where(allowed, d_scores, 0.0)
        d_keys = dot(d_scores.astype(BF16), queries)
        d_queries = dot(d_scores.T.astype(BF16), keys)
        d_running = (
            jnp.concatenate([later_sums, jnp.zeros((CHUNK - 16, CHUNK), F32)], axis=0).T
            - early_sums
            + out_sums
            - source_sums
        )
        if has_later:
            d_keys = d_keys + dot_nt(source_in[...], d_state[...].astype(BF16))
            at_end = jnp.sum(source_sums, axis=0, keepdims=True) + kept_sums[0:1, :]
            d_running = d_running + jnp.where(row == CHUNK - 1, at_end, 0.0)
        if ci:
            d_queries = d_queries + dot_nt(out_in[...], st_ref[0, ci - 1])
            queries_t = queries.astype(F32).T.astype(BF16)
            for pair in range(heads // 2):
                columns = slice(pair * LANES, (pair + 1) * LANES)
                fresh = dot(queries_t, out_in[:, columns])
                if has_later:
                    fresh = fresh + d_state[:, columns] * pair_of(low_row, kept, first_head + 2 * pair)
                d_state[:, columns] = fresh
        dkq_ref[start : start + CHUNK, :LANES] = d_keys
        dkq_ref[start : start + CHUNK, LANES:] = d_queries
        d_rate = dot((row <= column).astype(F32), d_running, HIGHEST)
        d_step = direct_sums - jnp.exp(hp_ref[1:2, :]) * d_rate
        d_raw = d_step * sigmoid(raw)
        ddt_ref[start : start + CHUNK, :] = d_raw.astype(BF16)
        hg_ref[0:1, :] += jnp.sum(d_raw, axis=0, keepdims=True)
        hg_ref[1:2, :] += jnp.sum(d_rate * rate, axis=0, keepdims=True)


def prepare_kernel(heads, size, state, at_ref, in_ref, out_ref, mine_ref, other_ref):
    x, core = at_ref[0], at_ref[1]
    inner = out_ref.shape[0]
    width = heads * size
    steps_at = 2 * inner + 2 * state
    steps = in_ref[:, steps_at : steps_at + 4 * heads].astype(F32)
    rows = steps.shape[0]
    steps = jnp.concatenate([steps, jnp.zeros((rows, LANES - 4 * heads), F32)], axis=1)
    column = lax.broadcasted_iota(jnp.int32, (rows, LANES), 1)
    for ref, c in ((mine_ref, core), (other_ref, 1 - core)):
        p = 2 * x + c
        keys_at = pl.multiple_of(2 * inner + c * state, LANES)
        ref[:, :state] = in_ref[:, pl.ds(keys_at, state)]
        values_at = pl.multiple_of(inner + p * width, LANES)
        ref[:, state : state + width] = in_ref[:, pl.ds(values_at, width)]
        drawn = pltpu.roll(steps, lax.rem(LANES - heads * p, LANES), 1)
        drawn = jnp.where(column < heads, drawn, 0.0).astype(BF16)
        ref[:, state + width : state + width + LANES] = drawn
        at = state + width + LANES
        gate_at = pl.multiple_of(p * width, LANES)
        ref[:, at : at + width] = in_ref[:, pl.ds(gate_at, width)]
        ref[:, at + width : at + 2 * width] = out_ref[pl.ds(gate_at, width), :].T


def prepare_call(heads, size, state, place, in_weight, out_weight):
    rows = in_weight.shape[0]
    columns = state + LANES + 3 * heads * size
    return pl.pallas_call(
        functools.partial(prepare_kernel, heads, size, state),
        in_specs=[
            pl.BlockSpec(memory_space=pltpu.SMEM),
            pl.BlockSpec(memory_space=pltpu.VMEM),
            pl.BlockSpec(memory_space=pltpu.VMEM),
        ],
        out_specs=[pl.BlockSpec(memory_space=pltpu.VMEM)] * 2,
        out_shape=[jax.ShapeDtypeStruct((rows, columns), BF16)] * 2,
        compiler_params=pltpu.CompilerParams(vmem_limit_bytes=24 * 1024 * 1024),
        name="prepare_weights",
    )(place, in_weight, out_weight)


def assemble_rows(links_shape, at_ref, own_ref, core_ref, pieces, whole_ref):
    sides, groups = links_shape
    a, g, c = at_ref[0], at_ref[1], at_ref[2]
    rows = own_ref.shape[0]
    part = 2 * rows // sides
    base = g * (2 * rows)
    whole_ref[pl.ds(pl.multiple_of(base + c * rows, 16), rows), :] = own_ref[...]
    whole_ref[pl.ds(pl.multiple_of(base + (1 - c) * rows, 16), rows), :] = core_ref[...]
    for k in range(1, groups):
        base = lax.rem(g + groups - k, groups) * (2 * rows)
        for j, ref in enumerate(pieces):
            at = base + lax.rem(a + sides - j, sides) * part
            whole_ref[pl.ds(pl.multiple_of(at, 16), part), :] = ref[(k - 1) * part : k * part, :]


def project_kernel(links_shape, at_ref, own_ref, core_ref, *refs):
    sides = links_shape[0]
    pieces, (rows_ref, whole_ref, out_ref) = refs[:sides], refs[sides:]

    @pl.when(pl.program_id(0) == 0)
    def _():
        assemble_rows(links_shape, at_ref, own_ref, core_ref, pieces, whole_ref)

    out_ref[...] = dot(rows_ref[...], whole_ref[...])


def whole_spec(array):
    return pl.BlockSpec(array.shape, lambda b: (0,) * array.ndim)


def project_call(links_shape, place, own, core, pieces, rows, tokens):
    columns, depth = own.shape[1], rows.shape[1]
    operands = [own, core, *pieces]
    return pl.pallas_call(
        functools.partial(project_kernel, links_shape),
        grid=(rows.shape[0] // tokens,),
        in_specs=[pl.BlockSpec(memory_space=pltpu.SMEM)]
        + [whole_spec(array) for array in operands]
        + [pl.BlockSpec((tokens, depth), lambda b: (b, 0))],
        out_specs=[
            pl.BlockSpec((depth, columns), lambda b: (0, 0)),
            pl.BlockSpec((tokens, columns), lambda b: (b, 0)),
        ],
        out_shape=[
            jax.ShapeDtypeStruct((depth, columns), BF16),
            jax.ShapeDtypeStruct((rows.shape[0], columns), F32),
        ],
        compiler_params=pltpu.CompilerParams(vmem_limit_bytes=40 * 1024 * 1024),
        cost_estimate=pl.CostEstimate(
            flops=2 * rows.size * columns, bytes_accessed=2 * rows.size, transcendentals=0
        ),
        name="project",
    )(place, *operands, rows)


def branch_back_kernel(links_shape, at_ref, own_ref, core_ref, *refs):
    sides = links_shape[0]
    pieces = refs[:sides]
    rows_refs = refs[sides : sides + 4]
    gate_ref, ssd_ref, cw_ref, whole_ref, out_ref, sums_ref = refs[sides + 4 :]
    block = pl.program_id(0)

    @pl.when(block == 0)
    def _():
        assemble_rows(links_shape, at_ref, own_ref, core_ref, pieces, whole_ref)

    for at, rows_ref in enumerate(rows_refs):

        @pl.when(block == at)
        def _():
            out_ref[...] = dot(rows_ref[...], whole_ref[...])

    tokens, width = out_ref.shape
    sums_ref[...] = jnp.zeros_like(sums_ref)
    for start in range(0, tokens, CHUNK):
        squares = jnp.zeros((CHUNK, LANES), F32)
        products = jnp.zeros((CHUNK, LANES), F32)
        for left in range(0, width, LANES):
            tile = (slice(start, start + CHUNK), slice(left, left + LANES))
            gate = gate_ref[tile]
            gated = ssd_ref[tile] * (gate * sigmoid(gate))
            squares = squares + gated * gated
            products = products + gated * (cw_ref[6:7, left : left + LANES] * out_ref[tile])
        sums_ref[0:1, start : start + CHUNK] = jnp.sum(squares.T, axis=0, keepdims=True)
        sums_ref[1:2, start : start + CHUNK] = jnp.sum(products.T, axis=0, keepdims=True)


def branch_back_call(links_shape, place, own, core, pieces, rows, gate, ssd_out, conv_rows):
    columns = own.shape[1]
    tokens, depth = rows[0].shape
    operands = [own, core, *pieces, *rows]
    return pl.pallas_call(
        functools.partial(branch_back_kernel, links_shape),
        grid=(4,),
        in_specs=[pl.BlockSpec(memory_space=pltpu.SMEM)]
        + [whole_spec(array) for array in operands]
        + [
            pl.BlockSpec((tokens, columns), lambda b: (b, 0)),
            pl.BlockSpec((tokens, columns), lambda b: (b, 0)),
            pl.BlockSpec((8, columns), lambda b: (0, 0)),
        ],
        out_specs=[
            pl.BlockSpec((depth, columns), lambda b: (0, 0)),
            pl.BlockSpec((tokens, columns), lambda b: (b, 0)),
            pl.BlockSpec((8, tokens), lambda b: (0, b)),
        ],
        out_shape=[
            jax.ShapeDtypeStruct((depth, columns), BF16),
            jax.ShapeDtypeStruct((4 * tokens, columns), F32),
            jax.ShapeDtypeStruct((8, 4 * tokens), F32),
        ],
        compiler_params=pltpu.CompilerParams(vmem_limit_bytes=56 * 1024 * 1024),
        cost_estimate=pl.CostEstimate(
            flops=8 * tokens * depth * columns, bytes_accessed=8 * tokens * depth, transcendentals=0
        ),
        name="branch_back",
    )(place, *operands, gate, ssd_out, conv_rows)


def gating_back_kernel(
    inner, sums_ref, core_ref, side_ref, both_ref, gate_ref, ssd_ref, db_ref, cw_ref,
    branch_ref, dgate_ref, dssd_ref, gain_ref
):
    @pl.when(pl.program_id(0) == 0)
    def _():
        gain_ref[...] = jnp.zeros_like(gain_ref)

    sums = sums_ref[...] + core_ref[...] + side_ref[...] + both_ref[...]
    scale_row = lax.rsqrt(sums[0:1, :] * (1.0 / inner) + EPS)
    cross_row = scale_row * scale_row * scale_row * (sums[1:2, :] * (1.0 / inner))
    tokens, width = gate_ref.shape
    for start in range(0, tokens, CHUNK):
        stacked = jnp.concatenate(
            [scale_row[:, start : start + CHUNK], cross_row[:, start : start + CHUNK],
             jnp.zeros((CHUNK - 2, CHUNK), F32)], axis=0
        ).T
        scale, cross = stacked[:, 0:1], stacked[:, 1:2]
        for left in range(0, width, LANES):
            columns = slice(left, left + LANES)
            tile = (slice(start, start + CHUNK), columns)
            gate, ssd, d_branch = gate_ref[tile], ssd_ref[tile], db_ref[tile]
            gain = cw_ref[6:7, columns]
            sig = sigmoid(gate)
            act = gate * sig
            gated = ssd * act
            scaled = gated * scale
            branch_ref[tile] = (scaled * gain).astype(BF16)
            gain_ref[0:1, columns] += jnp.sum(d_branch * scaled, axis=0, keepdims=True)
            d_gated = scale * (gain * d_branch) - gated * cross
            dssd_ref[tile] = d_gated * act
            dgate_ref[tile] = (d_gated * ssd * (sig * (1.0 + gate * (1.0 - sig)))).astype(BF16)


def gating_back_call(inner, sums, gate, ssd_out, d_branch, conv_rows):
    rows, columns = gate.shape
    tokens = rows // 4
    block = pl.BlockSpec((tokens, columns), lambda b: (b, 0))
    order = [lambda b: (0, b)]
    order.append(lambda b: (0, b + 1 - 2 * lax.rem(b, 2)))
    order.append(lambda b: (0, lax.rem(b + 2, 4)))
    order.append(lambda b: (0, 3 - b))
    return pl.pallas_call(
        functools.partial(gating_back_kernel, inner),
        grid=(4,),
        in_specs=[pl.BlockSpec((8, tokens), index) for index in order]
        + [block, block, block, pl.BlockSpec((8, columns), lambda b: (0, 0))],
        out_specs=[block, block, block, pl.BlockSpec((8, columns), lambda b: (0, 0))],
        out_shape=[
            jax.ShapeDtypeStruct((rows, columns), BF16),
            jax.ShapeDtypeStruct((rows, columns), BF16),
            jax.ShapeDtypeStruct((rows, columns), F32),
            jax.ShapeDtypeStruct((8, columns), F32),
        ],
        compiler_params=pltpu.CompilerParams(vmem_limit_bytes=40 * 1024 * 1024),
        cost_estimate=pl.CostEstimate(
            flops=20 * rows * columns, bytes_accessed=20 * rows * columns, transcendentals=0
        ),
        name="gating_back",
    )(*sums, gate, ssd_out, d_branch, conv_rows)


def normalize_kernel(*refs):
    rows_refs, (gain_ref, normed_ref, scale_ref) = refs[:4], refs[4:]
    for at, rows_ref in enumerate(rows_refs):

        @pl.when(pl.program_id(0) == at)
        def _():
            depth = rows_ref.shape[1]
            for start in range(0, rows_ref.shape[0], 64):
                rows = rows_ref[start : start + 64, :].astype(F32)
                mean = jnp.sum(rows * rows, axis=1, keepdims=True) * (1.0 / depth)
                scale = lax.rsqrt(mean + EPS)
                normed = rows * scale * gain_ref[0:1, :]
                normed_ref[start : start + 64, :] = normed.astype(BF16)
                scale_ref[start : start + 64, :] = jnp.broadcast_to(scale, (64, LANES))


def normalize_call(blocks, gain):
    tokens, depth = blocks[0].shape
    return pl.pallas_call(
        normalize_kernel,
        grid=(4,),
        in_specs=[whole_spec(block) for block in blocks] + [whole_spec(gain)],
        out_specs=[
            pl.BlockSpec((tokens, depth), lambda b: (b, 0)),
            pl.BlockSpec((tokens, LANES), lambda b: (b, 0)),
        ],
        out_shape=[
            jax.ShapeDtypeStruct((4 * tokens, depth), BF16),
            jax.ShapeDtypeStruct((4 * tokens, LANES), F32),
        ],
        compiler_params=pltpu.CompilerParams(vmem_limit_bytes=40 * 1024 * 1024),
        name="normalize",
    )(*blocks, gain)


def weight_grad_kernel(links_shape, at_ref, left_ref, right_ref, *refs):
    sides = links_shape[0]
    outs, scratch = refs[:sides], refs[sides]
    scratch[...] = lax.dot_general(
        left_ref[...], right_ref[...], (((0,), (0,)), ((), ())), preferred_element_type=F32
    ).astype(BF16)
    chips, part = outs[0].shape[0], outs[0].shape[1]
    for chip in range(chips):
        for j, out in enumerate(outs):
            at = (chip * sides + lax.rem(at_ref[0] + j, sides)) * part
            out[chip] = scratch[pl.ds(pl.multiple_of(at, 16), part), :]


def weight_grad_call(links_shape, place, left, right):
    sides, groups = links_shape
    tokens, depth = left.shape
    columns = right.shape[1]
    rows = depth // groups
    part = rows // sides
    chips = 1
    while chips * rows % LANES:
        chips += 1
    return pl.pallas_call(
        functools.partial(weight_grad_kernel, links_shape),
        grid=(groups // chips,),
        in_specs=[
            pl.BlockSpec(memory_space=pltpu.SMEM),
            pl.BlockSpec((tokens, chips * rows), lambda b: (0, b)),
            pl.BlockSpec((tokens, columns), lambda b: (0, 0)),
        ],
        out_specs=[pl.BlockSpec((chips, part, columns), lambda b: (b, 0, 0))] * sides,
        out_shape=[jax.ShapeDtypeStruct((groups, part, columns), BF16)] * sides,
        scratch_shapes=[pltpu.VMEM((chips * rows, columns), BF16)],
        compiler_params=pltpu.CompilerParams(vmem_limit_bytes=40 * 1024 * 1024),
        cost_estimate=pl.CostEstimate(
            flops=2 * left.size * columns, bytes_accessed=2 * left.size, transcendentals=0
        ),
        name="weight_grad",
    )(place, left, right)


def forward_call(heads, size, lengths, conv_in, keys_queries, conv_rows, head_rows):
    blocks = lengths.shape[0]
    total = conv_in.shape[0]
    tokens = total // blocks
    width = heads * size
    state = keys_queries.shape[1] // 2
    boundaries = tokens // CHUNK - 1
    return pl.pallas_call(
        functools.partial(forward_kernel, heads, size),
        grid=(blocks,),
        in_specs=[
            pl.BlockSpec(memory_space=pltpu.SMEM),
            pl.BlockSpec((tokens, width), lambda b: (b, 0)),
            pl.BlockSpec((tokens, LANES), lambda b: (b, width // LANES)),
            pl.BlockSpec((tokens, 2 * state), lambda b: (b, 0)),
            pl.BlockSpec((8, width), lambda b: (0, 0)),
            pl.BlockSpec((8, LANES), lambda b: (0, 0)),
        ],
        out_specs=[
            pl.BlockSpec((tokens, width), lambda b: (b, 0)),
            pl.BlockSpec((1, boundaries, state, width), lambda b: (b, 0, 0, 0)),
        ],
        out_shape=[
            jax.ShapeDtypeStruct((total, width), F32),
            jax.ShapeDtypeStruct((blocks, boundaries, state, width), BF16),
        ],
        scratch_shapes=[pltpu.VMEM((state, width), F32)],
        compiler_params=pltpu.CompilerParams(vmem_limit_bytes=40 * 1024 * 1024),
        cost_estimate=pl.CostEstimate(
            flops=blocks * 3_000_000_000, bytes_accessed=blocks * 8_000_000, transcendentals=0
        ),
        name="ssd_forward",
    )(lengths, conv_in, conv_in, keys_queries, conv_rows, head_rows)


def backward_call(
    heads, size, part, lengths, conv_in, keys_queries, d_out, states, conv_rows, head_rows
):
    blocks = lengths.shape[0]
    total = conv_in.shape[0]
    tokens = total // blocks
    width = heads * size
    steps_at = d_out.shape[1] // LANES
    state = keys_queries.shape[1] // 2
    boundaries = tokens // CHUNK - 1
    return pl.pallas_call(
        functools.partial(backward_kernel, heads, size, part * heads),
        grid=(blocks,),
        in_specs=[
            pl.BlockSpec(memory_space=pltpu.SMEM),
            pl.BlockSpec((tokens, width), lambda b: (b, part)),
            pl.BlockSpec((tokens, LANES), lambda b: (b, steps_at)),
            pl.BlockSpec((tokens, 2 * state), lambda b: (b, 0)),
            pl.BlockSpec((tokens, width), lambda b: (b, part)),
            pl.BlockSpec((1, boundaries, state, width), lambda b: (b, 0, 0, part)),
            pl.BlockSpec((8, width), lambda b: (0, part)),
            pl.BlockSpec((8, LANES), lambda b: (0, 0)),
        ],
        out_specs=[
            pl.BlockSpec((tokens, width), lambda b: (b, 0)),
            pl.BlockSpec((tokens, LANES), lambda b: (b, 0)),
            pl.BlockSpec((tokens, 2 * state), lambda b: (b, 0)),
            pl.BlockSpec((8, width), lambda b: (0, 0)),
            pl.BlockSpec((8, LANES), lambda b: (0, 0)),
        ],
        out_shape=[
            jax.ShapeDtypeStruct((total, width), BF16),
            jax.ShapeDtypeStruct((total, LANES), BF16),
            jax.ShapeDtypeStruct((total, 2 * state), F32),
            jax.ShapeDtypeStruct((8, width), F32),
            jax.ShapeDtypeStruct((8, LANES), F32),
        ],
        scratch_shapes=[
            pltpu.VMEM((state, width), F32),
            pltpu.VMEM((tokens + 8, width), F32),
            pltpu.VMEM((CHUNK, width), BF16),
            pltpu.VMEM((CHUNK, width), BF16),
        ],
        compiler_params=pltpu.CompilerParams(vmem_limit_bytes=48 * 1024 * 1024),
        cost_estimate=pl.CostEstimate(
            flops=blocks * 6_000_000_000, bytes_accessed=blocks * 8_000_000, transcendentals=0
        ),
        name="ssd_backward",
    )(lengths, conv_in, conv_in, keys_queries, d_out, states, conv_rows, head_rows)


def after(values):
    return lax.optimization_barrier(values)


def phase(sends, work=None, arguments=()):
    values, arguments = after(([value for _, value in sends], arguments))
    moved = [send(value) for (send, _), value in zip(sends, values)]
    done = work(*arguments) if work else ()
    return after((moved, done))


def total(first, others):
    result = first.astype(F32)
    for other in others:
        result = result + other.astype(F32)
    return result


class Links:
    def __init__(self, reps, shards):
        self.reps, self.shards = reps, shards
        self.sides, self.groups = reps // 2, shards // 2
        rep, shard = lax.axis_index("rep"), lax.axis_index("fsdp")
        self.rep, self.shard = rep, shard
        self.a, self.x = rep // 2, rep % 2
        self.g, self.c = shard // 2, shard % 2

    def send(self, value, target):
        pairs = []
        for r in range(self.reps):
            for f in range(self.shards):
                to_r, to_f = target(r, f)
                pairs.append((r * self.shards + f, to_r * self.shards + to_f))
        return lax.ppermute(value, ("rep", "fsdp"), pairs)

    def core(self, value):
        return self.send(value, lambda r, f: (r, f ^ 1))

    def side(self, value):
        return self.send(value, lambda r, f: (r ^ 1, f))

    def corner(self, value):
        return self.send(value, lambda r, f: (r ^ 1, f ^ 1))

    def along_a(self, value, by):
        return self.send(value, lambda r, f: (((r // 2 + by) % self.sides) * 2 + r % 2, f))

    def along_g(self, value, by):
        return self.send(value, lambda r, f: (r, ((f // 2 + by) % self.groups) * 2 + f % 2))

    def flip(self, value, bit_of_rep, bit_of_shard):
        return self.send(value, lambda r, f: (r ^ bit_of_rep, f ^ bit_of_shard))

    def round_g(self, piece):
        return [self.along_g(piece, k) for k in range(1, self.groups)]

    def piece_of(self, mine, from_core):
        if self.sides == 2:
            return jnp.where(self.a == self.c, mine, from_core)
        is_high = self.c == 1
        chip = jnp.concatenate(
            [jnp.where(is_high, from_core, mine), jnp.where(is_high, mine, from_core)], axis=0
        )
        part = chip.shape[0] // self.sides
        return lax.dynamic_slice_in_dim(chip, self.a * part, part, 0)

    def round_a(self, joined):
        return [self.along_a(joined, j) for j in range(1, self.sides)]

    def assemble(self, mine, from_core, joined, rounds):
        rows, columns = mine.shape
        part = 2 * rows // self.sides
        whole = jnp.zeros((rows * self.shards, columns), mine.dtype)
        base = self.g * 2 * rows
        whole = lax.dynamic_update_slice_in_dim(whole, mine, base + self.c * rows, 0)
        whole = lax.dynamic_update_slice_in_dim(whole, from_core, base + (1 - self.c) * rows, 0)
        for k in range(1, self.groups):
            base = ((self.g - k) % self.groups) * 2 * rows
            for j, pieces in enumerate([joined] + rounds):
                piece = pieces[(k - 1) * part : k * part]
                at = base + ((self.a - j) % self.sides) * part
                whole = lax.dynamic_update_slice_in_dim(whole, piece, at, 0)
        return whole

    def parts_for_a(self, view):
        axis = view.ndim - 3
        mine = lax.dynamic_index_in_dim(view, self.a, axis, keepdims=False)
        others = [
            lax.dynamic_index_in_dim(view, (self.a + j) % self.sides, axis, keepdims=False)
            for j in range(1, self.sides)
        ]
        return mine, others

    def parts_for_g(self, view):
        mine = lax.dynamic_index_in_dim(view, self.g, 0, keepdims=False)
        others = [
            lax.dynamic_index_in_dim(view, (self.g + k) % self.groups, 0, keepdims=False)
            for k in range(1, self.groups)
        ]
        return mine, others

    def send_a(self, others):
        return [self.along_a(part, j + 1) for j, part in enumerate(others)]

    def send_g(self, others):
        return [self.along_g(part, k + 1) for k, part in enumerate(others)]

    def chips_of(self, partial):
        rows = partial.shape[0] // (self.groups * self.sides)
        return partial.reshape(self.groups, self.sides, rows, partial.shape[1])

    def spread_a(self, piece):
        return [self.along_a(piece, j) for j in range(1, self.sides)]

    def join_a(self, piece, others):
        if self.sides == 2:
            is_high = self.a == 1
            return jnp.concatenate(
                [jnp.where(is_high, others[0], piece), jnp.where(is_high, piece, others[0])],
                axis=0,
            )
        part = piece.shape[0]
        chip = jnp.zeros((part * self.sides, piece.shape[1]), piece.dtype)
        for j, value in enumerate([piece] + others):
            at = ((self.a - j) % self.sides) * part
            chip = lax.dynamic_update_slice_in_dim(chip, value, at, 0)
        return chip

    def join_x(self, piece, other):
        is_far = self.x == 1
        return jnp.concatenate(
            [jnp.where(is_far, other, piece), jnp.where(is_far, piece, other)], axis=1
        )

    def rows_of_core(self, chip):
        rows = chip.shape[0] // 2
        is_high = self.c == 1
        mine = jnp.where(is_high, chip[rows:], chip[:rows])
        return mine, jnp.where(is_high, chip[:rows], chip[rows:])

    def shares(self, mine, from_core):
        columns = mine.shape[1] // 2
        is_high = self.c == 1
        low = jnp.where(is_high, from_core, mine)
        high = jnp.where(is_high, mine, from_core)
        return [low[:, :columns], high[:, :columns], low[:, columns:], high[:, columns:]]

    def sum_all(self, value):
        bit = 1
        while bit < self.shards:
            value = value + self.flip(value, 0, bit)
            bit *= 2
        bit = 1
        while bit < self.reps:
            value = value + self.flip(value, bit, 0)
            bit *= 2
        return value

    def group_blocks(self, value):
        far = self.side(value)
        return [value, self.core(value), far, self.core(far)]

    def core_sum(self, partials, link_type):
        tokens = partials.shape[0] // 2
        return partials[:tokens].astype(F32) + self.core(
            partials[tokens:].astype(link_type)
        ).astype(F32)


def shift_rows(values, by):
    zeros = jnp.zeros((values.shape[0], abs(by), values.shape[2]), values.dtype)
    if by > 0:
        return jnp.concatenate([zeros, values[:, :-by]], axis=1)
    return jnp.concatenate([values[:, -by:], zeros], axis=1)


def causal_conv(inputs, begin, taps, bias):
    position = jnp.arange(inputs.shape[1], dtype=jnp.int32)[None, :]
    result = bias + taps[3] * inputs
    shifted = [inputs]
    for delay in range(1, 4):
        inside = (position - delay >= begin)[..., None]
        shifted.append(jnp.where(inside, shift_rows(inputs, delay), 0.0))
        result = result + taps[3 - delay] * shifted[delay]
    return result, shifted


def causal_conv_back(d_result, begin, taps):
    position = jnp.arange(d_result.shape[1], dtype=jnp.int32)[None, :]
    d_inputs = taps[3] * d_result
    for delay in range(1, 4):
        inside = (position - delay >= begin)[..., None]
        moved = shift_rows(jnp.where(inside, d_result, 0.0), -delay)
        d_inputs = d_inputs + taps[3 - delay] * moved
    return d_inputs


def per_device(
    reps,
    shards,
    hidden_in,
    lengths,
    norm_gain,
    in_weight,
    conv_weight,
    conv_bias,
    dt_bias,
    a_log,
    skip_gain,
    gate_gain,
    out_weight,
    cotangent,
):
    links = Links(reps, shards)
    tokens, depth = hidden_in.shape
    inner = gate_gain.shape[0] * shards
    channels = conv_bias.shape[0] * shards
    all_heads = dt_bias.shape[0] * shards
    state = (channels - inner) // 2
    size = inner // all_heads
    heads, width = all_heads // 4, inner // 4
    x, c = links.x, links.c
    p = 2 * x + c

    is_high = c == 1
    far_hidden = links.side(hidden_in)
    mine, for_core = prepare_call(
        heads, size, state, jnp.stack([x, c]).astype(jnp.int32), in_weight, out_weight
    )
    ends = jnp.cumsum(lengths[0])
    positions = jnp.arange(tokens, dtype=jnp.int32)
    is_valid = (positions < ends[1])[:, None]
    back_own = jnp.where(is_valid, cotangent, jnp.zeros_like(cotangent))

    small_in = [conv_weight, conv_bias, norm_gain, gate_gain, dt_bias, a_log, skip_gain]
    sizes = [piece.size for piece in small_in]
    length = sum(sizes)
    padded = -(-length // LANES) * LANES
    packed = jnp.concatenate([piece.reshape(-1) for piece in small_in])
    packed = jnp.pad(packed, (0, padded - length)).reshape(1, padded)
    def parameters(far_pairs):
        gathered = jnp.zeros((shards, padded), BF16)
        gathered = lax.dynamic_update_slice_in_dim(gathered, pair_packed, links.g * 2, 0)
        for k in range(1, links.groups):
            at = ((links.g - k) % links.groups) * 2
            gathered = lax.dynamic_update_slice_in_dim(gathered, far_pairs[k - 1], at, 0)
        gathered = gathered.astype(F32)
        offsets = [sum(sizes[:i]) for i in range(len(sizes) + 1)]
        parts = [gathered[:, offsets[i] : offsets[i + 1]] for i in range(len(sizes))]
        taps = parts[0].reshape(shards, 4, -1).transpose(1, 0, 2).reshape(4, channels)
        bias = parts[1].reshape(channels)
        n_gain = parts[2].reshape(depth)
        g_gain = parts[3].reshape(inner)
        head_params = jnp.stack([parts[i].reshape(-1) for i in (4, 5, 6)])

        def of_group(array, step):
            return lax.dynamic_slice_in_dim(array, p * step, step, array.ndim - 1)

        head_here = of_group(head_params, heads)
        head_rows = jnp.pad(head_here, ((0, 5), (0, LANES - heads)))
        conv_rows = jnp.concatenate(
            [
                of_group(taps[:, :inner], width),
                of_group(bias[:inner], width)[None],
                jnp.repeat(head_here[2], size)[None],
                of_group(g_gain, width)[None],
                jnp.zeros((1, width), F32),
            ],
            axis=0,
        )
        return taps, bias, n_gain, head_rows, conv_rows

    split_a, split_b = state + width + LANES, state + 2 * width + LANES

    def columns(start, stop):
        return mine[:, start:stop], from_core[:, start:stop]

    def turn(k):
        return lambda value: links.along_g(value, k)

    def rounds(joined):
        return [(lambda value, j=j: links.along_a(value, j), joined) for j in range(1, links.sides)]

    others = list(range(1, links.groups))
    few = len(others) // 2
    (from_core, packed_core, lengths_core), _ = phase(
        [(links.core, for_core), (links.core, packed), (links.core, lengths)]
    )
    piece = links.piece_of(mine, from_core)
    pair_packed = jnp.concatenate(
        [jnp.where(is_high, packed_core, packed), jnp.where(is_high, packed, packed_core)], axis=0
    )
    first = piece[:, :split_a]
    moved, _ = phase(
        [(turn(k), first) for k in others[:1]] + [(turn(k), pair_packed) for k in others]
    )
    z_first, small_far = moved[:1], moved[1:]

    moved, parameters_here = phase(
        [(turn(k), first) for k in others[1:]] + [(links.core, hidden_in)], parameters, (small_far,)
    )
    z_first, core_hidden = z_first + moved[:-1], moved[-1]
    taps, bias, n_gain, head_rows, conv_rows = parameters_here
    n_rows = jnp.broadcast_to(n_gain[None], (8, depth))
    z_kq = jnp.concatenate([part[:, :state] for part in z_first], axis=0)
    z_values = jnp.concatenate([part[:, state:] for part in z_first], axis=0)
    gate_part = piece[:, split_a:split_b]

    far_hidden, z_kq, z_values = after((far_hidden, z_kq, z_values))
    moved, _ = phase(
        rounds(z_kq)
        + [(turn(k), gate_part) for k in others[: few + 0]]
        + [(links.core, far_hidden)]
    )
    y_kq, z_gate, far_core_hidden = moved[: links.sides - 1], moved[links.sides - 1 : -1], moved[-1]
    w_kq = links.assemble(*columns(0, state), z_kq, y_kq)
    kq_columns = inner + c * state
    pair_lengths = jnp.concatenate([lengths, lengths_core], axis=0)
    pair_ends = jnp.cumsum(pair_lengths, axis=1)
    position = positions[None, :]
    begin = jnp.where(
        position >= pair_ends[:, 1:],
        pair_ends[:, 1:],
        jnp.where(position >= pair_ends[:, :1], pair_ends[:, :1], 0),
    )
    kq_taps = lax.dynamic_slice_in_dim(taps, kq_columns, state, 1)
    kq_bias = lax.dynamic_slice_in_dim(bias, kq_columns, state, 0)

    def keys_or_queries(w_kq, core_hidden, far_hidden, far_core_hidden):
        normed, scale = normalize_call(
            [hidden_in, core_hidden, far_hidden, far_core_hidden], n_rows
        )
        kq_in = dot(normed[: 2 * tokens], w_kq).reshape(2, tokens, state)
        kq_pre, kq_shifted = causal_conv(kq_in, begin, kq_taps, kq_bias)
        return scale[:tokens, :1], normed, kq_pre, kq_shifted

    moved, (scale_own, normed, kq_pre, kq_shifted) = phase(
        [(turn(k), gate_part) for k in others[few:-1]] + rounds(z_values),
        keys_or_queries,
        (w_kq, core_hidden, far_hidden, far_core_hidden),
    )
    z_gate, y_values = z_gate + moved[: 1 - links.sides], moved[1 - links.sides :]
    counts = jnp.stack([pair_lengths // 32, pair_lengths % 32], axis=2).reshape(2, 4).astype(BF16)
    counts = jnp.pad(counts, ((0, 14), (0, state - 4)))
    kq_near = jax.nn.silu(kq_pre).astype(BF16).reshape(2 * tokens, state)
    place = jnp.stack([links.a, links.g, c]).astype(jnp.int32)
    links_shape = (links.sides, links.groups)

    def project(start, stop, joined, rounds_of_it):
        operands = (*columns(start, stop), [joined, *rounds_of_it], normed)
        return functools.partial(project_call, links_shape, place, tokens=tokens), operands

    moved, (w_values, conv_in) = phase(
        [(turn(k), gate_part) for k in others[-1:]]
        + [(links.side, jnp.concatenate([kq_near, counts], axis=0))],
        *project(state, split_a, z_values, y_values),
    )
    z_gate, kq_far = z_gate + moved[:1], moved[1]
    all_counts = jnp.concatenate([counts[:2, :4], kq_far[2 * tokens : 2 * tokens + 2, :4]], axis=0)
    all_counts = all_counts.astype(jnp.int32)
    all_lengths = all_counts[:, 0::2] * 32 + all_counts[:, 1::2]
    kq_half = jnp.concatenate([kq_near, kq_far[: 2 * tokens]], axis=0)
    z_gate = jnp.concatenate(z_gate, axis=0)

    (kq_core,), _ = phase([(links.core, kq_half)])
    kq_core = kq_core.reshape(2, 2, tokens, state)[:, ::-1].reshape(4 * tokens, state)
    keys_queries = jnp.concatenate(
        [jnp.where(is_high, kq_core, kq_half), jnp.where(is_high, kq_half, kq_core)], axis=1
    )
    far_back = links.side(back_own)
    moved, (ssd_out, states) = phase(
        rounds(z_gate) + [(turn(k), piece[:, split_b:]) for k in others],
        functools.partial(forward_call, heads, size),
        (all_lengths, conv_in, keys_queries, conv_rows, head_rows),
    )
    y_gate, z_out = moved[: links.sides - 1], moved[links.sides - 1 :]
    z_out = jnp.concatenate(z_out, axis=0)

    moved, (w_gate, gate) = phase(
        rounds(z_out) + [(links.core, back_own)], *project(split_a, split_b, z_gate, y_gate)
    )
    y_out, core_back = moved[:-1], moved[-1]
    (far_core_back,), _ = phase([(links.core, far_back)])
    back_blocks = [back_own, core_back, far_back, far_core_back]
    w_out, d_branch, sums = branch_back_call(
        links_shape, place, *columns(split_b, split_b + width), [z_out, *y_out], back_blocks,
        gate, ssd_out, conv_rows,
    )
    moved, back = phase(
        [(links.core, sums), (links.side, sums), (links.corner, sums)],
        lambda *blocks: jnp.concatenate(blocks, axis=0),
        back_blocks,
    )
    branch, d_gate, d_ssd, gain_rows = gating_back_call(
        inner, [sums, *moved], gate, ssd_out, d_branch, conv_rows
    )
    grad_gate_gain = gain_rows[0]

    def weight_grad(left, right):
        return lax.dot_general(
            left, right, (((0,), (0,)), ((), ())), preferred_element_type=F32
        ).astype(BF16)

    half = heads // 2
    by_g = width // (3 * LANES) * 2 * LANES
    far_rows, near_rows = slice(2 * tokens, None), slice(0, 2 * tokens)

    def backward(part, d_out):
        return backward_call(
            half, size, part, all_lengths, conv_in, keys_queries, d_out, states, conv_rows, head_rows
        )

    def a_sends(parts):
        return [
            (lambda value, j=j: links.along_a(value, j + 1), part) for j, part in enumerate(parts)
        ]

    def g_sends(parts):
        return [(turn(k + 1), part) for k, part in enumerate(parts)]

    g_out_z = weight_grad(back, branch[:, :by_g])
    mixed_parts = dot_nt(branch, w_out).astype(BF16).reshape(2, 2, tokens, depth)
    def grad_parts(left, right):
        parts = weight_grad_call(links_shape, place, left, right)
        return parts[0], parts[1:]

    gate_mine, gate_others = grad_parts(normed, d_gate)
    out_y_mine, out_y_others = grad_parts(back, branch[:, by_g:])
    first_mine = jnp.concatenate([gate_mine, out_y_mine], axis=2)
    first_others = [jnp.concatenate(p, axis=2) for p in zip(gate_others, out_y_others)]
    out_mine, out_others = links.parts_for_g(g_out_z.reshape(links.groups, -1, by_g))
    moved, (d_in_0, d_steps_0, d_kq_0, conv_grads_0, head_grads_0) = phase(
        a_sends(first_others) + g_sends(out_others) + [(links.core, mixed_parts[:, 1])],
        functools.partial(backward, 0),
        (d_ssd,),
    )
    count_a, count_g = links.sides - 1, links.groups - 1
    first_held = total(first_mine, moved[:count_a]).astype(BF16)
    out_chip = total(out_mine, moved[count_a:-1]).astype(BF16)
    mixed_sum = mixed_parts[:, 0].astype(F32) + moved[-1].astype(F32)
    first_mine, first_others = links.parts_for_g(first_held)
    values_mine, values_others = grad_parts(normed, d_in_0)
    moved, (d_in_1, d_steps_1, d_kq_1, conv_grads_1, head_grads_1) = phase(
        g_sends(first_others) + a_sends(values_others) + [(links.side, mixed_sum[1].astype(BF16))],
        functools.partial(backward, 1),
        (d_ssd,),
    )
    first_piece = total(first_mine, moved[:count_g]).astype(BF16)
    held_0 = total(values_mine, moved[count_g:-1]).astype(BF16)
    mixed = hidden_in.astype(F32) + mixed_sum[0] + moved[-1].astype(F32)
    mixed = jnp.where(is_valid, mixed, 0.0).astype(BF16)

    d_kq_parts = (d_kq_0 + d_kq_1).reshape(2, 2, tokens, 2 * state)
    d_kq_mine = jnp.where(is_high, d_kq_parts[..., state:], d_kq_parts[..., :state])
    d_kq_core = jnp.where(is_high, d_kq_parts[..., :state], d_kq_parts[..., state:])
    d_kq_core = d_kq_core[:, ::-1].astype(BF16)
    d_steps = d_steps_0 + d_steps_1
    d_rest = jnp.concatenate([d_in_0, d_in_1, d_steps], axis=1)

    def d_normed_of(d_gate_rows, d_rest_rows):
        return (dot_nt(d_gate_rows, w_gate) + dot_nt(d_rest_rows, w_values)).astype(BF16)

    values_mine, values_others = grad_parts(normed, d_in_1)
    out_mine, out_others = links.parts_for_a(out_chip.reshape(links.sides, -1, by_g))
    moved, d_far = phase(
        [(links.core, d_kq_core)]
        + a_sends(values_others)
        + a_sends(out_others)
        + [(links.side, first_piece)],
        d_normed_of,
        (d_gate[far_rows], d_rest[far_rows]),
    )
    d_kq_sum = d_kq_mine + moved[0].astype(F32)
    held_1 = total(values_mine, moved[1 : 1 + count_a]).astype(BF16)
    out_piece = total(out_mine, moved[1 + count_a : -1]).astype(BF16)
    first_x = links.join_x(first_piece, moved[-1])

    values_mine, values_others = links.parts_for_g(jnp.concatenate([held_0, held_1], axis=2))
    d_far = d_far.reshape(2, tokens, depth)
    moved, d_near = phase(
        [(links.side, d_kq_sum[1].astype(BF16)), (links.core, d_far[1])] + g_sends(values_others),
        d_normed_of,
        (d_gate[near_rows], d_rest[near_rows]),
    )
    d_kq = d_kq_sum[0] + moved[0].astype(F32)
    d_far = total(d_far[0], [moved[1]]).astype(BF16)
    values_piece = total(values_mine, moved[2:]).astype(BF16)

    kq_sig = sigmoid(kq_pre)
    d_kq_pre = d_kq * (kq_sig * (1.0 + kq_pre * (1.0 - kq_sig)))
    d_kq_in = causal_conv_back(d_kq_pre, begin, kq_taps).astype(BF16).reshape(2 * tokens, state)
    last_piece = jnp.concatenate([out_piece, values_piece], axis=1)
    moved, _ = phase([(links.side, d_kq_in), (links.side, last_piece)] + rounds(first_x))
    quarter = state // 2
    d_kq_all = jnp.concatenate([d_kq_in, moved[0]], axis=0)
    d_tail = jnp.concatenate(
        [
            jnp.where(x == 1, d_kq_all[:, quarter:], d_kq_all[:, :quarter]),
            d_steps[:, :heads],
            jnp.zeros((4 * tokens, LANES - quarter - heads), BF16),
        ],
        axis=1,
    )
    tail_mine, tail_others = grad_parts(normed, d_tail)
    last_x = links.join_x(last_piece, moved[1])
    first_rows = links.rows_of_core(links.join_a(first_x, moved[2:]))
    d_near = (d_near.astype(F32) + dot_nt(d_kq_in, w_kq)).astype(BF16).reshape(2, tokens, depth)
    far_d = links.side(d_far)

    moved, _ = phase(
        a_sends(tail_others)
        + rounds(last_x)
        + [(links.core, first_rows[1]), (links.core, d_near[1])]
    )
    tail_held = total(tail_mine, moved[:count_a]).astype(BF16)
    last_rows = links.rows_of_core(links.join_a(last_x, moved[count_a : 2 * count_a]))
    first_shares = links.shares(first_rows[0], moved[-2])
    d_near = total(d_near[0], [moved[-1]])

    tail_mine, tail_others = links.parts_for_g(tail_held)
    moved, _ = phase(g_sends(tail_others) + [(links.core, last_rows[1])])
    tail_piece = total(tail_mine, moved[:-1]).astype(BF16)
    last_shares = links.shares(last_rows[0], moved[-1])
    moved, _ = phase(rounds(tail_piece))
    tail_rows = links.rows_of_core(links.join_a(tail_piece, moved))
    moved, _ = phase([(links.core, tail_rows[1])])
    tail_both = jnp.concatenate(
        [jnp.where(is_high, moved[0], tail_rows[0]), jnp.where(is_high, tail_rows[0], moved[0])],
        axis=1,
    )
    (tail_far,), _ = phase([(links.side, tail_both)])
    tail_low = jnp.where(x == 1, tail_far, tail_both)
    tail_high = jnp.where(x == 1, tail_both, tail_far)
    tail_shares = [tail_low[:, :LANES], tail_low[:, LANES:], tail_high[:, :LANES], tail_high[:, LANES:]]
    d_normed = d_near + far_d.astype(F32)

    own_hidden, own_scale = hidden_in.astype(F32), scale_own
    weighted = n_gain * d_normed
    inner_mean = jnp.mean(own_hidden * weighted, axis=-1, keepdims=True)
    grad_hidden = (
        back_own.astype(F32)
        + own_scale * weighted
        - own_hidden * (own_scale * own_scale * own_scale * inner_mean)
    )

    conv_grads = jnp.concatenate([conv_grads_0, conv_grads_1], axis=1)
    head_grads = head_grads_0 + head_grads_1
    small = jnp.zeros((8, channels), F32)
    small = lax.dynamic_update_slice(small, conv_grads[:5], (0, p * width))
    d_kq_rows = [jnp.sum(kq_shifted[delay] * d_kq_pre, axis=(0, 1)) for delay in (3, 2, 1, 0)]
    d_kq_rows = jnp.stack(d_kq_rows + [jnp.sum(d_kq_pre, axis=(0, 1))])
    small = lax.dynamic_update_slice(small, d_kq_rows, (0, kq_columns))
    small = lax.dynamic_update_slice(small, grad_gate_gain[None], (5, p * width))
    grad_skip = conv_grads[5].reshape(heads, size).sum(axis=1)
    head_all = jnp.stack([head_grads[0, :heads], head_grads[1, :heads], grad_skip])
    small_heads = jnp.zeros((3, all_heads), F32)
    small_heads = lax.dynamic_update_slice(small_heads, head_all, (0, p * heads))
    small = lax.dynamic_update_slice(small, small_heads.reshape(1, -1), (7, 0))
    small = links.sum_all(small)

    def own_slice(array, count):
        return lax.dynamic_slice_in_dim(array, links.shard * count, count, array.ndim - 1)

    grad_conv = own_slice(small[:5], channels // shards)
    grad_heads = own_slice(small[7, : 3 * all_heads].reshape(3, all_heads), all_heads // shards)

    grad_in = jnp.concatenate(
        [share[:, :width] for share in first_shares]
        + [share[:, by_g:] for share in last_shares]
        + [tail_shares[i][:, :quarter] for i in (0, 2, 1, 3)]
        + [share[:, quarter : quarter + heads] for share in tail_shares],
        axis=1,
    ).astype(F32)
    out_parts = [
        part
        for first, last in zip(first_shares, last_shares)
        for part in (last[:, :by_g], first[:, width:])
    ]
    grad_norm = jnp.sum(grad_in * in_weight.astype(F32), axis=1) / norm_gain.astype(F32)
    grad_out = jnp.concatenate(out_parts, axis=1).astype(F32).T
    return (
        mixed,
        grad_hidden,
        grad_norm,
        grad_in,
        grad_conv[:4],
        grad_conv[4],
        grad_heads[0],
        grad_heads[1],
        grad_heads[2],
        own_slice(small[5, :inner], inner // shards),
        grad_out,
    )


def solution(mesh):
    return jax.shard_map(
        functools.partial(per_device, mesh.shape["rep"], mesh.shape["fsdp"]),
        mesh=mesh,
        in_specs=(
            P(("rep", "fsdp"), None),
            P(("rep", "fsdp"), None),
            P("fsdp"),
            P("fsdp", None),
            P(None, "fsdp"),
            P("fsdp"),
            P("fsdp"),
            P("fsdp"),
            P("fsdp"),
            P("fsdp"),
            P(None, "fsdp"),
            P(("rep", "fsdp"), None),
        ),
        out_specs=(
            P(("rep", "fsdp"), None),
            P(("rep", "fsdp"), None),
            P("fsdp"),
            P("fsdp", None),
            P(None, "fsdp"),
            P("fsdp"),
            P("fsdp"),
            P("fsdp"),
            P("fsdp"),
            P("fsdp"),
            P(None, "fsdp"),
        ),
        check_vma=False,
    )
```

time: 1630 us -> 565 us (0.35)
  waiting for transfers between devices: 592 us -> 116 us
  local copies, waits for them, and re-layouts: 444 us -> 105 us
  matrix products: 290 us -> 29.1 us
  Pallas kernels: 0 us -> 149 us
  blocking collectives: 110 us -> 0 us
  starting transfers between devices: 0.24 us -> 88.5 us
  other arithmetic: 134 us -> 64.3 us
  between operations: 19.7 us -> 3.37 us
    reduce_scatter x2 -> x0, waiting for transfers between devices: 383 us -> none  [the longest x1 383 us: per_device(): lax.psum_scatter(jnp.einsum('td,te->de', columns, d_proj_low, preferred_e...]
    dynamic_update_slice x14 -> x16, local copies, waits for them, and re-layouts: 275 us -> 10.9 us  [the longest x6 6.14 us: assemble(): whole = lax.dynamic_update_slice_in_dim(whole, piece, at, 0)]
    dot_general x34 -> x8, matrix products: 290 us -> 29.1 us  [the longest x6 23.2 us: dot_nt(): lax.dot_general(left, right, (((1,), (1,)), ((), ())), preferred_element_...]
    pallas_call x0 -> x14, Pallas kernels: none -> 149 us  [the longest x2 54.9 us: backward_call(): pl.pallas_call(functools.partial(backward_kernel, heads, size, part * hea...]
    ppermute x0 -> x69, waiting for transfers between devices: none -> 116 us  [send(): return lax.ppermute(value, ('rep', 'fsdp'), pairs)]
    psum x1 -> x0, waiting for transfers between devices: 105 us -> none  [per_device(): lax.psum((part_in, part_out, s_kernel, s_offsets, s_bias, s_decay, s_skip...]
    all_gather x2 -> x0, waiting for transfers between devices: 103 us -> none  [the longest x1 103 us: per_device(): lax.all_gather(in_weight, 'fsdp', axis=0, tiled=True)]
    ppermute x0 -> x69, starting transfers between devices: none -> 88.5 us  [send(): return lax.ppermute(value, ('rep', 'fsdp'), pairs)]
  transfers between devices with their start and end apart: 6 -> 69, of which waited for: 3 -> 22; matrix products, arithmetic and copies ran while one was open for 53% -> 18% of each run, Pallas kernels for 0% -> 17%
where the time goes in v1:
time: 565 us; the launch traced here: 555 us
  Pallas kernels  149 us (26%)
  waiting for transfers between devices  116 us (21%)
  local copies, waits for them, and re-layouts  105 us (19%)
  starting transfers between devices  88.5 us (16%)
  other arithmetic  64.3 us (11%)
  matrix products  29.1 us (5%)
    ppermute x69, waiting for transfers between devices, send(): return lax.ppermute(value, ('rep', 'fsdp'), pairs)  116 us
    ppermute x69, starting transfers between devices, send(): return lax.ppermute(value, ('rep', 'fsdp'), pairs)  88.5 us
    pallas_call x2, Pallas kernels, backward_call(): pl.pallas_call(functools.partial(backward_kernel, heads, size, part * hea...  54.9 us
    unnamed x311, local copies, waits for them, and re-layouts  44.6 us
    pallas_call x5, Pallas kernels, weight_grad_call(): pl.pallas_call(functools.partial(weight_grad_kernel, links_shape), grid=(...  25.5 us
    dot_general x6, matrix products, dot_nt(): lax.dot_general(left, right, (((1,), (1,)), ((), ())), preferred_element_...  23.2 us
    pallas_call x1, Pallas kernels, forward_call(): pl.pallas_call(functools.partial(forward_kernel, heads, size), grid=(bloc...  20.1 us
    pallas_call x2, Pallas kernels, project_call(): pl.pallas_call(functools.partial(project_kernel, links_shape), grid=(rows...  16.5 us
  transfers between devices with their start and end apart: 69, of which 22 were waited for; matrix products, arithmetic and copies ran while one was open for 18% of the time, Pallas kernels for 17%

profile of v1, /device:TPU:0, one launch (start us, length us, event | category | flops | bytes accessed | tf_op | source)
XLA Modules:
  0.0 555.0 jit_solution(5881588874205537713)
XLA Ops:
  43.4 15.6 %collective-permute-done.8 = bf16[192,1024]{1,0:T(8,128)(2,1)} collective-permute-done((bf16[192,1024]{1,0:T(8,128)(2,1)}, bf16[192,1024]{1,0:T(8,128)(2,1)}, u32[]{:S(2)}, u32[]{:S(2)}) %collective-permute-start.8) | collective-permute-done | bytes 393248 | tf_op jit(solution)/shard_map/ppermute | solution.py:711
  71.8 9.0 %collective-permute-start.12 = (bf16[192,768]{1,0:T(8,128)(2,1)}, bf16[192,768]{1,0:T(8,128)(2,1)S(1)}, u32[]{:S(2)}, u32[]{:S(2)}) collective-permute-start(bf16[192,768]{1,0:T(8,128)(2,1)} %get-tuple-element.275), channel_id=1, source_target_pairs={{0,2},{1,3},{2,4},{3,5},{4,6},{5,7},{6,0},{7,1},{8,10},{9,11},{10,... | collective-permute-start | bytes 884744 | tf_op jit(solution)/shard_map/ppermute | solution.py:711
  106.9 5.6 %collective-permute-done.14 = bf16[192,768]{1,0:T(8,128)(2,1)S(1)} collective-permute-done((bf16[192,768]{1,0:T(8,128)(2,1)}, bf16[192,768]{1,0:T(8,128)(2,1)S(1)}, u32[]{:S(2)}, u32[]{:S(2)}) %collective-permute-start.14) | collective-permute-done | bytes 294944 | tf_op jit(solution)/shard_map/ppermute | solution.py:711
  112.6 6.9 %collective-permute-done.15.refs_1_ = bf16[576,896]{1,0:T(8,128)(2,1)S(1)} collective-permute-done((bf16[576,896]{1,0:T(8,128)(2,1)}, bf16[576,896]{1,0:T(8,128)(2,1)S(1)}, u32[]{:S(2)}, u32[]{:S(2)}) %collective-permute-start.15) | collective-permute-done | bytes 1032224 | tf_op jit(solution)/shard_map/ppermute | solution.py:711
  122.8 9.3 %project.2 = (bf16[1536,896]{1,0:T(8,128)(2,1)S(1)}, f32[2048,896]{1,0:T(8,128)}) custom-call(s32[3]{0:T(128)S(1)} %pad_add_fusion.2.at_ref, bf16[192,896]{1,0:T(8,128)(2,1)S(1)} %slice.431.own_ref, bf16[192,896]{1,0:T(8,128)(2,1)S(1)} %slice.432.core_ref, bf16[576,896]{1,0:T(8,128)(2,1)S(1)} %copy-done.21, ...), custom_call_target="tpu_custom_call" | custom-call | flops 5637144576 | bytes 6291456 | tf_op jit(solution)/shard_map/project/pallas_call | solution.py:368
  145.8 20.1 %ssd_forward.1 = (f32[2048,768]{1,0:T(8,128)S(1)}, bf16[4,3,128,768]{3,2,1,0:T(8,128)(2,1)S(1)}) custom-call(s32[4,2]{1,0:T(4,128)S(1)} %multiply_add_fusion.1.len_ref, f32[2048,896]{1,0:T(8,128)} %get-tuple-element.294.u_ref.dt_ref, f32[2048,896]{1,0:T(8,128)} %get-tuple-element.294.u_ref.dt_ref, bf16[2048,256]{1,0:T(8,128)(2,1)S(1)} %pad_maximum_fusion.3.kq_ref, ...), custom_call_target="tpu_custom_call" | custom-call | flops 12000000000 | bytes 32000000 | tf_op jit(solution)/shard_map/ssd_forward/pallas_call | solution.py:599
  174.8 7.2 %project.3 = (bf16[1536,768]{1,0:T(8,128)(2,1)S(1)}, f32[2048,768]{1,0:T(8,128)S(1)}) custom-call(s32[3]{0:T(128)S(1)} %pad_add_fusion.2.at_ref, bf16[192,768]{1,0:T(8,128)(2,1)S(1)} %copy-done.30, bf16[192,768]{1,0:T(8,128)(2,1)S(1)} %get-tuple-element.307.core_ref, bf16[576,768]{1,0:T(8,128)(2,1)S(1)} %copy-done.35, bf16[576,768]{1,0:T(8,128)(2,1)S(1)} %copy-done.49, ...), custom_call_target="tpu_custom_call" | custom-call | flops 4831838208 | bytes 6291456 | tf_op jit(solution)/shard_map/project/pallas_call | solution.py:368
  186.0 9.5 %collective-permute-done.23.refs_1_ = bf16[576,768]{1,0:T(8,128)(2,1)} collective-permute-done((bf16[576,768]{1,0:T(8,128)(2,1)}, bf16[576,768]{1,0:T(8,128)(2,1)}, u32[]{:S(2)}, u32[]{:S(2)}) %collective-permute-start.23) | collective-permute-done | bytes 884768 | tf_op jit(solution)/shard_map/ppermute | solution.py:711
  195.5 15.2 %branch_back.1 = (bf16[1536,768]{1,0:T(8,128)(2,1)}, f32[2048,768]{1,0:T(8,128)}, f32[8,2048]{1,0:T(8,128)}) custom-call(s32[3]{0:T(128)} %copy-done.37, bf16[192,768]{1,0:T(8,128)(2,1)} %get-tuple-element.541.own_ref, bf16[192,768]{1,0:T(8,128)(2,1)} %get-tuple-element.498.core_ref, bf16[576,768]{1,0:T(8,128)(2,1)} %constant_dynamic-update-slice_fusion.3.refs_0_, ...), custom_call_target="tpu_custom_call" | custom-call | flops 4831838208 | bytes 6291456 | tf_op jit(solution)/shard_map/branch_back/pallas_call | solution.py:426
  216.5 9.7 %gating_back.1 = (bf16[2048,768]{1,0:T(8,128)(2,1)S(1)}, bf16[2048,768]{1,0:T(8,128)(2,1)S(1)}, f32[2048,768]{1,0:T(8,128)S(1)}, f32[8,768]{1,0:T(8,128)S(1)}) custom-call(f32[8,2048]{1,0:T(8,128)S(1)} %copy-done.36, f32[8,2048]{1,0:T(8,128)S(1)} %collective-permute-done.27.core_ref, f32[8,2048]{1,0:T(8,128)S(1)} %collective-permute-done.28.side_ref, ...), custom_call_target="tpu_custom_call" | custom-call | flops 31457280 | bytes 31457280 | tf_op jit(solution)/shard_map/gating_back/pallas_call | solution.py:496
  240.8 7.4 %weight_grad.5 = (bf16[4,192,768]{2,1,0:T(8,128)(2,1)S(1)}, bf16[4,192,768]{2,1,0:T(8,128)(2,1)S(1)}) custom-call(s32[3]{0:T(128)S(1)} %copy-done.38, bf16[2048,1536]{1,0:T(8,128)(2,1)S(1)} %copy-done.6, bf16[2048,768]{1,0:T(8,128)(2,1)S(1)} %copy-done.12), custom_call_target="tpu_custom_call" | custom-call | flops 4831838208 | bytes 6291456 | tf_op jit(solution)/shard_map/weight_grad/pallas_call | solution.py:573
  248.2 5.4 convolution_convert_fusion
  270.8 27.4 %ssd_backward.2 = (bf16[2048,384]{1,0:T(8,128)(2,1)S(1)}, bf16[2048,128]{1,0:T(8,128)(2,1)S(1)}, f32[2048,256]{1,0:T(8,128)S(1)}, f32[8,384]{1,0:T(8,128)S(1)}, f32[8,128]{1,0:T(8,128)S(1)}) custom-call(s32[4,2]{1,0:T(4,128)S(1)} %copy-done.45, f32[2048,896]{1,0:T(8,128)} %get-tuple-element.294.u_ref.dt_ref, f32[2048,896]{1,0:T(8,128)} %get-tuple-element.294.u_ref.dt_ref, ...), custom_call_target="tpu_custom_call" | custom-call | flops 24000000000 | bytes 32000000 | tf_op jit(solution)/shard_map/ssd_backward/pallas_call | solution.py:637
  312.7 5.6 %convert_add_fusion = f32[2,512,1536]{2,1,0:T(8,128)} fusion(bf16[2,512,1536]{2,1,0:T(8,128)(2,1)} %collective-permute-done.34, bf16[2,2,512,1536]{3,2,1,0:T(8,128)(2,1)S(1)} %bitcast.145), kind=kLoop, calls=%fused_computation.2 | loop fusion | flops 4718592 | bytes 12582912 | tf_op jit(solution)/shard_map/add | solution.py:1117
  326.6 27.5 %ssd_backward.3 = (bf16[2048,384]{1,0:T(8,128)(2,1)S(1)}, bf16[2048,128]{1,0:T(8,128)(2,1)S(1)}, f32[2048,256]{1,0:T(8,128)S(1)}, f32[8,384]{1,0:T(8,128)S(1)}, f32[8,128]{1,0:T(8,128)S(1)}) custom-call(s32[4,2]{1,0:T(4,128)S(1)} %copy-done.45, f32[2048,896]{1,0:T(8,128)} %get-tuple-element.294.u_ref.dt_ref, f32[2048,896]{1,0:T(8,128)} %get-tuple-element.294.u_ref.dt_ref, ...), custom_call_target="tpu_custom_call" | custom-call | flops 24000000000 | bytes 32000000 | tf_op jit(solution)/shard_map/ssd_backward/pallas_call | solution.py:637
  370.0 5.4 weight_grad.8
  388.4 10.5 %collective-permute-done.42 = bf16[192,512]{1,0:T(8,128)(2,1)S(1)} collective-permute-done((bf16[192,512]{1,0:T(8,128)(2,1)S(1)}, bf16[192,512]{1,0:T(8,128)(2,1)S(1)}, u32[]{:S(2)}, u32[]{:S(2)}) %collective-permute-start.42) | collective-permute-done | bytes 196640 | tf_op jit(solution)/shard_map/ppermute | solution.py:711
  414.2 10.1 %collective-permute-done.47 = bf16[192,768]{1,0:T(8,128)(2,1)S(1)} collective-permute-done((bf16[192,768]{1,0:T(8,128)(2,1)S(1)}, bf16[192,768]{1,0:T(8,128)(2,1)S(1)}, u32[]{:S(2)}, u32[]{:S(2)}) %collective-permute-start.47) | collective-permute-done | bytes 294944 | tf_op jit(solution)/shard_map/ppermute | solution.py:711
  434.6 10.6 %collective-permute-done.49 = bf16[1024,128]{1,0:T(8,128)(2,1)S(1)} collective-permute-done((bf16[1024,128]{1,0:T(8,128)(2,1)S(1)}, bf16[1024,128]{1,0:T(8,128)(2,1)S(1)}, u32[]{:S(2)}, u32[]{:S(2)}) %collective-permute-start.49) | collective-permute-done | bytes 262176 | tf_op jit(solution)/shard_map/ppermute | solution.py:711
  462.3 7.0 %collective-permute-start.65 = (f32[8,3328]{1,0:T(8,128)S(1)}, f32[8,3328]{1,0:T(8,128)S(1)}, u32[]{:S(2)}, u32[]{:S(2)}) collective-permute-start(f32[8,3328]{1,0:T(8,128)S(1)} %add.503), channel_id=1, source_target_pairs={{0,2},{1,3},{2,0},{3,1},{4,6},{5,7},{6,4},{7,5},{8,10},{9,11},{10,... | collective-permute-start | bytes 319496 | tf_op jit(solution)/shard_map/ppermute | solution.py:711
  474.5 6.2 %collective-permute-done.66 = f32[8,3328]{1,0:T(8,128)S(1)} collective-permute-done((f32[8,3328]{1,0:T(8,128)S(1)}, f32[8,3328]{1,0:T(8,128)S(1)}, u32[]{:S(2)}, u32[]{:S(2)}) %collective-permute-start.66) | collective-permute-done | bytes 106528 | tf_op jit(solution)/shard_map/ppermute | solution.py:711
  481.4 14.6 %collective-permute-done.67 = f32[8,3328]{1,0:T(8,128)S(1)} collective-permute-done((f32[8,3328]{1,0:T(8,128)S(1)}, f32[8,3328]{1,0:T(8,128)S(1)}, u32[]{:S(2)}, u32[]{:S(2)}) %collective-permute-start.67) | collective-permute-done | bytes 106528 | tf_op jit(solution)/shard_map/ppermute | solution.py:711
  517.6 7.0 %collective-permute-start.57 = (bf16[192,128]{1,0:T(8,128)(2,1)S(1)}, bf16[192,128]{1,0:T(8,128)(2,1)S(1)}, u32[]{:S(2)}, u32[]{:S(2)}) collective-permute-start(bf16[192,128]{1,0:T(8,128)(2,1)S(1)} %get-tuple-element.424), channel_id=1, source_target_pairs={{0,2},{1,3},{2,4},{3,5},{4,6},{5,7},{6,0},{7,1},{8,10},{9,11},{10,... | collective-permute-start | bytes 147464 | tf_op jit(solution)/shard_map/ppermute | solution.py:711
  527.3 5.6 %fusion.4 = (f32[512,1536]{1,0:T(8,128)}, bf16[512,1536]{1,0:T(8,128)(2,1)}) fusion(bf16[512,1536]{1,0:T(8,128)(2,1)S(1)} %copy-done.2, bf16[512,1536]{1,0:T(8,128)(2,1)} %collective-permute-done.56, bf16[512,1536]{1,0:T(8,128)(2,1)} %collective-permute-done.55, f32[512]{0:T(512)S(1)} %get-tuple-element.447, f32[1536]{0:T(1024)S(1)} %copy-done.116, ...), kind=kLoop, calls=%fused_computation.15 | loop fusion | flops 14155776 | bytes 17312256 | tf_op jit(solution)/shard_map/sub | solution.py:1218
  (651 shorter events, 293.2 us)
Async XLA Ops:
  8.8 56.5 %collective-permute-start.3 = (bf16[512,1536]{1,0:T(8,128)(2,1)S(1)}, bf16[512,1536]{1,0:T(8,128)(2,1)}, u32[]{:S(2)}, u32[]{:S(2)}) collective-permute-start(bf16[512,1536]{1,0:T(8,128)(2,1)S(1)} %copy-done.2), channel_id=1, source_target_pairs={{0,8},{1,9},{2,10},{3,11},{4,12},{5,13},{6,14},{7,15},{8,0},{9,1},... | collective-permute-start | bytes 4718600 | tf_op jit(solution)/shard_map/ppermute | solution.py:711
  34.0 47.0 %collective-permute-start.25 = (bf16[512,1536]{1,0:T(8,128)(2,1)}, bf16[512,1536]{1,0:T(8,128)(2,1)}, u32[]{:S(2)}, u32[]{:S(2)}) collective-permute-start(bf16[512,1536]{1,0:T(8,128)(2,1)} %broadcast_select_fusion.refs_2_), channel_id=1, source_target_pairs={{0,8},{1,9},{2,10},{3,11},{4,12},{5,13},{6,14},{7,15},{8,0},{9,1},... | collective-permute-start | bytes 4718600 | tf_op jit(solution)/shard_map/ppermute | solution.py:711
  34.5 24.5 %collective-permute-start.10 = (bf16[512,1536]{1,0:T(8,128)(2,1)S(1)}, bf16[512,1536]{1,0:T(8,128)(2,1)}, u32[]{:S(2)}, u32[]{:S(2)}) collective-permute-start(bf16[512,1536]{1,0:T(8,128)(2,1)S(1)} %copy-done.2), channel_id=1, source_target_pairs={{0,1},{1,0},{2,3},{3,2},{4,5},{5,4},{6,7},{7,6},{8,9},{9,8},{10,11... | collective-permute-start | bytes 4718600 | tf_op jit(solution)/shard_map/ppermute | solution.py:711
  65.3 24.6 %collective-permute-start.13 = (bf16[512,1536]{1,0:T(8,128)(2,1)}, bf16[512,1536]{1,0:T(8,128)(2,1)}, u32[]{:S(2)}, u32[]{:S(2)}) collective-permute-start(bf16[512,1536]{1,0:T(8,128)(2,1)} %collective-permute-done.3.refs_2_), channel_id=1, source_target_pairs={{0,1},{1,0},{2,3},{3,2},{4,5},{5,4},{6,7},{7,6},{8,9},{9,8},{10,11... | collective-permute-start | bytes 4718600 | tf_op jit(solution)/shard_map/ppermute | solution.py:711
  81.0 92.6 %collective-permute-start.26 = (bf16[512,1536]{1,0:T(8,128)(2,1)}, bf16[512,1536]{1,0:T(8,128)(2,1)}, u32[]{:S(2)}, u32[]{:S(2)}) collective-permute-start(bf16[512,1536]{1,0:T(8,128)(2,1)} %collective-permute-done.25.refs_4_), channel_id=1, source_target_pairs={{0,1},{1,0},{2,3},{3,2},{4,5},{5,4},{6,7},{7,6},{8,9},{9,8},{10,11... | collective-permute-start | bytes 4718600 | tf_op jit(solution)/shard_map/ppermute | solution.py:711
  94.6 24.9 %collective-permute-start.15 = (bf16[576,896]{1,0:T(8,128)(2,1)}, bf16[576,896]{1,0:T(8,128)(2,1)S(1)}, u32[]{:S(2)}, u32[]{:S(2)}) collective-permute-start(bf16[576,896]{1,0:T(8,128)(2,1)} %pad_maximum_fusion.4.refs_0_), channel_id=1, source_target_pairs={{0,16},{1,17},{2,18},{3,19},{4,20},{5,21},{6,22},{7,23},{8,24},{9,... | collective-permute-start | bytes 3096584 | tf_op jit(solution)/shard_map/ppermute | solution.py:711
  140.4 29.6 %collective-permute-start.19 = (bf16[576,768]{1,0:T(8,128)(2,1)S(1)}, bf16[576,768]{1,0:T(8,128)(2,1)S(1)}, u32[]{:S(2)}, u32[]{:S(2)}) collective-permute-start(bf16[576,768]{1,0:T(8,128)(2,1)S(1)} %copy-done.35), channel_id=1, source_target_pairs={{0,16},{1,17},{2,18},{3,19},{4,20},{5,21},{6,22},{7,23},{8,24},{9,... | collective-permute-start | bytes 2654216 | tf_op jit(solution)/shard_map/ppermute | solution.py:711
  142.0 28.0 %collective-permute-start.20 = (bf16[192,768]{1,0:T(8,128)(2,1)S(1)}, bf16[192,768]{1,0:T(8,128)(2,1)S(1)}, u32[]{:S(2)}, u32[]{:S(2)}) collective-permute-start(bf16[192,768]{1,0:T(8,128)(2,1)S(1)} %copy-done.112), channel_id=1, source_target_pairs={{0,2},{1,3},{2,4},{3,5},{4,6},{5,7},{6,0},{7,1},{8,10},{9,11},{10,... | collective-permute-start | bytes 884744 | tf_op jit(solution)/shard_map/ppermute | solution.py:711
  142.5 27.5 %collective-permute-start.21 = (bf16[192,768]{1,0:T(8,128)(2,1)S(1)}, bf16[192,768]{1,0:T(8,128)(2,1)S(1)}, u32[]{:S(2)}, u32[]{:S(2)}) collective-permute-start(bf16[192,768]{1,0:T(8,128)(2,1)S(1)} %copy-done.112), channel_id=1, source_target_pairs={{0,4},{1,5},{2,6},{3,7},{4,0},{5,1},{6,2},{7,3},{8,12},{9,13},{10,... | collective-permute-start | bytes 884744 | tf_op jit(solution)/shard_map/ppermute | solution.py:711
  142.6 27.4 %collective-permute-start.22 = (bf16[192,768]{1,0:T(8,128)(2,1)S(1)}, bf16[192,768]{1,0:T(8,128)(2,1)S(1)}, u32[]{:S(2)}, u32[]{:S(2)}) collective-permute-start(bf16[192,768]{1,0:T(8,128)(2,1)S(1)} %copy-done.112), channel_id=1, source_target_pairs={{0,6},{1,7},{2,0},{3,1},{4,2},{5,3},{6,4},{7,5},{8,14},{9,15},{10,... | collective-permute-start | bytes 884744 | tf_op jit(solution)/shard_map/ppermute | solution.py:711
  259.8 41.8 %collective-permute-start.34 = (bf16[2,512,1536]{2,1,0:T(8,128)(2,1)}, bf16[2,512,1536]{2,1,0:T(8,128)(2,1)}, u32[]{:S(2)}, u32[]{:S(2)}) collective-permute-start(bf16[2,512,1536]{2,1,0:T(8,128)(2,1)} %slice_bitcast_fusion.1), channel_id=1, source_target_pairs={{0,1},{1,0},{2,3},{3,2},{4,5},{5,4},{6,7},{7,6},{8,9},{9,8},{10,11... | collective-permute-start | bytes 9437192 | tf_op jit(solution)/shard_map/ppermute | solution.py:711
  262.0 39.6 %collective-permute-start.30 = (bf16[4,192,1024]{2,1,0:T(8,128)(2,1)}, bf16[4,192,1024]{2,1,0:T(8,128)(2,1)S(1)}, u32[]{:S(2)}, u32[]{:S(2)}) collective-permute-start(bf16[4,192,1024]{2,1,0:T(8,128)(2,1)} %pad_maximum_fusion.2), channel_id=1, source_target_pairs={{0,16},{1,17},{2,18},{3,19},{4,20},{5,21},{6,22},{7,23},{8,24},{9,... | collective-permute-start | bytes 4718600 | tf_op jit(solution)/shard_map/ppermute | solution.py:711
  262.5 39.0 %collective-permute-start.31 = (bf16[384,512]{1,0:T(8,128)(2,1)}, bf16[384,512]{1,0:T(8,128)(2,1)S(1)}, u32[]{:S(2)}, u32[]{:S(2)}) collective-permute-start(bf16[384,512]{1,0:T(8,128)(2,1)} %get-tuple-element.337), channel_id=1, source_target_pairs={{0,2},{1,3},{2,4},{3,5},{4,6},{5,7},{6,0},{7,1},{8,10},{9,11},{10,... | collective-permute-start | bytes 1179656 | tf_op jit(solution)/shard_map/ppermute | solution.py:711
  264.2 37.4 %collective-permute-start.32 = (bf16[384,512]{1,0:T(8,128)(2,1)}, bf16[384,512]{1,0:T(8,128)(2,1)S(1)}, u32[]{:S(2)}, u32[]{:S(2)}) collective-permute-start(bf16[384,512]{1,0:T(8,128)(2,1)} %get-tuple-element.338), channel_id=1, source_target_pairs={{0,4},{1,5},{2,6},{3,7},{4,0},{5,1},{6,2},{7,3},{8,12},{9,13},{10,... | collective-permute-start | bytes 1179656 | tf_op jit(solution)/shard_map/ppermute | solution.py:711
  264.6 37.0 %collective-permute-start.33 = (bf16[384,512]{1,0:T(8,128)(2,1)}, bf16[384,512]{1,0:T(8,128)(2,1)S(1)}, u32[]{:S(2)}, u32[]{:S(2)}) collective-permute-start(bf16[384,512]{1,0:T(8,128)(2,1)} %get-tuple-element.339), channel_id=1, source_target_pairs={{0,6},{1,7},{2,0},{3,1},{4,2},{5,3},{6,4},{7,5},{8,14},{9,15},{10,... | collective-permute-start | bytes 1179656 | tf_op jit(solution)/shard_map/ppermute | solution.py:711
  320.5 35.9 %collective-permute-start.35 = (bf16[192,1024]{1,0:T(8,128)(2,1)}, bf16[192,1024]{1,0:T(8,128)(2,1)}, u32[]{:S(2)}, u32[]{:S(2)}) collective-permute-start(bf16[192,1024]{1,0:T(8,128)(2,1)} %get-tuple-element.354), channel_id=1, source_target_pairs={{0,2},{1,3},{2,4},{3,5},{4,6},{5,7},{6,0},{7,1},{8,10},{9,11},{10,... | collective-permute-start | bytes 1179656 | tf_op jit(solution)/shard_map/ppermute | solution.py:711
  320.6 35.8 %collective-permute-start.36 = (bf16[192,1024]{1,0:T(8,128)(2,1)S(1)}, bf16[192,1024]{1,0:T(8,128)(2,1)}, u32[]{:S(2)}, u32[]{:S(2)}) collective-permute-start(bf16[192,1024]{1,0:T(8,128)(2,1)S(1)} %get-tuple-element.355), channel_id=1, source_target_pairs={{0,4},{1,5},{2,6},{3,7},{4,0},{5,1},{6,2},{7,3},{8,12},{9,13},{10,... | collective-permute-start | bytes 1179656 | tf_op jit(solution)/shard_map/ppermute | solution.py:711
  322.2 34.2 %collective-permute-start.37 = (bf16[192,1024]{1,0:T(8,128)(2,1)S(1)}, bf16[192,1024]{1,0:T(8,128)(2,1)}, u32[]{:S(2)}, u32[]{:S(2)}) collective-permute-start(bf16[192,1024]{1,0:T(8,128)(2,1)S(1)} %get-tuple-element.356), channel_id=1, source_target_pairs={{0,6},{1,7},{2,0},{3,1},{4,2},{5,3},{6,4},{7,5},{8,14},{9,15},{10,... | collective-permute-start | bytes 1179656 | tf_op jit(solution)/shard_map/ppermute | solution.py:711
  324.4 32.0 %collective-permute-start.38 = (bf16[4,192,384]{2,1,0:T(8,128)(2,1)S(1)}, bf16[4,192,384]{2,1,0:T(8,128)(2,1)S(1)}, u32[]{:S(2)}, u32[]{:S(2)}) collective-permute-start(bf16[4,192,384]{2,1,0:T(8,128)(2,1)S(1)} %get-tuple-element.357), channel_id=1, source_target_pairs={{0,16},{1,17},{2,18},{3,19},{4,20},{5,21},{6,22},{7,23},{8,24},{9,... | collective-permute-start | bytes 1769480 | tf_op jit(solution)/shard_map/ppermute | solution.py:711
  325.9 34.6 %collective-permute-start.39 = (bf16[512,1536]{1,0:T(8,128)(2,1)S(1)}, bf16[512,1536]{1,0:T(8,128)(2,1)S(1)}, u32[]{:S(2)}, u32[]{:S(2)}) collective-permute-start(bf16[512,1536]{1,0:T(8,128)(2,1)S(1)} %fusion.8), channel_id=1, source_target_pairs={{0,8},{1,9},{2,10},{3,11},{4,12},{5,13},{6,14},{7,15},{8,0},{9,1},... | collective-permute-start | bytes 4718600 | tf_op jit(solution)/shard_map/ppermute | solution.py:711
  455.1 53.6 %collective-permute-start.55 = (bf16[512,1536]{1,0:T(8,128)(2,1)}, bf16[512,1536]{1,0:T(8,128)(2,1)}, u32[]{:S(2)}, u32[]{:S(2)}) collective-permute-start(bf16[512,1536]{1,0:T(8,128)(2,1)} %slice.535), channel_id=1, source_target_pairs={{0,1},{1,0},{2,3},{3,2},{4,5},{5,4},{6,7},{7,6},{8,9},{9,8},{10,11... | collective-permute-start | bytes 4718600 | tf_op jit(solution)/shard_map/ppermute | solution.py:711
  456.7 52.0 %collective-permute-start.56 = (bf16[512,1536]{1,0:T(8,128)(2,1)}, bf16[512,1536]{1,0:T(8,128)(2,1)}, u32[]{:S(2)}, u32[]{:S(2)}) collective-permute-start(bf16[512,1536]{1,0:T(8,128)(2,1)} %add_convert_fusion.3), channel_id=1, source_target_pairs={{0,8},{1,9},{2,10},{3,11},{4,12},{5,13},{6,14},{7,15},{8,0},{9,1},... | collective-permute-start | bytes 4718600 | tf_op jit(solution)/shard_map/ppermute | solution.py:711
  469.3 39.4 %collective-permute-start.53 = (bf16[192,2560]{1,0:T(8,128)(2,1)}, bf16[192,2560]{1,0:T(8,128)(2,1)}, u32[]{:S(2)}, u32[]{:S(2)}) collective-permute-start(bf16[192,2560]{1,0:T(8,128)(2,1)} %pad_maximum_fusion.5), channel_id=1, source_target_pairs={{0,16},{1,17},{2,18},{3,19},{4,20},{5,21},{6,22},{7,23},{8,24},{9,... | collective-permute-start | bytes 2949128 | tf_op jit(solution)/shard_map/ppermute | solution.py:711
  474.5 34.2 %collective-permute-start.54 = (bf16[192,2048]{1,0:T(8,128)(2,1)}, bf16[192,2048]{1,0:T(8,128)(2,1)}, u32[]{:S(2)}, u32[]{:S(2)}) collective-permute-start(bf16[192,2048]{1,0:T(8,128)(2,1)} %get-tuple-element.416), channel_id=1, source_target_pairs={{0,1},{1,0},{2,3},{3,2},{4,5},{5,4},{6,7},{7,6},{8,9},{9,8},{10,11... | collective-permute-start | bytes 2359304 | tf_op jit(solution)/shard_map/ppermute | solution.py:711
  (194 other events, 1824.9 us)

commit v2 on v1

--- a/solution.py
+++ b/solution.py
@@ -131,6 +131,7 @@
     heads,
     size,
     first_head,
+    first_block,
     len_ref,
     u_ref,
     dt_ref,
@@ -150,8 +151,8 @@
     source_in,
 ):
     block = pl.program_id(0)
-    first = len_ref[block, 0]
-    both = first + len_ref[block, 1]
+    first = len_ref[first_block + block, 0]
+    both = first + len_ref[first_block + block, 1]
     tokens, width = u_ref.shape
     chunks = tokens // CHUNK
     row, column = iotas(CHUNK, CHUNK)
@@ -291,10 +292,10 @@
         hg_ref[1:2, :] += jnp.sum(d_rate * rate, axis=0, keepdims=True)
 
 
-def prepare_kernel(heads, size, state, at_ref, in_ref, out_ref, mine_ref, other_ref):
+def prepare_first_kernel(heads, size, state, at_ref, in_ref, mine_ref, other_ref):
     x, core = at_ref[0], at_ref[1]
-    inner = out_ref.shape[0]
     width = heads * size
+    inner = 4 * width
     steps_at = 2 * inner + 2 * state
     steps = in_ref[:, steps_at : steps_at + 4 * heads].astype(F32)
     rows = steps.shape[0]
@@ -302,34 +303,100 @@
     column = lax.broadcasted_iota(jnp.int32, (rows, LANES), 1)
     for ref, c in ((mine_ref, core), (other_ref, 1 - core)):
         p = 2 * x + c
+        values_at = pl.multiple_of(inner + p * width, LANES)
+        ref[:, :width] = in_ref[:, pl.ds(values_at, width)]
+        drawn = pltpu.roll(steps, lax.rem(LANES - heads * p, LANES), 1)
+        ref[:, width : width + LANES] = jnp.where(column < heads, drawn, 0.0).astype(BF16)
         keys_at = pl.multiple_of(2 * inner + c * state, LANES)
-        ref[:, :state] = in_ref[:, pl.ds(keys_at, state)]
-        values_at = pl.multiple_of(inner + p * width, LANES)
-        ref[:, state : state + width] = in_ref[:, pl.ds(values_at, width)]
-        drawn = pltpu.roll(steps, lax.rem(LANES - heads * p, LANES), 1)
-        drawn = jnp.where(column < heads, drawn, 0.0).astype(BF16)
-        ref[:, state + width : state + width + LANES] = drawn
-        at = state + width + LANES
-        gate_at = pl.multiple_of(p * width, LANES)
-        ref[:, at : at + width] = in_ref[:, pl.ds(gate_at, width)]
-        ref[:, at + width : at + 2 * width] = out_ref[pl.ds(gate_at, width), :].T
-
-
-def prepare_call(heads, size, state, place, in_weight, out_weight):
-    rows = in_weight.shape[0]
-    columns = state + LANES + 3 * heads * size
+        ref[:, width + LANES : width + LANES + state] = in_ref[:, pl.ds(keys_at, state)]
+
+
+def prepare_last_kernel(width, at_ref, in_ref, out_ref, mine_ref, other_ref):
+    x, core = at_ref[0], at_ref[1]
+    for ref, c in ((mine_ref, core), (other_ref, 1 - core)):
+        at = pl.multiple_of((2 * x + c) * width, LANES)
+        ref[:, :width] = in_ref[:, pl.ds(at, width)]
+        ref[:, width:] = out_ref[pl.ds(at, width), :].T
+
+
+def prepare_call(kernel, columns, place, *weights):
+    rows = weights[0].shape[0]
     return pl.pallas_call(
-        functools.partial(prepare_kernel, heads, size, state),
+        kernel,
+        in_specs=[pl.BlockSpec(memory_space=pltpu.SMEM)]
+        + [pl.BlockSpec(memory_space=pltpu.VMEM)] * len(weights),
+        out_specs=[pl.BlockSpec(memory_space=pltpu.VMEM)] * 2,
+        out_shape=[jax.ShapeDtypeStruct((rows, columns), BF16)] * 2,
+        compiler_params=pltpu.CompilerParams(vmem_limit_bytes=24 * 1024 * 1024),
+        name="prepare",
+    )(place, *weights)
+
+
+def unpack_kernel(sizes, heads, size, state, at_ref, small_ref, n_ref, conv_ref, head_ref, kq_ref, all_ref):
+    conv_size, gate_size, norm_size, head_size = sizes
+    x, c = at_ref[0], at_ref[1]
+    p = 2 * x + c
+    shards = small_ref.shape[0] // 8
+    width = heads * size
+
+    def joined(first_row, rows, at, part, columns):
+        padded = -(-columns // LANES) * LANES
+        lanes = -(-part // LANES) * LANES
+        lane = lax.broadcasted_iota(jnp.int32, (8, lanes), 1)
+        result = jnp.zeros((8, padded), F32)
+        for f in range(shards):
+            rows_here = small_ref[8 * f : 8 * f + 8, at : at + lanes].astype(F32)
+            rows_here = jnp.where(lane < part, rows_here, 0.0)
+            if padded > lanes:
+                rows_here = jnp.concatenate(
+                    [rows_here, jnp.zeros((8, padded - lanes), F32)], axis=1
+                )
+            result = result + pltpu.roll(rows_here, (part * f) % padded, 1)
+        return result[first_row : first_row + rows]
+
+    conv_all = joined(0, 5, 0, conv_size, conv_size * shards)
+    gate_all = joined(5, 1, 0, gate_size, gate_size * shards)
+    norm_all = joined(6, 1, 0, norm_size, norm_size * shards)
+    n_ref[...] = jnp.broadcast_to(norm_all, n_ref.shape)
+    all_ref[...] = jnp.zeros_like(all_ref)
+    all_ref[0:5, : conv_all.shape[1]] = conv_all
+    all_ref[6:7, : gate_all.shape[1]] = gate_all
+    conv_ref[...] = all_ref[:, pl.ds(pl.multiple_of(p * width, LANES), width)]
+    kq_at = 4 * width + c * state
+    kq_ref[...] = all_ref[:, pl.ds(pl.multiple_of(kq_at, LANES), state)]
+    column = lax.broadcasted_iota(jnp.int32, (8, LANES), 1)
+    head_ref[...] = jnp.zeros_like(head_ref)
+    for row in range(3):
+        values = joined(7, 1, row * LANES, head_size, head_size * shards)
+        values = jnp.broadcast_to(values, (8, LANES))
+        values = pltpu.roll(values, lax.rem(LANES - heads * p, LANES), 1)
+        head_ref[row : row + 1, :] = jnp.where(column < heads, values, 0.0)[0:1]
+    row_at, column_at = iotas(LANES, width)
+    spread = (row_at == column_at // size).astype(F32)
+    conv_ref[5:6, :] = dot(head_ref[...], spread, HIGHEST)[2:3]
+
+
+def unpack_call(sizes, heads, size, state, place, small):
+    shards = small.shape[0] // 8
+    depth, width = sizes[2] * shards, heads * size
+    columns = -(-sizes[0] * shards // LANES) * LANES
+    return pl.pallas_call(
+        functools.partial(unpack_kernel, sizes, heads, size, state),
         in_specs=[
             pl.BlockSpec(memory_space=pltpu.SMEM),
             pl.BlockSpec(memory_space=pltpu.VMEM),
-            pl.BlockSpec(memory_space=pltpu.VMEM),
         ],
-        out_specs=[pl.BlockSpec(memory_space=pltpu.VMEM)] * 2,
-        out_shape=[jax.ShapeDtypeStruct((rows, columns), BF16)] * 2,
+        out_specs=[pl.BlockSpec(memory_space=pltpu.VMEM)] * 4,
+        out_shape=[
+            jax.ShapeDtypeStruct((8, depth), F32),
+            jax.ShapeDtypeStruct((8, width), F32),
+            jax.ShapeDtypeStruct((8, LANES), F32),
+            jax.ShapeDtypeStruct((8, state), F32),
+        ],
+        scratch_shapes=[pltpu.VMEM((8, columns), F32)],
         compiler_params=pltpu.CompilerParams(vmem_limit_bytes=24 * 1024 * 1024),
-        name="prepare_weights",
-    )(place, in_weight, out_weight)
+        name="unpack",
+    )(place, small)
 
 
 def assemble_rows(links_shape, at_ref, own_ref, core_ref, pieces, whole_ref):
@@ -342,14 +409,14 @@
     whole_ref[pl.ds(pl.multiple_of(base + (1 - c) * rows, 16), rows), :] = core_ref[...]
     for k in range(1, groups):
         base = lax.rem(g + groups - k, groups) * (2 * rows)
-        for j, ref in enumerate(pieces):
+        for j in range(sides):
             at = base + lax.rem(a + sides - j, sides) * part
-            whole_ref[pl.ds(pl.multiple_of(at, 16), part), :] = ref[(k - 1) * part : k * part, :]
+            piece = pieces[(k - 1) * sides + j]
+            whole_ref[pl.ds(pl.multiple_of(at, 16), part), :] = piece[...]
 
 
 def project_kernel(links_shape, at_ref, own_ref, core_ref, *refs):
-    sides = links_shape[0]
-    pieces, (rows_ref, whole_ref, out_ref) = refs[:sides], refs[sides:]
+    pieces, (rows_ref, whole_ref, out_ref) = refs[:-3], refs[-3:]
 
     @pl.when(pl.program_id(0) == 0)
     def _():
@@ -362,36 +429,39 @@
     return pl.BlockSpec(array.shape, lambda b: (0,) * array.ndim)
 
 
-def project_call(links_shape, place, own, core, pieces, rows, tokens):
-    columns, depth = own.shape[1], rows.shape[1]
-    operands = [own, core, *pieces]
+def columns_spec(array, width, index):
+    if array.shape[1] == width:
+        index = 0
+    return pl.BlockSpec((array.shape[0], width), lambda b: (0, index))
+
+
+def project_call(links_shape, width, index, blocks, tokens, place, parts, rows):
+    depth = rows.shape[1]
     return pl.pallas_call(
         functools.partial(project_kernel, links_shape),
-        grid=(rows.shape[0] // tokens,),
+        grid=(blocks,),
         in_specs=[pl.BlockSpec(memory_space=pltpu.SMEM)]
-        + [whole_spec(array) for array in operands]
+        + [columns_spec(array, width, index) for array in parts]
         + [pl.BlockSpec((tokens, depth), lambda b: (b, 0))],
         out_specs=[
-            pl.BlockSpec((depth, columns), lambda b: (0, 0)),
-            pl.BlockSpec((tokens, columns), lambda b: (b, 0)),
+            pl.BlockSpec((depth, width), lambda b: (0, 0)),
+            pl.BlockSpec((tokens, width), lambda b: (b, 0)),
         ],
         out_shape=[
-            jax.ShapeDtypeStruct((depth, columns), BF16),
-            jax.ShapeDtypeStruct((rows.shape[0], columns), F32),
+            jax.ShapeDtypeStruct((depth, width), BF16),
+            jax.ShapeDtypeStruct((blocks * tokens, width), F32),
         ],
         compiler_params=pltpu.CompilerParams(vmem_limit_bytes=40 * 1024 * 1024),
         cost_estimate=pl.CostEstimate(
-            flops=2 * rows.size * columns, bytes_accessed=2 * rows.size, transcendentals=0
+            flops=2 * rows.size * width, bytes_accessed=2 * rows.size, transcendentals=0
         ),
         name="project",
-    )(place, *operands, rows)
+    )(place, *parts, rows)
 
 
 def branch_back_kernel(links_shape, at_ref, own_ref, core_ref, *refs):
-    sides = links_shape[0]
-    pieces = refs[:sides]
-    rows_refs = refs[sides : sides + 4]
-    gate_ref, ssd_ref, cw_ref, whole_ref, out_ref, sums_ref = refs[sides + 4 :]
+    pieces, rows_refs = refs[:-10], refs[-10:-6]
+    gate_ref, ssd_ref, cw_ref, whole_ref, out_ref, sums_ref = refs[-6:]
     block = pl.program_id(0)
 
     @pl.when(block == 0)
@@ -419,36 +489,32 @@
         sums_ref[1:2, start : start + CHUNK] = jnp.sum(products.T, axis=0, keepdims=True)
 
 
-def branch_back_call(links_shape, place, own, core, pieces, rows, gate, ssd_out, conv_rows):
-    columns = own.shape[1]
+def branch_back_call(links_shape, width, index, place, parts, rows, gate, ssd_out, conv_rows):
     tokens, depth = rows[0].shape
-    operands = [own, core, *pieces, *rows]
+    block = pl.BlockSpec((tokens, width), lambda b: (b, 0))
     return pl.pallas_call(
         functools.partial(branch_back_kernel, links_shape),
         grid=(4,),
         in_specs=[pl.BlockSpec(memory_space=pltpu.SMEM)]
-        + [whole_spec(array) for array in operands]
-        + [
-            pl.BlockSpec((tokens, columns), lambda b: (b, 0)),
-            pl.BlockSpec((tokens, columns), lambda b: (b, 0)),
-            pl.BlockSpec((8, columns), lambda b: (0, 0)),
-        ],
+        + [columns_spec(array, width, index) for array in parts]
+        + [whole_spec(array) for array in rows]
+        + [block, block, pl.BlockSpec((8, width), lambda b: (0, 0))],
         out_specs=[
-            pl.BlockSpec((depth, columns), lambda b: (0, 0)),
-            pl.BlockSpec((tokens, columns), lambda b: (b, 0)),
+            pl.BlockSpec((depth, width), lambda b: (0, 0)),
+            block,
             pl.BlockSpec((8, tokens), lambda b: (0, b)),
         ],
         out_shape=[
-            jax.ShapeDtypeStruct((depth, columns), BF16),
-            jax.ShapeDtypeStruct((4 * tokens, columns), F32),
+            jax.ShapeDtypeStruct((depth, width), BF16),
+            jax.ShapeDtypeStruct((4 * tokens, width), F32),
             jax.ShapeDtypeStruct((8, 4 * tokens), F32),
         ],
         compiler_params=pltpu.CompilerParams(vmem_limit_bytes=56 * 1024 * 1024),
         cost_estimate=pl.CostEstimate(
-            flops=8 * tokens * depth * columns, bytes_accessed=8 * tokens * depth, transcendentals=0
+            flops=8 * tokens * depth * width, bytes_accessed=8 * tokens * depth, transcendentals=0
         ),
         name="branch_back",
-    )(place, *operands, gate, ssd_out, conv_rows)
+    )(place, *parts, *rows, gate, ssd_out, conv_rows)
 
 
 def gating_back_kernel(
@@ -548,45 +614,123 @@
     )(*blocks, gain)
 
 
-def weight_grad_kernel(links_shape, at_ref, left_ref, right_ref, *refs):
-    sides = links_shape[0]
-    outs, scratch = refs[:sides], refs[sides]
-    scratch[...] = lax.dot_general(
-        left_ref[...], right_ref[...], (((0,), (0,)), ((), ())), preferred_element_type=F32
-    ).astype(BF16)
-    chips, part = outs[0].shape[0], outs[0].shape[1]
+def weight_grad_kernel(links_shape, groups_of_terms, over_a, at_ref, *refs):
+    sides, groups = links_shape
+    count = sum(len(terms) for terms in groups_of_terms)
+    left_count = 1 + max(left_at for terms in groups_of_terms for left_at, _ in terms)
+    lefts, rights = refs[:left_count], refs[left_count : left_count + count]
+    outs, scratch = refs[left_count + count : -1], refs[-1]
+    at_column, at_term = 0, 0
+    for terms in groups_of_terms:
+        result = None
+        for left_at, first_row in terms:
+            right = rights[at_term][...]
+            term = lax.dot_general(
+                lefts[left_at][first_row : first_row + right.shape[0], :],
+                right,
+                (((0,), (0,)), ((), ())),
+                preferred_element_type=F32,
+            )
+            result = term if result is None else result + term
+            at_term += 1
+        width = result.shape[1]
+        scratch[:, at_column : at_column + width] = result.astype(BF16)
+        at_column += width
+    if over_a:
+        chips, part = outs[0].shape[0], outs[0].shape[1]
+        for chip in range(chips):
+            for j, out in enumerate(outs):
+                at = (chip * sides + lax.rem(at_ref[0] + j, sides)) * part
+                out[chip] = scratch[pl.ds(pl.multiple_of(at, 16), part), :]
+        return
+    rows = outs[0].shape[0]
+    chips = scratch.shape[0] // rows
     for chip in range(chips):
-        for j, out in enumerate(outs):
-            at = (chip * sides + lax.rem(at_ref[0] + j, sides)) * part
-            out[chip] = scratch[pl.ds(pl.multiple_of(at, 16), part), :]
-
-
-def weight_grad_call(links_shape, place, left, right):
+        turn = lax.rem(pl.program_id(0) * chips + chip + groups - at_ref[1], groups)
+        for k, out in enumerate(outs):
+
+            @pl.when(turn == k)
+            def _():
+                out[...] = scratch[chip * rows : (chip + 1) * rows, :]
+
+
+def weight_grad_call(links_shape, over_a, place, groups_of_terms):
     sides, groups = links_shape
-    tokens, depth = left.shape
-    columns = right.shape[1]
+    terms = [term for group in groups_of_terms for term in group]
+    depth = terms[0][0].shape[1]
+    columns = sum(group[0][5] for group in groups_of_terms)
     rows = depth // groups
     part = rows // sides
     chips = 1
     while chips * rows % LANES:
         chips += 1
+    lefts = []
+    for term in terms:
+        if not any(term[0] is left for left in lefts):
+            lefts.append(term[0])
+
+    def left_at(term):
+        return [term[0] is left for left in lefts].index(True)
+
+    def left_spec(left):
+        return pl.BlockSpec((left.shape[0], chips * rows), lambda b: (0, b))
+
+    def right_spec(term):
+        return pl.BlockSpec((term[1], term[5]), lambda b: (term[4], term[6]))
+
+    if over_a:
+        out_specs = [pl.BlockSpec((chips, part, columns), lambda b: (b, 0, 0))] * sides
+        out_shape = [jax.ShapeDtypeStruct((groups, part, columns), BF16)] * sides
+    else:
+        out_specs = [pl.BlockSpec((rows, columns), lambda b: (0, 0))] * groups
+        out_shape = [jax.ShapeDtypeStruct((rows, columns), BF16)] * groups
+    shapes = tuple(
+        tuple((left_at(term), term[1] * term[2]) for term in group) for group in groups_of_terms
+    )
     return pl.pallas_call(
-        functools.partial(weight_grad_kernel, links_shape),
+        functools.partial(weight_grad_kernel, links_shape, shapes, over_a),
         grid=(groups // chips,),
-        in_specs=[
-            pl.BlockSpec(memory_space=pltpu.SMEM),
-            pl.BlockSpec((tokens, chips * rows), lambda b: (0, b)),
-            pl.BlockSpec((tokens, columns), lambda b: (0, 0)),
-        ],
-        out_specs=[pl.BlockSpec((chips, part, columns), lambda b: (b, 0, 0))] * sides,
-        out_shape=[jax.ShapeDtypeStruct((groups, part, columns), BF16)] * sides,
+        in_specs=[pl.BlockSpec(memory_space=pltpu.SMEM)]
+        + [left_spec(left) for left in lefts]
+        + [right_spec(term) for term in terms],
+        out_specs=out_specs,
+        out_shape=out_shape,
         scratch_shapes=[pltpu.VMEM((chips * rows, columns), BF16)],
-        compiler_params=pltpu.CompilerParams(vmem_limit_bytes=40 * 1024 * 1024),
+        compiler_params=pltpu.CompilerParams(vmem_limit_bytes=48 * 1024 * 1024),
         cost_estimate=pl.CostEstimate(
-            flops=2 * left.size * columns, bytes_accessed=2 * left.size, transcendentals=0
+            flops=2 * terms[0][1] * depth * columns,
+            bytes_accessed=2 * terms[0][1] * depth,
+            transcendentals=0,
         ),
         name="weight_grad",
-    )(place, left, right)
+    )(place, *lefts, *[term[3] for term in terms])
+
+
+def combine_kernel(groups, at_ref, *refs):
+    parts, outs = refs[:-groups], refs[-groups:]
+    result = parts[0][0].astype(F32)
+    for part in parts[1:]:
+        result = result + part[0].astype(F32)
+    turn = lax.rem(pl.program_id(0) + groups - at_ref[1], groups)
+    for k, out in enumerate(outs):
+
+        @pl.when(turn == k)
+        def _():
+            out[...] = result.astype(BF16)
+
+
+def combine_call(groups, place, parts):
+    rows, columns = parts[0].shape[1:]
+    return pl.pallas_call(
+        functools.partial(combine_kernel, groups),
+        grid=(groups,),
+        in_specs=[pl.BlockSpec(memory_space=pltpu.SMEM)]
+        + [pl.BlockSpec((1, rows, columns), lambda b: (b, 0, 0))] * len(parts),
+        out_specs=[pl.BlockSpec((rows, columns), lambda b: (0, 0))] * groups,
+        out_shape=[jax.ShapeDtypeStruct((rows, columns), BF16)] * groups,
+        compiler_params=pltpu.CompilerParams(vmem_limit_bytes=24 * 1024 * 1024),
+        name="combine",
+    )(place, *parts)
 
 
 def forward_call(heads, size, lengths, conv_in, keys_queries, conv_rows, head_rows):
@@ -625,25 +769,32 @@
 
 
 def backward_call(
-    heads, size, part, lengths, conv_in, keys_queries, d_out, states, conv_rows, head_rows
+    heads, size, first_head, first_block, blocks,
+    lengths, conv_in, keys_queries, d_out, states, conv_rows, head_rows
 ):
-    blocks = lengths.shape[0]
-    total = conv_in.shape[0]
-    tokens = total // blocks
+    tokens = conv_in.shape[0] // lengths.shape[0]
+    total = blocks * tokens
     width = heads * size
+    part = first_head * size // width
     steps_at = d_out.shape[1] // LANES
     state = keys_queries.shape[1] // 2
     boundaries = tokens // CHUNK - 1
+
+    def rows_of(columns, index):
+        return pl.BlockSpec((tokens, columns), lambda b: (first_block + b, index))
+
     return pl.pallas_call(
-        functools.partial(backward_kernel, heads, size, part * heads),
+        functools.partial(backward_kernel, heads, size, first_head, first_block),
         grid=(blocks,),
         in_specs=[
             pl.BlockSpec(memory_space=pltpu.SMEM),
-            pl.BlockSpec((tokens, width), lambda b: (b, part)),
-            pl.BlockSpec((tokens, LANES), lambda b: (b, steps_at)),
-            pl.BlockSpec((tokens, 2 * state), lambda b: (b, 0)),
-            pl.BlockSpec((tokens, width), lambda b: (b, part)),
-            pl.BlockSpec((1, boundaries, state, width), lambda b: (b, 0, 0, part)),
+            rows_of(width, part),
+            rows_of(LANES, steps_at),
+            rows_of(2 * state, 0),
+            rows_of(width, part),
+            pl.BlockSpec(
+                (1, boundaries, state, width), lambda b: (first_block + b, 0, 0, part)
+            ),
             pl.BlockSpec((8, width), lambda b: (0, part)),
             pl.BlockSpec((8, LANES), lambda b: (0, 0)),
         ],
@@ -669,7 +820,9 @@
         ],
         compiler_params=pltpu.CompilerParams(vmem_limit_bytes=48 * 1024 * 1024),
         cost_estimate=pl.CostEstimate(
-            flops=blocks * 6_000_000_000, bytes_accessed=blocks * 8_000_000, transcendentals=0
+            flops=blocks * heads * 1_000_000_000,
+            bytes_accessed=blocks * 8_000_000,
+            transcendentals=0,
         ),
         name="ssd_backward",
     )(lengths, conv_in, conv_in, keys_queries, d_out, states, conv_rows, head_rows)
@@ -679,11 +832,12 @@
     return lax.optimization_barrier(values)
 
 
-def phase(sends, work=None, arguments=()):
+def phase(sends, work=None, arguments=(), until=None):
     values, arguments = after(([value for _, value in sends], arguments))
     moved = [send(value) for (send, _), value in zip(sends, values)]
     done = work(*arguments) if work else ()
-    return after((moved, done))
+    moved, done, until = after((moved, done, until))
+    return (moved, done) if until is None else (moved, done, until)
 
 
 def total(first, others):
@@ -724,6 +878,11 @@
 
     def along_g(self, value, by):
         return self.send(value, lambda r, f: (r, ((f // 2 + by) % self.groups) * 2 + f % 2))
+
+    def diagonal(self, value, by):
+        return self.send(
+            value, lambda r, f: (((r // 2 + by) % self.sides) * 2 + (r % 2 ^ 1), f)
+        )
 
     def flip(self, value, bit_of_rep, bit_of_shard):
         return self.send(value, lambda r, f: (r ^ bit_of_rep, f ^ bit_of_shard))
@@ -899,99 +1058,128 @@
     x, c = links.x, links.c
     p = 2 * x + c
 
-    is_high = c == 1
+    is_high, is_far = c == 1, x == 1
     far_hidden = links.side(hidden_in)
-    mine, for_core = prepare_call(
-        heads, size, state, jnp.stack([x, c]).astype(jnp.int32), in_weight, out_weight
-    )
     ends = jnp.cumsum(lengths[0])
     positions = jnp.arange(tokens, dtype=jnp.int32)
     is_valid = (positions < ends[1])[:, None]
     back_own = jnp.where(is_valid, cotangent, jnp.zeros_like(cotangent))
-
-    small_in = [conv_weight, conv_bias, norm_gain, gate_gain, dt_bias, a_log, skip_gain]
-    sizes = [piece.size for piece in small_in]
-    length = sum(sizes)
-    padded = -(-length // LANES) * LANES
-    packed = jnp.concatenate([piece.reshape(-1) for piece in small_in])
-    packed = jnp.pad(packed, (0, padded - length)).reshape(1, padded)
-    def parameters(far_pairs):
-        gathered = jnp.zeros((shards, padded), BF16)
-        gathered = lax.dynamic_update_slice_in_dim(gathered, pair_packed, links.g * 2, 0)
-        for k in range(1, links.groups):
-            at = ((links.g - k) % links.groups) * 2
-            gathered = lax.dynamic_update_slice_in_dim(gathered, far_pairs[k - 1], at, 0)
-        gathered = gathered.astype(F32)
-        offsets = [sum(sizes[:i]) for i in range(len(sizes) + 1)]
-        parts = [gathered[:, offsets[i] : offsets[i + 1]] for i in range(len(sizes))]
-        taps = parts[0].reshape(shards, 4, -1).transpose(1, 0, 2).reshape(4, channels)
-        bias = parts[1].reshape(channels)
-        n_gain = parts[2].reshape(depth)
-        g_gain = parts[3].reshape(inner)
-        head_params = jnp.stack([parts[i].reshape(-1) for i in (4, 5, 6)])
-
-        def of_group(array, step):
-            return lax.dynamic_slice_in_dim(array, p * step, step, array.ndim - 1)
-
-        head_here = of_group(head_params, heads)
-        head_rows = jnp.pad(head_here, ((0, 5), (0, LANES - heads)))
-        conv_rows = jnp.concatenate(
-            [
-                of_group(taps[:, :inner], width),
-                of_group(bias[:inner], width)[None],
-                jnp.repeat(head_here[2], size)[None],
-                of_group(g_gain, width)[None],
-                jnp.zeros((1, width), F32),
-            ],
-            axis=0,
+    sides, groups = links.sides, links.groups
+    links_shape = (sides, groups)
+    place = jnp.stack([links.a, links.g, c]).astype(jnp.int32)
+
+    lanes = max(conv_weight.shape[1], gate_gain.shape[0], norm_gain.shape[0], 3 * LANES)
+    lanes = -(-lanes // LANES) * LANES
+
+    def pack(conv_weight, conv_bias, gate_gain, norm_gain, *head_values):
+        heads_row = jnp.concatenate(
+            [jnp.pad(v, (0, LANES - v.shape[0])) for v in head_values]
         )
-        return taps, bias, n_gain, head_rows, conv_rows
-
-    split_a, split_b = state + width + LANES, state + 2 * width + LANES
-
-    def columns(start, stop):
-        return mine[:, start:stop], from_core[:, start:stop]
-
-    def turn(k):
-        return lambda value: links.along_g(value, k)
-
-    def rounds(joined):
-        return [(lambda value, j=j: links.along_a(value, j), joined) for j in range(1, links.sides)]
-
-    others = list(range(1, links.groups))
-    few = len(others) // 2
-    (from_core, packed_core, lengths_core), _ = phase(
-        [(links.core, for_core), (links.core, packed), (links.core, lengths)]
-    )
-    piece = links.piece_of(mine, from_core)
-    pair_packed = jnp.concatenate(
-        [jnp.where(is_high, packed_core, packed), jnp.where(is_high, packed, packed_core)], axis=0
-    )
-    first = piece[:, :split_a]
+        rows = [conv_bias, gate_gain, norm_gain, heads_row[:lanes]]
+        rows = [jnp.pad(row, (0, lanes - row.shape[0]))[None] for row in rows]
+        taps_rows = jnp.pad(conv_weight, ((0, 0), (0, lanes - conv_weight.shape[1])))
+        return jnp.concatenate([taps_rows, *rows], axis=0)
+
+    small_in = (conv_weight, conv_bias, gate_gain, norm_gain, dt_bias, a_log, skip_gain)
+    sizes = (conv_bias.shape[0], gate_gain.shape[0], norm_gain.shape[0], dt_bias.shape[0])
+
+    first_columns, last_columns = width + LANES + state, 2 * width
+    core_place = jnp.stack([x, c]).astype(jnp.int32)
+    mine_a, for_core_a = prepare_call(
+        functools.partial(prepare_first_kernel, heads, size, state),
+        first_columns,
+        core_place,
+        in_weight,
+    )
+
+    def hops(pieces, stage):
+        sends = [(stage, 1, pieces[stage - 1])]
+        if groups - stage != stage:
+            sends.append((groups - stage, groups - 1, pieces[(groups - stage + 1) % groups]))
+        return sends
+
+    def hop_sends(pieces, stage):
+        return [
+            ((lambda value, by=by: links.along_g(value, by)), value)
+            for _, by, value in hops(pieces, stage)
+        ]
+
+    def landed(pieces, stage, values):
+        at = [k for k, _, _ in hops(pieces, stage)]
+        return {**pieces, **dict(zip(at, values))}
+
+    def rounds(piece):
+        return [(lambda value, j=j: links.along_a(value, j), piece) for j in range(1, sides)]
+
+    def doubled(value, bit, other):
+        upper = (links.shard // bit) % 2 == 1
+        return jnp.concatenate(
+            [jnp.where(upper, other, value), jnp.where(upper, value, other)], axis=0
+        )
+
+    def swap(bit):
+        return lambda value: links.flip(value, 0, bit)
+
+    (from_core_a,), packed = phase([(links.core, for_core_a)], pack, small_in)
+    pieces_a = {0: links.piece_of(mine_a, from_core_a)}
+
+    def prepare_last(packed, in_weight, out_weight):
+        small_pair = doubled(packed, 1, links.core(packed))
+        small_four = doubled(small_pair, 2, links.flip(small_pair, 0, 2))
+        kernel = functools.partial(prepare_last_kernel, width)
+        last = prepare_call(kernel, last_columns, core_place, in_weight, out_weight)
+        return small_four, last
+
+    moved, (small_all, (mine_b, for_core_b)) = phase(
+        hop_sends(pieces_a, 1) + [(links.core, lengths)],
+        prepare_last,
+        (packed, in_weight, out_weight),
+    )
+    lengths_core = moved[-1]
+    pieces_a = landed(pieces_a, 1, moved[:-1])
+    y_a = {}
+    firsts = [k for k in pieces_a if k]
+    sends = [send for k in firsts for send in rounds(pieces_a[k])]
     moved, _ = phase(
-        [(turn(k), first) for k in others[:1]] + [(turn(k), pair_packed) for k in others]
-    )
-    z_first, small_far = moved[:1], moved[1:]
-
+        hop_sends(pieces_a, 2) + [(swap(4), small_all), (links.core, for_core_b)] + sends
+    )
+    for at, k in enumerate(reversed(firsts)):
+        stop = len(moved) - at * (sides - 1)
+        y_a[k] = moved[stop - (sides - 1) : stop]
+    hop_count = len(hops(pieces_a, 2))
+    small_all = doubled(small_all, 4, moved[hop_count])
+    from_core_b = moved[hop_count + 1]
+    pieces_b = {0: links.piece_of(mine_b, from_core_b)}
+    pieces_a = landed(pieces_a, 2, moved[:hop_count])
+    bit = 8
+    while bit < shards:
+        small_all = doubled(small_all, bit, links.flip(small_all, 0, bit))
+        bit *= 2
+    for stage in range(3, groups // 2 + 1):
+        values = [send(value) for send, value in hop_sends(pieces_a, stage)]
+        pieces_a = landed(pieces_a, stage, values)
+    pieces_a, pieces_b, far_hidden = after((pieces_a, pieces_b, far_hidden))
+    rest = [k for k in pieces_a if k and k not in y_a]
+    b_firsts = [send(value) for send, value in hop_sends(pieces_b, 1)]
+    sends = [send for k in rest for send in rounds(pieces_a[k])]
     moved, parameters_here = phase(
-        [(turn(k), first) for k in others[1:]] + [(links.core, hidden_in)], parameters, (small_far,)
-    )
-    z_first, core_hidden = z_first + moved[:-1], moved[-1]
-    taps, bias, n_gain, head_rows, conv_rows = parameters_here
-    n_rows = jnp.broadcast_to(n_gain[None], (8, depth))
-    z_kq = jnp.concatenate([part[:, :state] for part in z_first], axis=0)
-    z_values = jnp.concatenate([part[:, state:] for part in z_first], axis=0)
-    gate_part = piece[:, split_a:split_b]
-
-    far_hidden, z_kq, z_values = after((far_hidden, z_kq, z_values))
-    moved, _ = phase(
-        rounds(z_kq)
-        + [(turn(k), gate_part) for k in others[: few + 0]]
-        + [(links.core, far_hidden)]
-    )
-    y_kq, z_gate, far_core_hidden = moved[: links.sides - 1], moved[links.sides - 1 : -1], moved[-1]
-    w_kq = links.assemble(*columns(0, state), z_kq, y_kq)
-    kq_columns = inner + c * state
+        sends + [(links.core, hidden_in), (links.core, far_hidden)],
+        functools.partial(unpack_call, sizes, heads, size, state, core_place),
+        (small_all,),
+    )
+    core_hidden, far_core_hidden = moved[-2:]
+    for at, k in enumerate(rest):
+        y_a[k] = moved[at * (sides - 1) : (at + 1) * (sides - 1)]
+    n_rows, conv_rows, head_rows, kq_rows = parameters_here
+    n_gain = n_rows[0]
+
+    def parts_of(mine, from_core, pieces, rounds_of):
+        parts = [mine, from_core]
+        for k in range(1, groups):
+            parts += [pieces[k], *rounds_of[k]]
+        return parts
+
+    parts_a = parts_of(mine_a, from_core_a, pieces_a, y_a)
     pair_lengths = jnp.concatenate([lengths, lengths_core], axis=0)
     pair_ends = jnp.cumsum(pair_lengths, axis=1)
     position = positions[None, :]
@@ -1000,92 +1188,103 @@
         pair_ends[:, 1:],
         jnp.where(position >= pair_ends[:, :1], pair_ends[:, :1], 0),
     )
-    kq_taps = lax.dynamic_slice_in_dim(taps, kq_columns, state, 1)
-    kq_bias = lax.dynamic_slice_in_dim(bias, kq_columns, state, 0)
-
-    def keys_or_queries(w_kq, core_hidden, far_hidden, far_core_hidden):
-        normed, scale = normalize_call(
-            [hidden_in, core_hidden, far_hidden, far_core_hidden], n_rows
-        )
-        kq_in = dot(normed[: 2 * tokens], w_kq).reshape(2, tokens, state)
-        kq_pre, kq_shifted = causal_conv(kq_in, begin, kq_taps, kq_bias)
-        return scale[:tokens, :1], normed, kq_pre, kq_shifted
-
-    moved, (scale_own, normed, kq_pre, kq_shifted) = phase(
-        [(turn(k), gate_part) for k in others[few:-1]] + rounds(z_values),
-        keys_or_queries,
-        (w_kq, core_hidden, far_hidden, far_core_hidden),
-    )
-    z_gate, y_values = z_gate + moved[: 1 - links.sides], moved[1 - links.sides :]
+    kq_columns = inner + c * state
+    kq_taps, kq_bias = kq_rows[:4], kq_rows[4]
+    normed, scale = normalize_call([hidden_in, core_hidden, far_hidden, far_core_hidden], n_rows)
+    scale_own = scale[:tokens, :1]
+    kq_index = (width + LANES) // state
+    w_kq, kq_in = project_call(links_shape, state, kq_index, 2, tokens, place, parts_a, normed)
+    kq_pre, kq_shifted = causal_conv(kq_in.reshape(2, tokens, state), begin, kq_taps, kq_bias)
     counts = jnp.stack([pair_lengths // 32, pair_lengths % 32], axis=2).reshape(2, 4).astype(BF16)
     counts = jnp.pad(counts, ((0, 14), (0, state - 4)))
     kq_near = jax.nn.silu(kq_pre).astype(BF16).reshape(2 * tokens, state)
-    place = jnp.stack([links.a, links.g, c]).astype(jnp.int32)
-    links_shape = (links.sides, links.groups)
-
-    def project(start, stop, joined, rounds_of_it):
-        operands = (*columns(start, stop), [joined, *rounds_of_it], normed)
-        return functools.partial(project_call, links_shape, place, tokens=tokens), operands
-
-    moved, (w_values, conv_in) = phase(
-        [(turn(k), gate_part) for k in others[-1:]]
-        + [(links.side, jnp.concatenate([kq_near, counts], axis=0))],
-        *project(state, split_a, z_values, y_values),
-    )
-    z_gate, kq_far = z_gate + moved[:1], moved[1]
+    moved, (w_values, conv_in), b_firsts = phase(
+        [(links.side, jnp.concatenate([kq_near, counts], axis=0))],
+        functools.partial(project_call, links_shape, width + LANES, 0, 4, tokens, place),
+        (parts_a, normed),
+        b_firsts,
+    )
+    pieces_b = landed(pieces_b, 1, b_firsts)
+    kq_far = moved[0]
     all_counts = jnp.concatenate([counts[:2, :4], kq_far[2 * tokens : 2 * tokens + 2, :4]], axis=0)
     all_counts = all_counts.astype(jnp.int32)
     all_lengths = all_counts[:, 0::2] * 32 + all_counts[:, 1::2]
     kq_half = jnp.concatenate([kq_near, kq_far[: 2 * tokens]], axis=0)
-    z_gate = jnp.concatenate(z_gate, axis=0)
-
+
+    kq_half, pieces_b, back_own = after((kq_half, pieces_b, back_own))
+    firsts = [k for k in pieces_b if k]
+    b_seconds = [send(value) for send, value in hop_sends(pieces_b, 2)]
+    y_firsts = [[send(value) for send, value in rounds(pieces_b[k])] for k in firsts]
     (kq_core,), _ = phase([(links.core, kq_half)])
     kq_core = kq_core.reshape(2, 2, tokens, state)[:, ::-1].reshape(4 * tokens, state)
     keys_queries = jnp.concatenate(
         [jnp.where(is_high, kq_core, kq_half), jnp.where(is_high, kq_half, kq_core)], axis=1
     )
-    far_back = links.side(back_own)
-    moved, (ssd_out, states) = phase(
-        rounds(z_gate) + [(turn(k), piece[:, split_b:]) for k in others],
+    cuts = [slice(0, tokens // 2), slice(tokens // 2, tokens)]
+    moved, (ssd_out, states), (b_seconds, y_firsts) = phase(
+        [(links.side, back_own[cuts[0]])],
         functools.partial(forward_call, heads, size),
         (all_lengths, conv_in, keys_queries, conv_rows, head_rows),
-    )
-    y_gate, z_out = moved[: links.sides - 1], moved[links.sides - 1 :]
-    z_out = jnp.concatenate(z_out, axis=0)
+        (b_seconds, y_firsts),
+    )
+    far_back = [moved[0]]
+    y_b = dict(zip(firsts, y_firsts))
+    pieces_b = landed(pieces_b, 2, b_seconds)
+    for stage in range(3, groups // 2 + 1):
+        values = [send(value) for send, value in hop_sends(pieces_b, stage)]
+        pieces_b = landed(pieces_b, stage, values)
+    rest = [k for k in pieces_b if k and k not in y_b]
+    gate_sends = [send for k in rest for send in rounds(pieces_b[k][:, :width])]
+    out_sends = [send for k in rest for send in rounds(pieces_b[k][:, width:])]
+    moved, _ = phase(
+        gate_sends
+        + [(links.core, back_own), (links.side, back_own[cuts[1]]), (links.core, far_back[0])]
+    )
+    core_back = moved[-3]
+    far_back.append(moved[-2])
+    far_core_back = [moved[-1]]
+    moved = moved[:-3]
+
+    def last_parts(values):
+        latest = {k: values[at * (sides - 1) : (at + 1) * (sides - 1)] for at, k in enumerate(rest)}
+        return parts_of(mine_b, from_core_b, pieces_b, {**y_b, **latest})
 
     moved, (w_gate, gate) = phase(
-        rounds(z_out) + [(links.core, back_own)], *project(split_a, split_b, z_gate, y_gate)
-    )
-    y_out, core_back = moved[:-1], moved[-1]
-    (far_core_back,), _ = phase([(links.core, far_back)])
-    back_blocks = [back_own, core_back, far_back, far_core_back]
+        out_sends + [(links.core, far_back[1])],
+        functools.partial(project_call, links_shape, width, 0, 4, tokens, place),
+        (last_parts(moved), normed),
+    )
+    far_core_back.append(moved[-1])
+    moved = moved[:-1]
+    back_blocks = [
+        back_own,
+        core_back,
+        jnp.concatenate(far_back, axis=0),
+        jnp.concatenate(far_core_back, axis=0),
+    ]
     w_out, d_branch, sums = branch_back_call(
-        links_shape, place, *columns(split_b, split_b + width), [z_out, *y_out], back_blocks,
-        gate, ssd_out, conv_rows,
-    )
-    moved, back = phase(
-        [(links.core, sums), (links.side, sums), (links.corner, sums)],
-        lambda *blocks: jnp.concatenate(blocks, axis=0),
-        back_blocks,
-    )
+        links_shape, width, 1, place, last_parts(moved), back_blocks, gate, ssd_out, conv_rows
+    )
+    moved, _ = phase([(links.core, sums), (links.side, sums), (links.corner, sums)])
     branch, d_gate, d_ssd, gain_rows = gating_back_call(
         inner, [sums, *moved], gate, ssd_out, d_branch, conv_rows
     )
     grad_gate_gain = gain_rows[0]
 
-    def weight_grad(left, right):
-        return lax.dot_general(
-            left, right, (((0,), (0,)), ((), ())), preferred_element_type=F32
-        ).astype(BF16)
-
-    half = heads // 2
     by_g = width // (3 * LANES) * 2 * LANES
-    far_rows, near_rows = slice(2 * tokens, None), slice(0, 2 * tokens)
-
-    def backward(part, d_out):
+    most = heads // 3 * 2
+    less = heads - most
+    most_width, less_width = most * size, less * size
+    rows_all = 4 * tokens
+
+    def backward(first_head, count, first_block, blocks, d_out):
         return backward_call(
-            half, size, part, all_lengths, conv_in, keys_queries, d_out, states, conv_rows, head_rows
+            count, size, first_head, first_block, blocks,
+            all_lengths, conv_in, keys_queries, d_out, states, conv_rows, head_rows,
         )
+
+    def turn(k):
+        return lambda value: links.along_g(value, k)
 
     def a_sends(parts):
         return [
@@ -1095,137 +1294,149 @@
     def g_sends(parts):
         return [(turn(k + 1), part) for k, part in enumerate(parts)]
 
-    g_out_z = weight_grad(back, branch[:, :by_g])
+    def start(sends):
+        return [send(value) for send, value in sends]
+
+    count_a, count_g = sides - 1, groups - 1
     mixed_parts = dot_nt(branch, w_out).astype(BF16).reshape(2, 2, tokens, depth)
-    def grad_parts(left, right):
-        parts = weight_grad_call(links_shape, place, left, right)
-        return parts[0], parts[1:]
-
-    gate_mine, gate_others = grad_parts(normed, d_gate)
-    out_y_mine, out_y_others = grad_parts(back, branch[:, by_g:])
-    first_mine = jnp.concatenate([gate_mine, out_y_mine], axis=2)
-    first_others = [jnp.concatenate(p, axis=2) for p in zip(gate_others, out_y_others)]
-    out_mine, out_others = links.parts_for_g(g_out_z.reshape(links.groups, -1, by_g))
+    mixed_keep, mixed_send = mixed_parts[:, 0], mixed_parts[:, 1]
+
+    def first_grads(normed, d_gate, back_blocks, branch):
+        def out_terms(columns, index):
+            return [
+                (block, tokens, 0, branch, at, columns, index)
+                for at, block in enumerate(back_blocks)
+            ]
+
+        first = weight_grad_call(
+            links_shape, True, place,
+            [
+                [(normed, rows_all, 0, d_gate, 0, width, 0)],
+                out_terms(width - by_g, by_g // (width - by_g)),
+            ],
+        )
+        return first, weight_grad_call(links_shape, False, place, [out_terms(by_g, 0)])
+
+    moved, (first_parts, out_parts) = phase(
+        [(links.core, mixed_send)], first_grads, (normed, d_gate, back_blocks, branch)
+    )
+    mixed_sum = mixed_keep.astype(F32) + moved[0].astype(F32)
     moved, (d_in_0, d_steps_0, d_kq_0, conv_grads_0, head_grads_0) = phase(
-        a_sends(first_others) + g_sends(out_others) + [(links.core, mixed_parts[:, 1])],
-        functools.partial(backward, 0),
+        a_sends(first_parts[1:])
+        + g_sends(out_parts[1:])
+        + [(links.side, mixed_sum[1].astype(BF16))],
+        functools.partial(backward, 0, most, 0, 4),
         (d_ssd,),
     )
-    count_a, count_g = links.sides - 1, links.groups - 1
-    first_held = total(first_mine, moved[:count_a]).astype(BF16)
-    out_chip = total(out_mine, moved[count_a:-1]).astype(BF16)
-    mixed_sum = mixed_parts[:, 0].astype(F32) + moved[-1].astype(F32)
-    first_mine, first_others = links.parts_for_g(first_held)
-    values_mine, values_others = grad_parts(normed, d_in_0)
-    moved, (d_in_1, d_steps_1, d_kq_1, conv_grads_1, head_grads_1) = phase(
-        g_sends(first_others) + a_sends(values_others) + [(links.side, mixed_sum[1].astype(BF16))],
-        functools.partial(backward, 1),
-        (d_ssd,),
-    )
-    first_piece = total(first_mine, moved[:count_g]).astype(BF16)
-    held_0 = total(values_mine, moved[count_g:-1]).astype(BF16)
     mixed = hidden_in.astype(F32) + mixed_sum[0] + moved[-1].astype(F32)
     mixed = jnp.where(is_valid, mixed, 0.0).astype(BF16)
-
-    d_kq_parts = (d_kq_0 + d_kq_1).reshape(2, 2, tokens, 2 * state)
-    d_kq_mine = jnp.where(is_high, d_kq_parts[..., state:], d_kq_parts[..., :state])
-    d_kq_core = jnp.where(is_high, d_kq_parts[..., :state], d_kq_parts[..., state:])
-    d_kq_core = d_kq_core[:, ::-1].astype(BF16)
-    d_steps = d_steps_0 + d_steps_1
-    d_rest = jnp.concatenate([d_in_0, d_in_1, d_steps], axis=1)
-
-    def d_normed_of(d_gate_rows, d_rest_rows):
-        return (dot_nt(d_gate_rows, w_gate) + dot_nt(d_rest_rows, w_values)).astype(BF16)
-
-    values_mine, values_others = grad_parts(normed, d_in_1)
-    out_mine, out_others = links.parts_for_a(out_chip.reshape(links.sides, -1, by_g))
-    moved, d_far = phase(
-        [(links.core, d_kq_core)]
-        + a_sends(values_others)
-        + a_sends(out_others)
-        + [(links.side, first_piece)],
-        d_normed_of,
-        (d_gate[far_rows], d_rest[far_rows]),
-    )
-    d_kq_sum = d_kq_mine + moved[0].astype(F32)
-    held_1 = total(values_mine, moved[1 : 1 + count_a]).astype(BF16)
-    out_piece = total(out_mine, moved[1 + count_a : -1]).astype(BF16)
-    first_x = links.join_x(first_piece, moved[-1])
-
-    values_mine, values_others = links.parts_for_g(jnp.concatenate([held_0, held_1], axis=2))
-    d_far = d_far.reshape(2, tokens, depth)
+    first_held = combine_call(groups, place, [first_parts[0], *moved[:count_a]])
+    values_0 = weight_grad_call(
+        links_shape, True, place, [[(normed, rows_all, 0, d_in_0, 0, most_width, 0)]]
+    )
+    out_chip = total(out_parts[0], moved[count_a:-1]).astype(BF16)
+    out_mine, out_others = links.parts_for_a(out_chip.reshape(sides, -1, by_g))
+    first_held, values_0, d_ssd, mixed, out_mine, out_others = after(
+        (first_held, values_0, d_ssd, mixed, out_mine, out_others)
+    )
+    first_sends = g_sends(first_held[1:])
+    first_sends = first_sends[:1] + first_sends[-1:] + first_sends[1:-1]
+
+    def back_project(first_row, d_in_1, d_steps):
+        rows = slice(first_row, first_row + 2 * tokens)
+        d_rest = jnp.concatenate([d_in_0[rows], d_in_1, d_steps], axis=1)
+        return dot_nt(d_gate[rows], w_gate) + dot_nt(d_rest, w_values)
+
+    def far_work(d_ssd):
+        results = backward(most, less, 2, 2, d_ssd)
+        d_steps = d_steps_0[2 * tokens :] + results[1]
+        return results, d_steps, back_project(2 * tokens, results[0], d_steps).astype(BF16)
+
+    moved, (results, d_steps_far, d_far_parts) = phase(
+        a_sends(values_0[1:]) + first_sends[:2], far_work, (d_ssd,)
+    )
+    first_far = moved[count_a:]
+    d_in_far, _, d_kq_far, conv_grads_far, head_grads_far = results
+    held_0 = combine_call(groups, place, [values_0[0], *moved[:count_a]])
+    held_sends = g_sends(held_0[1:])
+    held_sends = held_sends[:1] + held_sends[-1:] + held_sends[1:-1]
+
+    def halves(first_rows, second_rows):
+        rows = (first_rows + second_rows).reshape(2, tokens, 2 * state)
+        mine = jnp.where(is_high, rows[..., state:], rows[..., :state])
+        other = jnp.where(is_high, rows[..., :state], rows[..., state:])
+        return mine, other[::-1].astype(BF16)
+
+    kq_far_mine, kq_far_core = halves(d_kq_0[2 * tokens :], d_kq_far)
+    moved, _ = phase([(links.core, kq_far_core), (links.core, d_far_parts[tokens:])])
+    kq_far_sum = (kq_far_mine + moved[0].astype(F32)).astype(BF16)
+    d_far = (d_far_parts[:tokens].astype(F32) + moved[1].astype(F32)).astype(BF16)
+    moved, results = phase(
+        [(links.side, kq_far_sum)]
+        + first_sends[2:]
+        + [(links.side, d_far[cuts[0]])]
+        + a_sends(out_others),
+        functools.partial(backward, most, less, 0, 2),
+        (d_ssd,),
+    )
+    d_in_near, d_steps_near, d_kq_near, conv_grads_near, head_grads_near = results
+    kq_from_side = moved[0]
+    first_far = first_far + moved[1 : count_g - 1]
+    far_d = [moved[count_g - 1]]
+    out_piece = total(out_mine, moved[count_g:]).astype(BF16)
+    first_piece = total(first_held[0], first_far).astype(BF16)
+    first_piece = jnp.concatenate([first_piece, out_piece], axis=1)
+    kq_near_mine, kq_near_core = halves(d_kq_0[: 2 * tokens], d_kq_near)
+
+    d_steps_near = d_steps_0[: 2 * tokens] + d_steps_near
+    d_steps = jnp.concatenate([d_steps_near, d_steps_far], axis=0)
     moved, d_near = phase(
-        [(links.side, d_kq_sum[1].astype(BF16)), (links.core, d_far[1])] + g_sends(values_others),
-        d_normed_of,
-        (d_gate[near_rows], d_rest[near_rows]),
-    )
-    d_kq = d_kq_sum[0] + moved[0].astype(F32)
-    d_far = total(d_far[0], [moved[1]]).astype(BF16)
-    values_piece = total(values_mine, moved[2:]).astype(BF16)
-
+        [(links.core, kq_near_core)] + held_sends[:1],
+        functools.partial(back_project, 0),
+        (d_in_near, d_steps_near),
+    )
+    held_far = moved[1:]
+    d_kq = kq_near_mine + moved[0].astype(F32) + kq_from_side.astype(F32)
     kq_sig = sigmoid(kq_pre)
     d_kq_pre = d_kq * (kq_sig * (1.0 + kq_pre * (1.0 - kq_sig)))
     d_kq_in = causal_conv_back(d_kq_pre, begin, kq_taps).astype(BF16).reshape(2 * tokens, state)
-    last_piece = jnp.concatenate([out_piece, values_piece], axis=1)
-    moved, _ = phase([(links.side, d_kq_in), (links.side, last_piece)] + rounds(first_x))
-    quarter = state // 2
-    d_kq_all = jnp.concatenate([d_kq_in, moved[0]], axis=0)
-    d_tail = jnp.concatenate(
-        [
-            jnp.where(x == 1, d_kq_all[:, quarter:], d_kq_all[:, :quarter]),
-            d_steps[:, :heads],
-            jnp.zeros((4 * tokens, LANES - quarter - heads), BF16),
-        ],
-        axis=1,
-    )
-    tail_mine, tail_others = grad_parts(normed, d_tail)
-    last_x = links.join_x(last_piece, moved[1])
-    first_rows = links.rows_of_core(links.join_a(first_x, moved[2:]))
-    d_near = (d_near.astype(F32) + dot_nt(d_kq_in, w_kq)).astype(BF16).reshape(2, tokens, depth)
-    far_d = links.side(d_far)
-
-    moved, _ = phase(
-        a_sends(tail_others)
-        + rounds(last_x)
-        + [(links.core, first_rows[1]), (links.core, d_near[1])]
-    )
-    tail_held = total(tail_mine, moved[:count_a]).astype(BF16)
-    last_rows = links.rows_of_core(links.join_a(last_x, moved[count_a : 2 * count_a]))
-    first_shares = links.shares(first_rows[0], moved[-2])
-    d_near = total(d_near[0], [moved[-1]])
-
-    tail_mine, tail_others = links.parts_for_g(tail_held)
-    moved, _ = phase(g_sends(tail_others) + [(links.core, last_rows[1])])
-    tail_piece = total(tail_mine, moved[:-1]).astype(BF16)
-    last_shares = links.shares(last_rows[0], moved[-1])
-    moved, _ = phase(rounds(tail_piece))
-    tail_rows = links.rows_of_core(links.join_a(tail_piece, moved))
-    moved, _ = phase([(links.core, tail_rows[1])])
-    tail_both = jnp.concatenate(
-        [jnp.where(is_high, moved[0], tail_rows[0]), jnp.where(is_high, tail_rows[0], moved[0])],
-        axis=1,
-    )
-    (tail_far,), _ = phase([(links.side, tail_both)])
-    tail_low = jnp.where(x == 1, tail_far, tail_both)
-    tail_high = jnp.where(x == 1, tail_both, tail_far)
-    tail_shares = [tail_low[:, :LANES], tail_low[:, LANES:], tail_high[:, :LANES], tail_high[:, LANES:]]
-    d_normed = d_near + far_d.astype(F32)
-
-    own_hidden, own_scale = hidden_in.astype(F32), scale_own
-    weighted = n_gain * d_normed
-    inner_mean = jnp.mean(own_hidden * weighted, axis=-1, keepdims=True)
-    grad_hidden = (
-        back_own.astype(F32)
-        + own_scale * weighted
-        - own_hidden * (own_scale * own_scale * own_scale * inner_mean)
-    )
-
-    conv_grads = jnp.concatenate([conv_grads_0, conv_grads_1], axis=1)
-    head_grads = head_grads_0 + head_grads_1
+    half_rows = 2 * tokens
+
+    def last_grads(normed, d_in_near, d_in_far, d_steps, d_kq_in):
+        last = weight_grad_call(
+            links_shape, True, place,
+            [
+                [
+                    (normed, half_rows, 0, d_in_near, 0, less_width, 0),
+                    (normed, half_rows, 1, d_in_far, 0, less_width, 0),
+                ],
+                [
+                    (normed, half_rows, 0, d_steps, 0, LANES, 0),
+                    (normed, half_rows, 1, d_steps, 1, LANES, 0),
+                ],
+                [(normed, half_rows, 0, d_kq_in, 0, state, 0)],
+            ],
+        )
+        return last, dot_nt(d_kq_in, w_kq)
+
+    moved, (last_parts_here, kq_part) = phase(
+        rounds(first_piece) + held_sends[1:],
+        last_grads,
+        (normed, d_in_near, d_in_far, d_steps, d_kq_in),
+    )
+    first_y = moved[:count_a]
+    held_far = held_far + moved[count_a:]
+    held_piece = total(held_0[0], held_far).astype(BF16)
+    first_rows = links.rows_of_core(links.join_a(first_piece, first_y))
+    d_near = d_near + kq_part
+    d_near_keep, d_near_send = d_near[:tokens], d_near[tokens:].astype(BF16)
+
+    conv_grads = jnp.concatenate([conv_grads_0, conv_grads_far + conv_grads_near], axis=1)
+    head_grads = head_grads_0 + head_grads_far + head_grads_near
+    d_kq_rows = [jnp.sum(kq_shifted[delay] * d_kq_pre, axis=(0, 1)) for delay in (3, 2, 1, 0)]
+    d_kq_rows = jnp.stack(d_kq_rows + [jnp.sum(d_kq_pre, axis=(0, 1))])
     small = jnp.zeros((8, channels), F32)
     small = lax.dynamic_update_slice(small, conv_grads[:5], (0, p * width))
-    d_kq_rows = [jnp.sum(kq_shifted[delay] * d_kq_pre, axis=(0, 1)) for delay in (3, 2, 1, 0)]
-    d_kq_rows = jnp.stack(d_kq_rows + [jnp.sum(d_kq_pre, axis=(0, 1))])
     small = lax.dynamic_update_slice(small, d_kq_rows, (0, kq_columns))
     small = lax.dynamic_update_slice(small, grad_gate_gain[None], (5, p * width))
     grad_skip = conv_grads[5].reshape(heads, size).sum(axis=1)
@@ -1233,7 +1444,105 @@
     small_heads = jnp.zeros((3, all_heads), F32)
     small_heads = lax.dynamic_update_slice(small_heads, head_all, (0, p * heads))
     small = lax.dynamic_update_slice(small, small_heads.reshape(1, -1), (7, 0))
-    small = links.sum_all(small)
+
+    moved, _ = phase(
+        a_sends(last_parts_here[1:])
+        + [(links.side, d_far[cuts[1]]), (links.core, d_near_send), (links.core, small)]
+        + [(links.core, first_rows[1])]
+    )
+    far_d.append(moved[count_a])
+    d_near = d_near_keep + moved[count_a + 1].astype(F32)
+    small = small + moved[count_a + 2]
+    first_mine, first_core = first_rows[0], moved[-1]
+    first_both = jnp.concatenate(
+        [jnp.where(is_high, first_core, first_mine), jnp.where(is_high, first_mine, first_core)],
+        axis=1,
+    )
+    last_held = combine_call(groups, place, [last_parts_here[0], *moved[:count_a]])
+    first_half = first_both.shape[1] // 2
+    moved, _ = phase(
+        g_sends(last_held[1:])
+        + [(links.side, first_both[:, :first_half])]
+        + rounds(held_piece)
+    )
+    first_other = [moved[count_g]]
+    last_piece = total(last_held[0], moved[:count_g]).astype(BF16)
+    held_rows = links.rows_of_core(links.join_a(held_piece, moved[count_g + 1 :]))
+
+    def final_norm(d_near, far_d):
+        d_normed = d_near + far_d.astype(F32)
+        own_hidden, own_scale = hidden_in.astype(F32), scale_own
+        weighted = n_gain * d_normed
+        inner_mean = jnp.mean(own_hidden * weighted, axis=-1, keepdims=True)
+        return (
+            back_own.astype(F32)
+            + own_scale * weighted
+            - own_hidden * (own_scale * own_scale * own_scale * inner_mean)
+        )
+
+    diagonals = [(lambda value, j=j: links.diagonal(value, j), last_piece) for j in range(1, sides)]
+    moved, _ = phase(
+        rounds(last_piece)
+        + [(links.side, last_piece), (links.core, held_rows[1]), (swap(2), small)]
+        + diagonals
+    )
+    same_x = links.join_a(last_piece, moved[:count_a])
+    held_core, small = moved[count_a + 1], small + moved[count_a + 2]
+    other_x = links.join_a(moved[count_a], moved[count_a + 3 :])
+    at_kq = less_width + LANES
+    kq_both = same_x[:, at_kq:].astype(F32) + other_x[:, at_kq:].astype(F32)
+    last_rows = links.rows_of_core(
+        jnp.concatenate(
+            [
+                jnp.where(is_far, other_x, same_x)[:, :at_kq],
+                jnp.where(is_far, same_x, other_x)[:, :at_kq],
+                kq_both.astype(BF16),
+            ],
+            axis=1,
+        )
+    )
+    held_both = jnp.concatenate(
+        [jnp.where(is_high, held_core, held_rows[0]), jnp.where(is_high, held_rows[0], held_core)],
+        axis=1,
+    )
+    moved, grad_hidden = phase(
+        [(links.side, first_both[:, first_half:]), (links.side, held_both)]
+        + [(links.core, last_rows[1]), (swap(4), small)],
+        final_norm,
+        (d_near, jnp.concatenate(far_d, axis=0)),
+    )
+    small = small + moved[3]
+    bit = 8
+    while bit < shards:
+        small = small + links.flip(small, 0, bit)
+        bit *= 2
+    first_other = jnp.concatenate([first_other[0], moved[0]], axis=1)
+    held_other, last_core = moved[1], moved[2]
+    first_low = jnp.where(is_far, first_other, first_both)
+    first_high = jnp.where(is_far, first_both, first_other)
+    held_low = jnp.where(is_far, held_other, held_both)
+    held_high = jnp.where(is_far, held_both, held_other)
+    low = jnp.where(is_high, last_core, last_rows[0])
+    high = jnp.where(is_high, last_rows[0], last_core)
+    first_width = width + (width - by_g) + by_g
+    first_shares = [
+        first_low[:, :first_width], first_low[:, first_width:],
+        first_high[:, :first_width], first_high[:, first_width:],
+    ]
+    held_shares = [
+        held_low[:, :most_width], held_low[:, most_width:],
+        held_high[:, :most_width], held_high[:, most_width:],
+    ]
+    last_shares = [
+        low[:, :at_kq], high[:, :at_kq], low[:, at_kq : 2 * at_kq], high[:, at_kq : 2 * at_kq]
+    ]
+    kq_shares = [low[:, 2 * at_kq :], high[:, 2 * at_kq :]]
+    moved, _ = phase(
+        [(links.side, small)]
+        + rounds(small)
+        + [(lambda value, j=j: links.diagonal(value, j), small) for j in range(1, sides)]
+    )
+    small = total(small, moved)
 
     def own_slice(array, count):
         return lax.dynamic_slice_in_dim(array, links.shard * count, count, array.ndim - 1)
@@ -1243,18 +1552,18 @@
 
     grad_in = jnp.concatenate(
         [share[:, :width] for share in first_shares]
-        + [share[:, by_g:] for share in last_shares]
-        + [tail_shares[i][:, :quarter] for i in (0, 2, 1, 3)]
-        + [share[:, quarter : quarter + heads] for share in tail_shares],
+        + [part for pair in zip(held_shares, last_shares) for part in (pair[0], pair[1][:, :less_width])]
+        + kq_shares
+        + [share[:, less_width : less_width + heads] for share in last_shares],
         axis=1,
     ).astype(F32)
-    out_parts = [
+    out_shares = [
         part
-        for first, last in zip(first_shares, last_shares)
-        for part in (last[:, :by_g], first[:, width:])
+        for share in first_shares
+        for part in (share[:, 2 * width - by_g :], share[:, width : 2 * width - by_g])
     ]
     grad_norm = jnp.sum(grad_in * in_weight.astype(F32), axis=1) / norm_gain.astype(F32)
-    grad_out = jnp.concatenate(out_parts, axis=1).astype(F32).T
+    grad_out = jnp.concatenate(out_shares, axis=1).astype(F32).T
     return (
         mixed,
         grad_hidden,

time: 565 us -> 531 us (0.940)
  local copies, waits for them, and re-layouts: 105 us -> 78.1 us
  Pallas kernels: 149 us -> 163 us
  starting transfers between devices: 88.5 us -> 76.1 us
  waiting for transfers between devices: 116 us -> 106 us
    pallas_call x10 -> x16, Pallas kernels: 98.8 us -> 113 us  [the longest x3 53.6 us: backward_call(): pl.pallas_call(functools.partial(backward_kernel, heads, size, first_head...]
    ppermute x69 -> x74, starting transfers between devices: 88.5 us -> 76.1 us  [send(): return lax.ppermute(value, ('rep', 'fsdp'), pairs)]
    ppermute x69 -> x74, waiting for transfers between devices: 116 us -> 106 us  [send(): return lax.ppermute(value, ('rep', 'fsdp'), pairs)]
    add x11 -> x13, other arithmetic: 7.75 us -> 17.2 us  [the longest x1 6.83 us: per_device(): d_near = d_near + kq_part]
    dynamic_update_slice x11 -> x0, local copies, waits for them, and re-layouts: 9.05 us -> none  [the longest x6 6.14 us: assemble(): whole = lax.dynamic_update_slice_in_dim(whole, piece, at, 0)]
    unnamed x311 -> x314, local copies, waits for them, and re-layouts: 44.6 us -> 35.9 us
    dot_general x6, matrix products: 23.2 us -> 29.2 us  [dot_nt(): lax.dot_general(left, right, (((1,), (1,)), ((), ())), preferred_element_...]
    dot_general x2 -> x0, matrix products: 5.9 us -> none  [the longest x1 3.48 us: weight_grad(): lax.dot_general(left, right, (((0,), (0,)), ((), ())), preferred_element_...]
  transfers between devices with their start and end apart: 69 -> 74, of which waited for: 22 -> 25; matrix products, arithmetic and copies ran while one was open for 18% -> 13% of each run, Pallas kernels for 17% -> 22%
where the time goes in v2:
time: 531 us; the launch traced here: 522 us
  Pallas kernels  163 us (31%)
  waiting for transfers between devices  106 us (20%)
  local copies, waits for them, and re-layouts  78.1 us (15%)
  starting transfers between devices  76.1 us (14%)
  other arithmetic  65.5 us (12%)
  matrix products  29.2 us (5%)
    ppermute x74, waiting for transfers between devices, send(): return lax.ppermute(value, ('rep', 'fsdp'), pairs)  106 us
    ppermute x74, starting transfers between devices, send(): return lax.ppermute(value, ('rep', 'fsdp'), pairs)  76.1 us
    pallas_call x3, Pallas kernels, backward_call(): pl.pallas_call(functools.partial(backward_kernel, heads, size, first_head...  53.6 us
    unnamed x314, local copies, waits for them, and re-layouts  35.9 us
    pallas_call x4, Pallas kernels, weight_grad_call(): pl.pallas_call(functools.partial(weight_grad_kernel, links_shape, shapes,...  31.7 us
    dot_general x6, matrix products, dot_nt(): lax.dot_general(left, right, (((1,), (1,)), ((), ())), preferred_element_...  29.2 us
    pallas_call x3, Pallas kernels, project_call(): pl.pallas_call(functools.partial(project_kernel, links_shape), grid=(bloc...  20.1 us
    pallas_call x1, Pallas kernels, forward_call(): pl.pallas_call(functools.partial(forward_kernel, heads, size), grid=(bloc...  19.7 us
  transfers between devices with their start and end apart: 74, of which 25 were waited for; matrix products, arithmetic and copies ran while one was open for 13% of the time, Pallas kernels for 22%

profile of v2, /device:TPU:0, one launch (start us, length us, event | category | flops | bytes accessed | tf_op | source)
XLA Modules:
  0.0 521.6 jit_solution(8931107860920197963)
XLA Ops:
  19.4 9.9 %collective-permute-done.5 = bf16[16,512]{1,0:T(8,128)(2,1)} collective-permute-done((bf16[16,512]{1,0:T(8,128)(2,1)}, bf16[16,512]{1,0:T(8,128)(2,1)}, u32[]{:S(2)}, u32[]{:S(2)}) %collective-permute-start.5) | collective-permute-done | bytes 16416 | tf_op jit(solution)/shard_map/ppermute | solution.py:865
  45.8 5.5 %collective-permute-done.9.refs_1_ = bf16[192,1024]{1,0:T(8,128)(2,1)} collective-permute-done((bf16[192,1024]{1,0:T(8,128)(2,1)}, bf16[192,1024]{1,0:T(8,128)(2,1)}, u32[]{:S(2)}, u32[]{:S(2)}) %collective-permute-start.9) | collective-permute-done | bytes 393248 | tf_op jit(solution)/shard_map/ppermute | solution.py:865
  78.4 10.2 %project.4 = (bf16[1536,896]{1,0:T(8,128)(2,1)S(1)}, f32[2048,896]{1,0:T(8,128)}) custom-call(s32[3]{0:T(128)S(1)} %pad_add_fusion.2.at_ref, bf16[192,1024]{1,0:T(8,128)(2,1)S(1)} %get-tuple-element.377.own_ref, bf16[192,1024]{1,0:T(8,128)(2,1)S(1)} %copy-done.27, bf16[192,1024]{1,0:T(8,128)(2,1)} %collective-permute-done.1.refs_0_, ...), custom_call_target="tpu_custom_call" | custom-call | flops 5637144576 | bytes 6291456 | tf_op jit(solution)/shard_map/project/pallas_call | solution.py:440
  100.6 19.7 %ssd_forward.1 = (f32[2048,768]{1,0:T(8,128)S(1)}, bf16[4,3,128,768]{3,2,1,0:T(8,128)(2,1)S(1)}) custom-call(s32[4,2]{1,0:T(4,128)S(1)} %multiply_add_fusion.1.len_ref, f32[2048,896]{1,0:T(8,128)} %get-tuple-element.400.u_ref.dt_ref, f32[2048,896]{1,0:T(8,128)} %get-tuple-element.400.u_ref.dt_ref, bf16[2048,256]{1,0:T(8,128)(2,1)S(1)} %pad_maximum_fusion.2.kq_ref, ...), custom_call_target="tpu_custom_call" | custom-call | flops 12000000000 | bytes 32000000 | tf_op jit(solution)/shard_map/ssd_forward/pallas_call | solution.py:743
  125.8 8.3 %collective-permute-done.23.refs_3_ = bf16[192,768]{1,0:T(8,128)(2,1)S(1)} collective-permute-done((bf16[192,768]{1,0:T(8,128)(2,1)S(1)}, bf16[192,768]{1,0:T(8,128)(2,1)S(1)}, u32[]{:S(2)}, u32[]{:S(2)}) %collective-permute-start.23) | collective-permute-done | bytes 294944 | tf_op jit(solution)/shard_map/ppermute | solution.py:865
  134.2 9.0 %collective-permute-done.25 = bf16[256,1536]{1,0:T(8,128)(2,1)S(1)} collective-permute-done((bf16[256,1536]{1,0:T(8,128)(2,1)S(1)}, bf16[256,1536]{1,0:T(8,128)(2,1)S(1)}, u32[]{:S(2)}, u32[]{:S(2)}) %collective-permute-start.25) | collective-permute-done | bytes 786464 | tf_op jit(solution)/shard_map/ppermute | solution.py:865
  144.2 7.4 %project.5 = (bf16[1536,768]{1,0:T(8,128)(2,1)S(1)}, f32[2048,768]{1,0:T(8,128)S(1)}) custom-call(s32[3]{0:T(128)S(1)} %pad_add_fusion.2.at_ref, bf16[192,1536]{1,0:T(8,128)(2,1)S(1)} %copy-done.21, bf16[192,1536]{1,0:T(8,128)(2,1)S(1)} %copy-done.23, bf16[192,1536]{1,0:T(8,128)(2,1)} %collective-permute-done.16.refs_0_, ...), custom_call_target="tpu_custom_call" | custom-call | flops 4831838208 | bytes 6291456 | tf_op jit(solution)/shard_map/project/pallas_call | solution.py:440
  157.4 15.8 %branch_back.1 = (bf16[1536,768]{1,0:T(8,128)(2,1)}, f32[2048,768]{1,0:T(8,128)}, f32[8,2048]{1,0:T(8,128)}) custom-call(s32[3]{0:T(128)} %copy-done.57, bf16[192,1536]{1,0:T(8,128)(2,1)} %copy-done.20, bf16[192,1536]{1,0:T(8,128)(2,1)} %copy-done.22, bf16[192,1536]{1,0:T(8,128)(2,1)} %collective-permute-done.16.refs_0_, bf16[192,1536]{1,0:T(8,128)(2,1)} %copy-done.32, ...), custom_call_target="tpu_custom_call" | custom-call | flops 4831838208 | bytes 6291456 | tf_op jit(solution)/shard_map/branch_back/pallas_call | solution.py:495
  180.2 9.9 %gating_back.1 = (bf16[2048,768]{1,0:T(8,128)(2,1)S(1)}, bf16[2048,768]{1,0:T(8,128)(2,1)S(1)}, f32[2048,768]{1,0:T(8,128)S(1)}, f32[8,768]{1,0:T(8,128)S(1)}) custom-call(f32[8,2048]{1,0:T(8,128)S(1)} %copy-done.54, f32[8,2048]{1,0:T(8,128)S(1)} %collective-permute-done.29.core_ref, f32[8,2048]{1,0:T(8,128)S(1)} %collective-permute-done.30.side_ref, ...), custom_call_target="tpu_custom_call" | custom-call | flops 31457280 | bytes 31457280 | tf_op jit(solution)/shard_map/gating_back/pallas_call | solution.py:562
  199.8 6.4 %weight_grad.5 = (bf16[384,512]{1,0:T(8,128)(2,1)S(1)}, bf16[384,512]{1,0:T(8,128)(2,1)S(1)}, bf16[384,512]{1,0:T(8,128)(2,1)S(1)}, bf16[384,512]{1,0:T(8,128)(2,1)S(1)}) custom-call(s32[3]{0:T(128)S(1)} %copy-done.58, bf16[512,1536]{1,0:T(8,128)(2,1)S(1)} %copy-done.3, bf16[512,1536]{1,0:T(8,128)(2,1)S(1)} %copy-done.15, bf16[512,1536]{1,0:T(8,128)(2,1)} %copy-done.75, ...), custom_call_target="tpu_custom_call" | custom-call | flops 805306368 | bytes 1572864 | tf_op jit(solution)/shard_map/weight_grad/pallas_call | solution.py:690
  206.2 11.0 %weight_grad.4 = (bf16[4,192,1024]{2,1,0:T(8,128)(2,1)S(1)}, bf16[4,192,1024]{2,1,0:T(8,128)(2,1)S(1)}) custom-call(s32[3]{0:T(128)S(1)} %copy-done.58, bf16[2048,1536]{1,0:T(8,128)(2,1)} %copy-done.1, bf16[512,1536]{1,0:T(8,128)(2,1)S(1)} %copy-done.3, bf16[512,1536]{1,0:T(8,128)(2,1)} %copy-done.14, bf16[512,1536]{1,0:T(8,128)(2,1)} %copy-done.75, ...), custom_call_target="tpu_custom_call" | custom-call | flops 6442450944 | bytes 6291456 | tf_op jit(solution)/shard_map/weight_grad/pallas_call | solution.py:690
  227.6 32.1 %ssd_backward.3 = (bf16[2048,512]{1,0:T(8,128)(2,1)S(1)}, bf16[2048,128]{1,0:T(8,128)(2,1)S(1)}, f32[2048,256]{1,0:T(8,128)S(1)}, f32[8,512]{1,0:T(8,128)S(1)}, f32[8,128]{1,0:T(8,128)S(1)}) custom-call(s32[4,2]{1,0:T(4,128)S(1)} %multiply_add_fusion.1.len_ref, f32[2048,896]{1,0:T(8,128)} %get-tuple-element.400.u_ref.dt_ref, ...), custom_call_target="tpu_custom_call" | custom-call | flops 32000000000 | bytes 32000000 | tf_op jit(solution)/shard_map/ssd_backward/pallas_call | solution.py:786
  260.8 6.4 %weight_grad.6 = (bf16[4,192,512]{2,1,0:T(8,128)(2,1)S(1)}, bf16[4,192,512]{2,1,0:T(8,128)(2,1)S(1)}) custom-call(s32[3]{0:T(128)S(1)} %copy-done.58, bf16[2048,1536]{1,0:T(8,128)(2,1)} %copy-done.1, bf16[2048,512]{1,0:T(8,128)(2,1)S(1)} %get-tuple-element.485.refs_1_), custom_call_target="tpu_custom_call" | custom-call | flops 3221225472 | bytes 6291456 | tf_op jit(solution)/shard_map/weight_grad/pallas_call | solution.py:690
  277.1 10.9 %ssd_backward.4 = (bf16[1024,256]{1,0:T(8,128)(2,1)S(1)}, bf16[1024,128]{1,0:T(8,128)(2,1)S(1)}, f32[1024,256]{1,0:T(8,128)S(1)}, f32[8,256]{1,0:T(8,128)S(1)}, f32[8,128]{1,0:T(8,128)S(1)}) custom-call(s32[4,2]{1,0:T(4,128)S(1)} %multiply_add_fusion.1.len_ref, f32[2048,896]{1,0:T(8,128)} %get-tuple-element.400.u_ref.dt_ref, ...), custom_call_target="tpu_custom_call" | custom-call | flops 8000000000 | bytes 16000000 | tf_op jit(solution)/shard_map/ssd_backward/pallas_call | solution.py:786
  292.8 5.4 %fusion.5 = f32[1024,1536]{1,0:T(8,128)S(1)} fusion(bf16[1536,896]{1,0:T(8,128)(2,1)} %copy-done.71, bf16[1024,128]{1,0:T(8,128)(2,1)S(1)} %slice_add_fusion.4, bf16[1024,256]{1,0:T(8,128)(2,1)S(1)} %get-tuple-element.556.refs_2_, bf16[1024,512]{1,0:T(8,128)(2,1)S(1)} %copy-done.100), kind=kOutput, calls=%fused_computation.22 | convolution fusion | flops 2824077312 | bytes 10878976 | tf_op jit(solution)/shard_map/dot_general | solution.py:25
  302.8 5.6 %collective-permute-done.40 = bf16[192,1024]{1,0:T(8,128)(2,1)S(1)} collective-permute-done((bf16[192,1024]{1,0:T(8,128)(2,1)S(1)}, bf16[192,1024]{1,0:T(8,128)(2,1)S(1)}, u32[]{:S(2)}, u32[]{:S(2)}) %collective-permute-start.40) | collective-permute-done | bytes 393248 | tf_op jit(solution)/shard_map/ppermute | solution.py:865
  332.1 10.6 %ssd_backward.5 = (bf16[1024,256]{1,0:T(8,128)(2,1)S(1)}, bf16[1024,128]{1,0:T(8,128)(2,1)S(1)}, f32[1024,256]{1,0:T(8,128)S(1)}, f32[8,256]{1,0:T(8,128)S(1)}, f32[8,128]{1,0:T(8,128)S(1)}) custom-call(s32[4,2]{1,0:T(4,128)S(1)} %multiply_add_fusion.1.len_ref, f32[2048,896]{1,0:T(8,128)} %get-tuple-element.400.u_ref.dt_ref, ...), custom_call_target="tpu_custom_call" | custom-call | flops 8000000000 | bytes 16000000 | tf_op jit(solution)/shard_map/ssd_backward/pallas_call | solution.py:786
  350.9 5.7 %fusion.11 = f32[1024,1536]{1,0:T(8,128)S(1)} fusion(bf16[1536,896]{1,0:T(8,128)(2,1)} %copy-done.71, bf16[1024,128]{1,0:T(8,128)(2,1)S(1)} %slice_add_fusion.3, bf16[1024,256]{1,0:T(8,128)(2,1)S(1)} %get-tuple-element.555.refs_1_, bf16[1024,512]{1,0:T(8,128)(2,1)} %get-tuple-element.655), kind=kOutput, calls=%fused_computation.28 | convolution fusion | flops 2824077312 | bytes 10878976 | tf_op jit(solution)/shard_map/dot_general | solution.py:25
  364.1 6.6 %collective-permute-done.48 = bf16[192,512]{1,0:T(8,128)(2,1)} collective-permute-done((bf16[192,512]{1,0:T(8,128)(2,1)S(1)}, bf16[192,512]{1,0:T(8,128)(2,1)}, u32[]{:S(2)}, u32[]{:S(2)}) %collective-permute-start.48) | collective-permute-done | bytes 196640 | tf_op jit(solution)/shard_map/ppermute | solution.py:865
  387.8 7.9 %weight_grad.7 = (bf16[4,192,512]{2,1,0:T(8,128)(2,1)S(1)}, bf16[4,192,512]{2,1,0:T(8,128)(2,1)}) custom-call(s32[3]{0:T(128)S(1)} %copy-done.58, bf16[2048,1536]{1,0:T(8,128)(2,1)} %copy-done.1, bf16[1024,256]{1,0:T(8,128)(2,1)S(1)} %copy-done.39, bf16[1024,256]{1,0:T(8,128)(2,1)S(1)} %copy-done.35, ...), custom_call_target="tpu_custom_call" | custom-call | flops 1610612736 | bytes 3145728 | tf_op jit(solution)/shard_map/weight_grad/pallas_call | solution.py:690
  395.7 6.8 %add.327 = f32[1024,1536]{1,0:T(8,128)} add(f32[1024,1536]{1,0:T(8,128)} %convolution_add_fusion, f32[1024,1536]{1,0:T(8,128)S(1)} %copy-done.72) | non-fusion elementwise | flops 1572864 | bytes 18874368 | tf_op jit(solution)/shard_map/add | solution.py:1431
  413.3 15.5 %collective-permute-done.52.refs_1_ = bf16[4,192,512]{2,1,0:T(8,128)(2,1)S(1)} collective-permute-done((bf16[4,192,512]{2,1,0:T(8,128)(2,1)}, bf16[4,192,512]{2,1,0:T(8,128)(2,1)S(1)}, u32[]{:S(2)}, u32[]{:S(2)}) %collective-permute-start.52) | collective-permute-done | bytes 786464 | tf_op jit(solution)/shard_map/ppermute | solution.py:865
  447.6 6.8 %collective-permute-done.58 = bf16[192,512]{1,0:T(8,128)(2,1)S(1)} collective-permute-done((bf16[192,512]{1,0:T(8,128)(2,1)S(1)}, bf16[192,512]{1,0:T(8,128)(2,1)S(1)}, u32[]{:S(2)}, u32[]{:S(2)}) %collective-permute-start.58) | collective-permute-done | bytes 196640 | tf_op jit(solution)/shard_map/ppermute | solution.py:865
  483.9 10.9 %collective-permute-done.68 = bf16[192,1024]{1,0:T(8,128)(2,1)S(1)} collective-permute-done((bf16[192,1024]{1,0:T(8,128)(2,1)}, bf16[192,1024]{1,0:T(8,128)(2,1)S(1)}, u32[]{:S(2)}, u32[]{:S(2)}) %collective-permute-start.68) | collective-permute-done | bytes 393248 | tf_op jit(solution)/shard_map/ppermute | solution.py:865
  (620 shorter events, 274.1 us)
Async XLA Ops:
  6.4 23.7 %collective-permute-start.1 = (bf16[192,1024]{1,0:T(8,128)(2,1)}, bf16[192,1024]{1,0:T(8,128)(2,1)}, u32[]{:S(2)}, u32[]{:S(2)}) collective-permute-start(bf16[192,1024]{1,0:T(8,128)(2,1)} %broadcast_select_fusion.12), channel_id=1, source_target_pairs={{0,2},{1,3},{2,4},{3,5},{4,6},{5,7},{6,0},{7,1},{8,10},{9,11},{10,... | collective-permute-start | bytes 1179656 | tf_op jit(solution)/shard_map/ppermute | solution.py:865
  9.1 21.0 %collective-permute-start.2 = (bf16[192,1024]{1,0:T(8,128)(2,1)}, bf16[192,1024]{1,0:T(8,128)(2,1)}, u32[]{:S(2)}, u32[]{:S(2)}) collective-permute-start(bf16[192,1024]{1,0:T(8,128)(2,1)} %broadcast_select_fusion.12), channel_id=1, source_target_pairs={{0,6},{1,7},{2,0},{3,1},{4,2},{5,3},{6,4},{7,5},{8,14},{9,15},{10,... | collective-permute-start | bytes 1179656 | tf_op jit(solution)/shard_map/ppermute | solution.py:865
  11.8 42.2 %collective-permute-start.11 = (bf16[512,1536]{1,0:T(8,128)(2,1)S(1)}, bf16[512,1536]{1,0:T(8,128)(2,1)}, u32[]{:S(2)}, u32[]{:S(2)}) collective-permute-start(bf16[512,1536]{1,0:T(8,128)(2,1)S(1)} %copy-done.8), channel_id=1, source_target_pairs={{0,8},{1,9},{2,10},{3,11},{4,12},{5,13},{6,14},{7,15},{8,0},{9,1},... | collective-permute-start | bytes 4718600 | tf_op jit(solution)/shard_map/ppermute | solution.py:865
  30.1 21.2 %collective-permute-start.8 = (bf16[192,1536]{1,0:T(8,128)(2,1)}, bf16[192,1536]{1,0:T(8,128)(2,1)S(1)}, u32[]{:S(2)}, u32[]{:S(2)}) collective-permute-start(bf16[192,1536]{1,0:T(8,128)(2,1)} %get-tuple-element.348), channel_id=1, source_target_pairs={{0,1},{1,0},{2,3},{3,2},{4,5},{5,4},{6,7},{7,6},{8,9},{9,8},{10,11... | collective-permute-start | bytes 1769480 | tf_op jit(solution)/shard_map/ppermute | solution.py:865
  59.9 30.3 %collective-permute-start.16 = (bf16[192,1536]{1,0:T(8,128)(2,1)}, bf16[192,1536]{1,0:T(8,128)(2,1)}, u32[]{:S(2)}, u32[]{:S(2)}) collective-permute-start(bf16[192,1536]{1,0:T(8,128)(2,1)} %broadcast_select_fusion.9), channel_id=1, source_target_pairs={{0,2},{1,3},{2,4},{3,5},{4,6},{5,7},{6,0},{7,1},{8,10},{9,11},{10,... | collective-permute-start | bytes 1769480 | tf_op jit(solution)/shard_map/ppermute | solution.py:865
  61.6 28.5 %collective-permute-start.17 = (bf16[192,1536]{1,0:T(8,128)(2,1)}, bf16[192,1536]{1,0:T(8,128)(2,1)}, u32[]{:S(2)}, u32[]{:S(2)}) collective-permute-start(bf16[192,1536]{1,0:T(8,128)(2,1)} %broadcast_select_fusion.9), channel_id=1, source_target_pairs={{0,6},{1,7},{2,0},{3,1},{4,2},{5,3},{6,4},{7,5},{8,14},{9,15},{10,... | collective-permute-start | bytes 1769480 | tf_op jit(solution)/shard_map/ppermute | solution.py:865
  90.5 32.5 %collective-permute-start.20 = (bf16[192,1536]{1,0:T(8,128)(2,1)}, bf16[192,1536]{1,0:T(8,128)(2,1)S(1)}, u32[]{:S(2)}, u32[]{:S(2)}) collective-permute-start(bf16[192,1536]{1,0:T(8,128)(2,1)} %collective-permute-done.16.refs_0_), channel_id=1, source_target_pairs={{0,2},{1,3},{2,4},{3,5},{4,6},{5,7},{6,0},{7,1},{8,10},{9,11},{10,... | collective-permute-start | bytes 1769480 | tf_op jit(solution)/shard_map/ppermute | solution.py:865
  92.5 30.5 %collective-permute-start.21 = (bf16[192,1536]{1,0:T(8,128)(2,1)}, bf16[192,1536]{1,0:T(8,128)(2,1)S(1)}, u32[]{:S(2)}, u32[]{:S(2)}) collective-permute-start(bf16[192,1536]{1,0:T(8,128)(2,1)} %collective-permute-done.16.refs_0_), channel_id=1, source_target_pairs={{0,16},{1,17},{2,18},{3,19},{4,20},{5,21},{6,22},{7,23},{8,24},{9,... | collective-permute-start | bytes 1769480 | tf_op jit(solution)/shard_map/ppermute | solution.py:865
  93.4 29.6 %collective-permute-start.22 = (bf16[192,1536]{1,0:T(8,128)(2,1)}, bf16[192,1536]{1,0:T(8,128)(2,1)S(1)}, u32[]{:S(2)}, u32[]{:S(2)}) collective-permute-start(bf16[192,1536]{1,0:T(8,128)(2,1)} %collective-permute-done.17.refs_4_), channel_id=1, source_target_pairs={{0,16},{1,17},{2,18},{3,19},{4,20},{5,21},{6,22},{7,23},{8,24},{9,... | collective-permute-start | bytes 1769480 | tf_op jit(solution)/shard_map/ppermute | solution.py:865
  100.0 23.1 %collective-permute-start.19 = (bf16[256,1536]{1,0:T(8,128)(2,1)S(1)}, bf16[256,1536]{1,0:T(8,128)(2,1)S(1)}, u32[]{:S(2)}, u32[]{:S(2)}) collective-permute-start(bf16[256,1536]{1,0:T(8,128)(2,1)S(1)} %copy-done.102), channel_id=1, source_target_pairs={{0,8},{1,9},{2,10},{3,11},{4,12},{5,13},{6,14},{7,15},{8,0},{9,1},... | collective-permute-start | bytes 2359304 | tf_op jit(solution)/shard_map/ppermute | solution.py:865
  221.3 38.6 %collective-permute-start.33 = (bf16[4,192,1024]{2,1,0:T(8,128)(2,1)S(1)}, bf16[4,192,1024]{2,1,0:T(8,128)(2,1)S(1)}, u32[]{:S(2)}, u32[]{:S(2)}) collective-permute-start(bf16[4,192,1024]{2,1,0:T(8,128)(2,1)S(1)} %get-tuple-element.468), channel_id=1, source_target_pairs={{0,16},{1,17},{2,18},{3,19},{4,20},{5,21},{6,22},{7,23},{8,24},{9,... | collective-permute-start | bytes 4718600 | tf_op jit(solution)/shard_map/ppermute | solution.py:865
  222.5 37.4 %collective-permute-start.37 = (bf16[512,1536]{1,0:T(8,128)(2,1)S(1)}, bf16[512,1536]{1,0:T(8,128)(2,1)}, u32[]{:S(2)}, u32[]{:S(2)}) collective-permute-start(bf16[512,1536]{1,0:T(8,128)(2,1)S(1)} %fusion.17), channel_id=1, source_target_pairs={{0,8},{1,9},{2,10},{3,11},{4,12},{5,13},{6,14},{7,15},{8,0},{9,1},... | collective-permute-start | bytes 4718600 | tf_op jit(solution)/shard_map/ppermute | solution.py:865
  223.8 36.0 %collective-permute-start.34 = (bf16[384,512]{1,0:T(8,128)(2,1)S(1)}, bf16[384,512]{1,0:T(8,128)(2,1)S(1)}, u32[]{:S(2)}, u32[]{:S(2)}) collective-permute-start(bf16[384,512]{1,0:T(8,128)(2,1)S(1)} %get-tuple-element.469), channel_id=1, source_target_pairs={{0,2},{1,3},{2,4},{3,5},{4,6},{5,7},{6,0},{7,1},{8,10},{9,11},{10,... | collective-permute-start | bytes 1179656 | tf_op jit(solution)/shard_map/ppermute | solution.py:865
  224.4 35.4 %collective-permute-start.35 = (bf16[384,512]{1,0:T(8,128)(2,1)S(1)}, bf16[384,512]{1,0:T(8,128)(2,1)S(1)}, u32[]{:S(2)}, u32[]{:S(2)}) collective-permute-start(bf16[384,512]{1,0:T(8,128)(2,1)S(1)} %get-tuple-element.470), channel_id=1, source_target_pairs={{0,4},{1,5},{2,6},{3,7},{4,0},{5,1},{6,2},{7,3},{8,12},{9,13},{10,... | collective-permute-start | bytes 1179656 | tf_op jit(solution)/shard_map/ppermute | solution.py:865
  226.5 33.3 %collective-permute-start.36 = (bf16[384,512]{1,0:T(8,128)(2,1)S(1)}, bf16[384,512]{1,0:T(8,128)(2,1)S(1)}, u32[]{:S(2)}, u32[]{:S(2)}) collective-permute-start(bf16[384,512]{1,0:T(8,128)(2,1)S(1)} %get-tuple-element.471), channel_id=1, source_target_pairs={{0,6},{1,7},{2,0},{3,1},{4,2},{5,3},{6,4},{7,5},{8,14},{9,15},{10,... | collective-permute-start | bytes 1179656 | tf_op jit(solution)/shard_map/ppermute | solution.py:865
  288.0 20.4 %collective-permute-start.38 = (bf16[4,192,512]{2,1,0:T(8,128)(2,1)S(1)}, bf16[4,192,512]{2,1,0:T(8,128)(2,1)S(1)}, u32[]{:S(2)}, u32[]{:S(2)}) collective-permute-start(bf16[4,192,512]{2,1,0:T(8,128)(2,1)S(1)} %get-tuple-element.499), channel_id=1, source_target_pairs={{0,16},{1,17},{2,18},{3,19},{4,20},{5,21},{6,22},{7,23},{8,24},{9,... | collective-permute-start | bytes 2359304 | tf_op jit(solution)/shard_map/ppermute | solution.py:865
  321.1 26.6 %collective-permute-start.45 = (bf16[256,1536]{1,0:T(8,128)(2,1)}, bf16[256,1536]{1,0:T(8,128)(2,1)}, u32[]{:S(2)}, u32[]{:S(2)}) collective-permute-start(bf16[256,1536]{1,0:T(8,128)(2,1)} %get-tuple-element.524), channel_id=1, source_target_pairs={{0,8},{1,9},{2,10},{3,11},{4,12},{5,13},{6,14},{7,15},{8,0},{9,1},... | collective-permute-start | bytes 2359304 | tf_op jit(solution)/shard_map/ppermute | solution.py:865
  327.1 20.5 %collective-permute-start.44 = (bf16[192,1024]{1,0:T(8,128)(2,1)}, bf16[192,1024]{1,0:T(8,128)(2,1)S(1)}, u32[]{:S(2)}, u32[]{:S(2)}) collective-permute-start(bf16[192,1024]{1,0:T(8,128)(2,1)} %copy-done.60), channel_id=1, source_target_pairs={{0,4},{1,5},{2,6},{3,7},{4,0},{5,1},{6,2},{7,3},{8,12},{9,13},{10,... | collective-permute-start | bytes 1179656 | tf_op jit(solution)/shard_map/ppermute | solution.py:865
  374.0 21.7 %collective-permute-start.49 = (bf16[192,1536]{1,0:T(8,128)(2,1)}, bf16[192,1536]{1,0:T(8,128)(2,1)}, u32[]{:S(2)}, u32[]{:S(2)}) collective-permute-start(bf16[192,1536]{1,0:T(8,128)(2,1)} %pad_maximum_fusion.4), channel_id=1, source_target_pairs={{0,16},{1,17},{2,18},{3,19},{4,20},{5,21},{6,22},{7,23},{8,24},{9,... | collective-permute-start | bytes 1769480 | tf_op jit(solution)/shard_map/ppermute | solution.py:865
  408.6 20.9 %collective-permute-start.54 = (bf16[512,1536]{1,0:T(8,128)(2,1)}, bf16[512,1536]{1,0:T(8,128)(2,1)}, u32[]{:S(2)}, u32[]{:S(2)}) collective-permute-start(bf16[512,1536]{1,0:T(8,128)(2,1)} %slice.577), channel_id=1, source_target_pairs={{0,1},{1,0},{2,3},{3,2},{4,5},{5,4},{6,7},{7,6},{8,9},{9,8},{10,11... | collective-permute-start | bytes 4718600 | tf_op jit(solution)/shard_map/ppermute | solution.py:865
  408.6 20.2 %collective-permute-start.52 = (bf16[4,192,512]{2,1,0:T(8,128)(2,1)}, bf16[4,192,512]{2,1,0:T(8,128)(2,1)S(1)}, u32[]{:S(2)}, u32[]{:S(2)}) collective-permute-start(bf16[4,192,512]{2,1,0:T(8,128)(2,1)} %get-tuple-element.573), channel_id=1, source_target_pairs={{0,16},{1,17},{2,18},{3,19},{4,20},{5,21},{6,22},{7,23},{8,24},{9,... | collective-permute-start | bytes 2359304 | tf_op jit(solution)/shard_map/ppermute | solution.py:865
  432.5 21.9 %collective-permute-start.60 = (bf16[192,1536]{1,0:T(8,128)(2,1)S(1)}, bf16[192,1536]{1,0:T(8,128)(2,1)S(1)}, u32[]{:S(2)}, u32[]{:S(2)}) collective-permute-start(bf16[192,1536]{1,0:T(8,128)(2,1)S(1)} %get-tuple-element.592), channel_id=1, source_target_pairs={{0,8},{1,9},{2,10},{3,11},{4,12},{5,13},{6,14},{7,15},{8,0},{9,1},... | collective-permute-start | bytes 1769480 | tf_op jit(solution)/shard_map/ppermute | solution.py:865
  471.8 23.0 %collective-permute-start.67 = (bf16[192,1536]{1,0:T(8,128)(2,1)}, bf16[192,1536]{1,0:T(8,128)(2,1)S(1)}, u32[]{:S(2)}, u32[]{:S(2)}) collective-permute-start(bf16[192,1536]{1,0:T(8,128)(2,1)} %get-tuple-element.612), channel_id=1, source_target_pairs={{0,8},{1,9},{2,10},{3,11},{4,12},{5,13},{6,14},{7,15},{8,0},{9,1},... | collective-permute-start | bytes 1769480 | tf_op jit(solution)/shard_map/ppermute | solution.py:865
  472.7 22.1 %collective-permute-start.68 = (bf16[192,1024]{1,0:T(8,128)(2,1)}, bf16[192,1024]{1,0:T(8,128)(2,1)S(1)}, u32[]{:S(2)}, u32[]{:S(2)}) collective-permute-start(bf16[192,1024]{1,0:T(8,128)(2,1)} %pad_maximum_fusion.7), channel_id=1, source_target_pairs={{0,8},{1,9},{2,10},{3,11},{4,12},{5,13},{6,14},{7,15},{8,0},{9,1},... | collective-permute-start | bytes 1179656 | tf_op jit(solution)/shard_map/ppermute | solution.py:865
  (202 other events, 1789.0 us)

commit v3 on v2

--- a/solution.py
+++ b/solution.py
@@ -26,7 +26,7 @@
 
 
 def sigmoid(v):
-    return 1.0 / (1.0 + jnp.exp(-v))
+    return 0.5 * jnp.tanh(0.5 * v) + 0.5
 
 
 def softplus(v):
@@ -55,7 +55,7 @@
     pre = cw_ref[4:5, columns] + cw_ref[3:4, columns] * inputs[0]
     for delay in range(1, 4):
         pre = pre + cw_ref[3 - delay : 4 - delay, columns] * inputs[delay]
-    return pre, inputs
+    return pre
 
 
 def chunk_rates(dt_ref, hp_ref, start):
@@ -71,8 +71,9 @@
     return jnp.where(low, matrix[:, head : head + 1], matrix[:, head + 1 : head + 2])
 
 
-def forward_kernel(heads, size, len_ref, u_ref, dt_ref, kq_ref, cw_ref, hp_ref, y_ref, st_ref, state):
-    block = pl.program_id(0)
+def forward_kernel(heads, size, first_block, len_ref, u_ref, dt_ref, kq_ref, cw_ref, hp_ref, *refs):
+    y_ref, st_ref, pre_ref, state = refs[-4:]
+    block = first_block + pl.program_id(0)
     first = len_ref[block, 0]
     both = first + len_ref[block, 1]
     tokens = u_ref.shape[0]
@@ -100,7 +101,8 @@
         for pair in range(heads // 2):
             h = 2 * pair
             columns = slice(pair * LANES, (pair + 1) * LANES)
-            pre, _ = conv_tile(u_ref, cw_ref, start, columns, masks)
+            pre = conv_tile(u_ref, cw_ref, start, columns, masks)
+            pre_ref[start : start + CHUNK, columns] = pre
             values = pre * sigmoid(pre)
             scaled = values * pair_of(low, step, h)
             weights = []
@@ -133,23 +135,21 @@
     first_head,
     first_block,
     len_ref,
+    at_ref,
     u_ref,
+    pre_ref,
     dt_ref,
     kq_ref,
     dy_ref,
     st_ref,
     cw_ref,
     hp_ref,
-    du_ref,
-    ddt_ref,
-    dkq_ref,
-    cg_ref,
-    hg_ref,
-    d_state,
-    d_pre,
-    out_in,
-    source_in,
+    *refs,
 ):
+    added = refs[:-10]
+    du_ref, ddt_ref, mine_ref, other_ref, cg_ref, hg_ref = refs[-10:-4]
+    d_state, d_pre, out_in, source_in = refs[-4:]
+    is_high = at_ref[1] == 1
     block = pl.program_id(0)
     first = len_ref[first_block + block, 0]
     both = first + len_ref[first_block + block, 1]
@@ -172,7 +172,6 @@
         has_later = ci < chunks - 1
         position = row + start
         begin = begin_of(position, first, both)
-        masks = [position - delay >= begin for delay in range(1, 4)]
         ahead = [begin_of(position + delay, first, both) <= position for delay in range(1, 4)]
         raw, step, rate, running = chunk_rates(dt_ref, hp_ref, start)
         running_t = running.T
@@ -196,7 +195,8 @@
             h = first_head + 2 * pair
             columns = slice(pair * LANES, (pair + 1) * LANES)
             to_head = (column == h + (row >= size).astype(jnp.int32)).astype(BF16)
-            pre, inputs = conv_tile(u_ref, cw_ref, start, columns, masks)
+            pre = pre_ref[start : start + CHUNK, columns]
+            inputs = u_ref[start : start + CHUNK, columns]
             gate = sigmoid(pre)
             values = pre * gate
             steps = pair_of(low, step, h)
@@ -249,16 +249,15 @@
             d_here = d_values * (gate * (1.0 + pre * (1.0 - gate)))
             d_pre[start : start + CHUNK, columns] = d_here
             d_in = cw_ref[3:4, columns] * d_here
+            cg_ref[3:4, columns] += jnp.sum(inputs * d_here, axis=0, keepdims=True)
             for delay in range(1, 4):
                 shifted = d_pre[start + delay : start + delay + CHUNK, columns]
-                d_in = d_in + cw_ref[3 - delay : 4 - delay, columns] * jnp.where(
-                    ahead[delay - 1], shifted, 0.0
+                shifted = jnp.where(ahead[delay - 1], shifted, 0.0)
+                d_in = d_in + cw_ref[3 - delay : 4 - delay, columns] * shifted
+                cg_ref[3 - delay : 4 - delay, columns] += jnp.sum(
+                    inputs * shifted, axis=0, keepdims=True
                 )
             du_ref[start : start + CHUNK, columns] = d_in.astype(BF16)
-            for delay in range(4):
-                cg_ref[3 - delay : 4 - delay, columns] += jnp.sum(
-                    inputs[delay] * d_here, axis=0, keepdims=True
-                )
             cg_ref[4:5, columns] += jnp.sum(d_here, axis=0, keepdims=True)
         d_scores = jnp.where(allowed, d_scores, 0.0)
         d_keys = dot(d_scores.astype(BF16), queries)
@@ -282,8 +281,13 @@
                 if has_later:
                     fresh = fresh + d_state[:, columns] * pair_of(low_row, kept, first_head + 2 * pair)
                 d_state[:, columns] = fresh
-        dkq_ref[start : start + CHUNK, :LANES] = d_keys
-        dkq_ref[start : start + CHUNK, LANES:] = d_queries
+        here = slice(start, start + CHUNK)
+        mine = jnp.where(is_high, d_queries, d_keys)
+        other = jnp.where(is_high, d_keys, d_queries)
+        if added:
+            mine, other = mine + added[0][here, :], other + added[1][here, :]
+        mine_ref[here, :] = mine.astype(mine_ref.dtype)
+        other_ref[here, :] = other.astype(other_ref.dtype)
         d_rate = dot((row <= column).astype(F32), d_running, HIGHEST)
         d_step = direct_sums - jnp.exp(hp_ref[1:2, :]) * d_rate
         d_raw = d_step * sigmoid(raw)
@@ -316,7 +320,7 @@
     for ref, c in ((mine_ref, core), (other_ref, 1 - core)):
         at = pl.multiple_of((2 * x + c) * width, LANES)
         ref[:, :width] = in_ref[:, pl.ds(at, width)]
-        ref[:, width:] = out_ref[pl.ds(at, width), :].T
+        ref[:, width:] = out_ref[:, pl.ds(at, width)]
 
 
 def prepare_call(kernel, columns, place, *weights):
@@ -733,44 +737,208 @@
     )(place, *parts)
 
 
-def forward_call(heads, size, lengths, conv_in, keys_queries, conv_rows, head_rows):
-    blocks = lengths.shape[0]
+def keys_back_kernel(len_ref, mine_ref, core_ref, side_ref, in_ref, rows_ref, d_ref, grads_ref):
+    block = pl.program_id(0)
+    first = len_ref[block, 0]
+    both = first + len_ref[block, 1]
+    tokens, columns = in_ref.shape
+    position = lax.broadcasted_iota(jnp.int32, (tokens, columns), 0)
+    begin = begin_of(position, first, both)
+    inside = [position - delay >= begin for delay in range(1, 4)]
+    inputs = [in_ref[...]]
+    for delay in range(1, 4):
+        shifted = pltpu.roll(inputs[0], delay, 0)
+        inputs.append(jnp.where(inside[delay - 1], shifted, 0.0))
+    pre = rows_ref[4:5, :] + rows_ref[3:4, :] * inputs[0]
+    for delay in range(1, 4):
+        pre = pre + rows_ref[3 - delay : 4 - delay, :] * inputs[delay]
+    sig = sigmoid(pre)
+    d_out = mine_ref[...] + core_ref[...].astype(F32) + side_ref[...].astype(F32)
+    d_pre = d_out * (sig * (1.0 + pre * (1.0 - sig)))
+    d_in = rows_ref[3:4, :] * d_pre
+    for delay in range(1, 4):
+        moved = pltpu.roll(jnp.where(inside[delay - 1], d_pre, 0.0), tokens - delay, 0)
+        d_in = d_in + rows_ref[3 - delay : 4 - delay, :] * moved
+    d_ref[...] = d_in.astype(BF16)
+
+    @pl.when(block == 0)
+    def _():
+        grads_ref[...] = jnp.zeros_like(grads_ref)
+
+    for delay in range(4):
+        grads_ref[3 - delay : 4 - delay, :] += jnp.sum(
+            inputs[delay] * d_pre, axis=0, keepdims=True
+        )
+    grads_ref[4:5, :] += jnp.sum(d_pre, axis=0, keepdims=True)
+
+
+def keys_back_call(lengths, parts, inputs, rows):
+    total, columns = inputs.shape
+    block = pl.BlockSpec((total // 2, columns), lambda b: (b, 0))
+    small = pl.BlockSpec((8, columns), lambda b: (0, 0))
+    return pl.pallas_call(
+        keys_back_kernel,
+        grid=(2,),
+        in_specs=[pl.BlockSpec(memory_space=pltpu.SMEM)] + [block] * 4 + [small],
+        out_specs=[block, small],
+        out_shape=[
+            jax.ShapeDtypeStruct((total, columns), BF16),
+            jax.ShapeDtypeStruct((8, columns), F32),
+        ],
+        compiler_params=pltpu.CompilerParams(vmem_limit_bytes=24 * 1024 * 1024),
+        name="keys_back",
+    )(lengths, *parts, inputs, rows)
+
+
+def small_kernel(heads, size, at_ref, *refs):
+    convs, head_refs, (gain_ref, kq_ref, out_ref) = refs[:3], refs[3:6], refs[6:]
+    p = 2 * at_ref[0] + at_ref[1]
+    width = heads * size
+    most, less = convs[0].shape[1], convs[1].shape[1]
+    out_ref[...] = jnp.zeros_like(out_ref)
+    rest = convs[1][...] + convs[2][...]
+    at = pl.multiple_of(p * width, LANES)
+    out_ref[0:5, pl.ds(at, most)] = convs[0][0:5, :]
+    out_ref[0:5, pl.ds(pl.multiple_of(at + most, LANES), less)] = rest[0:5, :]
+    kq_at = pl.multiple_of(4 * width + at_ref[1] * kq_ref.shape[1], LANES)
+    out_ref[0:5, pl.ds(kq_at, kq_ref.shape[1])] = kq_ref[0:5, :]
+    out_ref[5:6, pl.ds(at, width)] = gain_ref[0:1, :]
+    skip = jnp.concatenate([convs[0][...], rest], axis=1)
+    row, column = iotas(width, LANES)
+    skip = dot(skip, (row // size == column).astype(F32), HIGHEST)
+    sums = head_refs[0][...] + head_refs[1][...] + head_refs[2][...]
+    for field, values in enumerate((sums[0:1], sums[1:2], skip[5:6])):
+        values = jnp.broadcast_to(values, (8, LANES))
+        lane = lax.broadcasted_iota(jnp.int32, (8, LANES), 1)
+        values = pltpu.roll(jnp.where(lane < heads, values, 0.0), heads * p, 1)
+        out_ref[7:8, field * LANES : (field + 1) * LANES] = values[0:1]
+
+
+def small_call(heads, size, channels, place, convs, head_grads, gains, kq_grads):
+    operands = [*convs, *head_grads, gains, kq_grads]
+    return pl.pallas_call(
+        functools.partial(small_kernel, heads, size),
+        in_specs=[pl.BlockSpec(memory_space=pltpu.SMEM)]
+        + [pl.BlockSpec(memory_space=pltpu.VMEM)] * len(operands),
+        out_specs=pl.BlockSpec(memory_space=pltpu.VMEM),
+        out_shape=jax.ShapeDtypeStruct((8, channels), F32),
+        compiler_params=pltpu.CompilerParams(vmem_limit_bytes=24 * 1024 * 1024),
+        name="small_gradients",
+    )(place, *operands)
+
+
+def final_kernel(heads, size, most, by_g, at_ref, *refs):
+    first_both, first_other, held_both, held_other, last_mine, last_core = refs[:6]
+    weight_ref, gain_ref, in_ref, out_ref, norm_ref = refs[6:]
+    far, high = at_ref[0] == 1, at_ref[1] == 1
+    width = heads * size
+    less = width - most
+    rows = in_ref.shape[0]
+    at_values, at_keys = 4 * width, 8 * width
+    state = last_mine.shape[1] - 2 * (less + LANES)
+    at_steps = at_keys + 2 * state
+    norm = jnp.zeros((rows, 1), F32)
+
+    def put(at, values):
+        stop = at + values.shape[1]
+        in_ref[:, at:stop] = values
+        weight = weight_ref[:, at:stop].astype(F32)
+        return jnp.sum(values * weight, axis=1, keepdims=True)
+
+    def share(both, other, p, count, start, stop):
+        columns = slice((p % 2) * count + start, (p % 2) * count + stop)
+        take_other = far if p < 2 else jnp.logical_not(far)
+        return jnp.where(take_other, other[:, columns], both[:, columns]).astype(F32)
+
+    def last_share(core, start, stop):
+        take_core = high if core == 0 else jnp.logical_not(high)
+        columns = slice(start, stop)
+        return jnp.where(take_core, last_core[:, columns], last_mine[:, columns]).astype(F32)
+
+    steps = jnp.zeros((rows, LANES), F32)
+    lane = lax.broadcasted_iota(jnp.int32, (rows, LANES), 1)
+    for p in range(4):
+        first = functools.partial(share, first_both, first_other, p, 2 * width)
+        norm = norm + put(p * width, first(0, width))
+        out_ref[:, p * width : p * width + by_g] = first(2 * width - by_g, 2 * width)
+        out_ref[:, p * width + by_g : (p + 1) * width] = first(width, 2 * width - by_g)
+        at = at_values + p * width
+        norm = norm + put(at, share(held_both, held_other, p, most, 0, most))
+        left = (p // 2) * (less + LANES)
+        norm = norm + put(at + most, last_share(p % 2, left, left + less))
+        drawn = last_share(p % 2, left + less, left + less + LANES)
+        steps = steps + pltpu.roll(jnp.where(lane < heads, drawn, 0.0), heads * p, 1)
+    for core in range(2):
+        at = 2 * (less + LANES)
+        norm = norm + put(at_keys + core * state, last_share(core, at, at + state))
+    norm = norm + put(at_steps, steps[:, : 4 * heads])
+    norm_ref[...] = norm / gain_ref[...]
+
+
+def final_call(heads, size, most, by_g, place, shares, weight, gain):
+    rows, columns = weight.shape
+    operands = [*shares, weight, gain]
+    return pl.pallas_call(
+        functools.partial(final_kernel, heads, size, most, by_g),
+        in_specs=[pl.BlockSpec(memory_space=pltpu.SMEM)]
+        + [pl.BlockSpec(memory_space=pltpu.VMEM)] * len(operands),
+        out_specs=[pl.BlockSpec(memory_space=pltpu.VMEM)] * 3,
+        out_shape=[
+            jax.ShapeDtypeStruct((rows, columns), F32),
+            jax.ShapeDtypeStruct((rows, 4 * heads * size), F32),
+            jax.ShapeDtypeStruct((rows, 1), F32),
+        ],
+        compiler_params=pltpu.CompilerParams(vmem_limit_bytes=40 * 1024 * 1024),
+        cost_estimate=pl.CostEstimate(
+            flops=5_000_000_000, bytes_accessed=16_000_000, transcendentals=0
+        ),
+        name="owner_gradients",
+    )(place, *operands)
+
+
+def forward_call(
+    heads, size, first_block, blocks, lengths, conv_in, keys_queries, conv_rows, head_rows, before=()
+):
     total = conv_in.shape[0]
-    tokens = total // blocks
+    tokens = total // lengths.shape[0]
     width = heads * size
     state = keys_queries.shape[1] // 2
     boundaries = tokens // CHUNK - 1
     return pl.pallas_call(
-        functools.partial(forward_kernel, heads, size),
+        functools.partial(forward_kernel, heads, size, first_block),
         grid=(blocks,),
         in_specs=[
             pl.BlockSpec(memory_space=pltpu.SMEM),
-            pl.BlockSpec((tokens, width), lambda b: (b, 0)),
-            pl.BlockSpec((tokens, LANES), lambda b: (b, width // LANES)),
-            pl.BlockSpec((tokens, 2 * state), lambda b: (b, 0)),
+            pl.BlockSpec((tokens, width), lambda b: (first_block + b, 0)),
+            pl.BlockSpec((tokens, LANES), lambda b: (first_block + b, width // LANES)),
+            pl.BlockSpec((tokens, 2 * state), lambda b: (first_block + b, 0)),
             pl.BlockSpec((8, width), lambda b: (0, 0)),
             pl.BlockSpec((8, LANES), lambda b: (0, 0)),
-        ],
+        ]
+        + [pl.BlockSpec(memory_space=pl.ANY)] * len(before),
         out_specs=[
-            pl.BlockSpec((tokens, width), lambda b: (b, 0)),
-            pl.BlockSpec((1, boundaries, state, width), lambda b: (b, 0, 0, 0)),
+            pl.BlockSpec((tokens, width), lambda b: (first_block + b, 0)),
+            pl.BlockSpec((1, boundaries, state, width), lambda b: (first_block + b, 0, 0, 0)),
+            pl.BlockSpec((tokens, width), lambda b: (first_block + b, 0)),
         ],
         out_shape=[
             jax.ShapeDtypeStruct((total, width), F32),
-            jax.ShapeDtypeStruct((blocks, boundaries, state, width), BF16),
+            jax.ShapeDtypeStruct((lengths.shape[0], boundaries, state, width), BF16),
+            jax.ShapeDtypeStruct((total, width), F32),
         ],
         scratch_shapes=[pltpu.VMEM((state, width), F32)],
+        input_output_aliases={6 + at: at for at in range(len(before))},
         compiler_params=pltpu.CompilerParams(vmem_limit_bytes=40 * 1024 * 1024),
         cost_estimate=pl.CostEstimate(
             flops=blocks * 3_000_000_000, bytes_accessed=blocks * 8_000_000, transcendentals=0
         ),
         name="ssd_forward",
-    )(lengths, conv_in, conv_in, keys_queries, conv_rows, head_rows)
+    )(lengths, conv_in, conv_in, keys_queries, conv_rows, head_rows, *before)
 
 
 def backward_call(
     heads, size, first_head, first_block, blocks,
-    lengths, conv_in, keys_queries, d_out, states, conv_rows, head_rows
+    lengths, place, conv_in, conv_pre, keys_queries, d_out, states, conv_rows, head_rows, before=()
 ):
     tokens = conv_in.shape[0] // lengths.shape[0]
     total = blocks * tokens
@@ -783,11 +951,16 @@
     def rows_of(columns, index):
         return pl.BlockSpec((tokens, columns), lambda b: (first_block + b, index))
 
+    def swapped(b):
+        return b + 1 - 2 * lax.rem(b, 2)
+
     return pl.pallas_call(
         functools.partial(backward_kernel, heads, size, first_head, first_block),
         grid=(blocks,),
         in_specs=[
             pl.BlockSpec(memory_space=pltpu.SMEM),
+            pl.BlockSpec(memory_space=pltpu.SMEM),
+            rows_of(width, part),
             rows_of(width, part),
             rows_of(LANES, steps_at),
             rows_of(2 * state, 0),
@@ -797,18 +970,24 @@
             ),
             pl.BlockSpec((8, width), lambda b: (0, part)),
             pl.BlockSpec((8, LANES), lambda b: (0, 0)),
-        ],
+        ]
+        + [
+            rows_of(state, 0),
+            pl.BlockSpec((tokens, state), lambda b: (swapped(first_block + b), 0)),
+        ][: len(before)],
         out_specs=[
             pl.BlockSpec((tokens, width), lambda b: (b, 0)),
             pl.BlockSpec((tokens, LANES), lambda b: (b, 0)),
-            pl.BlockSpec((tokens, 2 * state), lambda b: (b, 0)),
+            pl.BlockSpec((tokens, state), lambda b: (b, 0)),
+            pl.BlockSpec((tokens, state), lambda b: (swapped(b), 0)),
             pl.BlockSpec((8, width), lambda b: (0, 0)),
             pl.BlockSpec((8, LANES), lambda b: (0, 0)),
         ],
         out_shape=[
             jax.ShapeDtypeStruct((total, width), BF16),
             jax.ShapeDtypeStruct((total, LANES), BF16),
-            jax.ShapeDtypeStruct((total, 2 * state), F32),
+            jax.ShapeDtypeStruct((total, state), F32),
+            jax.ShapeDtypeStruct((total, state), BF16 if before else F32),
             jax.ShapeDtypeStruct((8, width), F32),
             jax.ShapeDtypeStruct((8, LANES), F32),
         ],
@@ -825,7 +1004,7 @@
             transcendentals=0,
         ),
         name="ssd_backward",
-    )(lengths, conv_in, conv_in, keys_queries, d_out, states, conv_rows, head_rows)
+    )(lengths, place, conv_in, conv_pre, conv_in, keys_queries, d_out, states, conv_rows, head_rows, *before)
 
 
 def after(values):
@@ -1133,24 +1312,24 @@
     moved, (small_all, (mine_b, for_core_b)) = phase(
         hop_sends(pieces_a, 1) + [(links.core, lengths)],
         prepare_last,
-        (packed, in_weight, out_weight),
+        (packed, in_weight, out_weight.T),
     )
     lengths_core = moved[-1]
     pieces_a = landed(pieces_a, 1, moved[:-1])
-    y_a = {}
     firsts = [k for k in pieces_a if k]
-    sends = [send for k in firsts for send in rounds(pieces_a[k])]
+    early, late = firsts[:1], firsts[1:]
+    early_sends = [send for k in early for send in rounds(pieces_a[k])]
     moved, _ = phase(
-        hop_sends(pieces_a, 2) + [(swap(4), small_all), (links.core, for_core_b)] + sends
-    )
-    for at, k in enumerate(reversed(firsts)):
-        stop = len(moved) - at * (sides - 1)
-        y_a[k] = moved[stop - (sides - 1) : stop]
+        hop_sends(pieces_a, 2)
+        + [(swap(4), small_all), (links.core, for_core_b)]
+        + early_sends
+    )
     hop_count = len(hops(pieces_a, 2))
     small_all = doubled(small_all, 4, moved[hop_count])
     from_core_b = moved[hop_count + 1]
+    y_moved = moved[hop_count + 2 :]
+    pieces_a = landed(pieces_a, 2, moved[:hop_count])
     pieces_b = {0: links.piece_of(mine_b, from_core_b)}
-    pieces_a = landed(pieces_a, 2, moved[:hop_count])
     bit = 8
     while bit < shards:
         small_all = doubled(small_all, bit, links.flip(small_all, 0, bit))
@@ -1159,17 +1338,19 @@
         values = [send(value) for send, value in hop_sends(pieces_a, stage)]
         pieces_a = landed(pieces_a, stage, values)
     pieces_a, pieces_b, far_hidden = after((pieces_a, pieces_b, far_hidden))
-    rest = [k for k in pieces_a if k and k not in y_a]
+    late = late + [k for k in pieces_a if k and k not in firsts]
+    late_sends = [send for k in late for send in rounds(pieces_a[k])]
     b_firsts = [send(value) for send, value in hop_sends(pieces_b, 1)]
-    sends = [send for k in rest for send in rounds(pieces_a[k])]
     moved, parameters_here = phase(
-        sends + [(links.core, hidden_in), (links.core, far_hidden)],
+        late_sends + [(links.core, hidden_in), (links.core, far_hidden)],
         functools.partial(unpack_call, sizes, heads, size, state, core_place),
         (small_all,),
     )
     core_hidden, far_core_hidden = moved[-2:]
-    for at, k in enumerate(rest):
-        y_a[k] = moved[at * (sides - 1) : (at + 1) * (sides - 1)]
+    y_moved = y_moved + moved[:-2]
+    y_a = {
+        k: y_moved[at * (sides - 1) : (at + 1) * (sides - 1)] for at, k in enumerate(early + late)
+    }
     n_rows, conv_rows, head_rows, kq_rows = parameters_here
     n_gain = n_rows[0]
 
@@ -1198,78 +1379,86 @@
     counts = jnp.stack([pair_lengths // 32, pair_lengths % 32], axis=2).reshape(2, 4).astype(BF16)
     counts = jnp.pad(counts, ((0, 14), (0, state - 4)))
     kq_near = jax.nn.silu(kq_pre).astype(BF16).reshape(2 * tokens, state)
+    count = tokens // 4
+    cuts = [slice(at, at + count) for at in range(0, tokens, count)]
     moved, (w_values, conv_in), b_firsts = phase(
-        [(links.side, jnp.concatenate([kq_near, counts], axis=0))],
+        [
+            (links.side, jnp.concatenate([kq_near, counts], axis=0)),
+            (links.side, back_own[cuts[0]]),
+        ],
         functools.partial(project_call, links_shape, width + LANES, 0, 4, tokens, place),
         (parts_a, normed),
         b_firsts,
     )
     pieces_b = landed(pieces_b, 1, b_firsts)
-    kq_far = moved[0]
+    kq_far, far_back = moved[0], [moved[1]]
     all_counts = jnp.concatenate([counts[:2, :4], kq_far[2 * tokens : 2 * tokens + 2, :4]], axis=0)
     all_counts = all_counts.astype(jnp.int32)
     all_lengths = all_counts[:, 0::2] * 32 + all_counts[:, 1::2]
     kq_half = jnp.concatenate([kq_near, kq_far[: 2 * tokens]], axis=0)
 
-    kq_half, pieces_b, back_own = after((kq_half, pieces_b, back_own))
-    firsts = [k for k in pieces_b if k]
-    b_seconds = [send(value) for send, value in hop_sends(pieces_b, 2)]
-    y_firsts = [[send(value) for send, value in rounds(pieces_b[k])] for k in firsts]
     (kq_core,), _ = phase([(links.core, kq_half)])
     kq_core = kq_core.reshape(2, 2, tokens, state)[:, ::-1].reshape(4 * tokens, state)
     keys_queries = jnp.concatenate(
         [jnp.where(is_high, kq_core, kq_half), jnp.where(is_high, kq_half, kq_core)], axis=1
     )
-    cuts = [slice(0, tokens // 2), slice(tokens // 2, tokens)]
-    moved, (ssd_out, states), (b_seconds, y_firsts) = phase(
-        [(links.side, back_own[cuts[0]])],
-        functools.partial(forward_call, heads, size),
+    firsts = [k for k in pieces_b if k]
+    hop_count = len(hops(pieces_b, 2))
+    moved, before = phase(
+        hop_sends(pieces_b, 2)
+        + rounds(pieces_b[firsts[0]])
+        + [(links.side, back_own[cuts[1]]), (links.core, back_own)],
+        functools.partial(forward_call, heads, size, 0, 2),
         (all_lengths, conv_in, keys_queries, conv_rows, head_rows),
-        (b_seconds, y_firsts),
-    )
-    far_back = [moved[0]]
-    y_b = dict(zip(firsts, y_firsts))
-    pieces_b = landed(pieces_b, 2, b_seconds)
+    )
+    y_b = {firsts[0]: moved[hop_count:-2]}
+    far_back.append(moved[-2])
+    core_back = moved[-1]
+    pieces_b = landed(pieces_b, 2, moved[:hop_count])
     for stage in range(3, groups // 2 + 1):
         values = [send(value) for send, value in hop_sends(pieces_b, stage)]
         pieces_b = landed(pieces_b, stage, values)
-    rest = [k for k in pieces_b if k and k not in y_b]
+    rest = [k for k in pieces_b if k and k not in firsts]
+    moved, (ssd_out, states, conv_pre) = phase(
+        [send for k in firsts[1:] for send in rounds(pieces_b[k])]
+        + [(links.side, back_own[cuts[2]])],
+        functools.partial(forward_call, heads, size, 2, 2),
+        (all_lengths, conv_in, keys_queries, conv_rows, head_rows, before),
+    )
+    far_back.append(moved[-1])
+    for at, k in enumerate(firsts[1:]):
+        y_b[k] = moved[at * (sides - 1) : (at + 1) * (sides - 1)]
     gate_sends = [send for k in rest for send in rounds(pieces_b[k][:, :width])]
     out_sends = [send for k in rest for send in rounds(pieces_b[k][:, width:])]
+    most_back = jnp.concatenate(far_back, axis=0)
     moved, _ = phase(
-        gate_sends
-        + [(links.core, back_own), (links.side, back_own[cuts[1]]), (links.core, far_back[0])]
-    )
-    core_back = moved[-3]
-    far_back.append(moved[-2])
-    far_core_back = [moved[-1]]
-    moved = moved[:-3]
+        gate_sends + [(links.side, back_own[cuts[3]]), (links.core, most_back)]
+    )
+    gate_moved, last_back, far_core_back = moved[:-2], moved[-2], moved[-1]
 
     def last_parts(values):
         latest = {k: values[at * (sides - 1) : (at + 1) * (sides - 1)] for at, k in enumerate(rest)}
         return parts_of(mine_b, from_core_b, pieces_b, {**y_b, **latest})
 
     moved, (w_gate, gate) = phase(
-        out_sends + [(links.core, far_back[1])],
+        out_sends + [(links.core, last_back)],
         functools.partial(project_call, links_shape, width, 0, 4, tokens, place),
-        (last_parts(moved), normed),
-    )
-    far_core_back.append(moved[-1])
-    moved = moved[:-1]
+        (last_parts(gate_moved), normed),
+    )
+    out_moved, last_core_back = moved[:-1], moved[-1]
     back_blocks = [
         back_own,
         core_back,
-        jnp.concatenate(far_back, axis=0),
-        jnp.concatenate(far_core_back, axis=0),
+        jnp.concatenate([most_back, last_back], axis=0),
+        jnp.concatenate([far_core_back, last_core_back], axis=0),
     ]
     w_out, d_branch, sums = branch_back_call(
-        links_shape, width, 1, place, last_parts(moved), back_blocks, gate, ssd_out, conv_rows
+        links_shape, width, 1, place, last_parts(out_moved), back_blocks, gate, ssd_out, conv_rows
     )
     moved, _ = phase([(links.core, sums), (links.side, sums), (links.corner, sums)])
     branch, d_gate, d_ssd, gain_rows = gating_back_call(
         inner, [sums, *moved], gate, ssd_out, d_branch, conv_rows
     )
-    grad_gate_gain = gain_rows[0]
 
     by_g = width // (3 * LANES) * 2 * LANES
     most = heads // 3 * 2
@@ -1277,10 +1466,10 @@
     most_width, less_width = most * size, less * size
     rows_all = 4 * tokens
 
-    def backward(first_head, count, first_block, blocks, d_out):
+    def backward(first_head, count, first_block, blocks, d_out, *before):
         return backward_call(
-            count, size, first_head, first_block, blocks,
-            all_lengths, conv_in, keys_queries, d_out, states, conv_rows, head_rows,
+            count, size, first_head, first_block, blocks, all_lengths, core_place,
+            conv_in, conv_pre, keys_queries, d_out, states, conv_rows, head_rows, before,
         )
 
     def turn(k):
@@ -1321,7 +1510,7 @@
         [(links.core, mixed_send)], first_grads, (normed, d_gate, back_blocks, branch)
     )
     mixed_sum = mixed_keep.astype(F32) + moved[0].astype(F32)
-    moved, (d_in_0, d_steps_0, d_kq_0, conv_grads_0, head_grads_0) = phase(
+    moved, (d_in_0, d_steps_0, kq_mine_0, kq_other_0, conv_grads_0, head_grads_0) = phase(
         a_sends(first_parts[1:])
         + g_sends(out_parts[1:])
         + [(links.side, mixed_sum[1].astype(BF16))],
@@ -1348,7 +1537,7 @@
         return dot_nt(d_gate[rows], w_gate) + dot_nt(d_rest, w_values)
 
     def far_work(d_ssd):
-        results = backward(most, less, 2, 2, d_ssd)
+        results = backward(most, less, 2, 2, d_ssd, kq_mine_0, kq_other_0)
         d_steps = d_steps_0[2 * tokens :] + results[1]
         return results, d_steps, back_project(2 * tokens, results[0], d_steps).astype(BF16)
 
@@ -1356,38 +1545,29 @@
         a_sends(values_0[1:]) + first_sends[:2], far_work, (d_ssd,)
     )
     first_far = moved[count_a:]
-    d_in_far, _, d_kq_far, conv_grads_far, head_grads_far = results
+    d_in_far, _, kq_far_mine, kq_far_core, conv_grads_far, head_grads_far = results
     held_0 = combine_call(groups, place, [values_0[0], *moved[:count_a]])
     held_sends = g_sends(held_0[1:])
     held_sends = held_sends[:1] + held_sends[-1:] + held_sends[1:-1]
 
-    def halves(first_rows, second_rows):
-        rows = (first_rows + second_rows).reshape(2, tokens, 2 * state)
-        mine = jnp.where(is_high, rows[..., state:], rows[..., :state])
-        other = jnp.where(is_high, rows[..., :state], rows[..., state:])
-        return mine, other[::-1].astype(BF16)
-
-    kq_far_mine, kq_far_core = halves(d_kq_0[2 * tokens :], d_kq_far)
     moved, _ = phase([(links.core, kq_far_core), (links.core, d_far_parts[tokens:])])
     kq_far_sum = (kq_far_mine + moved[0].astype(F32)).astype(BF16)
     d_far = (d_far_parts[:tokens].astype(F32) + moved[1].astype(F32)).astype(BF16)
     moved, results = phase(
         [(links.side, kq_far_sum)]
         + first_sends[2:]
-        + [(links.side, d_far[cuts[0]])]
+        + [(links.side, d_far[: tokens // 2])]
         + a_sends(out_others),
         functools.partial(backward, most, less, 0, 2),
-        (d_ssd,),
-    )
-    d_in_near, d_steps_near, d_kq_near, conv_grads_near, head_grads_near = results
+        (d_ssd, kq_mine_0, kq_other_0),
+    )
+    d_in_near, d_steps_near, kq_near_mine, kq_near_core, conv_grads_near, head_grads_near = results
     kq_from_side = moved[0]
     first_far = first_far + moved[1 : count_g - 1]
     far_d = [moved[count_g - 1]]
     out_piece = total(out_mine, moved[count_g:]).astype(BF16)
     first_piece = total(first_held[0], first_far).astype(BF16)
     first_piece = jnp.concatenate([first_piece, out_piece], axis=1)
-    kq_near_mine, kq_near_core = halves(d_kq_0[: 2 * tokens], d_kq_near)
-
     d_steps_near = d_steps_0[: 2 * tokens] + d_steps_near
     d_steps = jnp.concatenate([d_steps_near, d_steps_far], axis=0)
     moved, d_near = phase(
@@ -1396,10 +1576,9 @@
         (d_in_near, d_steps_near),
     )
     held_far = moved[1:]
-    d_kq = kq_near_mine + moved[0].astype(F32) + kq_from_side.astype(F32)
-    kq_sig = sigmoid(kq_pre)
-    d_kq_pre = d_kq * (kq_sig * (1.0 + kq_pre * (1.0 - kq_sig)))
-    d_kq_in = causal_conv_back(d_kq_pre, begin, kq_taps).astype(BF16).reshape(2 * tokens, state)
+    d_kq_in, kq_grads = keys_back_call(
+        all_lengths, [kq_near_mine, moved[0], kq_from_side], kq_in, kq_rows
+    )
     half_rows = 2 * tokens
 
     def last_grads(normed, d_in_near, d_in_far, d_steps, d_kq_in):
@@ -1417,9 +1596,9 @@
                 [(normed, half_rows, 0, d_kq_in, 0, state, 0)],
             ],
         )
-        return last, dot_nt(d_kq_in, w_kq)
-
-    moved, (last_parts_here, kq_part) = phase(
+        return last
+
+    moved, last_parts_here = phase(
         rounds(first_piece) + held_sends[1:],
         last_grads,
         (normed, d_in_near, d_in_far, d_steps, d_kq_in),
@@ -1428,26 +1607,17 @@
     held_far = held_far + moved[count_a:]
     held_piece = total(held_0[0], held_far).astype(BF16)
     first_rows = links.rows_of_core(links.join_a(first_piece, first_y))
-    d_near = d_near + kq_part
-    d_near_keep, d_near_send = d_near[:tokens], d_near[tokens:].astype(BF16)
-
-    conv_grads = jnp.concatenate([conv_grads_0, conv_grads_far + conv_grads_near], axis=1)
-    head_grads = head_grads_0 + head_grads_far + head_grads_near
-    d_kq_rows = [jnp.sum(kq_shifted[delay] * d_kq_pre, axis=(0, 1)) for delay in (3, 2, 1, 0)]
-    d_kq_rows = jnp.stack(d_kq_rows + [jnp.sum(d_kq_pre, axis=(0, 1))])
-    small = jnp.zeros((8, channels), F32)
-    small = lax.dynamic_update_slice(small, conv_grads[:5], (0, p * width))
-    small = lax.dynamic_update_slice(small, d_kq_rows, (0, kq_columns))
-    small = lax.dynamic_update_slice(small, grad_gate_gain[None], (5, p * width))
-    grad_skip = conv_grads[5].reshape(heads, size).sum(axis=1)
-    head_all = jnp.stack([head_grads[0, :heads], head_grads[1, :heads], grad_skip])
-    small_heads = jnp.zeros((3, all_heads), F32)
-    small_heads = lax.dynamic_update_slice(small_heads, head_all, (0, p * heads))
-    small = lax.dynamic_update_slice(small, small_heads.reshape(1, -1), (7, 0))
-
+    d_near_keep = d_near[:tokens] + dot_nt(d_kq_in[:tokens], w_kq)
+    d_near_send = (d_near[tokens:] + dot_nt(d_kq_in[tokens:], w_kq)).astype(BF16)
+    small = small_call(
+        heads, size, channels, core_place,
+        [conv_grads_0, conv_grads_far, conv_grads_near],
+        [head_grads_0, head_grads_far, head_grads_near],
+        gain_rows, kq_grads,
+    )
     moved, _ = phase(
         a_sends(last_parts_here[1:])
-        + [(links.side, d_far[cuts[1]]), (links.core, d_near_send), (links.core, small)]
+        + [(links.side, d_far[tokens // 2 :]), (links.core, d_near_send), (links.core, small)]
         + [(links.core, first_rows[1])]
     )
     far_d.append(moved[count_a])
@@ -1459,7 +1629,7 @@
         axis=1,
     )
     last_held = combine_call(groups, place, [last_parts_here[0], *moved[:count_a]])
-    first_half = first_both.shape[1] // 2
+    first_half = first_both.shape[1] // (3 * LANES) * 2 * LANES
     moved, _ = phase(
         g_sends(last_held[1:])
         + [(links.side, first_both[:, :first_half])]
@@ -1485,7 +1655,9 @@
         rounds(last_piece)
         + [(links.side, last_piece), (links.core, held_rows[1]), (swap(2), small)]
         + diagonals
-    )
+        + [(links.side, first_both[:, first_half:])]
+    )
+    first_other.append(moved.pop())
     same_x = links.join_a(last_piece, moved[:count_a])
     held_core, small = moved[count_a + 1], small + moved[count_a + 2]
     other_x = links.join_a(moved[count_a], moved[count_a + 3 :])
@@ -1506,41 +1678,27 @@
         axis=1,
     )
     moved, grad_hidden = phase(
-        [(links.side, first_both[:, first_half:]), (links.side, held_both)]
-        + [(links.core, last_rows[1]), (swap(4), small)],
+        [(links.side, held_both), (links.core, last_rows[1]), (swap(4), small)],
         final_norm,
         (d_near, jnp.concatenate(far_d, axis=0)),
     )
-    small = small + moved[3]
+    small = small + moved[2]
     bit = 8
     while bit < shards:
         small = small + links.flip(small, 0, bit)
         bit *= 2
-    first_other = jnp.concatenate([first_other[0], moved[0]], axis=1)
-    held_other, last_core = moved[1], moved[2]
-    first_low = jnp.where(is_far, first_other, first_both)
-    first_high = jnp.where(is_far, first_both, first_other)
-    held_low = jnp.where(is_far, held_other, held_both)
-    held_high = jnp.where(is_far, held_both, held_other)
-    low = jnp.where(is_high, last_core, last_rows[0])
-    high = jnp.where(is_high, last_rows[0], last_core)
-    first_width = width + (width - by_g) + by_g
-    first_shares = [
-        first_low[:, :first_width], first_low[:, first_width:],
-        first_high[:, :first_width], first_high[:, first_width:],
-    ]
-    held_shares = [
-        held_low[:, :most_width], held_low[:, most_width:],
-        held_high[:, :most_width], held_high[:, most_width:],
-    ]
-    last_shares = [
-        low[:, :at_kq], high[:, :at_kq], low[:, at_kq : 2 * at_kq], high[:, at_kq : 2 * at_kq]
-    ]
-    kq_shares = [low[:, 2 * at_kq :], high[:, 2 * at_kq :]]
-    moved, _ = phase(
+    first_other = jnp.concatenate(first_other, axis=1)
+    held_other, last_core = moved[0], moved[1]
+    moved, (grad_in, grad_out, grad_norm) = phase(
         [(links.side, small)]
         + rounds(small)
-        + [(lambda value, j=j: links.diagonal(value, j), small) for j in range(1, sides)]
+        + [(lambda value, j=j: links.diagonal(value, j), small) for j in range(1, sides)],
+        functools.partial(final_call, heads, size, most_width, by_g, core_place),
+        (
+            [first_both, first_other, held_both, held_other, last_rows[0], last_core],
+            in_weight,
+            norm_gain.astype(F32)[:, None],
+        ),
     )
     small = total(small, moved)
 
@@ -1548,26 +1706,14 @@
         return lax.dynamic_slice_in_dim(array, links.shard * count, count, array.ndim - 1)
 
     grad_conv = own_slice(small[:5], channels // shards)
-    grad_heads = own_slice(small[7, : 3 * all_heads].reshape(3, all_heads), all_heads // shards)
-
-    grad_in = jnp.concatenate(
-        [share[:, :width] for share in first_shares]
-        + [part for pair in zip(held_shares, last_shares) for part in (pair[0], pair[1][:, :less_width])]
-        + kq_shares
-        + [share[:, less_width : less_width + heads] for share in last_shares],
-        axis=1,
-    ).astype(F32)
-    out_shares = [
-        part
-        for share in first_shares
-        for part in (share[:, 2 * width - by_g :], share[:, width : 2 * width - by_g])
+    grad_heads = [
+        own_slice(small[7, field * LANES : field * LANES + all_heads], all_heads // shards)
+        for field in range(3)
     ]
-    grad_norm = jnp.sum(grad_in * in_weight.astype(F32), axis=1) / norm_gain.astype(F32)
-    grad_out = jnp.concatenate(out_shares, axis=1).astype(F32).T
     return (
         mixed,
         grad_hidden,
-        grad_norm,
+        grad_norm[:, 0],
         grad_in,
         grad_conv[:4],
         grad_conv[4],
@@ -1575,7 +1721,7 @@
         grad_heads[1],
         grad_heads[2],
         own_slice(small[5, :inner], inner // shards),
-        grad_out,
+        grad_out.T,
     )
 
 

time: 531 us -> 475 us (0.89)
  local copies, waits for them, and re-layouts: 78.1 us -> 39.4 us
  other arithmetic: 65.5 us -> 39.3 us
  waiting for transfers between devices: 106 us -> 120 us
  Pallas kernels: 163 us -> 173 us
  starting transfers between devices: 76.1 us -> 67.3 us
    ppermute x74 -> x76, waiting for transfers between devices: 106 us -> 120 us  [send(): return lax.ppermute(value, ('rep', 'fsdp'), pairs)]
    pallas_call x1 -> x5, Pallas kernels: 19.7 us -> 30.2 us  [the longest x2 23 us: forward_call(): pl.pallas_call(functools.partial(forward_kernel, heads, size, first_block...]
    slice x19 -> x4, local copies, waits for them, and re-layouts: 11.6 us -> 2.49 us  [the longest x1 1.24 us: per_device(): d_far[tokens // 2:]]
    unnamed x314 -> x224, local copies, waits for them, and re-layouts: 35.9 us -> 27 us
    ppermute x74 -> x76, starting transfers between devices: 76.1 us -> 67.3 us  [send(): return lax.ppermute(value, ('rep', 'fsdp'), pairs)]
    reduce_sum x3 -> x0, other arithmetic: 7.13 us -> none  [the longest x1 4.64 us: per_device(): jnp.sum(grad_in * in_weight.astype(F32), axis=1) / norm_gain.astype(F32)]
    add x6 -> x1, other arithmetic: 7.76 us -> 1.57 us  [per_device(): small = small + moved[2]]
    dynamic_update_slice x5 -> x0, local copies, waits for them, and re-layouts: 5.81 us -> none  [the longest x1 1.51 us: per_device(): small = lax.dynamic_update_slice(small, conv_grads[:5], (0, p * width))]
  transfers between devices with their start and end apart: 74 -> 76, of which waited for: 25 -> 25; matrix products, arithmetic and copies ran while one was open for 13% -> 9% of each run, Pallas kernels for 22% -> 29%
where the time goes in v3:
time: 475 us; the launch traced here: 468 us
  Pallas kernels  173 us (36%)
  waiting for transfers between devices  120 us (25%)
  starting transfers between devices  67.3 us (14%)
  local copies, waits for them, and re-layouts  39.4 us (8%)
  other arithmetic  39.3 us (8%)
  matrix products  26.2 us (6%)
    ppermute x76, waiting for transfers between devices, send(): return lax.ppermute(value, ('rep', 'fsdp'), pairs)  120 us
    ppermute x76, starting transfers between devices, send(): return lax.ppermute(value, ('rep', 'fsdp'), pairs)  67.3 us
    pallas_call x3, Pallas kernels, backward_call(): pl.pallas_call(functools.partial(backward_kernel, heads, size, first_head...  52.9 us
    pallas_call x4, Pallas kernels, weight_grad_call(): pl.pallas_call(functools.partial(weight_grad_kernel, links_shape, shapes,...  31.9 us
    unnamed x224, local copies, waits for them, and re-layouts  27 us
    dot_general x7, matrix products, dot_nt(): lax.dot_general(left, right, (((1,), (1,)), ((), ())), preferred_element_...  26.2 us
    pallas_call x2, Pallas kernels, forward_call(): pl.pallas_call(functools.partial(forward_kernel, heads, size, first_block...  23 us
    pallas_call x3, Pallas kernels, project_call(): pl.pallas_call(functools.partial(project_kernel, links_shape), grid=(bloc...  19.9 us
  transfers between devices with their start and end apart: 76, of which 25 were waited for; matrix products, arithmetic and copies ran while one was open for 9% of the time, Pallas kernels for 29%

profile of v3, /device:TPU:0, one launch (start us, length us, event | category | flops | bytes accessed | tf_op | source)
XLA Modules:
  0.0 467.9 jit_solution(16893116055946686088)
XLA Ops:
  18.7 13.1 %collective-permute-done.5 = bf16[16,512]{1,0:T(8,128)(2,1)S(1)} collective-permute-done((bf16[16,512]{1,0:T(8,128)(2,1)S(1)}, bf16[16,512]{1,0:T(8,128)(2,1)S(1)}, u32[]{:S(2)}, u32[]{:S(2)}) %collective-permute-start.5) | collective-permute-done | bytes 16416 | tf_op jit(solution)/shard_map/ppermute | solution.py:1044
  36.6 9.3 %collective-permute-done.7 = bf16[32,512]{1,0:T(8,128)(2,1)S(1)} collective-permute-done((bf16[32,512]{1,0:T(8,128)(2,1)S(1)}, bf16[32,512]{1,0:T(8,128)(2,1)S(1)}, u32[]{:S(2)}, u32[]{:S(2)}) %collective-permute-start.7) | collective-permute-done | bytes 32800 | tf_op jit(solution)/shard_map/ppermute | solution.py:1044
  54.5 6.7 %collective-permute-done.11.refs_5_ = bf16[192,1024]{1,0:T(8,128)(2,1)S(1)} collective-permute-done((bf16[192,1024]{1,0:T(8,128)(2,1)}, bf16[192,1024]{1,0:T(8,128)(2,1)S(1)}, u32[]{:S(2)}, u32[]{:S(2)}) %collective-permute-start.11) | collective-permute-done | bytes 393248 | tf_op jit(solution)/shard_map/ppermute | solution.py:1044
  61.2 7.5 %collective-permute-done.12.refs_3_ = bf16[192,1024]{1,0:T(8,128)(2,1)S(1)} collective-permute-done((bf16[192,1024]{1,0:T(8,128)(2,1)}, bf16[192,1024]{1,0:T(8,128)(2,1)S(1)}, u32[]{:S(2)}, u32[]{:S(2)}) %collective-permute-start.12) | collective-permute-done | bytes 393248 | tf_op jit(solution)/shard_map/ppermute | solution.py:1044
  79.6 10.2 %project.4 = (bf16[1536,896]{1,0:T(8,128)(2,1)S(1)}, f32[2048,896]{1,0:T(8,128)}) custom-call(s32[3]{0:T(128)S(1)} %pad_add_fusion.2.at_ref, bf16[192,1024]{1,0:T(8,128)(2,1)S(1)} %get-tuple-element.420.own_ref, bf16[192,1024]{1,0:T(8,128)(2,1)S(1)} %copy-done.26, bf16[192,1024]{1,0:T(8,128)(2,1)} %collective-permute-done.1.refs_0_, ...), custom_call_target="tpu_custom_call" | custom-call | flops 5637144576 | bytes 6291456 | tf_op jit(solution)/shard_map/project/pallas_call | solution.py:444
  102.0 11.5 %ssd_forward.2 = (f32[2048,768]{1,0:T(8,128)S(1)}, bf16[4,3,128,768]{3,2,1,0:T(8,128)(2,1)S(1)}, f32[2048,768]{1,0:T(8,128)}) custom-call(s32[4,2]{1,0:T(4,128)S(1)} %multiply_add_fusion.len_ref, f32[2048,896]{1,0:T(8,128)} %get-tuple-element.460.u_ref.dt_ref, f32[2048,896]{1,0:T(8,128)} %get-tuple-element.460.u_ref.dt_ref, ...), custom_call_target="tpu_custom_call" | custom-call | flops 6000000000 | bytes 16000000 | tf_op jit(solution)/shard_map/ssd_forward/pallas_call | solution.py:907
  118.9 11.5 %ssd_forward.3 = (f32[2048,768]{1,0:T(8,128)S(1)}, bf16[4,3,128,768]{3,2,1,0:T(8,128)(2,1)S(1)}, f32[2048,768]{1,0:T(8,128)}) custom-call(s32[4,2]{1,0:T(4,128)S(1)} %multiply_add_fusion.len_ref, f32[2048,896]{1,0:T(8,128)} %get-tuple-element.460.u_ref.dt_ref, ...), custom_call_target="tpu_custom_call", output_to_operand_aliasing={{0}: (6, {}), {1}: (7, {}), {2}: (8, {})} | custom-call | flops 6000000000 | bytes 16000000 | tf_op jit(solution)/shard_map/ssd_forward/pallas_call | solution.py:907
  135.9 6.9 %collective-permute-done.26.refs_3_ = bf16[192,768]{1,0:T(8,128)(2,1)S(1)} collective-permute-done((bf16[192,768]{1,0:T(8,128)(2,1)S(1)}, bf16[192,768]{1,0:T(8,128)(2,1)S(1)}, u32[]{:S(2)}, u32[]{:S(2)}) %collective-permute-start.26) | collective-permute-done | bytes 294944 | tf_op jit(solution)/shard_map/ppermute | solution.py:1044
  146.8 7.3 %project.5 = (bf16[1536,768]{1,0:T(8,128)(2,1)S(1)}, f32[2048,768]{1,0:T(8,128)S(1)}) custom-call(s32[3]{0:T(128)S(1)} %pad_add_fusion.2.at_ref, bf16[192,1536]{1,0:T(8,128)(2,1)S(1)} %copy-done.22, bf16[192,1536]{1,0:T(8,128)(2,1)S(1)} %copy-done.24, bf16[192,1536]{1,0:T(8,128)(2,1)} %collective-permute-done.17.refs_0_, ...), custom_call_target="tpu_custom_call" | custom-call | flops 4831838208 | bytes 6291456 | tf_op jit(solution)/shard_map/project/pallas_call | solution.py:444
  160.0 16.1 %branch_back.1 = (bf16[1536,768]{1,0:T(8,128)(2,1)}, f32[2048,768]{1,0:T(8,128)}, f32[8,2048]{1,0:T(8,128)}) custom-call(s32[3]{0:T(128)} %copy-done.43, bf16[192,1536]{1,0:T(8,128)(2,1)} %copy-done.20, bf16[192,1536]{1,0:T(8,128)(2,1)} %copy-done.23, bf16[192,1536]{1,0:T(8,128)(2,1)} %collective-permute-done.17.refs_0_, bf16[192,1536]{1,0:T(8,128)(2,1)} %copy-done.36, ...), custom_call_target="tpu_custom_call" | custom-call | flops 4831838208 | bytes 6291456 | tf_op jit(solution)/shard_map/branch_back/pallas_call | solution.py:499
  183.6 9.2 %gating_back.1 = (bf16[2048,768]{1,0:T(8,128)(2,1)S(1)}, bf16[2048,768]{1,0:T(8,128)(2,1)S(1)}, f32[2048,768]{1,0:T(8,128)S(1)}, f32[8,768]{1,0:T(8,128)S(1)}) custom-call(f32[8,2048]{1,0:T(8,128)S(1)} %copy-done.40, f32[8,2048]{1,0:T(8,128)S(1)} %collective-permute-done.31.core_ref, f32[8,2048]{1,0:T(8,128)S(1)} %collective-permute-done.32.side_ref, ...), custom_call_target="tpu_custom_call" | custom-call | flops 31457280 | bytes 31457280 | tf_op jit(solution)/shard_map/gating_back/pallas_call | solution.py:566
  202.6 6.4 %weight_grad.5 = (bf16[384,512]{1,0:T(8,128)(2,1)S(1)}, bf16[384,512]{1,0:T(8,128)(2,1)S(1)}, bf16[384,512]{1,0:T(8,128)(2,1)S(1)}, bf16[384,512]{1,0:T(8,128)(2,1)S(1)}) custom-call(s32[3]{0:T(128)S(1)} %copy-done.44, bf16[512,1536]{1,0:T(8,128)(2,1)S(1)} %copy-done.4, bf16[512,1536]{1,0:T(8,128)(2,1)S(1)} %copy-done.11, bf16[512,1536]{1,0:T(8,128)(2,1)} %copy-done.63, ...), custom_call_target="tpu_custom_call" | custom-call | flops 805306368 | bytes 1572864 | tf_op jit(solution)/shard_map/weight_grad/pallas_call | solution.py:694
  209.0 11.4 %weight_grad.4 = (bf16[4,192,1024]{2,1,0:T(8,128)(2,1)S(1)}, bf16[4,192,1024]{2,1,0:T(8,128)(2,1)S(1)}) custom-call(s32[3]{0:T(128)S(1)} %copy-done.44, bf16[2048,1536]{1,0:T(8,128)(2,1)} %copy-done.2, bf16[512,1536]{1,0:T(8,128)(2,1)S(1)} %copy-done.4, bf16[512,1536]{1,0:T(8,128)(2,1)} %copy-done.10, bf16[512,1536]{1,0:T(8,128)(2,1)} %copy-done.63, ...), custom_call_target="tpu_custom_call" | custom-call | flops 6442450944 | bytes 6291456 | tf_op jit(solution)/shard_map/weight_grad/pallas_call | solution.py:694
  229.9 31.2 %ssd_backward.3 = (bf16[2048,512]{1,0:T(8,128)(2,1)S(1)}, bf16[2048,128]{1,0:T(8,128)(2,1)S(1)}, f32[2048,128]{1,0:T(8,128)S(1)}, f32[2048,128]{1,0:T(8,128)S(1)...) custom-call(s32[4,2]{1,0:T(4,128)S(1)} %multiply_add_fusion.len_ref, s32[2]{0:T(128)S(1)} %pad_add_fusion.3.at_ref, ...), custom_call_target="tpu_custom_call" | custom-call | flops 32000000000 | bytes 32000000 | tf_op jit(solution)/shard_map/ssd_backward/pallas_call | solution.py:957
  264.9 6.1 %weight_grad.6 = (bf16[4,192,512]{2,1,0:T(8,128)(2,1)S(1)}, bf16[4,192,512]{2,1,0:T(8,128)(2,1)S(1)}) custom-call(s32[3]{0:T(128)S(1)} %copy-done.44, bf16[2048,1536]{1,0:T(8,128)(2,1)} %copy-done.2, bf16[2048,512]{1,0:T(8,128)(2,1)S(1)} %get-tuple-element.547.refs_1_), custom_call_target="tpu_custom_call" | custom-call | flops 3221225472 | bytes 6291456 | tf_op jit(solution)/shard_map/weight_grad/pallas_call | solution.py:694
  283.8 10.8 %ssd_backward.4 = (bf16[1024,256]{1,0:T(8,128)(2,1)S(1)}, bf16[1024,128]{1,0:T(8,128)(2,1)S(1)}, f32[1024,128]{1,0:T(8,128)S(1)}, bf16[1024,128]{1,0:T(8,128)(2,...) custom-call(s32[4,2]{1,0:T(4,128)S(1)} %multiply_add_fusion.len_ref, s32[2]{0:T(128)S(1)} %pad_add_fusion.3.at_ref, ...), custom_call_target="tpu_custom_call" | custom-call | flops 8000000000 | bytes 16000000 | tf_op jit(solution)/shard_map/ssd_backward/pallas_call | solution.py:957
  313.0 10.8 %ssd_backward.5 = (bf16[1024,256]{1,0:T(8,128)(2,1)S(1)}, bf16[1024,128]{1,0:T(8,128)(2,1)S(1)}, f32[1024,128]{1,0:T(8,128)S(1)}, bf16[1024,128]{1,0:T(8,128)(2,...) custom-call(s32[4,2]{1,0:T(4,128)S(1)} %multiply_add_fusion.len_ref, s32[2]{0:T(128)S(1)} %pad_add_fusion.3.at_ref, ...), custom_call_target="tpu_custom_call" | custom-call | flops 8000000000 | bytes 16000000 | tf_op jit(solution)/shard_map/ssd_backward/pallas_call | solution.py:957
  323.9 10.3 %collective-permute-done.45.side_ref = bf16[1024,128]{1,0:T(8,128)(2,1)S(1)} collective-permute-done((bf16[1024,128]{1,0:T(8,128)(2,1)S(1)}, bf16[1024,128]{1,0:T(8,128)(2,1)S(1)}, u32[]{:S(2)}, u32[]{:S(2)}) %collective-permute-start.45) | collective-permute-done | bytes 262176 | tf_op jit(solution)/shard_map/ppermute | solution.py:1044
  355.9 8.0 %weight_grad.7 = (bf16[4,192,512]{2,1,0:T(8,128)(2,1)S(1)}, bf16[4,192,512]{2,1,0:T(8,128)(2,1)}) custom-call(s32[3]{0:T(128)S(1)} %copy-done.44, bf16[2048,1536]{1,0:T(8,128)(2,1)} %copy-done.2, bf16[1024,256]{1,0:T(8,128)(2,1)S(1)} %copy-done.39, bf16[1024,256]{1,0:T(8,128)(2,1)S(1)} %get-tuple-element.626.refs_2_, ...), custom_call_target="tpu_custom_call" | custom-call | flops 1610612736 | bytes 3145728 | tf_op jit(solution)/shard_map/weight_grad/pallas_call | solution.py:694
  372.0 15.0 %collective-permute-done.54.refs_1_ = bf16[4,192,512]{2,1,0:T(8,128)(2,1)S(1)} collective-permute-done((bf16[4,192,512]{2,1,0:T(8,128)(2,1)}, bf16[4,192,512]{2,1,0:T(8,128)(2,1)S(1)}, u32[]{:S(2)}, u32[]{:S(2)}) %collective-permute-start.54) | collective-permute-done | bytes 786464 | tf_op jit(solution)/shard_map/ppermute | solution.py:1044
  399.6 6.7 %collective-permute-done.60 = bf16[192,512]{1,0:T(8,128)(2,1)S(1)} collective-permute-done((bf16[192,512]{1,0:T(8,128)(2,1)S(1)}, bf16[192,512]{1,0:T(8,128)(2,1)S(1)}, u32[]{:S(2)}, u32[]{:S(2)}) %collective-permute-start.60) | collective-permute-done | bytes 196640 | tf_op jit(solution)/shard_map/ppermute | solution.py:1044
  406.3 7.4 %collective-permute-done.62 = bf16[192,2048]{1,0:T(8,128)(2,1)S(1)} collective-permute-done((bf16[192,2048]{1,0:T(8,128)(2,1)S(1)}, bf16[192,2048]{1,0:T(8,128)(2,1)S(1)}, u32[]{:S(2)}, u32[]{:S(2)}) %collective-permute-start.62) | collective-permute-done | bytes 786464 | tf_op jit(solution)/shard_map/ppermute | solution.py:1044
  421.9 7.0 %collective-permute-done.65 = bf16[192,512]{1,0:T(8,128)(2,1)S(1)} collective-permute-done((bf16[192,512]{1,0:T(8,128)(2,1)S(1)}, bf16[192,512]{1,0:T(8,128)(2,1)S(1)}, u32[]{:S(2)}, u32[]{:S(2)}) %collective-permute-start.65) | collective-permute-done | bytes 196640 | tf_op jit(solution)/shard_map/ppermute | solution.py:1044
  438.4 5.8 %fusion.4 = f32[512,1536]{1,0:T(8,128)} fusion(bf16[512,1536]{1,0:T(8,128)(2,1)} %refs_0_.1, f32[512,1536]{1,0:T(8,128)} %copy-done.60, bf16[512,1536]{1,0:T(8,128)(2,1)S(1)} %pad_maximum_fusion, f32[512]{0:T(512)S(1)} %get-tuple-element.716, f32[1536]{0:T(1024)S(1)} %slice_reduce_fusion.1, f32[512]{0:T(512)S(1)} %get-tuple-element.715, ...), kind=kLoop, calls=%fused_computation.11 | loop fusion | flops 7864320 | bytes 11020800 | tf_op jit(solution)/shard_map/sub | solution.py:1648
  (493 shorter events, 218.3 us)
Async XLA Ops:
  7.2 39.8 %collective-permute-start.10 = (bf16[512,1536]{1,0:T(8,128)(2,1)}, bf16[512,1536]{1,0:T(8,128)(2,1)}, u32[]{:S(2)}, u32[]{:S(2)}) collective-permute-start(bf16[512,1536]{1,0:T(8,128)(2,1)} %refs_0_.1), channel_id=1, source_target_pairs={{0,8},{1,9},{2,10},{3,11},{4,12},{5,13},{6,14},{7,15},{8,0},{9,1},... | collective-permute-start | bytes 4718600 | tf_op jit(solution)/shard_map/ppermute | solution.py:1044
  10.5 21.4 %collective-permute-start.1 = (bf16[192,1024]{1,0:T(8,128)(2,1)}, bf16[192,1024]{1,0:T(8,128)(2,1)}, u32[]{:S(2)}, u32[]{:S(2)}) collective-permute-start(bf16[192,1024]{1,0:T(8,128)(2,1)} %broadcast_select_fusion.8), channel_id=1, source_target_pairs={{0,2},{1,3},{2,4},{3,5},{4,6},{5,7},{6,0},{7,1},{8,10},{9,11},{10,... | collective-permute-start | bytes 1179656 | tf_op jit(solution)/shard_map/ppermute | solution.py:1044
  12.0 19.9 %collective-permute-start.2 = (bf16[192,1024]{1,0:T(8,128)(2,1)}, bf16[192,1024]{1,0:T(8,128)(2,1)}, u32[]{:S(2)}, u32[]{:S(2)}) collective-permute-start(bf16[192,1024]{1,0:T(8,128)(2,1)} %broadcast_select_fusion.8), channel_id=1, source_target_pairs={{0,6},{1,7},{2,0},{3,1},{4,2},{5,3},{6,4},{7,5},{8,14},{9,15},{10,... | collective-permute-start | bytes 1179656 | tf_op jit(solution)/shard_map/ppermute | solution.py:1044
  46.9 21.8 %collective-permute-start.13 = (bf16[512,1536]{1,0:T(8,128)(2,1)}, bf16[512,1536]{1,0:T(8,128)(2,1)}, u32[]{:S(2)}, u32[]{:S(2)}) collective-permute-start(bf16[512,1536]{1,0:T(8,128)(2,1)} %refs_0_.1), channel_id=1, source_target_pairs={{0,1},{1,0},{2,3},{3,2},{4,5},{5,4},{6,7},{7,6},{8,9},{9,8},{10,11... | collective-permute-start | bytes 4718600 | tf_op jit(solution)/shard_map/ppermute | solution.py:1044
  47.0 21.8 %collective-permute-start.14 = (bf16[512,1536]{1,0:T(8,128)(2,1)}, bf16[512,1536]{1,0:T(8,128)(2,1)}, u32[]{:S(2)}, u32[]{:S(2)}) collective-permute-start(bf16[512,1536]{1,0:T(8,128)(2,1)} %collective-permute-done.10.refs_2_), channel_id=1, source_target_pairs={{0,1},{1,0},{2,3},{3,2},{4,5},{5,4},{6,7},{7,6},{8,9},{9,8},{10,11... | collective-permute-start | bytes 4718600 | tf_op jit(solution)/shard_map/ppermute | solution.py:1044
  50.6 18.2 %collective-permute-start.12 = (bf16[192,1024]{1,0:T(8,128)(2,1)}, bf16[192,1024]{1,0:T(8,128)(2,1)S(1)}, u32[]{:S(2)}, u32[]{:S(2)}) collective-permute-start(bf16[192,1024]{1,0:T(8,128)(2,1)} %collective-permute-done.6.refs_2_), channel_id=1, source_target_pairs={{0,16},{1,17},{2,18},{3,19},{4,20},{5,21},{6,22},{7,23},{8,24},{9,... | collective-permute-start | bytes 1179656 | tf_op jit(solution)/shard_map/ppermute | solution.py:1044
  52.5 38.9 %collective-permute-start.18 = (bf16[192,1536]{1,0:T(8,128)(2,1)}, bf16[192,1536]{1,0:T(8,128)(2,1)S(1)}, u32[]{:S(2)}, u32[]{:S(2)}) collective-permute-start(bf16[192,1536]{1,0:T(8,128)(2,1)} %broadcast_select_fusion.7), channel_id=1, source_target_pairs={{0,6},{1,7},{2,0},{3,1},{4,2},{5,3},{6,4},{7,5},{8,14},{9,15},{10,... | collective-permute-start | bytes 1769480 | tf_op jit(solution)/shard_map/ppermute | solution.py:1044
  61.2 30.9 %collective-permute-start.17 = (bf16[192,1536]{1,0:T(8,128)(2,1)}, bf16[192,1536]{1,0:T(8,128)(2,1)}, u32[]{:S(2)}, u32[]{:S(2)}) collective-permute-start(bf16[192,1536]{1,0:T(8,128)(2,1)} %broadcast_select_fusion.7), channel_id=1, source_target_pairs={{0,2},{1,3},{2,4},{3,5},{4,6},{5,7},{6,0},{7,1},{8,10},{9,11},{10,... | collective-permute-start | bytes 1769480 | tf_op jit(solution)/shard_map/ppermute | solution.py:1044
  98.8 18.0 %collective-permute-start.23 = (bf16[512,1536]{1,0:T(8,128)(2,1)S(1)}, bf16[512,1536]{1,0:T(8,128)(2,1)S(1)}, u32[]{:S(2)}, u32[]{:S(2)}) collective-permute-start(bf16[512,1536]{1,0:T(8,128)(2,1)S(1)} %broadcast_select_fusion.refs_6_.refs_1_.refs_0_), channel_id=1, source_target_pairs={{0,1},{1,0},{2,3},{3,2},{4,5},{5,4},{6,7},{7,6},{8,9},{9,8},{10,11... | collective-permute-start | bytes 4718600 | tf_op jit(solution)/shard_map/ppermute | solution.py:1044
  202.5 17.9 %collective-permute-start.34 = (bf16[2,512,1536]{2,1,0:T(8,128)(2,1)}, bf16[2,512,1536]{2,1,0:T(8,128)(2,1)}, u32[]{:S(2)}, u32[]{:S(2)}) collective-permute-start(bf16[2,512,1536]{2,1,0:T(8,128)(2,1)} %slice_bitcast_fusion.2), channel_id=1, source_target_pairs={{0,1},{1,0},{2,3},{3,2},{4,5},{5,4},{6,7},{7,6},{8,9},{9,8},{10,11... | collective-permute-start | bytes 9437192 | tf_op jit(solution)/shard_map/ppermute | solution.py:1044
  224.5 36.6 %collective-permute-start.36 = (bf16[384,512]{1,0:T(8,128)(2,1)S(1)}, bf16[384,512]{1,0:T(8,128)(2,1)S(1)}, u32[]{:S(2)}, u32[]{:S(2)}) collective-permute-start(bf16[384,512]{1,0:T(8,128)(2,1)S(1)} %get-tuple-element.529), channel_id=1, source_target_pairs={{0,2},{1,3},{2,4},{3,5},{4,6},{5,7},{6,0},{7,1},{8,10},{9,11},{10,... | collective-permute-start | bytes 1179656 | tf_op jit(solution)/shard_map/ppermute | solution.py:1044
  224.6 36.6 %collective-permute-start.37 = (bf16[384,512]{1,0:T(8,128)(2,1)S(1)}, bf16[384,512]{1,0:T(8,128)(2,1)S(1)}, u32[]{:S(2)}, u32[]{:S(2)}) collective-permute-start(bf16[384,512]{1,0:T(8,128)(2,1)S(1)} %get-tuple-element.530), channel_id=1, source_target_pairs={{0,4},{1,5},{2,6},{3,7},{4,0},{5,1},{6,2},{7,3},{8,12},{9,13},{10,... | collective-permute-start | bytes 1179656 | tf_op jit(solution)/shard_map/ppermute | solution.py:1044
  226.8 34.3 %collective-permute-start.38 = (bf16[384,512]{1,0:T(8,128)(2,1)S(1)}, bf16[384,512]{1,0:T(8,128)(2,1)S(1)}, u32[]{:S(2)}, u32[]{:S(2)}) collective-permute-start(bf16[384,512]{1,0:T(8,128)(2,1)S(1)} %get-tuple-element.531), channel_id=1, source_target_pairs={{0,6},{1,7},{2,0},{3,1},{4,2},{5,3},{6,4},{7,5},{8,14},{9,15},{10,... | collective-permute-start | bytes 1179656 | tf_op jit(solution)/shard_map/ppermute | solution.py:1044
  228.4 36.2 %collective-permute-start.35 = (bf16[4,192,1024]{2,1,0:T(8,128)(2,1)S(1)}, bf16[4,192,1024]{2,1,0:T(8,128)(2,1)S(1)}, u32[]{:S(2)}, u32[]{:S(2)}) collective-permute-start(bf16[4,192,1024]{2,1,0:T(8,128)(2,1)S(1)} %get-tuple-element.528), channel_id=1, source_target_pairs={{0,16},{1,17},{2,18},{3,19},{4,20},{5,21},{6,22},{7,23},{8,24},{9,... | collective-permute-start | bytes 4718600 | tf_op jit(solution)/shard_map/ppermute | solution.py:1044
  228.9 36.0 %collective-permute-start.39 = (bf16[512,1536]{1,0:T(8,128)(2,1)S(1)}, bf16[512,1536]{1,0:T(8,128)(2,1)}, u32[]{:S(2)}, u32[]{:S(2)}) collective-permute-start(bf16[512,1536]{1,0:T(8,128)(2,1)S(1)} %fusion.17), channel_id=1, source_target_pairs={{0,8},{1,9},{2,10},{3,11},{4,12},{5,13},{6,14},{7,15},{8,0},{9,1},... | collective-permute-start | bytes 4718600 | tf_op jit(solution)/shard_map/ppermute | solution.py:1044
  278.4 24.6 %collective-permute-start.41 = (bf16[192,1024]{1,0:T(8,128)(2,1)S(1)}, bf16[192,1024]{1,0:T(8,128)(2,1)S(1)}, u32[]{:S(2)}, u32[]{:S(2)}) collective-permute-start(bf16[192,1024]{1,0:T(8,128)(2,1)S(1)} %get-tuple-element.562), channel_id=1, source_target_pairs={{0,2},{1,3},{2,4},{3,5},{4,6},{5,7},{6,0},{7,1},{8,10},{9,11},{10,... | collective-permute-start | bytes 1179656 | tf_op jit(solution)/shard_map/ppermute | solution.py:1044
  279.0 24.0 %collective-permute-start.42 = (bf16[192,1024]{1,0:T(8,128)(2,1)S(1)}, bf16[192,1024]{1,0:T(8,128)(2,1)S(1)}, u32[]{:S(2)}, u32[]{:S(2)}) collective-permute-start(bf16[192,1024]{1,0:T(8,128)(2,1)S(1)} %get-tuple-element.563), channel_id=1, source_target_pairs={{0,6},{1,7},{2,0},{3,1},{4,2},{5,3},{6,4},{7,5},{8,14},{9,15},{10,... | collective-permute-start | bytes 1179656 | tf_op jit(solution)/shard_map/ppermute | solution.py:1044
  282.3 20.8 %collective-permute-start.40 = (bf16[4,192,512]{2,1,0:T(8,128)(2,1)S(1)}, bf16[4,192,512]{2,1,0:T(8,128)(2,1)S(1)}, u32[]{:S(2)}, u32[]{:S(2)}) collective-permute-start(bf16[4,192,512]{2,1,0:T(8,128)(2,1)S(1)} %get-tuple-element.561), channel_id=1, source_target_pairs={{0,16},{1,17},{2,18},{3,19},{4,20},{5,21},{6,22},{7,23},{8,24},{9,... | collective-permute-start | bytes 2359304 | tf_op jit(solution)/shard_map/ppermute | solution.py:1044
  308.7 25.5 %collective-permute-start.47 = (bf16[256,1536]{1,0:T(8,128)(2,1)}, bf16[256,1536]{1,0:T(8,128)(2,1)S(1)}, u32[]{:S(2)}, u32[]{:S(2)}) collective-permute-start(bf16[256,1536]{1,0:T(8,128)(2,1)} %get-tuple-element.589), channel_id=1, source_target_pairs={{0,8},{1,9},{2,10},{3,11},{4,12},{5,13},{6,14},{7,15},{8,0},{9,1},... | collective-permute-start | bytes 2359304 | tf_op jit(solution)/shard_map/ppermute | solution.py:1044
  311.6 22.6 %collective-permute-start.45 = (bf16[1024,128]{1,0:T(8,128)(2,1)S(1)}, bf16[1024,128]{1,0:T(8,128)(2,1)S(1)}, u32[]{:S(2)}, u32[]{:S(2)}) collective-permute-start(bf16[1024,128]{1,0:T(8,128)(2,1)S(1)} %add_convert_fusion.5), channel_id=1, source_target_pairs={{0,8},{1,9},{2,10},{3,11},{4,12},{5,13},{6,14},{7,15},{8,0},{9,1},... | collective-permute-start | bytes 786440 | tf_op jit(solution)/shard_map/ppermute | solution.py:1044
  313.0 21.2 %collective-permute-start.46 = (bf16[192,1024]{1,0:T(8,128)(2,1)S(1)}, bf16[192,1024]{1,0:T(8,128)(2,1)S(1)}, u32[]{:S(2)}, u32[]{:S(2)}) collective-permute-start(bf16[192,1024]{1,0:T(8,128)(2,1)S(1)} %get-tuple-element.588), channel_id=1, source_target_pairs={{0,4},{1,5},{2,6},{3,7},{4,0},{5,1},{6,2},{7,3},{8,12},{9,13},{10,... | collective-permute-start | bytes 1179656 | tf_op jit(solution)/shard_map/ppermute | solution.py:1044
  366.8 21.5 %collective-permute-start.56 = (bf16[512,1536]{1,0:T(8,128)(2,1)}, bf16[512,1536]{1,0:T(8,128)(2,1)}, u32[]{:S(2)}, u32[]{:S(2)}) collective-permute-start(bf16[512,1536]{1,0:T(8,128)(2,1)} %add_convert_fusion.1), channel_id=1, source_target_pairs={{0,1},{1,0},{2,3},{3,2},{4,5},{5,4},{6,7},{7,6},{8,9},{9,8},{10,11... | collective-permute-start | bytes 4718600 | tf_op jit(solution)/shard_map/ppermute | solution.py:1044
  366.9 20.2 %collective-permute-start.54 = (bf16[4,192,512]{2,1,0:T(8,128)(2,1)}, bf16[4,192,512]{2,1,0:T(8,128)(2,1)S(1)}, u32[]{:S(2)}, u32[]{:S(2)}) collective-permute-start(bf16[4,192,512]{2,1,0:T(8,128)(2,1)} %get-tuple-element.644), channel_id=1, source_target_pairs={{0,16},{1,17},{2,18},{3,19},{4,20},{5,21},{6,22},{7,23},{8,24},{9,... | collective-permute-start | bytes 2359304 | tf_op jit(solution)/shard_map/ppermute | solution.py:1044
  368.5 19.9 %collective-permute-start.55 = (bf16[256,1536]{1,0:T(8,128)(2,1)}, bf16[256,1536]{1,0:T(8,128)(2,1)}, u32[]{:S(2)}, u32[]{:S(2)}) collective-permute-start(bf16[256,1536]{1,0:T(8,128)(2,1)} %get-tuple-element.645), channel_id=1, source_target_pairs={{0,8},{1,9},{2,10},{3,11},{4,12},{5,13},{6,14},{7,15},{8,0},{9,1},... | collective-permute-start | bytes 2359304 | tf_op jit(solution)/shard_map/ppermute | solution.py:1044
  (162 other events, 1581.6 us)

commit v4 on v3

--- a/solution.py
+++ b/solution.py
@@ -426,7 +426,7 @@
     def _():
         assemble_rows(links_shape, at_ref, own_ref, core_ref, pieces, whole_ref)
 
-    out_ref[...] = dot(rows_ref[...], whole_ref[...])
+    out_ref[...] = dot(rows_ref[...], whole_ref[...]).astype(out_ref.dtype)
 
 
 def whole_spec(array):
@@ -439,7 +439,7 @@
     return pl.BlockSpec((array.shape[0], width), lambda b: (0, index))
 
 
-def project_call(links_shape, width, index, blocks, tokens, place, parts, rows):
+def project_call(links_shape, width, index, blocks, tokens, kind, place, parts, rows):
     depth = rows.shape[1]
     return pl.pallas_call(
         functools.partial(project_kernel, links_shape),
@@ -453,7 +453,7 @@
         ],
         out_shape=[
             jax.ShapeDtypeStruct((depth, width), BF16),
-            jax.ShapeDtypeStruct((blocks * tokens, width), F32),
+            jax.ShapeDtypeStruct((blocks * tokens, width), kind),
         ],
         compiler_params=pltpu.CompilerParams(vmem_limit_bytes=40 * 1024 * 1024),
         cost_estimate=pl.CostEstimate(
@@ -463,8 +463,8 @@
     )(place, *parts, rows)
 
 
-def branch_back_kernel(links_shape, at_ref, own_ref, core_ref, *refs):
-    pieces, rows_refs = refs[:-10], refs[-10:-6]
+def branch_back_kernel(links_shape, counts, at_ref, own_ref, core_ref, *refs):
+    pieces, rows_refs = refs[: -6 - sum(counts)], list(refs[-6 - sum(counts) : -6])
     gate_ref, ssd_ref, cw_ref, whole_ref, out_ref, sums_ref = refs[-6:]
     block = pl.program_id(0)
 
@@ -472,11 +472,16 @@
     def _():
         assemble_rows(links_shape, at_ref, own_ref, core_ref, pieces, whole_ref)
 
-    for at, rows_ref in enumerate(rows_refs):
+    for at, count in enumerate(counts):
+        parts = [rows_refs.pop(0) for _ in range(count)]
 
         @pl.when(block == at)
         def _():
-            out_ref[...] = dot(rows_ref[...], whole_ref[...])
+            first_row = 0
+            for part in parts:
+                stop = first_row + part.shape[0]
+                out_ref[first_row:stop, :] = dot(part[...], whole_ref[...])
+                first_row = stop
 
     tokens, width = out_ref.shape
     sums_ref[...] = jnp.zeros_like(sums_ref)
@@ -485,7 +490,7 @@
         products = jnp.zeros((CHUNK, LANES), F32)
         for left in range(0, width, LANES):
             tile = (slice(start, start + CHUNK), slice(left, left + LANES))
-            gate = gate_ref[tile]
+            gate = gate_ref[tile].astype(F32)
             gated = ssd_ref[tile] * (gate * sigmoid(gate))
             squares = squares + gated * gated
             products = products + gated * (cw_ref[6:7, left : left + LANES] * out_ref[tile])
@@ -494,10 +499,12 @@
 
 
 def branch_back_call(links_shape, width, index, place, parts, rows, gate, ssd_out, conv_rows):
-    tokens, depth = rows[0].shape
+    tokens, depth = ssd_out.shape[0] // 4, rows[0][0].shape[1]
+    counts = [len(block) for block in rows]
+    rows = [part for block in rows for part in block]
     block = pl.BlockSpec((tokens, width), lambda b: (b, 0))
     return pl.pallas_call(
-        functools.partial(branch_back_kernel, links_shape),
+        functools.partial(branch_back_kernel, links_shape, counts),
         grid=(4,),
         in_specs=[pl.BlockSpec(memory_space=pltpu.SMEM)]
         + [columns_spec(array, width, index) for array in parts]
@@ -542,7 +549,7 @@
         for left in range(0, width, LANES):
             columns = slice(left, left + LANES)
             tile = (slice(start, start + CHUNK), columns)
-            gate, ssd, d_branch = gate_ref[tile], ssd_ref[tile], db_ref[tile]
+            gate, ssd, d_branch = gate_ref[tile].astype(F32), ssd_ref[tile], db_ref[tile]
             gain = cw_ref[6:7, columns]
             sig = sigmoid(gate)
             act = gate * sig
@@ -737,6 +744,81 @@
     )(place, *parts)
 
 
+def keys_front_kernel(len_ref, in_ref, rows_ref, out_ref):
+    tokens, columns = in_ref.shape[0] // 2, in_ref.shape[1]
+    position = lax.broadcasted_iota(jnp.int32, (tokens, columns), 0)
+    row, lane = iotas(16, columns)
+    counts = jnp.zeros((16, columns), jnp.int32)
+    for block in range(2):
+        first = len_ref[block, 0]
+        both = first + len_ref[block, 1]
+        begin = begin_of(position, first, both)
+        inputs = in_ref[block * tokens : (block + 1) * tokens, :]
+        pre = rows_ref[4:5, :] + rows_ref[3:4, :] * inputs
+        for delay in range(1, 4):
+            shifted = jnp.where(position - delay >= begin, pltpu.roll(inputs, delay, 0), 0.0)
+            pre = pre + rows_ref[3 - delay : 4 - delay, :] * shifted
+        out_ref[block * tokens : (block + 1) * tokens, :] = (pre * sigmoid(pre)).astype(BF16)
+        for sequence in range(2):
+            length = len_ref[block, sequence]
+            here = row == block
+            counts = jnp.where(here & (lane == 2 * sequence), lax.div(length, 32), counts)
+            counts = jnp.where(here & (lane == 2 * sequence + 1), lax.rem(length, 32), counts)
+    out_ref[2 * tokens :, :] = counts.astype(F32).astype(BF16)
+
+
+def keys_front_call(lengths, inputs, rows):
+    total, columns = inputs.shape
+    return pl.pallas_call(
+        keys_front_kernel,
+        in_specs=[
+            pl.BlockSpec(memory_space=pltpu.SMEM),
+            pl.BlockSpec(memory_space=pltpu.VMEM),
+            pl.BlockSpec(memory_space=pltpu.VMEM),
+        ],
+        out_specs=pl.BlockSpec(memory_space=pltpu.VMEM),
+        out_shape=jax.ShapeDtypeStruct((total + 16, columns), BF16),
+        compiler_params=pltpu.CompilerParams(vmem_limit_bytes=24 * 1024 * 1024),
+        name="keys_front",
+    )(lengths, inputs, rows)
+
+
+def norm_back_kernel(keep_ref, core_ref, *refs):
+    far_refs, (hidden_ref, back_ref, scale_ref, gain_ref, out_ref) = refs[:3], refs[3:]
+    block = pl.program_id(0)
+    far = jnp.where(block == 0, far_refs[0][...], far_refs[1][...])
+    far = jnp.where(block <= 1, far, far_refs[2][...]).astype(F32)
+    hidden, scale = hidden_ref[...].astype(F32), scale_ref[:, 0:1]
+    weighted = gain_ref[0:1, :] * (keep_ref[...] + core_ref[...].astype(F32) + far)
+    mean = jnp.sum(hidden * weighted, axis=1, keepdims=True) * (1.0 / hidden.shape[1])
+    cross = scale * scale * scale * mean
+    out_ref[...] = back_ref[...].astype(F32) + scale * weighted - hidden * cross
+
+
+def norm_back_call(keep, core, far, hidden, back, scale, gain):
+    tokens, depth = keep.shape
+    rows = tokens // 4
+    block = pl.BlockSpec((rows, depth), lambda b: (b, 0))
+    quarter = pl.BlockSpec((rows, depth), lambda b: (0, 0))
+    later = pl.BlockSpec((rows, depth), lambda b: (jnp.maximum(b - 2, 0), 0))
+    return pl.pallas_call(
+        norm_back_kernel,
+        grid=(4,),
+        in_specs=[
+            block, block, quarter, quarter, later, block, block,
+            pl.BlockSpec((rows, LANES), lambda b: (b, 0)),
+            whole_spec(gain),
+        ],
+        out_specs=block,
+        out_shape=jax.ShapeDtypeStruct((tokens, depth), F32),
+        compiler_params=pltpu.CompilerParams(vmem_limit_bytes=32 * 1024 * 1024),
+        cost_estimate=pl.CostEstimate(
+            flops=4_000_000_000, bytes_accessed=12_000_000, transcendentals=0
+        ),
+        name="norm_back",
+    )(keep, core, *far, hidden, back, scale, gain)
+
+
 def keys_back_kernel(len_ref, mine_ref, core_ref, side_ref, in_ref, rows_ref, d_ref, grads_ref):
     block = pl.program_id(0)
     first = len_ref[block, 0]
@@ -828,7 +910,7 @@
 
 
 def final_kernel(heads, size, most, by_g, at_ref, *refs):
-    first_both, first_other, held_both, held_other, last_mine, last_core = refs[:6]
+    first_both, first_other, held_mine, held_core, last_mine, last_core = refs[:6]
     weight_ref, gain_ref, in_ref, out_ref, norm_ref = refs[6:]
     far, high = at_ref[0] == 1, at_ref[1] == 1
     width = heads * size
@@ -850,20 +932,24 @@
         take_other = far if p < 2 else jnp.logical_not(far)
         return jnp.where(take_other, other[:, columns], both[:, columns]).astype(F32)
 
-    def last_share(core, start, stop):
-        take_core = high if core == 0 else jnp.logical_not(high)
+    def core_share(mine, other, core, start, stop):
+        take_other = high if core == 0 else jnp.logical_not(high)
         columns = slice(start, stop)
-        return jnp.where(take_core, last_core[:, columns], last_mine[:, columns]).astype(F32)
+        return jnp.where(take_other, other[:, columns], mine[:, columns]).astype(F32)
+
+    last_share = functools.partial(core_share, last_mine, last_core)
+    held_share = functools.partial(core_share, held_mine, held_core)
 
     steps = jnp.zeros((rows, LANES), F32)
     lane = lax.broadcasted_iota(jnp.int32, (rows, LANES), 1)
     for p in range(4):
-        first = functools.partial(share, first_both, first_other, p, 2 * width)
+        first = functools.partial(share, first_both, first_other, p, 2 * width - by_g)
         norm = norm + put(p * width, first(0, width))
-        out_ref[:, p * width : p * width + by_g] = first(2 * width - by_g, 2 * width)
+        left = (p // 2) * (by_g + most)
+        out_ref[:, p * width : p * width + by_g] = held_share(p % 2, left, left + by_g)
         out_ref[:, p * width + by_g : (p + 1) * width] = first(width, 2 * width - by_g)
         at = at_values + p * width
-        norm = norm + put(at, share(held_both, held_other, p, most, 0, most))
+        norm = norm + put(at, held_share(p % 2, left + by_g, left + by_g + most))
         left = (p // 2) * (less + LANES)
         norm = norm + put(at + most, last_share(p % 2, left, left + less))
         drawn = last_share(p % 2, left + less, left + less + LANES)
@@ -1182,34 +1268,6 @@
         ).astype(F32)
 
 
-def shift_rows(values, by):
-    zeros = jnp.zeros((values.shape[0], abs(by), values.shape[2]), values.dtype)
-    if by > 0:
-        return jnp.concatenate([zeros, values[:, :-by]], axis=1)
-    return jnp.concatenate([values[:, -by:], zeros], axis=1)
-
-
-def causal_conv(inputs, begin, taps, bias):
-    position = jnp.arange(inputs.shape[1], dtype=jnp.int32)[None, :]
-    result = bias + taps[3] * inputs
-    shifted = [inputs]
-    for delay in range(1, 4):
-        inside = (position - delay >= begin)[..., None]
-        shifted.append(jnp.where(inside, shift_rows(inputs, delay), 0.0))
-        result = result + taps[3 - delay] * shifted[delay]
-    return result, shifted
-
-
-def causal_conv_back(d_result, begin, taps):
-    position = jnp.arange(d_result.shape[1], dtype=jnp.int32)[None, :]
-    d_inputs = taps[3] * d_result
-    for delay in range(1, 4):
-        inside = (position - delay >= begin)[..., None]
-        moved = shift_rows(jnp.where(inside, d_result, 0.0), -delay)
-        d_inputs = d_inputs + taps[3 - delay] * moved
-    return d_inputs
-
-
 def per_device(
     reps,
     shards,
@@ -1299,10 +1357,11 @@
     def swap(bit):
         return lambda value: links.flip(value, 0, bit)
 
-    (from_core_a,), packed = phase([(links.core, for_core_a)], pack, small_in)
+    (from_core_a,), _ = phase([(links.core, for_core_a)])
     pieces_a = {0: links.piece_of(mine_a, from_core_a)}
 
-    def prepare_last(packed, in_weight, out_weight):
+    def prepare_last(small_in, in_weight, out_weight):
+        packed = pack(*small_in)
         small_pair = doubled(packed, 1, links.core(packed))
         small_four = doubled(small_pair, 2, links.flip(small_pair, 0, 2))
         kernel = functools.partial(prepare_last_kernel, width)
@@ -1312,7 +1371,7 @@
     moved, (small_all, (mine_b, for_core_b)) = phase(
         hop_sends(pieces_a, 1) + [(links.core, lengths)],
         prepare_last,
-        (packed, in_weight, out_weight.T),
+        (small_in, in_weight, out_weight.T),
     )
     lengths_core = moved[-1]
     pieces_a = landed(pieces_a, 1, moved[:-1])
@@ -1352,7 +1411,6 @@
         k: y_moved[at * (sides - 1) : (at + 1) * (sides - 1)] for at, k in enumerate(early + late)
     }
     n_rows, conv_rows, head_rows, kq_rows = parameters_here
-    n_gain = n_rows[0]
 
     def parts_of(mine, from_core, pieces, rounds_of):
         parts = [mine, from_core]
@@ -1362,40 +1420,30 @@
 
     parts_a = parts_of(mine_a, from_core_a, pieces_a, y_a)
     pair_lengths = jnp.concatenate([lengths, lengths_core], axis=0)
-    pair_ends = jnp.cumsum(pair_lengths, axis=1)
-    position = positions[None, :]
-    begin = jnp.where(
-        position >= pair_ends[:, 1:],
-        pair_ends[:, 1:],
-        jnp.where(position >= pair_ends[:, :1], pair_ends[:, :1], 0),
-    )
-    kq_columns = inner + c * state
-    kq_taps, kq_bias = kq_rows[:4], kq_rows[4]
     normed, scale = normalize_call([hidden_in, core_hidden, far_hidden, far_core_hidden], n_rows)
-    scale_own = scale[:tokens, :1]
     kq_index = (width + LANES) // state
-    w_kq, kq_in = project_call(links_shape, state, kq_index, 2, tokens, place, parts_a, normed)
-    kq_pre, kq_shifted = causal_conv(kq_in.reshape(2, tokens, state), begin, kq_taps, kq_bias)
-    counts = jnp.stack([pair_lengths // 32, pair_lengths % 32], axis=2).reshape(2, 4).astype(BF16)
-    counts = jnp.pad(counts, ((0, 14), (0, state - 4)))
-    kq_near = jax.nn.silu(kq_pre).astype(BF16).reshape(2 * tokens, state)
-    count = tokens // 4
-    cuts = [slice(at, at + count) for at in range(0, tokens, count)]
+    w_kq, kq_in = project_call(
+        links_shape, state, kq_index, 2, tokens, F32, place, parts_a, normed
+    )
+    kq_near = keys_front_call(pair_lengths, kq_in, kq_rows)
+    half, quarter = tokens // 2, tokens // 4
+    cuts = [slice(0, half), slice(half, half + quarter), slice(half + quarter, tokens)]
     moved, (w_values, conv_in), b_firsts = phase(
         [
-            (links.side, jnp.concatenate([kq_near, counts], axis=0)),
-            (links.side, back_own[cuts[0]]),
-        ],
-        functools.partial(project_call, links_shape, width + LANES, 0, 4, tokens, place),
+            (links.side, kq_near),
+            (links.side, back_own[cuts[1]]),
+        ],
+        functools.partial(project_call, links_shape, width + LANES, 0, 4, tokens, F32, place),
         (parts_a, normed),
         b_firsts,
     )
     pieces_b = landed(pieces_b, 1, b_firsts)
-    kq_far, far_back = moved[0], [moved[1]]
-    all_counts = jnp.concatenate([counts[:2, :4], kq_far[2 * tokens : 2 * tokens + 2, :4]], axis=0)
+    kq_far, far_back = moved[0], [None, moved[1]]
+    counts_at = slice(2 * tokens, 2 * tokens + 2)
+    all_counts = jnp.concatenate([kq_near[counts_at, :4], kq_far[counts_at, :4]], axis=0)
     all_counts = all_counts.astype(jnp.int32)
     all_lengths = all_counts[:, 0::2] * 32 + all_counts[:, 1::2]
-    kq_half = jnp.concatenate([kq_near, kq_far[: 2 * tokens]], axis=0)
+    kq_half = jnp.concatenate([kq_near[: 2 * tokens], kq_far[: 2 * tokens]], axis=0)
 
     (kq_core,), _ = phase([(links.core, kq_half)])
     kq_core = kq_core.reshape(2, 2, tokens, state)[:, ::-1].reshape(4 * tokens, state)
@@ -1407,12 +1455,12 @@
     moved, before = phase(
         hop_sends(pieces_b, 2)
         + rounds(pieces_b[firsts[0]])
-        + [(links.side, back_own[cuts[1]]), (links.core, back_own)],
+        + [(links.side, back_own[cuts[0]]), (links.core, back_own)],
         functools.partial(forward_call, heads, size, 0, 2),
         (all_lengths, conv_in, keys_queries, conv_rows, head_rows),
     )
     y_b = {firsts[0]: moved[hop_count:-2]}
-    far_back.append(moved[-2])
+    far_back[0] = moved[-2]
     core_back = moved[-1]
     pieces_b = landed(pieces_b, 2, moved[:hop_count])
     for stage in range(3, groups // 2 + 1):
@@ -1430,28 +1478,19 @@
         y_b[k] = moved[at * (sides - 1) : (at + 1) * (sides - 1)]
     gate_sends = [send for k in rest for send in rounds(pieces_b[k][:, :width])]
     out_sends = [send for k in rest for send in rounds(pieces_b[k][:, width:])]
-    most_back = jnp.concatenate(far_back, axis=0)
-    moved, _ = phase(
-        gate_sends + [(links.side, back_own[cuts[3]]), (links.core, most_back)]
-    )
-    gate_moved, last_back, far_core_back = moved[:-2], moved[-2], moved[-1]
+    moved, _ = phase(gate_sends + [(links.core, part) for part in far_back])
+    gate_moved, far_core_back = moved[: len(gate_sends)], moved[len(gate_sends) :]
 
     def last_parts(values):
         latest = {k: values[at * (sides - 1) : (at + 1) * (sides - 1)] for at, k in enumerate(rest)}
         return parts_of(mine_b, from_core_b, pieces_b, {**y_b, **latest})
 
-    moved, (w_gate, gate) = phase(
-        out_sends + [(links.core, last_back)],
-        functools.partial(project_call, links_shape, width, 0, 4, tokens, place),
+    out_moved, (w_gate, gate) = phase(
+        out_sends,
+        functools.partial(project_call, links_shape, width, 0, 4, tokens, F32, place),
         (last_parts(gate_moved), normed),
     )
-    out_moved, last_core_back = moved[:-1], moved[-1]
-    back_blocks = [
-        back_own,
-        core_back,
-        jnp.concatenate([most_back, last_back], axis=0),
-        jnp.concatenate([far_core_back, last_core_back], axis=0),
-    ]
+    back_blocks = [[back_own], [core_back], far_back, far_core_back]
     w_out, d_branch, sums = branch_back_call(
         links_shape, width, 1, place, last_parts(out_moved), back_blocks, gate, ssd_out, conv_rows
     )
@@ -1492,10 +1531,12 @@
 
     def first_grads(normed, d_gate, back_blocks, branch):
         def out_terms(columns, index):
-            return [
-                (block, tokens, 0, branch, at, columns, index)
-                for at, block in enumerate(back_blocks)
-            ]
+            terms, first_row = [], 0
+            for part in [part for block in back_blocks for part in block]:
+                rows = part.shape[0]
+                terms.append((part, rows, 0, branch, first_row // rows, columns, index))
+                first_row += rows
+            return terms
 
         first = weight_grad_call(
             links_shape, True, place,
@@ -1509,24 +1550,24 @@
     moved, (first_parts, out_parts) = phase(
         [(links.core, mixed_send)], first_grads, (normed, d_gate, back_blocks, branch)
     )
-    mixed_sum = mixed_keep.astype(F32) + moved[0].astype(F32)
+    mixed_core = moved[0]
+    mixed_far = (mixed_keep[1].astype(F32) + mixed_core[1].astype(F32)).astype(BF16)
     moved, (d_in_0, d_steps_0, kq_mine_0, kq_other_0, conv_grads_0, head_grads_0) = phase(
         a_sends(first_parts[1:])
         + g_sends(out_parts[1:])
-        + [(links.side, mixed_sum[1].astype(BF16))],
+        + [(links.side, mixed_far)],
         functools.partial(backward, 0, most, 0, 4),
         (d_ssd,),
     )
-    mixed = hidden_in.astype(F32) + mixed_sum[0] + moved[-1].astype(F32)
-    mixed = jnp.where(is_valid, mixed, 0.0).astype(BF16)
+    mixed_side = moved[-1]
     first_held = combine_call(groups, place, [first_parts[0], *moved[:count_a]])
     values_0 = weight_grad_call(
         links_shape, True, place, [[(normed, rows_all, 0, d_in_0, 0, most_width, 0)]]
     )
     out_chip = total(out_parts[0], moved[count_a:-1]).astype(BF16)
     out_mine, out_others = links.parts_for_a(out_chip.reshape(sides, -1, by_g))
-    first_held, values_0, d_ssd, mixed, out_mine, out_others = after(
-        (first_held, values_0, d_ssd, mixed, out_mine, out_others)
+    first_held, values_0, d_ssd, out_mine, out_others = after(
+        (first_held, values_0, d_ssd, out_mine, out_others)
     )
     first_sends = g_sends(first_held[1:])
     first_sends = first_sends[:1] + first_sends[-1:] + first_sends[1:-1]
@@ -1556,7 +1597,7 @@
     moved, results = phase(
         [(links.side, kq_far_sum)]
         + first_sends[2:]
-        + [(links.side, d_far[: tokens // 2])]
+        + [(links.side, d_far[:quarter])]
         + a_sends(out_others),
         functools.partial(backward, most, less, 0, 2),
         (d_ssd, kq_mine_0, kq_other_0),
@@ -1567,15 +1608,15 @@
     far_d = [moved[count_g - 1]]
     out_piece = total(out_mine, moved[count_g:]).astype(BF16)
     first_piece = total(first_held[0], first_far).astype(BF16)
-    first_piece = jnp.concatenate([first_piece, out_piece], axis=1)
     d_steps_near = d_steps_0[: 2 * tokens] + d_steps_near
     d_steps = jnp.concatenate([d_steps_near, d_steps_far], axis=0)
     moved, d_near = phase(
-        [(links.core, kq_near_core)] + held_sends[:1],
+        [(links.core, kq_near_core), (links.side, d_far[quarter:half])] + held_sends[:1],
         functools.partial(back_project, 0),
         (d_in_near, d_steps_near),
     )
-    held_far = moved[1:]
+    far_d.append(moved[1])
+    held_far = moved[2:]
     d_kq_in, kq_grads = keys_back_call(
         all_lengths, [kq_near_mine, moved[0], kq_from_side], kq_in, kq_rows
     )
@@ -1599,13 +1640,17 @@
         return last
 
     moved, last_parts_here = phase(
-        rounds(first_piece) + held_sends[1:],
+        rounds(first_piece)
+        + held_sends[1:]
+        + [(links.side, d_far[half:])],
         last_grads,
         (normed, d_in_near, d_in_far, d_steps, d_kq_in),
     )
     first_y = moved[:count_a]
-    held_far = held_far + moved[count_a:]
+    held_far = held_far + moved[count_a:-1]
+    far_d.append(moved[-1])
     held_piece = total(held_0[0], held_far).astype(BF16)
+    held_piece = jnp.concatenate([out_piece, held_piece], axis=1)
     first_rows = links.rows_of_core(links.join_a(first_piece, first_y))
     d_near_keep = d_near[:tokens] + dot_nt(d_kq_in[:tokens], w_kq)
     d_near_send = (d_near[tokens:] + dot_nt(d_kq_in[tokens:], w_kq)).astype(BF16)
@@ -1615,52 +1660,52 @@
         [head_grads_0, head_grads_far, head_grads_near],
         gain_rows, kq_grads,
     )
-    moved, _ = phase(
+    def finish_mixed(keep, core, side):
+        mixed = hidden_in.astype(F32) + keep.astype(F32) + core.astype(F32) + side.astype(F32)
+        return jnp.where(is_valid, mixed, 0.0).astype(BF16)
+
+    moved, mixed = phase(
         a_sends(last_parts_here[1:])
-        + [(links.side, d_far[tokens // 2 :]), (links.core, d_near_send), (links.core, small)]
-        + [(links.core, first_rows[1])]
-    )
-    far_d.append(moved[count_a])
-    d_near = d_near_keep + moved[count_a + 1].astype(F32)
-    small = small + moved[count_a + 2]
-    first_mine, first_core = first_rows[0], moved[-1]
+        + [(links.core, d_near_send)]
+        + [(links.core, first_rows[1]), (links.side, held_piece), (links.core, small)],
+        finish_mixed,
+        (mixed_keep[0], mixed_core[0], mixed_side),
+    )
+    d_near_core = moved[count_a]
+    first_mine, first_core = first_rows[0], moved[count_a + 1]
+    held_both = links.join_x(held_piece, moved[count_a + 2])
+    small = small + moved[-1]
     first_both = jnp.concatenate(
         [jnp.where(is_high, first_core, first_mine), jnp.where(is_high, first_mine, first_core)],
         axis=1,
     )
     last_held = combine_call(groups, place, [last_parts_here[0], *moved[:count_a]])
-    first_half = first_both.shape[1] // (3 * LANES) * 2 * LANES
-    moved, _ = phase(
+
+    moved, grad_hidden = phase(
         g_sends(last_held[1:])
-        + [(links.side, first_both[:, :first_half])]
-        + rounds(held_piece)
-    )
-    first_other = [moved[count_g]]
+        + [(links.side, first_both)]
+        + rounds(held_both)
+        + [(swap(2), small)],
+        norm_back_call,
+        (d_near_keep, d_near_core, far_d, hidden_in, back_own, scale, n_rows),
+    )
+    first_other = moved[count_g]
+    held_rows = links.rows_of_core(links.join_a(held_both, moved[count_g + 1 : -1]))
+    small = small + moved[-1]
     last_piece = total(last_held[0], moved[:count_g]).astype(BF16)
-    held_rows = links.rows_of_core(links.join_a(held_piece, moved[count_g + 1 :]))
-
-    def final_norm(d_near, far_d):
-        d_normed = d_near + far_d.astype(F32)
-        own_hidden, own_scale = hidden_in.astype(F32), scale_own
-        weighted = n_gain * d_normed
-        inner_mean = jnp.mean(own_hidden * weighted, axis=-1, keepdims=True)
-        return (
-            back_own.astype(F32)
-            + own_scale * weighted
-            - own_hidden * (own_scale * own_scale * own_scale * inner_mean)
-        )
-
     diagonals = [(lambda value, j=j: links.diagonal(value, j), last_piece) for j in range(1, sides)]
     moved, _ = phase(
         rounds(last_piece)
-        + [(links.side, last_piece), (links.core, held_rows[1]), (swap(2), small)]
+        + [(links.side, last_piece), (links.core, held_rows[1]), (swap(4), small)]
         + diagonals
-        + [(links.side, first_both[:, first_half:])]
-    )
-    first_other.append(moved.pop())
+    )
     same_x = links.join_a(last_piece, moved[:count_a])
     held_core, small = moved[count_a + 1], small + moved[count_a + 2]
     other_x = links.join_a(moved[count_a], moved[count_a + 3 :])
+    bit = 8
+    while bit < shards:
+        small = small + links.flip(small, 0, bit)
+        bit *= 2
     at_kq = less_width + LANES
     kq_both = same_x[:, at_kq:].astype(F32) + other_x[:, at_kq:].astype(F32)
     last_rows = links.rows_of_core(
@@ -1673,29 +1718,15 @@
             axis=1,
         )
     )
-    held_both = jnp.concatenate(
-        [jnp.where(is_high, held_core, held_rows[0]), jnp.where(is_high, held_rows[0], held_core)],
-        axis=1,
-    )
-    moved, grad_hidden = phase(
-        [(links.side, held_both), (links.core, last_rows[1]), (swap(4), small)],
-        final_norm,
-        (d_near, jnp.concatenate(far_d, axis=0)),
-    )
-    small = small + moved[2]
-    bit = 8
-    while bit < shards:
-        small = small + links.flip(small, 0, bit)
-        bit *= 2
-    first_other = jnp.concatenate(first_other, axis=1)
-    held_other, last_core = moved[0], moved[1]
+    (last_core,), _ = phase([(links.core, last_rows[1])])
+    held_rows_pair = [held_rows[0], held_core]
     moved, (grad_in, grad_out, grad_norm) = phase(
         [(links.side, small)]
         + rounds(small)
         + [(lambda value, j=j: links.diagonal(value, j), small) for j in range(1, sides)],
         functools.partial(final_call, heads, size, most_width, by_g, core_place),
         (
-            [first_both, first_other, held_both, held_other, last_rows[0], last_core],
+            [first_both, first_other, *held_rows_pair, last_rows[0], last_core],
             in_weight,
             norm_gain.astype(F32)[:, None],
         ),

time: 475 us -> 467 us (0.983)
  waiting for transfers between devices: 120 us -> 91.8 us
  local copies, waits for them, and re-layouts: 39.4 us -> 56.4 us
  other arithmetic: 39.3 us -> 26.7 us
  starting transfers between devices: 67.3 us -> 76.4 us
  Pallas kernels: 173 us -> 179 us
    ppermute x76, waiting for transfers between devices: 120 us -> 91.8 us  [send(): return lax.ppermute(value, ('rep', 'fsdp'), pairs)]
    ppermute x76, starting transfers between devices: 67.3 us -> 76.4 us  [send(): return lax.ppermute(value, ('rep', 'fsdp'), pairs)]
    unnamed x224 -> x316, local copies, waits for them, and re-layouts: 27 us -> 35.6 us
    add x4 -> x2, other arithmetic: 8.29 us -> 0.03 us  [per_device(): small = small + moved[-1]]
    pallas_call x1 -> x3, Pallas kernels: 16.1 us -> 22 us  [the longest x1 16.1 us: branch_back_call(): pl.pallas_call(functools.partial(branch_back_kernel, links_shape, counts)...]
    sub x3 -> x0, other arithmetic: 5.8 us -> none  [the longest x1 5.79 us: final_norm(): back_own.astype(F32) + own_scale * weighted]
    squeeze x0 -> x2, local copies, waits for them, and re-layouts: none -> 5.55 us  [the longest x1 2.9 us: per_device(): mixed_keep[0]]
  transfers between devices with their start and end apart: 76 -> 76, of which waited for: 25 -> 24; matrix products, arithmetic and copies ran while one was open for 9% -> 9% of each run, Pallas kernels for 29% -> 31%
where the time goes in v4:
time: 467 us; the launch traced here: 459 us
  Pallas kernels  179 us (38%)
  waiting for transfers between devices  91.8 us (20%)
  starting transfers between devices  76.4 us (16%)
  local copies, waits for them, and re-layouts  56.4 us (12%)
  other arithmetic  26.7 us (6%)
  matrix products  25.1 us (5%)
    ppermute x76, waiting for transfers between devices, send(): return lax.ppermute(value, ('rep', 'fsdp'), pairs)  91.8 us
    ppermute x76, starting transfers between devices, send(): return lax.ppermute(value, ('rep', 'fsdp'), pairs)  76.4 us
    pallas_call x3, Pallas kernels, backward_call(): pl.pallas_call(functools.partial(backward_kernel, heads, size, first_head...  52.7 us
    unnamed x316, local copies, waits for them, and re-layouts  35.6 us
    pallas_call x4, Pallas kernels, weight_grad_call(): pl.pallas_call(functools.partial(weight_grad_kernel, links_shape, shapes,...  33.2 us
    dot_general x7, matrix products, dot_nt(): lax.dot_general(left, right, (((1,), (1,)), ((), ())), preferred_element_...  25.1 us
    pallas_call x2, Pallas kernels, forward_call(): pl.pallas_call(functools.partial(forward_kernel, heads, size, first_block...  22.7 us
    pallas_call x3, Pallas kernels, project_call(): pl.pallas_call(functools.partial(project_kernel, links_shape), grid=(bloc...  19.5 us
  transfers between devices with their start and end apart: 76, of which 24 were waited for; matrix products, arithmetic and copies ran while one was open for 9% of the time, Pallas kernels for 31%

profile of v4, /device:TPU:0, one launch (start us, length us, event | category | flops | bytes accessed | tf_op | source)
XLA Modules:
  0.0 458.7 jit_solution(14598188021822099256)
XLA Ops:
  16.8 13.6 %collective-permute-done.5 = bf16[16,512]{1,0:T(8,128)(2,1)} collective-permute-done((bf16[16,512]{1,0:T(8,128)(2,1)S(1)}, bf16[16,512]{1,0:T(8,128)(2,1)}, u32[]{:S(2)}, u32[]{:S(2)}) %collective-permute-start.5) | collective-permute-done | bytes 16416 | tf_op jit(solution)/shard_map/ppermute | solution.py:1130
  35.7 10.5 %collective-permute-done.7 = bf16[32,512]{1,0:T(8,128)(2,1)S(1)} collective-permute-done((bf16[32,512]{1,0:T(8,128)(2,1)S(1)}, bf16[32,512]{1,0:T(8,128)(2,1)S(1)}, u32[]{:S(2)}, u32[]{:S(2)}) %collective-permute-start.7) | collective-permute-done | bytes 32800 | tf_op jit(solution)/shard_map/ppermute | solution.py:1130
  67.2 5.8 %collective-permute-done.12.refs_3_ = bf16[192,1024]{1,0:T(8,128)(2,1)S(1)} collective-permute-done((bf16[192,1024]{1,0:T(8,128)(2,1)S(1)}, bf16[192,1024]{1,0:T(8,128)(2,1)S(1)}, u32[]{:S(2)}, u32[]{:S(2)}) %collective-permute-start.12) | collective-permute-done | bytes 393248 | tf_op jit(solution)/shard_map/ppermute | solution.py:1130
  73.0 5.0 %normalize.1 = (bf16[2048,1536]{1,0:T(8,128)(2,1)S(1)}, f32[2048,128]{1,0:T(8,128)S(1)}) custom-call(bf16[512,1536]{1,0:T(8,128)(2,1)S(1)} %copy-done.17, bf16[512,1536]{1,0:T(8,128)(2,1)} %collective-permute-done.13.refs_1_, bf16[512,1536]{1,0:T(8,128)(2,1)} %collective-permute-done.10.refs_2_, bf16[512,1536]{1,0:T(8,128)(2,1)} %collective-permute-done.14.refs_3_, ...), custom_call_target="tpu_custom_call" | custom-call | tf_op jit(solution)/shard_map/normalize/pallas_call | solution.py:611
  84.7 9.9 %project.4 = (bf16[1536,896]{1,0:T(8,128)(2,1)S(1)}, f32[2048,896]{1,0:T(8,128)}) custom-call(s32[3]{0:T(128)S(1)} %pad_add_fusion.1.at_ref, bf16[192,1024]{1,0:T(8,128)(2,1)S(1)} %copy-done.45, bf16[192,1024]{1,0:T(8,128)(2,1)S(1)} %copy-done.47, bf16[192,1024]{1,0:T(8,128)(2,1)} %collective-permute-done.1.refs_0_, bf16[192,1024]{1,0:T(8,128)(2,1)S(1)} %copy-done.80, ...), custom_call_target="tpu_custom_call" | custom-call | flops 5637144576 | bytes 6291456 | tf_op jit(solution)/shard_map/project/pallas_call | solution.py:444
  110.5 11.4 %ssd_forward.2 = (f32[2048,768]{1,0:T(8,128)S(1)}, bf16[4,3,128,768]{3,2,1,0:T(8,128)(2,1)S(1)}, f32[2048,768]{1,0:T(8,128)}) custom-call(s32[4,2]{1,0:T(4,128)S(1)} %multiply_add_fusion.len_ref, f32[2048,896]{1,0:T(8,128)} %get-tuple-element.464.u_ref.dt_ref, f32[2048,896]{1,0:T(8,128)} %get-tuple-element.464.u_ref.dt_ref, ...), custom_call_target="tpu_custom_call" | custom-call | flops 6000000000 | bytes 16000000 | tf_op jit(solution)/shard_map/ssd_forward/pallas_call | solution.py:993
  129.7 11.4 %ssd_forward.3 = (f32[2048,768]{1,0:T(8,128)S(1)}, bf16[4,3,128,768]{3,2,1,0:T(8,128)(2,1)S(1)}, f32[2048,768]{1,0:T(8,128)}) custom-call(s32[4,2]{1,0:T(4,128)S(1)} %multiply_add_fusion.len_ref, f32[2048,896]{1,0:T(8,128)} %get-tuple-element.464.u_ref.dt_ref, ...), custom_call_target="tpu_custom_call", output_to_operand_aliasing={{0}: (6, {}), {1}: (7, {}), {2}: (8, {})} | custom-call | flops 6000000000 | bytes 16000000 | tf_op jit(solution)/shard_map/ssd_forward/pallas_call | solution.py:993
  144.5 8.1 %collective-permute-done.26.refs_3_ = bf16[192,768]{1,0:T(8,128)(2,1)S(1)} collective-permute-done((bf16[192,768]{1,0:T(8,128)(2,1)S(1)}, bf16[192,768]{1,0:T(8,128)(2,1)S(1)}, u32[]{:S(2)}, u32[]{:S(2)}) %collective-permute-start.26) | collective-permute-done | bytes 294944 | tf_op jit(solution)/shard_map/ppermute | solution.py:1130
  157.1 7.3 %project.5 = (bf16[1536,768]{1,0:T(8,128)(2,1)S(1)}, f32[2048,768]{1,0:T(8,128)S(1)}) custom-call(s32[3]{0:T(128)S(1)} %pad_add_fusion.1.at_ref, bf16[192,1536]{1,0:T(8,128)(2,1)S(1)} %copy-done.39, bf16[192,1536]{1,0:T(8,128)(2,1)S(1)} %copy-done.41, bf16[192,1536]{1,0:T(8,128)(2,1)S(1)} %copy-done.67, bf16[192,1536]{1,0:T(8,128)(2,1)S(1)} %copy-done.69, ...), custom_call_target="tpu_custom_call" | custom-call | flops 4831838208 | bytes 6291456 | tf_op jit(solution)/shard_map/project/pallas_call | solution.py:444
  169.3 16.1 %branch_back.1 = (bf16[1536,768]{1,0:T(8,128)(2,1)}, f32[2048,768]{1,0:T(8,128)}, f32[8,2048]{1,0:T(8,128)}) custom-call(s32[3]{0:T(128)} %copy-done.86, bf16[192,1536]{1,0:T(8,128)(2,1)} %copy-done.38, bf16[192,1536]{1,0:T(8,128)(2,1)} %copy-done.40, bf16[192,1536]{1,0:T(8,128)(2,1)} %copy-done.65, bf16[192,1536]{1,0:T(8,128)(2,1)} %copy-done.68, ...), custom_call_target="tpu_custom_call" | custom-call | flops 4831838208 | bytes 6291456 | tf_op jit(solution)/shard_map/branch_back/pallas_call | solution.py:506
  192.0 9.2 %gating_back.1 = (bf16[2048,768]{1,0:T(8,128)(2,1)S(1)}, bf16[2048,768]{1,0:T(8,128)(2,1)S(1)}, f32[2048,768]{1,0:T(8,128)S(1)}, f32[8,768]{1,0:T(8,128)S(1)}) custom-call(f32[8,2048]{1,0:T(8,128)S(1)} %copy-done.83, f32[8,2048]{1,0:T(8,128)S(1)} %collective-permute-done.31.core_ref, f32[8,2048]{1,0:T(8,128)S(1)} %collective-permute-done.32.side_ref, ...), custom_call_target="tpu_custom_call" | custom-call | flops 31457280 | bytes 31457280 | tf_op jit(solution)/shard_map/gating_back/pallas_call | solution.py:573
  201.3 5.3 %convolution_convert_fusion = bf16[2048,1536]{1,0:T(8,128)(2,1)S(1)} fusion(bf16[2048,768]{1,0:T(8,128)(2,1)S(1)} %get-tuple-element.522.refs_10_.refs_11_.refs_12_.refs_13_.refs_14_.refs_15_.refs_16_.refs_17_.refs_8_.refs_9_, bf16[1536,768]{1,0:T(8,128)(2,1)S(1)} %copy-done.157), kind=kOutput, calls=%fused_computation | convolution fusion | flops 4834983936 | bytes 11796480 | tf_op jit(solution)/shard_map/dot_general | solution.py:25
  214.7 7.2 %weight_grad.5 = (bf16[384,512]{1,0:T(8,128)(2,1)S(1)}, bf16[384,512]{1,0:T(8,128)(2,1)S(1)}, bf16[384,512]{1,0:T(8,128)(2,1)S(1)}, bf16[384,512]{1,0:T(8,128)(2,1)S(1)}) custom-call(s32[3]{0:T(128)S(1)} %copy-done.87, bf16[512,1536]{1,0:T(8,128)(2,1)} %copy-done.3, bf16[512,1536]{1,0:T(8,128)(2,1)} %copy-done.113, bf16[256,1536]{1,0:T(8,128)(2,1)S(1)} %copy-done.14, ...), custom_call_target="tpu_custom_call" | custom-call | flops 805306368 | bytes 1572864 | tf_op jit(solution)/shard_map/weight_grad/pallas_call | solution.py:701
  222.0 12.8 %weight_grad.4 = (bf16[4,192,1024]{2,1,0:T(8,128)(2,1)S(1)}, bf16[4,192,1024]{2,1,0:T(8,128)(2,1)}) custom-call(s32[3]{0:T(128)S(1)} %copy-done.87, bf16[2048,1536]{1,0:T(8,128)(2,1)} %copy-done.2, bf16[512,1536]{1,0:T(8,128)(2,1)} %copy-done.3, bf16[512,1536]{1,0:T(8,128)(2,1)} %copy-done.113, bf16[256,1536]{1,0:T(8,128)(2,1)S(1)} %copy-done.14, ...), custom_call_target="tpu_custom_call" | custom-call | flops 6442450944 | bytes 6291456 | tf_op jit(solution)/shard_map/weight_grad/pallas_call | solution.py:701
  243.7 31.1 %ssd_backward.3 = (bf16[2048,512]{1,0:T(8,128)(2,1)S(1)}, bf16[2048,128]{1,0:T(8,128)(2,1)S(1)}, f32[2048,128]{1,0:T(8,128)S(1)}, f32[2048,128]{1,0:T(8,128)S(1)...) custom-call(s32[4,2]{1,0:T(4,128)S(1)} %multiply_add_fusion.len_ref, s32[2]{0:T(128)S(1)} %pad_add_fusion.2.at_ref, ...), custom_call_target="tpu_custom_call" | custom-call | flops 32000000000 | bytes 32000000 | tf_op jit(solution)/shard_map/ssd_backward/pallas_call | solution.py:1043
  278.5 6.1 %weight_grad.6 = (bf16[4,192,512]{2,1,0:T(8,128)(2,1)S(1)}, bf16[4,192,512]{2,1,0:T(8,128)(2,1)S(1)}) custom-call(s32[3]{0:T(128)S(1)} %copy-done.87, bf16[2048,1536]{1,0:T(8,128)(2,1)} %copy-done.2, bf16[2048,512]{1,0:T(8,128)(2,1)S(1)} %get-tuple-element.555.refs_1_), custom_call_target="tpu_custom_call" | custom-call | flops 3221225472 | bytes 6291456 | tf_op jit(solution)/shard_map/weight_grad/pallas_call | solution.py:701
  293.6 10.8 %ssd_backward.4 = (bf16[1024,256]{1,0:T(8,128)(2,1)S(1)}, bf16[1024,128]{1,0:T(8,128)(2,1)S(1)}, f32[1024,128]{1,0:T(8,128)S(1)}, bf16[1024,128]{1,0:T(8,128)(2,...) custom-call(s32[4,2]{1,0:T(4,128)S(1)} %multiply_add_fusion.len_ref, s32[2]{0:T(128)S(1)} %pad_add_fusion.2.at_ref, ...), custom_call_target="tpu_custom_call" | custom-call | flops 8000000000 | bytes 16000000 | tf_op jit(solution)/shard_map/ssd_backward/pallas_call | solution.py:1043
  304.5 5.1 %fusion.1 = f32[1024,1536]{1,0:T(8,128)S(1)} fusion(bf16[1536,896]{1,0:T(8,128)(2,1)S(1)} %copy-done.111, bf16[1024,128]{1,0:T(8,128)(2,1)S(1)} %slice_add_fusion.2, bf16[1024,256]{1,0:T(8,128)(2,1)S(1)} %get-tuple-element.632.refs_2_, bf16[1024,512]{1,0:T(8,128)(2,1)} %get-tuple-element.735), kind=kOutput, calls=%fused_computation.10 | convolution fusion | flops 2824077312 | bytes 10878976 | tf_op jit(solution)/shard_map/dot_general | solution.py:25
  328.3 10.8 %ssd_backward.5 = (bf16[1024,256]{1,0:T(8,128)(2,1)S(1)}, bf16[1024,128]{1,0:T(8,128)(2,1)S(1)}, f32[1024,128]{1,0:T(8,128)S(1)}, bf16[1024,128]{1,0:T(8,128)(2,...) custom-call(s32[4,2]{1,0:T(4,128)S(1)} %multiply_add_fusion.len_ref, s32[2]{0:T(128)S(1)} %pad_add_fusion.2.at_ref, ...), custom_call_target="tpu_custom_call" | custom-call | flops 8000000000 | bytes 16000000 | tf_op jit(solution)/shard_map/ssd_backward/pallas_call | solution.py:1043
  339.2 5.1 %collective-permute-done.46 = bf16[192,1024]{1,0:T(8,128)(2,1)S(1)} collective-permute-done((bf16[192,1024]{1,0:T(8,128)(2,1)S(1)}, bf16[192,1024]{1,0:T(8,128)(2,1)S(1)}, u32[]{:S(2)}, u32[]{:S(2)}) %collective-permute-start.46) | collective-permute-done | bytes 393248 | tf_op jit(solution)/shard_map/ppermute | solution.py:1130
  370.0 7.2 %weight_grad.7 = (bf16[4,192,512]{2,1,0:T(8,128)(2,1)S(1)}, bf16[4,192,512]{2,1,0:T(8,128)(2,1)S(1)}) custom-call(s32[3]{0:T(128)S(1)} %copy-done.87, bf16[2048,1536]{1,0:T(8,128)(2,1)} %copy-done.2, bf16[1024,256]{1,0:T(8,128)(2,1)S(1)} %get-tuple-element.631.refs_1_, bf16[1024,256]{1,0:T(8,128)(2,1)S(1)} %copy-done.72, ...), custom_call_target="tpu_custom_call" | custom-call | flops 1610612736 | bytes 3145728 | tf_op jit(solution)/shard_map/weight_grad/pallas_call | solution.py:701
  389.5 7.2 %collective-permute-done.59 = bf16[192,1024]{1,0:T(8,128)(2,1)S(1)} collective-permute-done((bf16[192,1024]{1,0:T(8,128)(2,1)S(1)}, bf16[192,1024]{1,0:T(8,128)(2,1)S(1)}, u32[]{:S(2)}, u32[]{:S(2)}) %collective-permute-start.59) | collective-permute-done | bytes 393248 | tf_op jit(solution)/shard_map/ppermute | solution.py:1130
  409.5 5.0 %collective-permute-done.66 = f32[8,3328]{1,0:T(8,128)S(1)} collective-permute-done((f32[8,3328]{1,0:T(8,128)S(1)}, f32[8,3328]{1,0:T(8,128)S(1)}, u32[]{:S(2)}, u32[]{:S(2)}) %collective-permute-start.66) | collective-permute-done | bytes 106528 | tf_op jit(solution)/shard_map/ppermute | solution.py:1130
  448.9 4.9 %owner_gradients.1 = (f32[192,6448]{1,0:T(8,128)}, f32[192,3072]{1,0:T(8,128)}, f32[192,1]{1,0:T(8,128)S(1)}) custom-call(s32[2]{0:T(128)S(1)} %pad_add_fusion.2.at_ref, bf16[192,2048]{1,0:T(8,128)(2,1)S(1)} %copy-done.52, bf16[192,2048]{1,0:T(8,128)(2,1)S(1)} %copy-done.95, bf16[192,2048]{1,0:T(8,128)(2,1)S(1)} %copy-done.57, ...), custom_call_target="tpu_custom_call" | custom-call | flops 5000000000 | bytes 16000000 | tf_op jit(solution)/shard_map/owner_gradients/pallas_call | solution.py:967
  (564 shorter events, 228.8 us)
Async XLA Ops:
  7.5 23.7 %collective-permute-start.1 = (bf16[192,1024]{1,0:T(8,128)(2,1)}, bf16[192,1024]{1,0:T(8,128)(2,1)}, u32[]{:S(2)}, u32[]{:S(2)}) collective-permute-start(bf16[192,1024]{1,0:T(8,128)(2,1)} %broadcast_select_fusion.14), channel_id=1, source_target_pairs={{0,2},{1,3},{2,4},{3,5},{4,6},{5,7},{6,0},{7,1},{8,10},{9,11},{10,... | collective-permute-start | bytes 1179656 | tf_op jit(solution)/shard_map/ppermute | solution.py:1130
  10.2 20.9 %collective-permute-start.2 = (bf16[192,1024]{1,0:T(8,128)(2,1)}, bf16[192,1024]{1,0:T(8,128)(2,1)}, u32[]{:S(2)}, u32[]{:S(2)}) collective-permute-start(bf16[192,1024]{1,0:T(8,128)(2,1)} %broadcast_select_fusion.14), channel_id=1, source_target_pairs={{0,6},{1,7},{2,0},{3,1},{4,2},{5,3},{6,4},{7,5},{8,14},{9,15},{10,... | collective-permute-start | bytes 1179656 | tf_op jit(solution)/shard_map/ppermute | solution.py:1130
  12.2 18.1 %collective-permute-start.5 = (bf16[16,512]{1,0:T(8,128)(2,1)S(1)}, bf16[16,512]{1,0:T(8,128)(2,1)}, u32[]{:S(2)}, u32[]{:S(2)}) collective-permute-start(bf16[16,512]{1,0:T(8,128)(2,1)S(1)} %pad_maximum_fusion.11), channel_id=1, source_target_pairs={{0,2},{1,3},{2,0},{3,1},{4,6},{5,7},{6,4},{7,5},{8,10},{9,11},{10,... | collective-permute-start | bytes 49160 | tf_op jit(solution)/shard_map/ppermute | solution.py:1130
  12.3 36.8 %collective-permute-start.10 = (bf16[512,1536]{1,0:T(8,128)(2,1)}, bf16[512,1536]{1,0:T(8,128)(2,1)}, u32[]{:S(2)}, u32[]{:S(2)}) collective-permute-start(bf16[512,1536]{1,0:T(8,128)(2,1)} %refs_3_), channel_id=1, source_target_pairs={{0,8},{1,9},{2,10},{3,11},{4,12},{5,13},{6,14},{7,15},{8,0},{9,1},... | collective-permute-start | bytes 4718600 | tf_op jit(solution)/shard_map/ppermute | solution.py:1130
  49.1 23.9 %collective-permute-start.13 = (bf16[512,1536]{1,0:T(8,128)(2,1)}, bf16[512,1536]{1,0:T(8,128)(2,1)}, u32[]{:S(2)}, u32[]{:S(2)}) collective-permute-start(bf16[512,1536]{1,0:T(8,128)(2,1)} %refs_3_), channel_id=1, source_target_pairs={{0,1},{1,0},{2,3},{3,2},{4,5},{5,4},{6,7},{7,6},{8,9},{9,8},{10,11... | collective-permute-start | bytes 4718600 | tf_op jit(solution)/shard_map/ppermute | solution.py:1130
  49.1 23.9 %collective-permute-start.14 = (bf16[512,1536]{1,0:T(8,128)(2,1)}, bf16[512,1536]{1,0:T(8,128)(2,1)}, u32[]{:S(2)}, u32[]{:S(2)}) collective-permute-start(bf16[512,1536]{1,0:T(8,128)(2,1)} %collective-permute-done.10.refs_2_), channel_id=1, source_target_pairs={{0,1},{1,0},{2,3},{3,2},{4,5},{5,4},{6,7},{7,6},{8,9},{9,8},{10,11... | collective-permute-start | bytes 4718600 | tf_op jit(solution)/shard_map/ppermute | solution.py:1130
  59.3 36.9 %collective-permute-start.18 = (bf16[192,1536]{1,0:T(8,128)(2,1)S(1)}, bf16[192,1536]{1,0:T(8,128)(2,1)S(1)}, u32[]{:S(2)}, u32[]{:S(2)}) collective-permute-start(bf16[192,1536]{1,0:T(8,128)(2,1)S(1)} %copy-done.131), channel_id=1, source_target_pairs={{0,6},{1,7},{2,0},{3,1},{4,2},{5,3},{6,4},{7,5},{8,14},{9,15},{10,... | collective-permute-start | bytes 1769480 | tf_op jit(solution)/shard_map/ppermute | solution.py:1130
  65.5 30.6 %collective-permute-start.17 = (bf16[192,1536]{1,0:T(8,128)(2,1)S(1)}, bf16[192,1536]{1,0:T(8,128)(2,1)S(1)}, u32[]{:S(2)}, u32[]{:S(2)}) collective-permute-start(bf16[192,1536]{1,0:T(8,128)(2,1)S(1)} %copy-done.131), channel_id=1, source_target_pairs={{0,2},{1,3},{2,4},{3,5},{4,6},{5,7},{6,0},{7,1},{8,10},{9,11},{10,... | collective-permute-start | bytes 1769480 | tf_op jit(solution)/shard_map/ppermute | solution.py:1130
  105.1 20.1 %collective-permute-start.23 = (bf16[512,1536]{1,0:T(8,128)(2,1)S(1)}, bf16[512,1536]{1,0:T(8,128)(2,1)S(1)}, u32[]{:S(2)}, u32[]{:S(2)}) collective-permute-start(bf16[512,1536]{1,0:T(8,128)(2,1)S(1)} %broadcast_select_fusion.refs_6_.refs_1_.refs_0_.refs_4_), channel_id=1, source_target_pairs={{0,1},{1,0},{2,3},{3,2},{4,5},{5,4},{6,7},{7,6},{8,9},{9,8},{10,11... | collective-permute-start | bytes 4718600 | tf_op jit(solution)/shard_map/ppermute | solution.py:1130
  105.6 19.5 %collective-permute-start.22 = (bf16[256,1536]{1,0:T(8,128)(2,1)S(1)}, bf16[256,1536]{1,0:T(8,128)(2,1)S(1)}, u32[]{:S(2)}, u32[]{:S(2)}) collective-permute-start(bf16[256,1536]{1,0:T(8,128)(2,1)S(1)} %copy-done.129), channel_id=1, source_target_pairs={{0,8},{1,9},{2,10},{3,11},{4,12},{5,13},{6,14},{7,15},{8,0},{9,1},... | collective-permute-start | bytes 2359304 | tf_op jit(solution)/shard_map/ppermute | solution.py:1130
  211.3 23.5 %collective-permute-start.34 = (bf16[2,512,1536]{2,1,0:T(8,128)(2,1)}, bf16[2,512,1536]{2,1,0:T(8,128)(2,1)}, u32[]{:S(2)}, u32[]{:S(2)}) collective-permute-start(bf16[2,512,1536]{2,1,0:T(8,128)(2,1)} %slice_bitcast_fusion), channel_id=1, source_target_pairs={{0,1},{1,0},{2,3},{3,2},{4,5},{5,4},{6,7},{7,6},{8,9},{9,8},{10,11... | collective-permute-start | bytes 9437192 | tf_op jit(solution)/shard_map/ppermute | solution.py:1130
  237.2 37.7 %collective-permute-start.36 = (bf16[384,512]{1,0:T(8,128)(2,1)S(1)}, bf16[384,512]{1,0:T(8,128)(2,1)S(1)}, u32[]{:S(2)}, u32[]{:S(2)}) collective-permute-start(bf16[384,512]{1,0:T(8,128)(2,1)S(1)} %get-tuple-element.537), channel_id=1, source_target_pairs={{0,2},{1,3},{2,4},{3,5},{4,6},{5,7},{6,0},{7,1},{8,10},{9,11},{10,... | collective-permute-start | bytes 1179656 | tf_op jit(solution)/shard_map/ppermute | solution.py:1130
  238.9 36.0 %collective-permute-start.37 = (bf16[384,512]{1,0:T(8,128)(2,1)S(1)}, bf16[384,512]{1,0:T(8,128)(2,1)S(1)}, u32[]{:S(2)}, u32[]{:S(2)}) collective-permute-start(bf16[384,512]{1,0:T(8,128)(2,1)S(1)} %get-tuple-element.538), channel_id=1, source_target_pairs={{0,4},{1,5},{2,6},{3,7},{4,0},{5,1},{6,2},{7,3},{8,12},{9,13},{10,... | collective-permute-start | bytes 1179656 | tf_op jit(solution)/shard_map/ppermute | solution.py:1130
  239.6 35.3 %collective-permute-start.38 = (bf16[384,512]{1,0:T(8,128)(2,1)S(1)}, bf16[384,512]{1,0:T(8,128)(2,1)S(1)}, u32[]{:S(2)}, u32[]{:S(2)}) collective-permute-start(bf16[384,512]{1,0:T(8,128)(2,1)S(1)} %get-tuple-element.539), channel_id=1, source_target_pairs={{0,6},{1,7},{2,0},{3,1},{4,2},{5,3},{6,4},{7,5},{8,14},{9,15},{10,... | collective-permute-start | bytes 1179656 | tf_op jit(solution)/shard_map/ppermute | solution.py:1130
  242.1 35.9 %collective-permute-start.35 = (bf16[4,192,1024]{2,1,0:T(8,128)(2,1)}, bf16[4,192,1024]{2,1,0:T(8,128)(2,1)S(1)}, u32[]{:S(2)}, u32[]{:S(2)}) collective-permute-start(bf16[4,192,1024]{2,1,0:T(8,128)(2,1)} %get-tuple-element.536), channel_id=1, source_target_pairs={{0,16},{1,17},{2,18},{3,19},{4,20},{5,21},{6,22},{7,23},{8,24},{9,... | collective-permute-start | bytes 4718600 | tf_op jit(solution)/shard_map/ppermute | solution.py:1130
  242.9 35.6 %collective-permute-start.39 = (bf16[512,1536]{1,0:T(8,128)(2,1)S(1)}, bf16[512,1536]{1,0:T(8,128)(2,1)}, u32[]{:S(2)}, u32[]{:S(2)}) collective-permute-start(bf16[512,1536]{1,0:T(8,128)(2,1)S(1)} %fusion), channel_id=1, source_target_pairs={{0,8},{1,9},{2,10},{3,11},{4,12},{5,13},{6,14},{7,15},{8,0},{9,1},... | collective-permute-start | bytes 4718600 | tf_op jit(solution)/shard_map/ppermute | solution.py:1130
  288.6 24.1 %collective-permute-start.41 = (bf16[192,1024]{1,0:T(8,128)(2,1)S(1)}, bf16[192,1024]{1,0:T(8,128)(2,1)S(1)}, u32[]{:S(2)}, u32[]{:S(2)}) collective-permute-start(bf16[192,1024]{1,0:T(8,128)(2,1)S(1)} %get-tuple-element.568), channel_id=1, source_target_pairs={{0,2},{1,3},{2,4},{3,5},{4,6},{5,7},{6,0},{7,1},{8,10},{9,11},{10,... | collective-permute-start | bytes 1179656 | tf_op jit(solution)/shard_map/ppermute | solution.py:1130
  288.6 24.1 %collective-permute-start.42 = (bf16[192,1024]{1,0:T(8,128)(2,1)S(1)}, bf16[192,1024]{1,0:T(8,128)(2,1)S(1)}, u32[]{:S(2)}, u32[]{:S(2)}) collective-permute-start(bf16[192,1024]{1,0:T(8,128)(2,1)S(1)} %get-tuple-element.569), channel_id=1, source_target_pairs={{0,6},{1,7},{2,0},{3,1},{4,2},{5,3},{6,4},{7,5},{8,14},{9,15},{10,... | collective-permute-start | bytes 1179656 | tf_op jit(solution)/shard_map/ppermute | solution.py:1130
  292.4 20.3 %collective-permute-start.40 = (bf16[4,192,512]{2,1,0:T(8,128)(2,1)S(1)}, bf16[4,192,512]{2,1,0:T(8,128)(2,1)S(1)}, u32[]{:S(2)}, u32[]{:S(2)}) collective-permute-start(bf16[4,192,512]{2,1,0:T(8,128)(2,1)S(1)} %get-tuple-element.567), channel_id=1, source_target_pairs={{0,16},{1,17},{2,18},{3,19},{4,20},{5,21},{6,22},{7,23},{8,24},{9,... | collective-permute-start | bytes 2359304 | tf_op jit(solution)/shard_map/ppermute | solution.py:1130
  358.2 20.0 %collective-permute-start.55 = (bf16[256,1536]{1,0:T(8,128)(2,1)S(1)}, bf16[256,1536]{1,0:T(8,128)(2,1)S(1)}, u32[]{:S(2)}, u32[]{:S(2)}) collective-permute-start(bf16[256,1536]{1,0:T(8,128)(2,1)S(1)} %slice.198), channel_id=1, source_target_pairs={{0,8},{1,9},{2,10},{3,11},{4,12},{5,13},{6,14},{7,15},{8,0},{9,1},... | collective-permute-start | bytes 2359304 | tf_op jit(solution)/shard_map/ppermute | solution.py:1130
  380.9 20.3 %collective-permute-start.57 = (bf16[512,1536]{1,0:T(8,128)(2,1)}, bf16[512,1536]{1,0:T(8,128)(2,1)}, u32[]{:S(2)}, u32[]{:S(2)}) collective-permute-start(bf16[512,1536]{1,0:T(8,128)(2,1)} %add_convert_fusion.1), channel_id=1, source_target_pairs={{0,1},{1,0},{2,3},{3,2},{4,5},{5,4},{6,7},{7,6},{8,9},{9,8},{10,11... | collective-permute-start | bytes 4718600 | tf_op jit(solution)/shard_map/ppermute | solution.py:1130
  381.0 20.2 %collective-permute-start.56 = (bf16[4,192,512]{2,1,0:T(8,128)(2,1)}, bf16[4,192,512]{2,1,0:T(8,128)(2,1)S(1)}, u32[]{:S(2)}, u32[]{:S(2)}) collective-permute-start(bf16[4,192,512]{2,1,0:T(8,128)(2,1)} %copy-done.100), channel_id=1, source_target_pairs={{0,16},{1,17},{2,18},{3,19},{4,20},{5,21},{6,22},{7,23},{8,24},{9,... | collective-permute-start | bytes 2359304 | tf_op jit(solution)/shard_map/ppermute | solution.py:1130
  402.8 20.0 %collective-permute-start.64 = (bf16[192,2048]{1,0:T(8,128)(2,1)S(1)}, bf16[192,2048]{1,0:T(8,128)(2,1)S(1)}, u32[]{:S(2)}, u32[]{:S(2)}) collective-permute-start(bf16[192,2048]{1,0:T(8,128)(2,1)S(1)} %pad_maximum_fusion.1.refs_0_), channel_id=1, source_target_pairs={{0,8},{1,9},{2,10},{3,11},{4,12},{5,13},{6,14},{7,15},{8,0},{9,1},... | collective-permute-start | bytes 2359304 | tf_op jit(solution)/shard_map/ppermute | solution.py:1130
  403.4 19.4 %collective-permute-start.65 = (bf16[192,2048]{1,0:T(8,128)(2,1)S(1)}, bf16[192,2048]{1,0:T(8,128)(2,1)S(1)}, u32[]{:S(2)}, u32[]{:S(2)}) collective-permute-start(bf16[192,2048]{1,0:T(8,128)(2,1)S(1)} %pad_maximum_fusion.2), channel_id=1, source_target_pairs={{0,16},{1,17},{2,18},{3,19},{4,20},{5,21},{6,22},{7,23},{8,24},{9,... | collective-permute-start | bytes 2359304 | tf_op jit(solution)/shard_map/ppermute | solution.py:1130
  (210 other events, 1993.0 us)

commit v5 on v4

--- a/solution.py
+++ b/solution.py
@@ -71,7 +71,15 @@
     return jnp.where(low, matrix[:, head : head + 1], matrix[:, head + 1 : head + 2])
 
 
-def forward_kernel(heads, size, first_block, len_ref, u_ref, dt_ref, kq_ref, cw_ref, hp_ref, *refs):
+def keys_queries_of(is_high, mine_ref, other_ref, start):
+    here = slice(start, start + CHUNK)
+    mine, other = mine_ref[here, :], other_ref[here, :]
+    return jnp.where(is_high, other, mine), jnp.where(is_high, mine, other)
+
+
+def forward_kernel(
+    heads, size, first_block, len_ref, at_ref, u_ref, dt_ref, kq_ref, kq_other_ref, cw_ref, hp_ref, *refs
+):
     y_ref, st_ref, pre_ref, state = refs[-4:]
     block = first_block + pl.program_id(0)
     first = len_ref[block, 0]
@@ -88,8 +96,7 @@
         masks = [position - delay >= begin for delay in range(1, 4)]
         raw, step, rate, running = chunk_rates(dt_ref, hp_ref, start)
         running_t = running.T
-        keys = kq_ref[start : start + CHUNK, :LANES]
-        queries = kq_ref[start : start + CHUNK, LANES:]
+        keys, queries = keys_queries_of(at_ref[1] == 1, kq_ref, kq_other_ref, start)
         keys_t = keys.astype(F32).T.astype(BF16)
         allowed = (column <= row) & (column + start >= begin)
         scores = jnp.where(allowed, dot_nt(queries, keys), 0.0)
@@ -140,6 +147,7 @@
     pre_ref,
     dt_ref,
     kq_ref,
+    kq_other_ref,
     dy_ref,
     st_ref,
     cw_ref,
@@ -175,8 +183,7 @@
         ahead = [begin_of(position + delay, first, both) <= position for delay in range(1, 4)]
         raw, step, rate, running = chunk_rates(dt_ref, hp_ref, start)
         running_t = running.T
-        keys = kq_ref[start : start + CHUNK, :LANES]
-        queries = kq_ref[start : start + CHUNK, LANES:]
+        keys, queries = keys_queries_of(is_high, kq_ref, kq_other_ref, start)
         allowed = (row <= column) & (position >= begin_of(column + start, first, both))
         scores = jnp.where(allowed, dot_nt(keys, queries), 0.0)
         last_begin = begin_of(start + CHUNK - 1, first, both)
@@ -983,21 +990,23 @@
 
 
 def forward_call(
-    heads, size, first_block, blocks, lengths, conv_in, keys_queries, conv_rows, head_rows, before=()
+    heads, size, first_block, blocks, lengths, place, conv_in, keys_queries, conv_rows, head_rows, before=()
 ):
     total = conv_in.shape[0]
     tokens = total // lengths.shape[0]
     width = heads * size
-    state = keys_queries.shape[1] // 2
+    state = keys_queries[0].shape[1]
     boundaries = tokens // CHUNK - 1
     return pl.pallas_call(
         functools.partial(forward_kernel, heads, size, first_block),
         grid=(blocks,),
         in_specs=[
             pl.BlockSpec(memory_space=pltpu.SMEM),
+            pl.BlockSpec(memory_space=pltpu.SMEM),
             pl.BlockSpec((tokens, width), lambda b: (first_block + b, 0)),
             pl.BlockSpec((tokens, LANES), lambda b: (first_block + b, width // LANES)),
-            pl.BlockSpec((tokens, 2 * state), lambda b: (first_block + b, 0)),
+            pl.BlockSpec((tokens, state), lambda b: (first_block + b, 0)),
+            pl.BlockSpec((tokens, state), lambda b: (first_block + b + 1 - 2 * lax.rem(b, 2), 0)),
             pl.BlockSpec((8, width), lambda b: (0, 0)),
             pl.BlockSpec((8, LANES), lambda b: (0, 0)),
         ]
@@ -1013,13 +1022,13 @@
             jax.ShapeDtypeStruct((total, width), F32),
         ],
         scratch_shapes=[pltpu.VMEM((state, width), F32)],
-        input_output_aliases={6 + at: at for at in range(len(before))},
+        input_output_aliases={8 + at: at for at in range(len(before))},
         compiler_params=pltpu.CompilerParams(vmem_limit_bytes=40 * 1024 * 1024),
         cost_estimate=pl.CostEstimate(
             flops=blocks * 3_000_000_000, bytes_accessed=blocks * 8_000_000, transcendentals=0
         ),
         name="ssd_forward",
-    )(lengths, conv_in, conv_in, keys_queries, conv_rows, head_rows, *before)
+    )(lengths, place, conv_in, conv_in, *keys_queries, conv_rows, head_rows, *before)
 
 
 def backward_call(
@@ -1031,7 +1040,7 @@
     width = heads * size
     part = first_head * size // width
     steps_at = d_out.shape[1] // LANES
-    state = keys_queries.shape[1] // 2
+    state = keys_queries[0].shape[1]
     boundaries = tokens // CHUNK - 1
 
     def rows_of(columns, index):
@@ -1049,7 +1058,8 @@
             rows_of(width, part),
             rows_of(width, part),
             rows_of(LANES, steps_at),
-            rows_of(2 * state, 0),
+            rows_of(state, 0),
+            pl.BlockSpec((tokens, state), lambda b: (swapped(first_block + b), 0)),
             rows_of(width, part),
             pl.BlockSpec(
                 (1, boundaries, state, width), lambda b: (first_block + b, 0, 0, part)
@@ -1090,7 +1100,7 @@
             transcendentals=0,
         ),
         name="ssd_backward",
-    )(lengths, place, conv_in, conv_pre, conv_in, keys_queries, d_out, states, conv_rows, head_rows, *before)
+    )(lengths, place, conv_in, conv_pre, conv_in, *keys_queries, d_out, states, conv_rows, head_rows, *before)
 
 
 def after(values):
@@ -1446,10 +1456,7 @@
     kq_half = jnp.concatenate([kq_near[: 2 * tokens], kq_far[: 2 * tokens]], axis=0)
 
     (kq_core,), _ = phase([(links.core, kq_half)])
-    kq_core = kq_core.reshape(2, 2, tokens, state)[:, ::-1].reshape(4 * tokens, state)
-    keys_queries = jnp.concatenate(
-        [jnp.where(is_high, kq_core, kq_half), jnp.where(is_high, kq_half, kq_core)], axis=1
-    )
+    keys_queries = [kq_half, kq_core]
     firsts = [k for k in pieces_b if k]
     hop_count = len(hops(pieces_b, 2))
     moved, before = phase(
@@ -1457,7 +1464,7 @@
         + rounds(pieces_b[firsts[0]])
         + [(links.side, back_own[cuts[0]]), (links.core, back_own)],
         functools.partial(forward_call, heads, size, 0, 2),
-        (all_lengths, conv_in, keys_queries, conv_rows, head_rows),
+        (all_lengths, core_place, conv_in, keys_queries, conv_rows, head_rows),
     )
     y_b = {firsts[0]: moved[hop_count:-2]}
     far_back[0] = moved[-2]
@@ -1471,7 +1478,7 @@
         [send for k in firsts[1:] for send in rounds(pieces_b[k])]
         + [(links.side, back_own[cuts[2]])],
         functools.partial(forward_call, heads, size, 2, 2),
-        (all_lengths, conv_in, keys_queries, conv_rows, head_rows, before),
+        (all_lengths, core_place, conv_in, keys_queries, conv_rows, head_rows, before),
     )
     far_back.append(moved[-1])
     for at, k in enumerate(firsts[1:]):

time: 467 us -> 452 us (0.968)
  local copies, waits for them, and re-layouts: 56.4 us -> 46.2 us
  other arithmetic: 26.7 us -> 21 us
  waiting for transfers between devices: 91.8 us -> 96.9 us
    unnamed x316 -> x308, local copies, waits for them, and re-layouts: 35.6 us -> 29.2 us
    ppermute x76, waiting for transfers between devices: 91.8 us -> 96.9 us  [send(): return lax.ppermute(value, ('rep', 'fsdp'), pairs)]
  transfers between devices with their start and end apart: 76 -> 76, of which waited for: 24 -> 27; matrix products, arithmetic and copies ran while one was open for 9% -> 8% of each run, Pallas kernels for 31% -> 32%
where the time goes in v5:
time: 452 us; the launch traced here: 445 us
  Pallas kernels  178 us (39%)
  waiting for transfers between devices  96.9 us (21%)
  starting transfers between devices  76.5 us (17%)
  local copies, waits for them, and re-layouts  46.2 us (10%)
  matrix products  22.4 us (5%)
  other arithmetic  21 us (5%)
    ppermute x76, waiting for transfers between devices, send(): return lax.ppermute(value, ('rep', 'fsdp'), pairs)  96.9 us
    ppermute x76, starting transfers between devices, send(): return lax.ppermute(value, ('rep', 'fsdp'), pairs)  76.5 us
    pallas_call x3, Pallas kernels, backward_call(): pl.pallas_call(functools.partial(backward_kernel, heads, size, first_head...  52.7 us
    pallas_call x4, Pallas kernels, weight_grad_call(): pl.pallas_call(functools.partial(weight_grad_kernel, links_shape, shapes,...  33.7 us
    unnamed x308, local copies, waits for them, and re-layouts  29.2 us
    pallas_call x2, Pallas kernels, forward_call(): pl.pallas_call(functools.partial(forward_kernel, heads, size, first_block...  22.9 us
    dot_general x7, matrix products, dot_nt(): lax.dot_general(left, right, (((1,), (1,)), ((), ())), preferred_element_...  22.4 us
    pallas_call x3, Pallas kernels, project_call(): pl.pallas_call(functools.partial(project_kernel, links_shape), grid=(bloc...  19.5 us
  transfers between devices with their start and end apart: 76, of which 27 were waited for; matrix products, arithmetic and copies ran while one was open for 8% of the time, Pallas kernels for 32%

profile of v5, /device:TPU:0, one launch (start us, length us, event | category | flops | bytes accessed | tf_op | source)
XLA Modules:
  0.0 444.6 jit_solution(9654061505216997083)
XLA Ops:
  16.8 13.6 %collective-permute-done.5 = bf16[16,512]{1,0:T(8,128)(2,1)} collective-permute-done((bf16[16,512]{1,0:T(8,128)(2,1)S(1)}, bf16[16,512]{1,0:T(8,128)(2,1)}, u32[]{:S(2)}, u32[]{:S(2)}) %collective-permute-start.5) | collective-permute-done | bytes 16416 | tf_op jit(solution)/shard_map/ppermute | solution.py:1140
  35.7 10.5 %collective-permute-done.7 = bf16[32,512]{1,0:T(8,128)(2,1)S(1)} collective-permute-done((bf16[32,512]{1,0:T(8,128)(2,1)S(1)}, bf16[32,512]{1,0:T(8,128)(2,1)S(1)}, u32[]{:S(2)}, u32[]{:S(2)}) %collective-permute-start.7) | collective-permute-done | bytes 32800 | tf_op jit(solution)/shard_map/ppermute | solution.py:1140
  59.8 5.1 %collective-permute-done.11.refs_5_ = bf16[192,1024]{1,0:T(8,128)(2,1)S(1)} collective-permute-done((bf16[192,1024]{1,0:T(8,128)(2,1)}, bf16[192,1024]{1,0:T(8,128)(2,1)S(1)}, u32[]{:S(2)}, u32[]{:S(2)}) %collective-permute-start.11) | collective-permute-done | bytes 393248 | tf_op jit(solution)/shard_map/ppermute | solution.py:1140
  66.6 5.8 %collective-permute-done.12.refs_3_ = bf16[192,1024]{1,0:T(8,128)(2,1)S(1)} collective-permute-done((bf16[192,1024]{1,0:T(8,128)(2,1)S(1)}, bf16[192,1024]{1,0:T(8,128)(2,1)S(1)}, u32[]{:S(2)}, u32[]{:S(2)}) %collective-permute-start.12) | collective-permute-done | bytes 393248 | tf_op jit(solution)/shard_map/ppermute | solution.py:1140
  72.4 5.0 %normalize.1 = (bf16[2048,1536]{1,0:T(8,128)(2,1)S(1)}, f32[2048,128]{1,0:T(8,128)S(1)}) custom-call(bf16[512,1536]{1,0:T(8,128)(2,1)S(1)} %copy-done.18, bf16[512,1536]{1,0:T(8,128)(2,1)} %collective-permute-done.13.refs_1_, bf16[512,1536]{1,0:T(8,128)(2,1)} %collective-permute-done.10.refs_2_, bf16[512,1536]{1,0:T(8,128)(2,1)} %collective-permute-done.14.refs_3_, ...), custom_call_target="tpu_custom_call" | custom-call | tf_op jit(solution)/shard_map/normalize/pallas_call | solution.py:618
  83.1 9.9 %project.4 = (bf16[1536,896]{1,0:T(8,128)(2,1)S(1)}, f32[2048,896]{1,0:T(8,128)}) custom-call(s32[3]{0:T(128)S(1)} %pad_add_fusion.1.at_ref, bf16[192,1024]{1,0:T(8,128)(2,1)S(1)} %get-tuple-element.428.own_ref, bf16[192,1024]{1,0:T(8,128)(2,1)S(1)} %copy-done.43, bf16[192,1024]{1,0:T(8,128)(2,1)} %collective-permute-done.1.refs_0_, ...), custom_call_target="tpu_custom_call" | custom-call | flops 5637144576 | bytes 6291456 | tf_op jit(solution)/shard_map/project/pallas_call | solution.py:451
  105.0 11.5 %ssd_forward.2 = (f32[2048,768]{1,0:T(8,128)S(1)}, bf16[4,3,128,768]{3,2,1,0:T(8,128)(2,1)S(1)}, f32[2048,768]{1,0:T(8,128)}) custom-call(s32[4,2]{1,0:T(4,128)S(1)} %multiply_add_fusion.len_ref, s32[2]{0:T(128)S(1)} %pad_add_fusion.2.at_ref, f32[2048,896]{1,0:T(8,128)} %get-tuple-element.471.u_ref.dt_ref, f32[2048,896]{1,0:T(8,128)} %get-tuple-element.471.u_ref.dt_ref, ...), custom_call_target="tpu_custom_call" | custom-call | flops 6000000000 | bytes 16000000 | tf_op jit(solution)/shard_map/ssd_forward/pallas_call | solution.py:1000
  123.6 11.4 %ssd_forward.3 = (f32[2048,768]{1,0:T(8,128)S(1)}, bf16[4,3,128,768]{3,2,1,0:T(8,128)(2,1)S(1)}, f32[2048,768]{1,0:T(8,128)}) custom-call(s32[4,2]{1,0:T(4,128)S(1)} %multiply_add_fusion.len_ref, s32[2]{0:T(128)S(1)} %pad_add_fusion.2.at_ref, ...), custom_call_target="tpu_custom_call", output_to_operand_aliasing={{0}: (8, {}), {1}: (9, {}), {2}: (10, {})} | custom-call | flops 6000000000 | bytes 16000000 | tf_op jit(solution)/shard_map/ssd_forward/pallas_call | solution.py:1000
  138.7 7.8 %collective-permute-done.26.refs_3_ = bf16[192,768]{1,0:T(8,128)(2,1)S(1)} collective-permute-done((bf16[192,768]{1,0:T(8,128)(2,1)S(1)}, bf16[192,768]{1,0:T(8,128)(2,1)S(1)}, u32[]{:S(2)}, u32[]{:S(2)}) %collective-permute-start.26) | collective-permute-done | bytes 294944 | tf_op jit(solution)/shard_map/ppermute | solution.py:1140
  149.3 7.3 %project.5 = (bf16[1536,768]{1,0:T(8,128)(2,1)S(1)}, f32[2048,768]{1,0:T(8,128)S(1)}) custom-call(s32[3]{0:T(128)S(1)} %pad_add_fusion.1.at_ref, bf16[192,1536]{1,0:T(8,128)(2,1)S(1)} %copy-done.37, bf16[192,1536]{1,0:T(8,128)(2,1)S(1)} %copy-done.39, bf16[192,1536]{1,0:T(8,128)(2,1)S(1)} %copy-done.56, ...), custom_call_target="tpu_custom_call" | custom-call | flops 4831838208 | bytes 6291456 | tf_op jit(solution)/shard_map/project/pallas_call | solution.py:451
  161.4 16.1 %branch_back.1 = (bf16[1536,768]{1,0:T(8,128)(2,1)}, f32[2048,768]{1,0:T(8,128)}, f32[8,2048]{1,0:T(8,128)}) custom-call(s32[3]{0:T(128)} %copy-done.74, bf16[192,1536]{1,0:T(8,128)(2,1)} %copy-done.36, bf16[192,1536]{1,0:T(8,128)(2,1)} %copy-done.38, bf16[192,1536]{1,0:T(8,128)(2,1)} %copy-done.55, bf16[192,1536]{1,0:T(8,128)(2,1)} %copy-done.57, ...), custom_call_target="tpu_custom_call" | custom-call | flops 4831838208 | bytes 6291456 | tf_op jit(solution)/shard_map/branch_back/pallas_call | solution.py:513
  184.1 9.2 %gating_back.1 = (bf16[2048,768]{1,0:T(8,128)(2,1)S(1)}, bf16[2048,768]{1,0:T(8,128)(2,1)S(1)}, f32[2048,768]{1,0:T(8,128)S(1)}, f32[8,768]{1,0:T(8,128)S(1)}) custom-call(f32[8,2048]{1,0:T(8,128)S(1)} %copy-done.71, f32[8,2048]{1,0:T(8,128)S(1)} %collective-permute-done.31.core_ref, f32[8,2048]{1,0:T(8,128)S(1)} %collective-permute-done.32.side_ref, ...), custom_call_target="tpu_custom_call" | custom-call | flops 31457280 | bytes 31457280 | tf_op jit(solution)/shard_map/gating_back/pallas_call | solution.py:580
  193.4 5.3 %convolution_convert_fusion = bf16[2048,1536]{1,0:T(8,128)(2,1)S(1)} fusion(bf16[2048,768]{1,0:T(8,128)(2,1)S(1)} %get-tuple-element.530.refs_10_.refs_11_.refs_12_.refs_13_.refs_14_.refs_15_.refs_16_.refs_17_.refs_8_.refs_9_, bf16[1536,768]{1,0:T(8,128)(2,1)S(1)} %copy-done.153), kind=kOutput, calls=%fused_computation | convolution fusion | flops 4834983936 | bytes 11796480 | tf_op jit(solution)/shard_map/dot_general | solution.py:25
  204.1 7.2 %weight_grad.5 = (bf16[384,512]{1,0:T(8,128)(2,1)S(1)}, bf16[384,512]{1,0:T(8,128)(2,1)S(1)}, bf16[384,512]{1,0:T(8,128)(2,1)S(1)}, bf16[384,512]{1,0:T(8,128)(2,1)S(1)}) custom-call(s32[3]{0:T(128)S(1)} %copy-done.75, bf16[512,1536]{1,0:T(8,128)(2,1)} %copy-done.3, bf16[512,1536]{1,0:T(8,128)(2,1)} %copy-done.102, bf16[256,1536]{1,0:T(8,128)(2,1)S(1)} %copy-done.15, ...), custom_call_target="tpu_custom_call" | custom-call | flops 805306368 | bytes 1572864 | tf_op jit(solution)/shard_map/weight_grad/pallas_call | solution.py:708
  211.3 12.8 %weight_grad.4 = (bf16[4,192,1024]{2,1,0:T(8,128)(2,1)S(1)}, bf16[4,192,1024]{2,1,0:T(8,128)(2,1)}) custom-call(s32[3]{0:T(128)S(1)} %copy-done.75, bf16[2048,1536]{1,0:T(8,128)(2,1)} %copy-done.2, bf16[512,1536]{1,0:T(8,128)(2,1)} %copy-done.3, bf16[512,1536]{1,0:T(8,128)(2,1)} %copy-done.102, bf16[256,1536]{1,0:T(8,128)(2,1)S(1)} %copy-done.15, ...), custom_call_target="tpu_custom_call" | custom-call | flops 6442450944 | bytes 6291456 | tf_op jit(solution)/shard_map/weight_grad/pallas_call | solution.py:708
  232.5 31.1 %ssd_backward.3 = (bf16[2048,512]{1,0:T(8,128)(2,1)S(1)}, bf16[2048,128]{1,0:T(8,128)(2,1)S(1)}, f32[2048,128]{1,0:T(8,128)S(1)}, f32[2048,128]{1,0:T(8,128)S(1)...) custom-call(s32[4,2]{1,0:T(4,128)S(1)} %multiply_add_fusion.len_ref, s32[2]{0:T(128)S(1)} %pad_add_fusion.2.at_ref, ...), custom_call_target="tpu_custom_call" | custom-call | flops 32000000000 | bytes 32000000 | tf_op jit(solution)/shard_map/ssd_backward/pallas_call | solution.py:1052
  267.3 6.6 %weight_grad.6 = (bf16[4,192,512]{2,1,0:T(8,128)(2,1)S(1)}, bf16[4,192,512]{2,1,0:T(8,128)(2,1)S(1)}) custom-call(s32[3]{0:T(128)S(1)} %copy-done.75, bf16[2048,1536]{1,0:T(8,128)(2,1)} %copy-done.2, bf16[2048,512]{1,0:T(8,128)(2,1)S(1)} %get-tuple-element.563.refs_1_), custom_call_target="tpu_custom_call" | custom-call | flops 3221225472 | bytes 6291456 | tf_op jit(solution)/shard_map/weight_grad/pallas_call | solution.py:708
  283.2 10.8 %ssd_backward.4 = (bf16[1024,256]{1,0:T(8,128)(2,1)S(1)}, bf16[1024,128]{1,0:T(8,128)(2,1)S(1)}, f32[1024,128]{1,0:T(8,128)S(1)}, bf16[1024,128]{1,0:T(8,128)(2,...) custom-call(s32[4,2]{1,0:T(4,128)S(1)} %multiply_add_fusion.len_ref, s32[2]{0:T(128)S(1)} %pad_add_fusion.2.at_ref, ...), custom_call_target="tpu_custom_call" | custom-call | flops 8000000000 | bytes 16000000 | tf_op jit(solution)/shard_map/ssd_backward/pallas_call | solution.py:1052
  313.0 10.9 %ssd_backward.5 = (bf16[1024,256]{1,0:T(8,128)(2,1)S(1)}, bf16[1024,128]{1,0:T(8,128)(2,1)S(1)}, f32[1024,128]{1,0:T(8,128)S(1)}, bf16[1024,128]{1,0:T(8,128)(2,...) custom-call(s32[4,2]{1,0:T(4,128)S(1)} %multiply_add_fusion.len_ref, s32[2]{0:T(128)S(1)} %pad_add_fusion.2.at_ref, ...), custom_call_target="tpu_custom_call" | custom-call | flops 8000000000 | bytes 16000000 | tf_op jit(solution)/shard_map/ssd_backward/pallas_call | solution.py:1052
  324.0 5.2 %collective-permute-done.46 = bf16[192,1024]{1,0:T(8,128)(2,1)S(1)} collective-permute-done((bf16[192,1024]{1,0:T(8,128)(2,1)S(1)}, bf16[192,1024]{1,0:T(8,128)(2,1)S(1)}, u32[]{:S(2)}, u32[]{:S(2)}) %collective-permute-start.46) | collective-permute-done | bytes 393248 | tf_op jit(solution)/shard_map/ppermute | solution.py:1140
  354.8 7.2 %weight_grad.7 = (bf16[4,192,512]{2,1,0:T(8,128)(2,1)S(1)}, bf16[4,192,512]{2,1,0:T(8,128)(2,1)S(1)}) custom-call(s32[3]{0:T(128)S(1)} %copy-done.75, bf16[2048,1536]{1,0:T(8,128)(2,1)} %copy-done.2, bf16[1024,256]{1,0:T(8,128)(2,1)S(1)} %get-tuple-element.639.refs_1_, bf16[1024,256]{1,0:T(8,128)(2,1)S(1)} %copy-done.60, ...), custom_call_target="tpu_custom_call" | custom-call | flops 1610612736 | bytes 3145728 | tf_op jit(solution)/shard_map/weight_grad/pallas_call | solution.py:708
  373.1 8.6 %collective-permute-done.59 = bf16[192,1024]{1,0:T(8,128)(2,1)S(1)} collective-permute-done((bf16[192,1024]{1,0:T(8,128)(2,1)}, bf16[192,1024]{1,0:T(8,128)(2,1)S(1)}, u32[]{:S(2)}, u32[]{:S(2)}) %collective-permute-start.59) | collective-permute-done | bytes 393248 | tf_op jit(solution)/shard_map/ppermute | solution.py:1140
  395.0 5.7 %collective-permute-done.66 = f32[8,3328]{1,0:T(8,128)S(1)} collective-permute-done((f32[8,3328]{1,0:T(8,128)S(1)}, f32[8,3328]{1,0:T(8,128)S(1)}, u32[]{:S(2)}, u32[]{:S(2)}) %collective-permute-start.66) | collective-permute-done | bytes 106528 | tf_op jit(solution)/shard_map/ppermute | solution.py:1140
  434.9 4.9 %owner_gradients.1 = (f32[192,6448]{1,0:T(8,128)}, f32[192,3072]{1,0:T(8,128)}, f32[192,1]{1,0:T(8,128)S(1)}) custom-call(s32[2]{0:T(128)S(1)} %pad_add_fusion.2.at_ref, bf16[192,2048]{1,0:T(8,128)(2,1)S(1)} %pad_maximum_fusion.refs_0_, bf16[192,2048]{1,0:T(8,128)(2,1)S(1)} %copy-done.83, bf16[192,2048]{1,0:T(8,128)(2,1)S(1)} %copy-done.49, ...), custom_call_target="tpu_custom_call" | custom-call | flops 5000000000 | bytes 16000000 | tf_op jit(solution)/shard_map/owner_gradients/pallas_call | solution.py:974
  (553 shorter events, 211.9 us)
Async XLA Ops:
  7.5 23.7 %collective-permute-start.1 = (bf16[192,1024]{1,0:T(8,128)(2,1)}, bf16[192,1024]{1,0:T(8,128)(2,1)}, u32[]{:S(2)}, u32[]{:S(2)}) collective-permute-start(bf16[192,1024]{1,0:T(8,128)(2,1)} %broadcast_select_fusion.14), channel_id=1, source_target_pairs={{0,2},{1,3},{2,4},{3,5},{4,6},{5,7},{6,0},{7,1},{8,10},{9,11},{10,... | collective-permute-start | bytes 1179656 | tf_op jit(solution)/shard_map/ppermute | solution.py:1140
  10.2 21.0 %collective-permute-start.2 = (bf16[192,1024]{1,0:T(8,128)(2,1)}, bf16[192,1024]{1,0:T(8,128)(2,1)}, u32[]{:S(2)}, u32[]{:S(2)}) collective-permute-start(bf16[192,1024]{1,0:T(8,128)(2,1)} %broadcast_select_fusion.14), channel_id=1, source_target_pairs={{0,6},{1,7},{2,0},{3,1},{4,2},{5,3},{6,4},{7,5},{8,14},{9,15},{10,... | collective-permute-start | bytes 1179656 | tf_op jit(solution)/shard_map/ppermute | solution.py:1140
  12.2 18.1 %collective-permute-start.5 = (bf16[16,512]{1,0:T(8,128)(2,1)S(1)}, bf16[16,512]{1,0:T(8,128)(2,1)}, u32[]{:S(2)}, u32[]{:S(2)}) collective-permute-start(bf16[16,512]{1,0:T(8,128)(2,1)S(1)} %pad_maximum_fusion.10), channel_id=1, source_target_pairs={{0,2},{1,3},{2,0},{3,1},{4,6},{5,7},{6,4},{7,5},{8,10},{9,11},{10,... | collective-permute-start | bytes 49160 | tf_op jit(solution)/shard_map/ppermute | solution.py:1140
  12.3 36.8 %collective-permute-start.10 = (bf16[512,1536]{1,0:T(8,128)(2,1)}, bf16[512,1536]{1,0:T(8,128)(2,1)}, u32[]{:S(2)}, u32[]{:S(2)}) collective-permute-start(bf16[512,1536]{1,0:T(8,128)(2,1)} %refs_3_), channel_id=1, source_target_pairs={{0,8},{1,9},{2,10},{3,11},{4,12},{5,13},{6,14},{7,15},{8,0},{9,1},... | collective-permute-start | bytes 4718600 | tf_op jit(solution)/shard_map/ppermute | solution.py:1140
  49.1 23.3 %collective-permute-start.13 = (bf16[512,1536]{1,0:T(8,128)(2,1)}, bf16[512,1536]{1,0:T(8,128)(2,1)}, u32[]{:S(2)}, u32[]{:S(2)}) collective-permute-start(bf16[512,1536]{1,0:T(8,128)(2,1)} %refs_3_), channel_id=1, source_target_pairs={{0,1},{1,0},{2,3},{3,2},{4,5},{5,4},{6,7},{7,6},{8,9},{9,8},{10,11... | collective-permute-start | bytes 4718600 | tf_op jit(solution)/shard_map/ppermute | solution.py:1140
  49.1 23.3 %collective-permute-start.14 = (bf16[512,1536]{1,0:T(8,128)(2,1)}, bf16[512,1536]{1,0:T(8,128)(2,1)}, u32[]{:S(2)}, u32[]{:S(2)}) collective-permute-start(bf16[512,1536]{1,0:T(8,128)(2,1)} %collective-permute-done.10.refs_2_), channel_id=1, source_target_pairs={{0,1},{1,0},{2,3},{3,2},{4,5},{5,4},{6,7},{7,6},{8,9},{9,8},{10,11... | collective-permute-start | bytes 4718600 | tf_op jit(solution)/shard_map/ppermute | solution.py:1140
  58.0 36.5 %collective-permute-start.18 = (bf16[192,1536]{1,0:T(8,128)(2,1)S(1)}, bf16[192,1536]{1,0:T(8,128)(2,1)S(1)}, u32[]{:S(2)}, u32[]{:S(2)}) collective-permute-start(bf16[192,1536]{1,0:T(8,128)(2,1)S(1)} %copy-done.122), channel_id=1, source_target_pairs={{0,6},{1,7},{2,0},{3,1},{4,2},{5,3},{6,4},{7,5},{8,14},{9,15},{10,... | collective-permute-start | bytes 1769480 | tf_op jit(solution)/shard_map/ppermute | solution.py:1140
  64.9 29.6 %collective-permute-start.17 = (bf16[192,1536]{1,0:T(8,128)(2,1)S(1)}, bf16[192,1536]{1,0:T(8,128)(2,1)S(1)}, u32[]{:S(2)}, u32[]{:S(2)}) collective-permute-start(bf16[192,1536]{1,0:T(8,128)(2,1)S(1)} %copy-done.122), channel_id=1, source_target_pairs={{0,2},{1,3},{2,4},{3,5},{4,6},{5,7},{6,0},{7,1},{8,10},{9,11},{10,... | collective-permute-start | bytes 1769480 | tf_op jit(solution)/shard_map/ppermute | solution.py:1140
  98.9 20.2 %collective-permute-start.23 = (bf16[512,1536]{1,0:T(8,128)(2,1)S(1)}, bf16[512,1536]{1,0:T(8,128)(2,1)S(1)}, u32[]{:S(2)}, u32[]{:S(2)}) collective-permute-start(bf16[512,1536]{1,0:T(8,128)(2,1)S(1)} %broadcast_select_fusion.refs_6_.refs_1_.refs_0_.refs_4_), channel_id=1, source_target_pairs={{0,1},{1,0},{2,3},{3,2},{4,5},{5,4},{6,7},{7,6},{8,9},{9,8},{10,11... | collective-permute-start | bytes 4718600 | tf_op jit(solution)/shard_map/ppermute | solution.py:1140
  99.1 20.0 %collective-permute-start.22 = (bf16[256,1536]{1,0:T(8,128)(2,1)}, bf16[256,1536]{1,0:T(8,128)(2,1)S(1)}, u32[]{:S(2)}, u32[]{:S(2)}) collective-permute-start(bf16[256,1536]{1,0:T(8,128)(2,1)} %slice.191), channel_id=1, source_target_pairs={{0,8},{1,9},{2,10},{3,11},{4,12},{5,13},{6,14},{7,15},{8,0},{9,1},... | collective-permute-start | bytes 2359304 | tf_op jit(solution)/shard_map/ppermute | solution.py:1140
  202.8 21.3 %collective-permute-start.34 = (bf16[2,512,1536]{2,1,0:T(8,128)(2,1)}, bf16[2,512,1536]{2,1,0:T(8,128)(2,1)}, u32[]{:S(2)}, u32[]{:S(2)}) collective-permute-start(bf16[2,512,1536]{2,1,0:T(8,128)(2,1)} %slice_bitcast_fusion), channel_id=1, source_target_pairs={{0,1},{1,0},{2,3},{3,2},{4,5},{5,4},{6,7},{7,6},{8,9},{9,8},{10,11... | collective-permute-start | bytes 9437192 | tf_op jit(solution)/shard_map/ppermute | solution.py:1140
  226.4 37.2 %collective-permute-start.36 = (bf16[384,512]{1,0:T(8,128)(2,1)S(1)}, bf16[384,512]{1,0:T(8,128)(2,1)S(1)}, u32[]{:S(2)}, u32[]{:S(2)}) collective-permute-start(bf16[384,512]{1,0:T(8,128)(2,1)S(1)} %get-tuple-element.545), channel_id=1, source_target_pairs={{0,2},{1,3},{2,4},{3,5},{4,6},{5,7},{6,0},{7,1},{8,10},{9,11},{10,... | collective-permute-start | bytes 1179656 | tf_op jit(solution)/shard_map/ppermute | solution.py:1140
  228.1 35.5 %collective-permute-start.37 = (bf16[384,512]{1,0:T(8,128)(2,1)S(1)}, bf16[384,512]{1,0:T(8,128)(2,1)S(1)}, u32[]{:S(2)}, u32[]{:S(2)}) collective-permute-start(bf16[384,512]{1,0:T(8,128)(2,1)S(1)} %get-tuple-element.546), channel_id=1, source_target_pairs={{0,4},{1,5},{2,6},{3,7},{4,0},{5,1},{6,2},{7,3},{8,12},{9,13},{10,... | collective-permute-start | bytes 1179656 | tf_op jit(solution)/shard_map/ppermute | solution.py:1140
  228.9 34.8 %collective-permute-start.38 = (bf16[384,512]{1,0:T(8,128)(2,1)S(1)}, bf16[384,512]{1,0:T(8,128)(2,1)S(1)}, u32[]{:S(2)}, u32[]{:S(2)}) collective-permute-start(bf16[384,512]{1,0:T(8,128)(2,1)S(1)} %get-tuple-element.547), channel_id=1, source_target_pairs={{0,6},{1,7},{2,0},{3,1},{4,2},{5,3},{6,4},{7,5},{8,14},{9,15},{10,... | collective-permute-start | bytes 1179656 | tf_op jit(solution)/shard_map/ppermute | solution.py:1140
  231.3 35.9 %collective-permute-start.35 = (bf16[4,192,1024]{2,1,0:T(8,128)(2,1)}, bf16[4,192,1024]{2,1,0:T(8,128)(2,1)S(1)}, u32[]{:S(2)}, u32[]{:S(2)}) collective-permute-start(bf16[4,192,1024]{2,1,0:T(8,128)(2,1)} %get-tuple-element.544), channel_id=1, source_target_pairs={{0,16},{1,17},{2,18},{3,19},{4,20},{5,21},{6,22},{7,23},{8,24},{9,... | collective-permute-start | bytes 4718600 | tf_op jit(solution)/shard_map/ppermute | solution.py:1140
  231.9 35.4 %collective-permute-start.39 = (bf16[512,1536]{1,0:T(8,128)(2,1)S(1)}, bf16[512,1536]{1,0:T(8,128)(2,1)S(1)}, u32[]{:S(2)}, u32[]{:S(2)}) collective-permute-start(bf16[512,1536]{1,0:T(8,128)(2,1)S(1)} %fusion), channel_id=1, source_target_pairs={{0,8},{1,9},{2,10},{3,11},{4,12},{5,13},{6,14},{7,15},{8,0},{9,1},... | collective-permute-start | bytes 4718600 | tf_op jit(solution)/shard_map/ppermute | solution.py:1140
  277.9 22.7 %collective-permute-start.41 = (bf16[192,1024]{1,0:T(8,128)(2,1)S(1)}, bf16[192,1024]{1,0:T(8,128)(2,1)S(1)}, u32[]{:S(2)}, u32[]{:S(2)}) collective-permute-start(bf16[192,1024]{1,0:T(8,128)(2,1)S(1)} %get-tuple-element.576), channel_id=1, source_target_pairs={{0,2},{1,3},{2,4},{3,5},{4,6},{5,7},{6,0},{7,1},{8,10},{9,11},{10,... | collective-permute-start | bytes 1179656 | tf_op jit(solution)/shard_map/ppermute | solution.py:1140
  277.9 22.7 %collective-permute-start.42 = (bf16[192,1024]{1,0:T(8,128)(2,1)S(1)}, bf16[192,1024]{1,0:T(8,128)(2,1)S(1)}, u32[]{:S(2)}, u32[]{:S(2)}) collective-permute-start(bf16[192,1024]{1,0:T(8,128)(2,1)S(1)} %get-tuple-element.577), channel_id=1, source_target_pairs={{0,6},{1,7},{2,0},{3,1},{4,2},{5,3},{6,4},{7,5},{8,14},{9,15},{10,... | collective-permute-start | bytes 1179656 | tf_op jit(solution)/shard_map/ppermute | solution.py:1140
  281.7 18.9 %collective-permute-start.40 = (bf16[4,192,512]{2,1,0:T(8,128)(2,1)S(1)}, bf16[4,192,512]{2,1,0:T(8,128)(2,1)S(1)}, u32[]{:S(2)}, u32[]{:S(2)}) collective-permute-start(bf16[4,192,512]{2,1,0:T(8,128)(2,1)S(1)} %get-tuple-element.575), channel_id=1, source_target_pairs={{0,16},{1,17},{2,18},{3,19},{4,20},{5,21},{6,22},{7,23},{8,24},{9,... | collective-permute-start | bytes 2359304 | tf_op jit(solution)/shard_map/ppermute | solution.py:1140
  342.9 19.8 %collective-permute-start.55 = (bf16[256,1536]{1,0:T(8,128)(2,1)S(1)}, bf16[256,1536]{1,0:T(8,128)(2,1)S(1)}, u32[]{:S(2)}, u32[]{:S(2)}) collective-permute-start(bf16[256,1536]{1,0:T(8,128)(2,1)S(1)} %slice.198), channel_id=1, source_target_pairs={{0,8},{1,9},{2,10},{3,11},{4,12},{5,13},{6,14},{7,15},{8,0},{9,1},... | collective-permute-start | bytes 2359304 | tf_op jit(solution)/shard_map/ppermute | solution.py:1140
  365.0 20.3 %collective-permute-start.57 = (bf16[512,1536]{1,0:T(8,128)(2,1)}, bf16[512,1536]{1,0:T(8,128)(2,1)S(1)}, u32[]{:S(2)}, u32[]{:S(2)}) collective-permute-start(bf16[512,1536]{1,0:T(8,128)(2,1)} %add_convert_fusion.1), channel_id=1, source_target_pairs={{0,1},{1,0},{2,3},{3,2},{4,5},{5,4},{6,7},{7,6},{8,9},{9,8},{10,11... | collective-permute-start | bytes 4718600 | tf_op jit(solution)/shard_map/ppermute | solution.py:1140
  365.1 20.2 %collective-permute-start.56 = (bf16[4,192,512]{2,1,0:T(8,128)(2,1)}, bf16[4,192,512]{2,1,0:T(8,128)(2,1)S(1)}, u32[]{:S(2)}, u32[]{:S(2)}) collective-permute-start(bf16[4,192,512]{2,1,0:T(8,128)(2,1)} %copy-done.88), channel_id=1, source_target_pairs={{0,16},{1,17},{2,18},{3,19},{4,20},{5,21},{6,22},{7,23},{8,24},{9,... | collective-permute-start | bytes 2359304 | tf_op jit(solution)/shard_map/ppermute | solution.py:1140
  388.0 20.4 %collective-permute-start.64 = (bf16[192,2048]{1,0:T(8,128)(2,1)S(1)}, bf16[192,2048]{1,0:T(8,128)(2,1)S(1)}, u32[]{:S(2)}, u32[]{:S(2)}) collective-permute-start(bf16[192,2048]{1,0:T(8,128)(2,1)S(1)} %pad_maximum_fusion.refs_0_), channel_id=1, source_target_pairs={{0,8},{1,9},{2,10},{3,11},{4,12},{5,13},{6,14},{7,15},{8,0},{9,1},... | collective-permute-start | bytes 2359304 | tf_op jit(solution)/shard_map/ppermute | solution.py:1140
  388.9 19.5 %collective-permute-start.65 = (bf16[192,2048]{1,0:T(8,128)(2,1)S(1)}, bf16[192,2048]{1,0:T(8,128)(2,1)S(1)}, u32[]{:S(2)}, u32[]{:S(2)}) collective-permute-start(bf16[192,2048]{1,0:T(8,128)(2,1)S(1)} %pad_maximum_fusion.1), channel_id=1, source_target_pairs={{0,16},{1,17},{2,18},{3,19},{4,20},{5,21},{6,22},{7,23},{8,24},{9,... | collective-permute-start | bytes 2359304 | tf_op jit(solution)/shard_map/ppermute | solution.py:1140
  (206 other events, 1930.4 us)

commit v6 on v5

--- a/solution.py
+++ b/solution.py
@@ -1310,7 +1310,6 @@
     ends = jnp.cumsum(lengths[0])
     positions = jnp.arange(tokens, dtype=jnp.int32)
     is_valid = (positions < ends[1])[:, None]
-    back_own = jnp.where(is_valid, cotangent, jnp.zeros_like(cotangent))
     sides, groups = links.sides, links.groups
     links_shape = (sides, groups)
     place = jnp.stack([links.a, links.g, c]).astype(jnp.int32)
@@ -1370,18 +1369,22 @@
     (from_core_a,), _ = phase([(links.core, for_core_a)])
     pieces_a = {0: links.piece_of(mine_a, from_core_a)}
 
-    def prepare_last(small_in, in_weight, out_weight):
+    half, quarter = tokens // 2, tokens // 4
+    cuts = [slice(0, half), slice(half, half + quarter), slice(half + quarter, tokens)]
+
+    def prepare_last(small_in, in_weight, out_weight, cotangent):
+        back = jnp.where(is_valid, cotangent, jnp.zeros_like(cotangent))
         packed = pack(*small_in)
         small_pair = doubled(packed, 1, links.core(packed))
         small_four = doubled(small_pair, 2, links.flip(small_pair, 0, 2))
         kernel = functools.partial(prepare_last_kernel, width)
         last = prepare_call(kernel, last_columns, core_place, in_weight, out_weight)
-        return small_four, last
-
-    moved, (small_all, (mine_b, for_core_b)) = phase(
+        return small_four, last, back, [back[cut] for cut in cuts]
+
+    moved, (small_all, (mine_b, for_core_b), back_own, back_parts) = phase(
         hop_sends(pieces_a, 1) + [(links.core, lengths)],
         prepare_last,
-        (small_in, in_weight, out_weight.T),
+        (small_in, in_weight, out_weight.T, cotangent),
     )
     lengths_core = moved[-1]
     pieces_a = landed(pieces_a, 1, moved[:-1])
@@ -1436,12 +1439,10 @@
         links_shape, state, kq_index, 2, tokens, F32, place, parts_a, normed
     )
     kq_near = keys_front_call(pair_lengths, kq_in, kq_rows)
-    half, quarter = tokens // 2, tokens // 4
-    cuts = [slice(0, half), slice(half, half + quarter), slice(half + quarter, tokens)]
     moved, (w_values, conv_in), b_firsts = phase(
         [
             (links.side, kq_near),
-            (links.side, back_own[cuts[1]]),
+            (links.side, back_parts[1]),
         ],
         functools.partial(project_call, links_shape, width + LANES, 0, 4, tokens, F32, place),
         (parts_a, normed),
@@ -1462,7 +1463,7 @@
     moved, before = phase(
         hop_sends(pieces_b, 2)
         + rounds(pieces_b[firsts[0]])
-        + [(links.side, back_own[cuts[0]]), (links.core, back_own)],
+        + [(links.side, back_parts[0]), (links.core, back_own)],
         functools.partial(forward_call, heads, size, 0, 2),
         (all_lengths, core_place, conv_in, keys_queries, conv_rows, head_rows),
     )
@@ -1476,7 +1477,7 @@
     rest = [k for k in pieces_b if k and k not in firsts]
     moved, (ssd_out, states, conv_pre) = phase(
         [send for k in firsts[1:] for send in rounds(pieces_b[k])]
-        + [(links.side, back_own[cuts[2]])],
+        + [(links.side, back_parts[2])],
         functools.partial(forward_call, heads, size, 2, 2),
         (all_lengths, core_place, conv_in, keys_queries, conv_rows, head_rows, before),
     )

time: 452 us -> 447 us (0.989)
  starting transfers between devices: 76.5 us -> 67.6 us
    ppermute x76, starting transfers between devices: 76.5 us -> 67.6 us  [send(): return lax.ppermute(value, ('rep', 'fsdp'), pairs)]
    unnamed x308 -> x294, local copies, waits for them, and re-layouts: 29.2 us -> 27.7 us
  transfers between devices with their start and end apart: 76 -> 76, of which waited for: 27 -> 26; matrix products, arithmetic and copies ran while one was open for 8% -> 8% of each run, Pallas kernels for 32% -> 32%
where the time goes in v6:
time: 447 us; the launch traced here: 439 us
  Pallas kernels  179 us (40%)
  waiting for transfers between devices  101 us (23%)
  starting transfers between devices  67.6 us (15%)
  local copies, waits for them, and re-layouts  44.8 us (10%)
  matrix products  22.6 us (5%)
  other arithmetic  21.5 us (5%)
    ppermute x76, waiting for transfers between devices, send(): return lax.ppermute(value, ('rep', 'fsdp'), pairs)  101 us
    ppermute x76, starting transfers between devices, send(): return lax.ppermute(value, ('rep', 'fsdp'), pairs)  67.6 us
    pallas_call x3, Pallas kernels, backward_call(): pl.pallas_call(functools.partial(backward_kernel, heads, size, first_head...  52.8 us
    pallas_call x4, Pallas kernels, weight_grad_call(): pl.pallas_call(functools.partial(weight_grad_kernel, links_shape, shapes,...  33.8 us
    unnamed x294, local copies, waits for them, and re-layouts  27.7 us
    pallas_call x2, Pallas kernels, forward_call(): pl.pallas_call(functools.partial(forward_kernel, heads, size, first_block...  22.9 us
    dot_general x7, matrix products, dot_nt(): lax.dot_general(left, right, (((1,), (1,)), ((), ())), preferred_element_...  22.6 us
    pallas_call x3, Pallas kernels, project_call(): pl.pallas_call(functools.partial(project_kernel, links_shape), grid=(bloc...  20.2 us
  transfers between devices with their start and end apart: 76, of which 26 were waited for; matrix products, arithmetic and copies ran while one was open for 8% of the time, Pallas kernels for 32%

profile of v6, /device:TPU:0, one launch (start us, length us, event | category | flops | bytes accessed | tf_op | source)
XLA Modules:
  0.0 439.3 jit_solution(2554932025580837842)
XLA Ops:
  18.6 12.7 %collective-permute-done.5 = bf16[16,512]{1,0:T(8,128)(2,1)S(1)} collective-permute-done((bf16[16,512]{1,0:T(8,128)(2,1)S(1)}, bf16[16,512]{1,0:T(8,128)(2,1)S(1)}, u32[]{:S(2)}, u32[]{:S(2)}) %collective-permute-start.5) | collective-permute-done | bytes 16416 | tf_op jit(solution)/shard_map/ppermute | solution.py:1140
  36.9 10.6 %collective-permute-done.7 = bf16[32,512]{1,0:T(8,128)(2,1)} collective-permute-done((bf16[32,512]{1,0:T(8,128)(2,1)}, bf16[32,512]{1,0:T(8,128)(2,1)}, u32[]{:S(2)}, u32[]{:S(2)}) %collective-permute-start.7) | collective-permute-done | bytes 32800 | tf_op jit(solution)/shard_map/ppermute | solution.py:1140
  54.6 7.6 %collective-permute-done.11.refs_5_ = bf16[192,1024]{1,0:T(8,128)(2,1)S(1)} collective-permute-done((bf16[192,1024]{1,0:T(8,128)(2,1)}, bf16[192,1024]{1,0:T(8,128)(2,1)S(1)}, u32[]{:S(2)}, u32[]{:S(2)}) %collective-permute-start.11) | collective-permute-done | bytes 393248 | tf_op jit(solution)/shard_map/ppermute | solution.py:1140
  62.2 7.6 %collective-permute-done.12.refs_3_ = bf16[192,1024]{1,0:T(8,128)(2,1)S(1)} collective-permute-done((bf16[192,1024]{1,0:T(8,128)(2,1)}, bf16[192,1024]{1,0:T(8,128)(2,1)S(1)}, u32[]{:S(2)}, u32[]{:S(2)}) %collective-permute-start.12) | collective-permute-done | bytes 393248 | tf_op jit(solution)/shard_map/ppermute | solution.py:1140
  79.9 10.1 %project.4 = (bf16[1536,896]{1,0:T(8,128)(2,1)S(1)}, f32[2048,896]{1,0:T(8,128)}) custom-call(s32[3]{0:T(128)S(1)} %pad_add_fusion.1.at_ref, bf16[192,1024]{1,0:T(8,128)(2,1)S(1)} %get-tuple-element.435.own_ref, bf16[192,1024]{1,0:T(8,128)(2,1)S(1)} %copy-done.41, bf16[192,1024]{1,0:T(8,128)(2,1)} %collective-permute-done.1.refs_0_, ...), custom_call_target="tpu_custom_call" | custom-call | flops 5637144576 | bytes 6291456 | tf_op jit(solution)/shard_map/project/pallas_call | solution.py:451
  99.3 11.5 %ssd_forward.2 = (f32[2048,768]{1,0:T(8,128)S(1)}, bf16[4,3,128,768]{3,2,1,0:T(8,128)(2,1)S(1)}, f32[2048,768]{1,0:T(8,128)}) custom-call(s32[4,2]{1,0:T(4,128)S(1)} %multiply_add_fusion.len_ref, s32[2]{0:T(128)S(1)} %pad_add_fusion.2.at_ref, f32[2048,896]{1,0:T(8,128)} %get-tuple-element.481.u_ref.dt_ref, f32[2048,896]{1,0:T(8,128)} %get-tuple-element.481.u_ref.dt_ref, ...), custom_call_target="tpu_custom_call" | custom-call | flops 6000000000 | bytes 16000000 | tf_op jit(solution)/shard_map/ssd_forward/pallas_call | solution.py:1000
  117.9 11.4 %ssd_forward.3 = (f32[2048,768]{1,0:T(8,128)S(1)}, bf16[4,3,128,768]{3,2,1,0:T(8,128)(2,1)S(1)}, f32[2048,768]{1,0:T(8,128)}) custom-call(s32[4,2]{1,0:T(4,128)S(1)} %multiply_add_fusion.len_ref, s32[2]{0:T(128)S(1)} %pad_add_fusion.2.at_ref, ...), custom_call_target="tpu_custom_call", output_to_operand_aliasing={{0}: (8, {}), {1}: (9, {}), {2}: (10, {})} | custom-call | flops 6000000000 | bytes 16000000 | tf_op jit(solution)/shard_map/ssd_forward/pallas_call | solution.py:1000
  133.0 8.2 %collective-permute-done.26.refs_3_ = bf16[192,768]{1,0:T(8,128)(2,1)S(1)} collective-permute-done((bf16[192,768]{1,0:T(8,128)(2,1)S(1)}, bf16[192,768]{1,0:T(8,128)(2,1)S(1)}, u32[]{:S(2)}, u32[]{:S(2)}) %collective-permute-start.26) | collective-permute-done | bytes 294944 | tf_op jit(solution)/shard_map/ppermute | solution.py:1140
  144.6 7.3 %project.5 = (bf16[1536,768]{1,0:T(8,128)(2,1)S(1)}, f32[2048,768]{1,0:T(8,128)S(1)}) custom-call(s32[3]{0:T(128)S(1)} %pad_add_fusion.1.at_ref, bf16[192,1536]{1,0:T(8,128)(2,1)S(1)} %copy-done.37, bf16[192,1536]{1,0:T(8,128)(2,1)} %collective-permute-done.8.core_ref, bf16[192,1536]{1,0:T(8,128)(2,1)S(1)} %copy-done.56, bf16[192,1536]{1,0:T(8,128)(2,1)S(1)} %copy-done.58, ...), custom_call_target="tpu_custom_call" | custom-call | flops 4831838208 | bytes 6291456 | tf_op jit(solution)/shard_map/project/pallas_call | solution.py:451
  156.8 16.0 %branch_back.1 = (bf16[1536,768]{1,0:T(8,128)(2,1)}, f32[2048,768]{1,0:T(8,128)}, f32[8,2048]{1,0:T(8,128)}) custom-call(s32[3]{0:T(128)} %copy-done.70, bf16[192,1536]{1,0:T(8,128)(2,1)} %copy-done.36, bf16[192,1536]{1,0:T(8,128)(2,1)} %collective-permute-done.8.core_ref, bf16[192,1536]{1,0:T(8,128)(2,1)} %copy-done.55, bf16[192,1536]{1,0:T(8,128)(2,1)} %copy-done.57, ...), custom_call_target="tpu_custom_call" | custom-call | flops 4831838208 | bytes 6291456 | tf_op jit(solution)/shard_map/branch_back/pallas_call | solution.py:513
  179.7 9.2 %gating_back.1 = (bf16[2048,768]{1,0:T(8,128)(2,1)S(1)}, bf16[2048,768]{1,0:T(8,128)(2,1)S(1)}, f32[2048,768]{1,0:T(8,128)S(1)}, f32[8,768]{1,0:T(8,128)S(1)}) custom-call(f32[8,2048]{1,0:T(8,128)S(1)} %copy-done.67, f32[8,2048]{1,0:T(8,128)S(1)} %collective-permute-done.31.core_ref, f32[8,2048]{1,0:T(8,128)S(1)} %collective-permute-done.32.side_ref, ...), custom_call_target="tpu_custom_call" | custom-call | flops 31457280 | bytes 31457280 | tf_op jit(solution)/shard_map/gating_back/pallas_call | solution.py:580
  188.9 5.4 %convolution_convert_fusion = bf16[2048,1536]{1,0:T(8,128)(2,1)S(1)} fusion(bf16[2048,768]{1,0:T(8,128)(2,1)S(1)} %get-tuple-element.540.refs_10_.refs_11_.refs_12_.refs_13_.refs_14_.refs_15_.refs_16_.refs_17_.refs_8_.refs_9_, bf16[1536,768]{1,0:T(8,128)(2,1)S(1)} %copy-done.146), kind=kOutput, calls=%fused_computation | convolution fusion | flops 4834983936 | bytes 11796480 | tf_op jit(solution)/shard_map/dot_general | solution.py:25
  199.5 7.2 %weight_grad.5 = (bf16[384,512]{1,0:T(8,128)(2,1)S(1)}, bf16[384,512]{1,0:T(8,128)(2,1)S(1)}, bf16[384,512]{1,0:T(8,128)(2,1)S(1)}, bf16[384,512]{1,0:T(8,128)(2,1)S(1)}) custom-call(s32[3]{0:T(128)S(1)} %copy-done.71, bf16[512,1536]{1,0:T(8,128)(2,1)} %copy-done.3, bf16[512,1536]{1,0:T(8,128)(2,1)} %copy-done.95, bf16[256,1536]{1,0:T(8,128)(2,1)S(1)} %copy-done.15, ...), custom_call_target="tpu_custom_call" | custom-call | flops 805306368 | bytes 1572864 | tf_op jit(solution)/shard_map/weight_grad/pallas_call | solution.py:708
  206.7 12.8 %weight_grad.4 = (bf16[4,192,1024]{2,1,0:T(8,128)(2,1)S(1)}, bf16[4,192,1024]{2,1,0:T(8,128)(2,1)}) custom-call(s32[3]{0:T(128)S(1)} %copy-done.71, bf16[2048,1536]{1,0:T(8,128)(2,1)} %copy-done.2, bf16[512,1536]{1,0:T(8,128)(2,1)} %copy-done.3, bf16[512,1536]{1,0:T(8,128)(2,1)} %copy-done.95, bf16[256,1536]{1,0:T(8,128)(2,1)S(1)} %copy-done.15, ...), custom_call_target="tpu_custom_call" | custom-call | flops 6442450944 | bytes 6291456 | tf_op jit(solution)/shard_map/weight_grad/pallas_call | solution.py:708
  228.1 31.1 %ssd_backward.3 = (bf16[2048,512]{1,0:T(8,128)(2,1)S(1)}, bf16[2048,128]{1,0:T(8,128)(2,1)S(1)}, f32[2048,128]{1,0:T(8,128)S(1)}, f32[2048,128]{1,0:T(8,128)S(1)...) custom-call(s32[4,2]{1,0:T(4,128)S(1)} %multiply_add_fusion.len_ref, s32[2]{0:T(128)S(1)} %pad_add_fusion.2.at_ref, ...), custom_call_target="tpu_custom_call" | custom-call | flops 32000000000 | bytes 32000000 | tf_op jit(solution)/shard_map/ssd_backward/pallas_call | solution.py:1052
  262.5 6.6 %weight_grad.6 = (bf16[4,192,512]{2,1,0:T(8,128)(2,1)S(1)}, bf16[4,192,512]{2,1,0:T(8,128)(2,1)S(1)}) custom-call(s32[3]{0:T(128)S(1)} %copy-done.71, bf16[2048,1536]{1,0:T(8,128)(2,1)} %copy-done.2, bf16[2048,512]{1,0:T(8,128)(2,1)S(1)} %get-tuple-element.573.refs_1_), custom_call_target="tpu_custom_call" | custom-call | flops 3221225472 | bytes 6291456 | tf_op jit(solution)/shard_map/weight_grad/pallas_call | solution.py:708
  278.1 10.8 %ssd_backward.4 = (bf16[1024,256]{1,0:T(8,128)(2,1)S(1)}, bf16[1024,128]{1,0:T(8,128)(2,1)S(1)}, f32[1024,128]{1,0:T(8,128)S(1)}, bf16[1024,128]{1,0:T(8,128)(2,...) custom-call(s32[4,2]{1,0:T(4,128)S(1)} %multiply_add_fusion.len_ref, s32[2]{0:T(128)S(1)} %pad_add_fusion.2.at_ref, ...), custom_call_target="tpu_custom_call" | custom-call | flops 8000000000 | bytes 16000000 | tf_op jit(solution)/shard_map/ssd_backward/pallas_call | solution.py:1052
  308.2 10.9 %ssd_backward.5 = (bf16[1024,256]{1,0:T(8,128)(2,1)S(1)}, bf16[1024,128]{1,0:T(8,128)(2,1)S(1)}, f32[1024,128]{1,0:T(8,128)S(1)}, bf16[1024,128]{1,0:T(8,128)(2,...) custom-call(s32[4,2]{1,0:T(4,128)S(1)} %multiply_add_fusion.len_ref, s32[2]{0:T(128)S(1)} %pad_add_fusion.2.at_ref, ...), custom_call_target="tpu_custom_call" | custom-call | flops 8000000000 | bytes 16000000 | tf_op jit(solution)/shard_map/ssd_backward/pallas_call | solution.py:1052
  319.2 6.2 %collective-permute-done.46 = bf16[192,1024]{1,0:T(8,128)(2,1)S(1)} collective-permute-done((bf16[192,1024]{1,0:T(8,128)(2,1)S(1)}, bf16[192,1024]{1,0:T(8,128)(2,1)S(1)}, u32[]{:S(2)}, u32[]{:S(2)}) %collective-permute-start.46) | collective-permute-done | bytes 393248 | tf_op jit(solution)/shard_map/ppermute | solution.py:1140
  350.2 7.1 %weight_grad.7 = (bf16[4,192,512]{2,1,0:T(8,128)(2,1)S(1)}, bf16[4,192,512]{2,1,0:T(8,128)(2,1)S(1)}) custom-call(s32[3]{0:T(128)S(1)} %copy-done.71, bf16[2048,1536]{1,0:T(8,128)(2,1)} %copy-done.2, bf16[1024,256]{1,0:T(8,128)(2,1)S(1)} %get-tuple-element.649.refs_1_, bf16[1024,256]{1,0:T(8,128)(2,1)S(1)} %copy-done.61, ...), custom_call_target="tpu_custom_call" | custom-call | flops 1610612736 | bytes 3145728 | tf_op jit(solution)/shard_map/weight_grad/pallas_call | solution.py:708
  369.0 8.0 %collective-permute-done.59 = bf16[192,1024]{1,0:T(8,128)(2,1)S(1)} collective-permute-done((bf16[192,1024]{1,0:T(8,128)(2,1)S(1)}, bf16[192,1024]{1,0:T(8,128)(2,1)S(1)}, u32[]{:S(2)}, u32[]{:S(2)}) %collective-permute-start.59) | collective-permute-done | bytes 393248 | tf_op jit(solution)/shard_map/ppermute | solution.py:1140
  389.4 4.7 %collective-permute-done.66 = f32[8,3328]{1,0:T(8,128)S(1)} collective-permute-done((f32[8,3328]{1,0:T(8,128)S(1)}, f32[8,3328]{1,0:T(8,128)S(1)}, u32[]{:S(2)}, u32[]{:S(2)}) %collective-permute-start.66) | collective-permute-done | bytes 106528 | tf_op jit(solution)/shard_map/ppermute | solution.py:1140
  395.2 4.7 %norm_back.1 = f32[512,1536]{1,0:T(8,128)} custom-call(f32[512,1536]{1,0:T(8,128)S(1)} %slice_add_fusion.keep_ref, bf16[512,1536]{1,0:T(8,128)(2,1)} %collective-permute-done.57.core_ref, bf16[128,1536]{1,0:T(8,128)(2,1)S(1)} %copy-done.83, bf16[128,1536]{1,0:T(8,128)(2,1)S(1)} %copy-done.85, bf16[256,1536]{1,0:T(8,128)(2,1)S(1)} %copy-done.79, ...), custom_call_target="tpu_custom_call" | custom-call | flops 4000000000 | bytes 12000000 | tf_op jit(solution)/shard_map/norm_back/pallas_call | solution.py:811
  429.5 4.9 %owner_gradients.1 = (f32[192,6448]{1,0:T(8,128)}, f32[192,3072]{1,0:T(8,128)}, f32[192,1]{1,0:T(8,128)S(1)}) custom-call(s32[2]{0:T(128)S(1)} %pad_add_fusion.2.at_ref, bf16[192,2048]{1,0:T(8,128)(2,1)S(1)} %pad_maximum_fusion.refs_0_, bf16[192,2048]{1,0:T(8,128)(2,1)S(1)} %copy-done.77, bf16[192,2048]{1,0:T(8,128)(2,1)S(1)} %copy-done.47, ...), custom_call_target="tpu_custom_call" | custom-call | flops 5000000000 | bytes 16000000 | tf_op jit(solution)/shard_map/owner_gradients/pallas_call | solution.py:974
  (539 shorter events, 203.6 us)
Async XLA Ops:
  3.7 45.7 %collective-permute-start.10 = (bf16[512,1536]{1,0:T(8,128)(2,1)}, bf16[512,1536]{1,0:T(8,128)(2,1)}, u32[]{:S(2)}, u32[]{:S(2)}) collective-permute-start(bf16[512,1536]{1,0:T(8,128)(2,1)} %refs_3_), channel_id=1, source_target_pairs={{0,8},{1,9},{2,10},{3,11},{4,12},{5,13},{6,14},{7,15},{8,0},{9,1},... | collective-permute-start | bytes 4718600 | tf_op jit(solution)/shard_map/ppermute | solution.py:1140
  9.6 22.8 %collective-permute-start.1 = (bf16[192,1024]{1,0:T(8,128)(2,1)}, bf16[192,1024]{1,0:T(8,128)(2,1)}, u32[]{:S(2)}, u32[]{:S(2)}) collective-permute-start(bf16[192,1024]{1,0:T(8,128)(2,1)} %broadcast_select_fusion.14), channel_id=1, source_target_pairs={{0,2},{1,3},{2,4},{3,5},{4,6},{5,7},{6,0},{7,1},{8,10},{9,11},{10,... | collective-permute-start | bytes 1179656 | tf_op jit(solution)/shard_map/ppermute | solution.py:1140
  11.2 21.2 %collective-permute-start.2 = (bf16[192,1024]{1,0:T(8,128)(2,1)}, bf16[192,1024]{1,0:T(8,128)(2,1)}, u32[]{:S(2)}, u32[]{:S(2)}) collective-permute-start(bf16[192,1024]{1,0:T(8,128)(2,1)} %broadcast_select_fusion.14), channel_id=1, source_target_pairs={{0,6},{1,7},{2,0},{3,1},{4,2},{5,3},{6,4},{7,5},{8,14},{9,15},{10,... | collective-permute-start | bytes 1179656 | tf_op jit(solution)/shard_map/ppermute | solution.py:1140
  49.4 20.3 %collective-permute-start.13 = (bf16[512,1536]{1,0:T(8,128)(2,1)S(1)}, bf16[512,1536]{1,0:T(8,128)(2,1)S(1)}, u32[]{:S(2)}, u32[]{:S(2)}) collective-permute-start(bf16[512,1536]{1,0:T(8,128)(2,1)S(1)} %copy-done.18), channel_id=1, source_target_pairs={{0,1},{1,0},{2,3},{3,2},{4,5},{5,4},{6,7},{7,6},{8,9},{9,8},{10,11... | collective-permute-start | bytes 4718600 | tf_op jit(solution)/shard_map/ppermute | solution.py:1140
  49.5 20.2 %collective-permute-start.14 = (bf16[512,1536]{1,0:T(8,128)(2,1)}, bf16[512,1536]{1,0:T(8,128)(2,1)S(1)}, u32[]{:S(2)}, u32[]{:S(2)}) collective-permute-start(bf16[512,1536]{1,0:T(8,128)(2,1)} %collective-permute-done.10.refs_2_), channel_id=1, source_target_pairs={{0,1},{1,0},{2,3},{3,2},{4,5},{5,4},{6,7},{7,6},{8,9},{9,8},{10,11... | collective-permute-start | bytes 4718600 | tf_op jit(solution)/shard_map/ppermute | solution.py:1140
  51.2 18.6 %collective-permute-start.12 = (bf16[192,1024]{1,0:T(8,128)(2,1)}, bf16[192,1024]{1,0:T(8,128)(2,1)S(1)}, u32[]{:S(2)}, u32[]{:S(2)}) collective-permute-start(bf16[192,1024]{1,0:T(8,128)(2,1)} %collective-permute-done.6.refs_2_), channel_id=1, source_target_pairs={{0,16},{1,17},{2,18},{3,19},{4,20},{5,21},{6,22},{7,23},{8,24},{9,... | collective-permute-start | bytes 1179656 | tf_op jit(solution)/shard_map/ppermute | solution.py:1140
  54.3 37.2 %collective-permute-start.18 = (bf16[192,1536]{1,0:T(8,128)(2,1)S(1)}, bf16[192,1536]{1,0:T(8,128)(2,1)S(1)}, u32[]{:S(2)}, u32[]{:S(2)}) collective-permute-start(bf16[192,1536]{1,0:T(8,128)(2,1)S(1)} %broadcast_select_fusion.5), channel_id=1, source_target_pairs={{0,6},{1,7},{2,0},{3,1},{4,2},{5,3},{6,4},{7,5},{8,14},{9,15},{10,... | collective-permute-start | bytes 1769480 | tf_op jit(solution)/shard_map/ppermute | solution.py:1140
  62.2 29.3 %collective-permute-start.17 = (bf16[192,1536]{1,0:T(8,128)(2,1)S(1)}, bf16[192,1536]{1,0:T(8,128)(2,1)S(1)}, u32[]{:S(2)}, u32[]{:S(2)}) collective-permute-start(bf16[192,1536]{1,0:T(8,128)(2,1)S(1)} %broadcast_select_fusion.5), channel_id=1, source_target_pairs={{0,2},{1,3},{2,4},{3,5},{4,6},{5,7},{6,0},{7,1},{8,10},{9,11},{10,... | collective-permute-start | bytes 1769480 | tf_op jit(solution)/shard_map/ppermute | solution.py:1140
  95.9 20.2 %collective-permute-start.23 = (bf16[512,1536]{1,0:T(8,128)(2,1)S(1)}, bf16[512,1536]{1,0:T(8,128)(2,1)S(1)}, u32[]{:S(2)}, u32[]{:S(2)}) collective-permute-start(bf16[512,1536]{1,0:T(8,128)(2,1)S(1)} %broadcast_select_fusion.refs_6_.refs_1_.refs_0_.refs_4_), channel_id=1, source_target_pairs={{0,1},{1,0},{2,3},{3,2},{4,5},{5,4},{6,7},{7,6},{8,9},{9,8},{10,11... | collective-permute-start | bytes 4718600 | tf_op jit(solution)/shard_map/ppermute | solution.py:1140
  96.0 20.0 %collective-permute-start.22 = (bf16[256,1536]{1,0:T(8,128)(2,1)}, bf16[256,1536]{1,0:T(8,128)(2,1)S(1)}, u32[]{:S(2)}, u32[]{:S(2)}) collective-permute-start(bf16[256,1536]{1,0:T(8,128)(2,1)} %slice.190), channel_id=1, source_target_pairs={{0,8},{1,9},{2,10},{3,11},{4,12},{5,13},{6,14},{7,15},{8,0},{9,1},... | collective-permute-start | bytes 2359304 | tf_op jit(solution)/shard_map/ppermute | solution.py:1140
  198.4 21.2 %collective-permute-start.34 = (bf16[2,512,1536]{2,1,0:T(8,128)(2,1)}, bf16[2,512,1536]{2,1,0:T(8,128)(2,1)}, u32[]{:S(2)}, u32[]{:S(2)}) collective-permute-start(bf16[2,512,1536]{2,1,0:T(8,128)(2,1)} %slice_bitcast_fusion), channel_id=1, source_target_pairs={{0,1},{1,0},{2,3},{3,2},{4,5},{5,4},{6,7},{7,6},{8,9},{9,8},{10,11... | collective-permute-start | bytes 9437192 | tf_op jit(solution)/shard_map/ppermute | solution.py:1140
  221.9 37.3 %collective-permute-start.36 = (bf16[384,512]{1,0:T(8,128)(2,1)S(1)}, bf16[384,512]{1,0:T(8,128)(2,1)S(1)}, u32[]{:S(2)}, u32[]{:S(2)}) collective-permute-start(bf16[384,512]{1,0:T(8,128)(2,1)S(1)} %get-tuple-element.555), channel_id=1, source_target_pairs={{0,2},{1,3},{2,4},{3,5},{4,6},{5,7},{6,0},{7,1},{8,10},{9,11},{10,... | collective-permute-start | bytes 1179656 | tf_op jit(solution)/shard_map/ppermute | solution.py:1140
  222.3 36.9 %collective-permute-start.37 = (bf16[384,512]{1,0:T(8,128)(2,1)S(1)}, bf16[384,512]{1,0:T(8,128)(2,1)S(1)}, u32[]{:S(2)}, u32[]{:S(2)}) collective-permute-start(bf16[384,512]{1,0:T(8,128)(2,1)S(1)} %get-tuple-element.556), channel_id=1, source_target_pairs={{0,4},{1,5},{2,6},{3,7},{4,0},{5,1},{6,2},{7,3},{8,12},{9,13},{10,... | collective-permute-start | bytes 1179656 | tf_op jit(solution)/shard_map/ppermute | solution.py:1140
  223.2 36.0 %collective-permute-start.38 = (bf16[384,512]{1,0:T(8,128)(2,1)S(1)}, bf16[384,512]{1,0:T(8,128)(2,1)S(1)}, u32[]{:S(2)}, u32[]{:S(2)}) collective-permute-start(bf16[384,512]{1,0:T(8,128)(2,1)S(1)} %get-tuple-element.557), channel_id=1, source_target_pairs={{0,6},{1,7},{2,0},{3,1},{4,2},{5,3},{6,4},{7,5},{8,14},{9,15},{10,... | collective-permute-start | bytes 1179656 | tf_op jit(solution)/shard_map/ppermute | solution.py:1140
  225.8 36.3 %collective-permute-start.35 = (bf16[4,192,1024]{2,1,0:T(8,128)(2,1)}, bf16[4,192,1024]{2,1,0:T(8,128)(2,1)S(1)}, u32[]{:S(2)}, u32[]{:S(2)}) collective-permute-start(bf16[4,192,1024]{2,1,0:T(8,128)(2,1)} %get-tuple-element.554), channel_id=1, source_target_pairs={{0,16},{1,17},{2,18},{3,19},{4,20},{5,21},{6,22},{7,23},{8,24},{9,... | collective-permute-start | bytes 4718600 | tf_op jit(solution)/shard_map/ppermute | solution.py:1140
  226.7 35.8 %collective-permute-start.39 = (bf16[512,1536]{1,0:T(8,128)(2,1)S(1)}, bf16[512,1536]{1,0:T(8,128)(2,1)S(1)}, u32[]{:S(2)}, u32[]{:S(2)}) collective-permute-start(bf16[512,1536]{1,0:T(8,128)(2,1)S(1)} %fusion), channel_id=1, source_target_pairs={{0,8},{1,9},{2,10},{3,11},{4,12},{5,13},{6,14},{7,15},{8,0},{9,1},... | collective-permute-start | bytes 4718600 | tf_op jit(solution)/shard_map/ppermute | solution.py:1140
  273.1 22.4 %collective-permute-start.41 = (bf16[192,1024]{1,0:T(8,128)(2,1)S(1)}, bf16[192,1024]{1,0:T(8,128)(2,1)S(1)}, u32[]{:S(2)}, u32[]{:S(2)}) collective-permute-start(bf16[192,1024]{1,0:T(8,128)(2,1)S(1)} %get-tuple-element.586), channel_id=1, source_target_pairs={{0,2},{1,3},{2,4},{3,5},{4,6},{5,7},{6,0},{7,1},{8,10},{9,11},{10,... | collective-permute-start | bytes 1179656 | tf_op jit(solution)/shard_map/ppermute | solution.py:1140
  273.6 21.8 %collective-permute-start.42 = (bf16[192,1024]{1,0:T(8,128)(2,1)S(1)}, bf16[192,1024]{1,0:T(8,128)(2,1)S(1)}, u32[]{:S(2)}, u32[]{:S(2)}) collective-permute-start(bf16[192,1024]{1,0:T(8,128)(2,1)S(1)} %get-tuple-element.587), channel_id=1, source_target_pairs={{0,6},{1,7},{2,0},{3,1},{4,2},{5,3},{6,4},{7,5},{8,14},{9,15},{10,... | collective-permute-start | bytes 1179656 | tf_op jit(solution)/shard_map/ppermute | solution.py:1140
  276.9 18.6 %collective-permute-start.40 = (bf16[4,192,512]{2,1,0:T(8,128)(2,1)S(1)}, bf16[4,192,512]{2,1,0:T(8,128)(2,1)S(1)}, u32[]{:S(2)}, u32[]{:S(2)}) collective-permute-start(bf16[4,192,512]{2,1,0:T(8,128)(2,1)S(1)} %get-tuple-element.585), channel_id=1, source_target_pairs={{0,16},{1,17},{2,18},{3,19},{4,20},{5,21},{6,22},{7,23},{8,24},{9,... | collective-permute-start | bytes 2359304 | tf_op jit(solution)/shard_map/ppermute | solution.py:1140
  339.0 19.2 %collective-permute-start.55 = (bf16[256,1536]{1,0:T(8,128)(2,1)S(1)}, bf16[256,1536]{1,0:T(8,128)(2,1)S(1)}, u32[]{:S(2)}, u32[]{:S(2)}) collective-permute-start(bf16[256,1536]{1,0:T(8,128)(2,1)S(1)} %slice.198), channel_id=1, source_target_pairs={{0,8},{1,9},{2,10},{3,11},{4,12},{5,13},{6,14},{7,15},{8,0},{9,1},... | collective-permute-start | bytes 2359304 | tf_op jit(solution)/shard_map/ppermute | solution.py:1140
  360.9 20.1 %collective-permute-start.57 = (bf16[512,1536]{1,0:T(8,128)(2,1)}, bf16[512,1536]{1,0:T(8,128)(2,1)}, u32[]{:S(2)}, u32[]{:S(2)}) collective-permute-start(bf16[512,1536]{1,0:T(8,128)(2,1)} %add_convert_fusion.1), channel_id=1, source_target_pairs={{0,1},{1,0},{2,3},{3,2},{4,5},{5,4},{6,7},{7,6},{8,9},{9,8},{10,11... | collective-permute-start | bytes 4718600 | tf_op jit(solution)/shard_map/ppermute | solution.py:1140
  361.0 20.0 %collective-permute-start.56 = (bf16[4,192,512]{2,1,0:T(8,128)(2,1)S(1)}, bf16[4,192,512]{2,1,0:T(8,128)(2,1)S(1)}, u32[]{:S(2)}, u32[]{:S(2)}) collective-permute-start(bf16[4,192,512]{2,1,0:T(8,128)(2,1)S(1)} %get-tuple-element.674), channel_id=1, source_target_pairs={{0,16},{1,17},{2,18},{3,19},{4,20},{5,21},{6,22},{7,23},{8,24},{9,... | collective-permute-start | bytes 2359304 | tf_op jit(solution)/shard_map/ppermute | solution.py:1140
  382.5 20.5 %collective-permute-start.64 = (bf16[192,2048]{1,0:T(8,128)(2,1)S(1)}, bf16[192,2048]{1,0:T(8,128)(2,1)S(1)}, u32[]{:S(2)}, u32[]{:S(2)}) collective-permute-start(bf16[192,2048]{1,0:T(8,128)(2,1)S(1)} %pad_maximum_fusion.refs_0_), channel_id=1, source_target_pairs={{0,8},{1,9},{2,10},{3,11},{4,12},{5,13},{6,14},{7,15},{8,0},{9,1},... | collective-permute-start | bytes 2359304 | tf_op jit(solution)/shard_map/ppermute | solution.py:1140
  383.5 19.5 %collective-permute-start.65 = (bf16[192,2048]{1,0:T(8,128)(2,1)S(1)}, bf16[192,2048]{1,0:T(8,128)(2,1)S(1)}, u32[]{:S(2)}, u32[]{:S(2)}) collective-permute-start(bf16[192,2048]{1,0:T(8,128)(2,1)S(1)} %pad_maximum_fusion.1), channel_id=1, source_target_pairs={{0,16},{1,17},{2,18},{3,19},{4,20},{5,21},{6,22},{7,23},{8,24},{9,... | collective-permute-start | bytes 2359304 | tf_op jit(solution)/shard_map/ppermute | solution.py:1140
  (199 other events, 1973.1 us)
